TPU v7x, 32 devices: a whole 2x2x4 slice. The times are simulated.
32 devices in a mesh: req: 2 (over x), mlp: 16 (over z, y, core).
Axes of the slice: x: 2, y: 2, z: 4, core: 2. Of those that a mesh axis runs over, the one named last changes fastest.
Arguments:
- tokens: bfloat16 [2048, 4096], P(('req', 'mlp')), may hold values from -6 to 6
- layer_norm_gain: float32 [4096], replicated, may hold values from 0.1 to 1.9
- layer_norm_bias: float32 [4096], replicated, may hold values from -2 to 2
- query_key_weight: bfloat16 [4096, 16, 768], P(None, 'mlp')
- output_weight: bfloat16 [16, 256, 4096], P('mlp'), may hold values from -0.09375 to 0.09375
- up_weight: bfloat16 [4096, 8192], P(None, 'mlp'), may hold values from -0.09375 to 0.09375
- input_bias: float32 [8192], P('mlp'), may hold values from -3 to 3
- down_weight: bfloat16 [8192, 4096], P('mlp'), may hold values from -0.0625 to 0.0625
- output_bias: float32 [4096], replicated, may hold values from -2 to 2
- input_adapter_left: bfloat16 [4096, 2048], P(None, 'mlp'), may hold values from -0.09375 to 0.09375
- query_key_value_right: bfloat16 [1024, 16, 768], P(None, 'mlp'), may hold values from -1.5 to 1.5
- up_adapter_right: bfloat16 [1024, 8192], P(None, 'mlp'), may hold values from -1.5 to 1.5
- output_adapter_left: bfloat16 [16, 256, 1024], P('mlp'), may hold values from -0.09375 to 0.09375
- down_adapter_left: bfloat16 [8192, 1024], P('mlp'), may hold values from -0.0625 to 0.0625
- output_adapter_right: bfloat16 [2048, 4096], P('mlp'), may hold values from -1 to 1
- lengths: int32 [65], replicated, may hold values from 8 to 1024, as said below
- request_adapter: int32 [65], replicated, may hold values from 0 to 63
- slot_adapter: int32 [64], P('mlp'), may hold values from 0 to 63, each once
Outputs:
- mixed: bfloat16 [2048, 4096], P(('req', 'mlp'))
Inputs may be any that keep to these rules, and one draw needn't show every extreme that they name: `lengths`: one request holds exactly 1024 tokens, every other one 8 to 24; together they hold 2048 tokens. `slot_adapter`: every adapter id stands in exactly one slot.
All inputs are finite; a program needn't handle non-finite values.
Results may differ from a plain program's by a relative error of at most 0.017.
Values may be sent and summed in bfloat16 or wider, within the bound.
No kernel may reach another device: no remote copies, remote signals or barrier semaphores. Data moves between devices by JAX's collectives and lax.ppermute only.
A program may use at most 128 MiB of HBM per device.

v0:
```python
import functools
import math

import jax
import jax.numpy as jnp
import numpy as np
from jax import lax
from jax.experimental import pallas as pl
from jax.experimental.pallas import tpu as pltpu
from jax.sharding import PartitionSpec as P

HEAD_SIZE = 256
ROT = 64
ADAPTER_RANK = 16
EPSILON = 1e-05
NEGATIVE_FILL = -1e30
RING = (0, 2, 4, 6, 7, 5, 3, 1)
PLACE = tuple(RING.index(pair) for pair in range(8))
CORE_PERM = [(i, i ^ 1) for i in range(16)]
RING_PERM = [(RING[i] * 2, RING[(i + 1) % 8] * 2) for i in range(8)] + [
    (RING[i] * 2 + 1, RING[(i - 1) % 8] * 2 + 1) for i in range(8)
]
SLOTS = 8
BLOCKS = 4
CORE, MLP, PAIRS, BASES = 0, 1, 2, 2 + SLOTS


def to_partner(value):
    return lax.ppermute(value, "mlp", CORE_PERM)


def along_ring(value):
    return lax.ppermute(value, "mlp", RING_PERM)


def rank_product(left_side, right_side):
    return jnp.dot(left_side, right_side, preferred_element_type=jnp.float32)


def across(left_side, right_side):
    return lax.dot_general(
        left_side, right_side, (((1,), (1,)), ((), ())), preferred_element_type=jnp.float32
    )


def spread_table(period, first, width):
    row = np.arange(32)[:, None]
    column = np.arange(width)[None, :]
    return jnp.asarray((row - first == column % period).astype(np.float32), jnp.bfloat16)


def swap_halves(info, lanes):
    half = lanes.shape[1] // 2
    return jnp.where(info[CORE] == 1, pltpu.roll(lanes, half, 1), lanes)


def lane_ids(shape, period):
    return (lax.broadcasted_iota(jnp.int32, shape, 1) // period).astype(jnp.float32)


def pair_at(info, slot, rows):
    return pl.ds(pl.multiple_of(info[PAIRS + slot] * rows, rows), rows)


def store_lanes(info, out_ref, lanes, slot):
    width = out_ref.shape[1] // SLOTS
    for k in range(lanes.shape[1] // width):
        part = lanes[:, k * width : (k + 1) * width]
        out_ref[:, pair_at(info, slot + k, width)] = swap_halves(info, part).astype(out_ref.dtype)


def rank_rows(info, rank_ref, slot, count):
    width = rank_ref.shape[1] // SLOTS
    lanes = [
        swap_halves(info, rank_ref[:, pair_at(info, slot + k, width)].astype(jnp.float32))
        for k in range(count)
    ]
    lanes = lanes[0] if count == 1 else jnp.concatenate(lanes, axis=1)
    return jnp.transpose(lanes).astype(jnp.bfloat16)


def widened(rows, spread_ref, own):
    return jnp.where(own, rank_product(rows, spread_ref[...]), 0.0).astype(jnp.bfloat16)


def cosine(angle):
    turns = jnp.floor(angle * (1.0 / math.pi) + 0.5)
    rest = ((angle - turns * 3.140625) - turns * 9.67502593994140625e-4) - turns * 1.509957990978376e-7
    square = rest * rest
    value = jnp.full_like(square, 1.0 / 479001600.0)
    for factor in (-1.0 / 3628800.0, 1.0 / 40320.0, -1.0 / 720.0, 1.0 / 24.0, -0.5, 1.0):
        value = value * square + factor
    odd = turns - 2.0 * jnp.floor(turns * 0.5)
    return value * (1.0 - 2.0 * odd)


def norm_kernel(x_ref, gain_ref, bias_ref, out_ref):
    values = x_ref[...].astype(jnp.float32)
    center = values - jnp.mean(values, axis=1, keepdims=True)
    spread = jnp.mean(center * center, axis=1, keepdims=True)
    scaled = center * lax.rsqrt(spread + EPSILON)
    out_ref[...] = (scaled * gain_ref[...] + bias_ref[...]).astype(out_ref.dtype)


def local_tokens(info, slot, shape, dim):
    rows = shape[dim] // 2
    at = lax.broadcasted_iota(jnp.int32, shape, dim)
    second = at >= rows
    at = jnp.where(second, at - rows, at) + info[CORE] * (rows // 2)
    at = jnp.where(at >= rows, at - rows, at)
    return (at + jnp.where(second, info[BASES + slot + 1], info[BASES + slot])).astype(jnp.float32)


def token_kernel(info, column_ref, row_ref, ids_ref, table_ref, meta_ref, turn_ref):
    rows = 2 * 128
    count = row_ref.shape[1]
    earlier = lax.broadcasted_iota(jnp.int32, (count, count), 0) < lax.broadcasted_iota(
        jnp.int32, (count, count), 1
    )
    anchors = jnp.sum(jnp.where(earlier, column_ref[...], 0.0), axis=0, keepdims=True)
    endings = anchors + row_ref[...]
    ids = ids_ref[...]
    lane = lax.broadcasted_iota(jnp.int32, (rows, 128), 1)

    def one(block, _):
        token = local_tokens(info, 2 * block, (rows, 1), 0)
        inside = jnp.logical_and(anchors <= token, token < endings)
        start = jnp.sum(jnp.where(inside, anchors, 0.0), axis=1, keepdims=True)
        adapter = jnp.sum(jnp.where(inside, ids, 0.0), axis=1, keepdims=True)
        at = pl.ds(pl.multiple_of(block * rows, rows), rows)
        meta_ref[at, :] = jnp.where(lane < 64, start, adapter)
        angle = (token - start) * table_ref[0:1, :] - table_ref[1:2, :]
        turn_ref[at, :] = cosine(angle) * table_ref[2:3, :]
        return 0

    lax.fori_loop(0, meta_ref.shape[0] // rows, one, 0)


def rank_kernel(count, first_slot, info, *refs):
    x = jnp.concatenate([ref[...] for ref in refs[:count]], axis=0)
    left_ref, meta_ref, slot_ref, fold_ref, held_ref, out_ref = refs[count:]
    products = rank_product(x, left_ref[...])
    adapter = meta_ref[first_slot * 128 : first_slot * 128 + x.shape[0], 64:65]
    chosen = jnp.where(slot_ref[...] == adapter, products, 0.0).astype(jnp.bfloat16)
    out_ref[...] = held_ref[...]
    store_lanes(info, out_ref, across(fold_ref[...], chosen), first_slot)


def base_kernel(count, *refs):
    x = jnp.concatenate([ref[...] for ref in refs[:count]], axis=0)
    qkv_ref, up_ref, base_ref, up_base_ref, shared_ref = refs[count:]
    first = rank_product(x, qkv_ref[...])
    base_ref[...] = first
    shared_ref[...] = first[:, HEAD_SIZE:].astype(shared_ref.dtype)
    up_base_ref[...] = rank_product(x, up_ref[...])


def turn(part, table):
    width = table.shape[1]
    lane = lax.broadcasted_iota(jnp.int32, table.shape, 1)
    cos = jnp.where(lane < ROT, table, 1.0)
    sin = jnp.where(lane < ROT, pltpu.roll(table, width - ROT, 1), 0.0)
    head = part[:, :width]
    swapped = jnp.where(
        lane % 2 == 0, pltpu.roll(head, width - 1, 1), pltpu.roll(head, 1, 1)
    )
    return jnp.concatenate([head * cos + swapped * sin, part[:, width:]], axis=1)


def block_rows_of(refs, block):
    if block:
        return refs[block][...]
    return jnp.concatenate([refs[0][...], refs[4][...]], axis=0)


def inner_kernel(info, *refs):
    base_refs, up_refs, (rank_ref, meta_ref, turn_ref, first_ref, last_ref) = refs[:5], refs[5:10], refs[10:15]
    qkv_right_ref, up_right_ref, bias_ref, left_ref = refs[15:19]
    q_ref, k_ref, v_ref, hidden_ref, out_ref = refs[19:]
    rows = 256
    column_id = lane_ids((rows, first_ref.shape[1]), ADAPTER_RANK)
    for block in range(BLOCKS):
        at = slice(block * rows, (block + 1) * rows)
        own = column_id == meta_ref[at, 64:65]
        ranks = rank_rows(info, rank_ref, 2 * block, 2)
        total = block_rows_of(base_refs, block) + rank_product(
            widened(ranks, first_ref, own), qkv_right_ref[...]
        )
        table = turn_ref[at, :]
        q_ref[at, :] = (turn(total[:, :HEAD_SIZE], table) * HEAD_SIZE ** (-0.5)).astype(jnp.bfloat16)
        k_ref[at, :] = turn(total[:, HEAD_SIZE : 2 * HEAD_SIZE], table).astype(jnp.bfloat16)
        v_ref[at, :] = total[:, 2 * HEAD_SIZE :].astype(jnp.bfloat16)
        x = block_rows_of(up_refs, block) + rank_product(widened(ranks, last_ref, own), up_right_ref[...])
        x = x + bias_ref[...]
        inner = math.sqrt(2.0 / math.pi) * (x + 0.044715 * (x * x * x))
        hidden = (0.5 * x * (1.0 + jnp.tanh(inner))).astype(jnp.bfloat16)
        hidden_ref[at, :] = hidden
        chosen = jnp.where(own, rank_product(hidden, left_ref[...]), 0.0).astype(jnp.bfloat16)
        store_lanes(info, out_ref, across(last_ref[...], chosen), 2 * block)


def far_kernel(first_row, info, *refs):
    shared_refs, (rank_ref, meta_ref, turn_ref, spread_ref, right_ref, k_ref, v_ref) = refs[:5], refs[5:]
    rows = 256
    column_id = lane_ids((rows, spread_ref.shape[1]), ADAPTER_RANK)
    for block in range(BLOCKS):
        at = slice(block * rows, (block + 1) * rows)
        far_at = slice(first_row + block * rows, first_row + (block + 1) * rows)
        own = column_id == meta_ref[far_at, 64:65]
        wide = widened(rank_rows(info, rank_ref, 2 * block, 2), spread_ref, own)
        total = block_rows_of(shared_refs, block).astype(jnp.float32)
        total = total + rank_product(wide, right_ref[:, HEAD_SIZE:])
        k_ref[at, :] = turn(total[:, :HEAD_SIZE], turn_ref[far_at, :]).astype(jnp.bfloat16)
        v_ref[at, :] = total[:, HEAD_SIZE:].astype(jnp.bfloat16)


def attention_kernel(req_count, info, *refs):
    q_ref, refs = refs[0], refs[1:]
    key_refs, value_refs, refs = refs[:req_count], refs[req_count : 2 * req_count], refs[2 * req_count :]
    meta_ref, spread_ref, left_ref, hidden_rank_ref, attended_ref, out_ref = refs[:6]
    top_ref, sum_ref, acc_ref, fold_ref = refs[6:]
    rows = 256
    pair = rows // 2
    column_id = lane_ids((rows, left_ref.shape[1]), ADAPTER_RANK)

    def twice(lanes):
        return jnp.concatenate([lanes] * (HEAD_SIZE // lanes.shape[1]), axis=1)

    def one(block, _):
        at = pl.ds(pl.multiple_of(block * rows, rows), rows)
        start = meta_ref[at, 0:1]
        query = local_tokens(info, 2 * block, (rows, 1), 0)
        q = q_ref[at, :]

        def scores_of(d):
            scores = across(q, key_refs[d][...])
            key = jnp.concatenate(
                [local_tokens(info, d * SLOTS + k, (1, rows), 1) for k in range(0, SLOTS, 2)], axis=1
            )
            allowed = jnp.logical_and(key <= query, key >= start)
            return jnp.where(allowed, scores, NEGATIVE_FILL), allowed

        scores, _ = scores_of(0)
        top = jnp.max(scores, axis=1, keepdims=True)
        weights = jnp.exp(scores - top)
        top_ref[...] = jnp.broadcast_to(top, top_ref.shape)
        sum_ref[...] = jnp.broadcast_to(jnp.sum(weights, axis=1, keepdims=True), sum_ref.shape)
        acc_ref[...] = rank_product(weights.astype(jnp.bfloat16), value_refs[0][...])
        lowest = jnp.min(start)
        for d in range(1, req_count):
            highest = info[BASES + d * SLOTS] + pair
            for k in range(1, SLOTS):
                highest = jnp.maximum(highest, info[BASES + d * SLOTS + k] + pair)

            @pl.when(highest.astype(jnp.float32) > lowest)
            def _(d=d):
                scores, allowed = scores_of(d)
                top = top_ref[...]
                new_top = jnp.maximum(top, jnp.max(scores, axis=1, keepdims=True))
                weights = jnp.where(allowed, jnp.exp(scores - new_top[:, 0:1]), 0.0)
                scale = jnp.exp(top - new_top)
                top_ref[...] = new_top
                sum_ref[...] = sum_ref[...] * scale + jnp.sum(weights, axis=1, keepdims=True)
                acc_ref[...] = acc_ref[...] * twice(scale) + rank_product(
                    weights.astype(jnp.bfloat16), value_refs[d][...]
                )

        attended = (acc_ref[...] / twice(sum_ref[...])).astype(jnp.bfloat16)
        attended_ref[at, :] = attended
        chosen = jnp.where(column_id == meta_ref[at, 64:65], rank_product(attended, left_ref[...]), 0.0)
        store_lanes(info, fold_ref, across(spread_ref[...], chosen.astype(jnp.bfloat16)), 2 * block)
        return 0

    lax.fori_loop(0, BLOCKS, one, 0)
    out_ref[...] = (fold_ref[...] + hidden_rank_ref[...].astype(jnp.float32)).astype(out_ref.dtype)


def main_kernel(block, attended_ref, hidden_ref, output_ref, down_ref, kept_ref, sent_ref):
    rows = 256
    sent = sent_ref.shape[0]
    width = 512
    attended = attended_ref[block * rows : (block + 1) * rows, :]
    hidden = hidden_ref[block * rows : (block + 1) * rows, :]

    def one(step, _):
        at = pl.ds(pl.multiple_of(step * width, width), width)
        total = rank_product(attended, output_ref[:, at]) + rank_product(hidden, down_ref[:, at])
        if block:
            sent_ref[:, at] = total[:sent].astype(sent_ref.dtype)
            kept_ref[:, at] = total[sent:]
        else:
            kept_ref[:, at] = total[: rows - sent]
            sent_ref[:, at] = total[rows - sent :].astype(sent_ref.dtype)
        return 0

    lax.fori_loop(0, output_ref.shape[1] // width, one, 0)


def adapt_kernel(slot, first, info, rank_ref, meta_ref, spread_ref, right_ref, kept_ref, arrived_ref, *out_refs):
    pair = 128
    half = pair // 2
    columns = spread_ref.shape[1]
    count = columns // (4 * ADAPTER_RANK)
    column_id = lax.broadcasted_iota(jnp.int32, (pair, columns), 1) // (2 * ADAPTER_RANK)
    partner = info[MLP] + 1 - 2 * info[CORE]
    column_id = column_id + jnp.where(column_id < count, info[MLP] * count, (partner - 1) * count)
    own = column_id.astype(jnp.float32) == meta_ref[slot * pair : (slot + 1) * pair, 64:65]
    wide = widened(rank_rows(info, rank_ref, slot, 1), spread_ref, own)
    width = 512

    def one(step, _):
        at = pl.ds(pl.multiple_of(step * width, width), width)
        if len(out_refs) == 1:
            total = rank_product(wide[:half], right_ref[:, at]) + kept_ref[first : first + half, at]
            total = total + arrived_ref[:, at].astype(jnp.float32)
            out_refs[0][:, at] = total.astype(out_refs[0].dtype)
        else:
            total = rank_product(wide, right_ref[:, at]) + kept_ref[:, at]
            out_refs[0][:, at] = total[:half] + arrived_ref[half:, at].astype(jnp.float32)
            out_refs[1][:, at] = total[half:] + arrived_ref[:half, at].astype(jnp.float32)
        return 0

    lax.fori_loop(0, right_ref.shape[1] // width, one, 0)


def call(kernel, operands, outs, info=None, scratch=(), mib=24):
    vmem = pl.BlockSpec(memory_space=pltpu.VMEM)
    specs = [vmem] * len(operands)
    if info is not None:
        operands, specs = [info] + operands, [pl.BlockSpec(memory_space=pltpu.SMEM)] + specs
    return pl.pallas_call(
        kernel,
        in_specs=specs,
        out_specs=[vmem] * len(outs),
        out_shape=outs,
        scratch_shapes=scratch,
        compiler_params=pltpu.CompilerParams(vmem_limit_bytes=mib * 1024 * 1024),
        cost_estimate=pl.CostEstimate(flops=1000, bytes_accessed=1000, transcendentals=0),
    )(*operands)


def shape(rows, width, dtype=jnp.bfloat16):
    return jax.ShapeDtypeStruct((rows, width), dtype)


def sum_over_mlp(value, bits):
    for bit in bits:
        value = value + lax.ppermute(value, "mlp", [(i, i ^ bit) for i in range(16)])
    return value


def narrow(value):
    return value.astype(jnp.bfloat16)


def wide(value):
    return value.astype(jnp.float32)


def per_device(
    tokens,
    layer_norm_gain,
    layer_norm_bias,
    query_key_weight,
    output_weight,
    up_weight,
    input_bias,
    down_weight,
    output_bias,
    input_adapter_left,
    query_key_value_right,
    up_adapter_right,
    output_adapter_left,
    down_adapter_left,
    output_adapter_right,
    lengths,
    request_adapter,
    slot_adapter,
):
    block = tokens.shape[0]
    model_width = tokens.shape[1]
    pair_rows = 2 * block
    group_rows = SLOTS * pair_rows
    req_count = lax.axis_size("req")
    group = lax.axis_index("req")
    me = lax.axis_index("mlp")
    block_rows = 2 * pair_rows
    table = np.zeros((req_count, 16, 2 + SLOTS * (1 + req_count)), np.int32)
    for g in range(req_count):
        for m in range(16):
            side = 2 * (m % 2) - 1
            steps = [0, 4] + [t for s in (1, 2, 3) for t in (side * s, -side * s)]
            pairs = [RING[(PLACE[m // 2] + t) % 8] for t in steps]
            firsts = [(g - d) * group_rows + p * pair_rows for d in range(req_count) for p in pairs]
            table[g, m] = [m % 2, m] + pairs + firsts
    info = lax.dynamic_slice(jnp.asarray(table), (group, me, 0), (1, 1, table.shape[2])).reshape(-1)

    own = call(
        norm_kernel,
        [tokens, layer_norm_gain.reshape(1, -1), layer_norm_bias.reshape(1, -1)],
        [shape(block, model_width)],
    )[0]
    other = to_partner(own)
    ring_a, ring_b = along_ring(own), along_ring(other)
    pair_left = jnp.concatenate([input_adapter_left, to_partner(input_adapter_left)], axis=1)

    float_lengths = wide(lengths)
    lane = np.arange(128)
    turn_rows = np.zeros((8, 128), np.float32)
    turn_rows[0] = np.exp(lane % ROT // 2 * (-2.0 * math.log(10000.0) / ROT))
    turn_rows[1] = np.where(lane < ROT, 0.0, math.pi / 2)
    turn_rows[2] = np.where(lane < ROT, 1.0, np.where(lane % 2 == 0, -1.0, 1.0))
    token_rows = req_count * group_rows
    token_args = [
        float_lengths[:, None],
        float_lengths[None, :],
        wide(request_adapter)[None, :],
        jnp.asarray(turn_rows),
    ]
    meta, turns = call(token_kernel, token_args, [shape(token_rows, 128, jnp.float32)] * 2, info)

    qkv_rows = query_key_weight.reshape(model_width, 3 * HEAD_SIZE)
    adapter_columns = query_key_value_right.shape[0]
    qkv_right = query_key_value_right.reshape(adapter_columns, 3 * HEAD_SIZE)
    spread_first = spread_table(ADAPTER_RANK, 0, adapter_columns)
    spread_last = spread_table(ADAPTER_RANK, ADAPTER_RANK, adapter_columns)
    near_right = output_adapter_right
    slot_columns = wide(jnp.repeat(slot_adapter, 2 * ADAPTER_RANK))[None, :]
    slot_columns = jnp.concatenate([slot_columns, to_partner(slot_columns)], axis=1)
    own_columns = near_right.shape[0]
    spread_own = spread_table(2 * ADAPTER_RANK, 0, 2 * own_columns)
    hidden_width = up_weight.shape[1]

    def to_group(value, d):
        return lax.ppermute(value, "req", [(g, g + d) for g in range(req_count - d)])

    held = functools.partial(pltpu.VMEM, dtype=jnp.float32)

    def add_ranks(part, first_slot, so_far):
        return call(
            functools.partial(rank_kernel, len(part), first_slot),
            list(part) + [pair_left, meta, slot_columns, spread_own, so_far],
            [shape(32, group_rows)],
            info,
        )[0]

    def products_of(part):
        rows = len(part) * block
        return call(
            functools.partial(base_kernel, len(part)),
            list(part) + [qkv_rows, up_weight],
            [
                shape(rows, 3 * HEAD_SIZE, jnp.float32),
                shape(rows, hidden_width, jnp.float32),
                shape(rows, 2 * HEAD_SIZE),
            ],
        )

    def to_groups(value):
        return [to_group(value, d) for d in range(1, req_count)]

    def arrivals(a, b):
        return a, b, to_partner(b), to_partner(a)

    tie = lax.optimization_barrier
    own_part = (own, other)
    ring_a, meta, turns = tie((ring_a, meta, turns))
    zeroth = products_of(own_part)
    ring_b, zeroth, pair_left = tie((ring_b, zeroth, pair_left))
    part = arrivals(ring_a, ring_b)
    ring_a, ring_b = along_ring(ring_a), along_ring(ring_b)
    ranks = add_ranks(own_part, 0, jnp.zeros((32, group_rows), jnp.bfloat16))
    ranks = add_ranks(part, 2, ranks)
    first = products_of(part)
    ring_b, ranks, first = tie((ring_b, ranks, first))
    part = arrivals(ring_a, ring_b)
    ring_a, ring_b = along_ring(ring_a), along_ring(ring_b)
    far_right = to_partner(near_right)
    far_early = to_groups(jnp.concatenate([zeroth[2], first[2]], axis=0))
    ranks = add_ranks(part, 4, ranks)
    second = products_of(part)
    ring_b, ranks, second, far_right, far_early = tie((ring_b, ranks, second, far_right, far_early))
    far_middle = to_groups(second[2])
    part = arrivals(ring_a, ring_b)
    ring_a = along_ring(ring_a)
    ranks = add_ranks(part, 6, ranks)
    third = products_of(part)
    ring_a, ranks, third, far_middle = tie((ring_a, ranks, third, far_middle))
    part = (ring_a, to_partner(ring_a))
    ranks = add_ranks(part, 1, ranks)
    moved = lax.ppermute(ranks, "mlp", [(i, i ^ 2) for i in range(16)])
    fourth = products_of(part)
    ranks, fourth = tie((ranks + moved, fourth))
    far_late = to_groups(jnp.concatenate([third[2], fourth[2]], axis=0))
    rank_in = sum_over_mlp(ranks, (4, 8))
    products = (zeroth, first, second, third, fourth)

    bias_row = input_bias.reshape(1, -1)
    far_rank = to_groups(rank_in)
    queries, own_keys, own_values, hidden, hidden_rank = call(
        inner_kernel,
        [part[0] for part in products]
        + [part[1] for part in products]
        + [rank_in, meta, turns, spread_first, spread_last]
        + [qkv_right, up_adapter_right, bias_row, down_adapter_left],
        [shape(group_rows, HEAD_SIZE)] * 3 + [shape(group_rows, hidden_width), shape(32, group_rows)],
        info,
    )
    keys, values = [own_keys], [own_values]
    for d in range(1, req_count):
        early, late = far_early[d - 1], far_late[d - 1]
        shared = [early[:pair_rows], early[pair_rows:], far_middle[d - 1]]
        shared += [late[:block_rows], late[block_rows:]]
        far_keys, far_values = call(
            functools.partial(far_kernel, d * group_rows),
            shared + [far_rank[d - 1], meta, turns, spread_first, qkv_right],
            [shape(group_rows, HEAD_SIZE)] * 2,
            info,
        )
        keys.append(far_keys)
        values.append(far_values)

    output_left = output_adapter_left.reshape(HEAD_SIZE, adapter_columns)
    attended, rank_out = call(
        functools.partial(attention_kernel, req_count),
        [queries] + keys + values + [meta, spread_first, output_left, hidden_rank],
        [shape(group_rows, HEAD_SIZE), shape(32, group_rows)],
        info,
        [
            held((block_rows, 128)),
            held((block_rows, 128)),
            held((block_rows, HEAD_SIZE)),
            held((32, group_rows)),
        ],
    )
    output_rows = output_weight.reshape(HEAD_SIZE, model_width)

    def main(k, attended, hidden):
        sent = block if k == 0 else pair_rows
        return call(
            functools.partial(main_kernel, k),
            [attended, hidden, output_rows, down_weight],
            [shape(block_rows - sent, model_width, jnp.float32), shape(sent, model_width)],
        )

    kept, arrived, before = {}, {}, None
    for bit, k in zip((1, 2, 4, 8), (0, 3, 2, 1)):
        moved = lax.ppermute(rank_out, "mlp", [(i, i ^ bit) for i in range(16)])
        kept[k], sent = main(k, attended, hidden)
        rank_out, attended, sent = tie((rank_out + moved, attended, sent))
        if before is not None:
            rank_out, arrived[before] = tie((rank_out, arrived[before]))
        arrived[k], before = to_partner(sent), k

    pair_right = jnp.concatenate([near_right, far_right], axis=0)

    def adapt(slot, half, kept, first, arrived):
        if half:
            outs = [shape(block, model_width, jnp.bfloat16 if slot else jnp.float32)]
        else:
            outs = [shape(block, model_width, jnp.float32)] * 2
        return call(
            functools.partial(adapt_kernel, slot, first),
            [rank_out, meta, spread_own, pair_right, kept, arrived],
            outs,
            info,
        )

    chain_a = along_ring(adapt(1, True, kept[0], 2 * block, arrived[0])[0])
    chain_b = None
    for s in (3, 2, 1):
        add_a, add_b = adapt(2 * s + 1, False, kept[s], 0, arrived[s])
        if chain_b is None:
            chain_b = along_ring(narrow(add_b))
            chain_a = along_ring(narrow(wide(chain_a) + add_a))
        else:
            chain_a = along_ring(narrow(wide(chain_a) + add_a))
            chain_b = along_ring(narrow(wide(chain_b) + add_b))
    arrived = to_partner(narrow(wide(chain_b) + kept[0][block : 2 * block]))
    total = adapt(0, True, kept[0], 0, chain_a)[0] + wide(arrived)
    return narrow(total + wide(tokens) + output_bias)


def solution(mesh):
    in_specs = (
        P(("req", "mlp"), None),
        P(),
        P(),
        P(None, "mlp", None),
        P("mlp", None, None),
        P(None, "mlp"),
        P("mlp"),
        P("mlp", None),
        P(),
        P(None, "mlp"),
        P(None, "mlp", None),
        P(None, "mlp"),
        P("mlp", None, None),
        P("mlp", None),
        P("mlp", None),
        P(),
        P(),
        P("mlp"),
    )
    out_specs = P(("req", "mlp"), None)
    return jax.shard_map(
        per_device, mesh=mesh, in_specs=in_specs, out_specs=out_specs, check_vma=False
    )
```

profile of v0, /device:TPU:0, one launch (start us, length us, event | category | flops | bytes accessed | tf_op | source)
XLA Modules:
  0.0 172.2 jit_solution(922083121928360898)
XLA Ops:
  3.6 3.0 %collective-permute-start.4 = (bf16[64,4096]{1,0:T(8,128)(2,1)S(1)}, bf16[64,4096]{1,0:T(8,128)(2,1)S(1)}, u32[]{:S(2)}, u32[]{:S(2)}) collective-permute-start(bf16[64,4096]{1,0:T(8,128)(2,1)S(1)} %shard_map.217.refs_0_), channel_id=1, source_target_pairs={{0,4},{4,8},{8,12},{12,14},{14,10},{10,6},{6,2},{2,0},{1,3},{5,1},... | collective-permute-start | bytes 1572872 | tf_op jit(solution)/shard_map/ppermute | solution.py:33
  15.8 2.8 %copy-done = bf16[4096,1,768]{2,0,1:T(8,128)(2,1)S(1)} copy-done((bf16[4096,1,768]{2,0,1:T(8,128)(2,1)S(1)}, bf16[4096,1,768]{2,0,1:T(8,128)(2,1)}, u32[]{:S(2)}) %copy-start) | copy-done | bytes 6291480
  20.8 2.7 %shard_map.218 = (f32[128,768]{1,0:T(8,128)S(1)}, f32[128,512]{1,0:T(8,128)S(1)}, bf16[128,512]{1,0:T(8,128)(2,1)S(1)}) custom-call(bf16[64,4096]{1,0:T(8,128)(2,1)S(1)} %shard_map.217.refs_0_, bf16[64,4096]{1,0:T(8,128)(2,1)} %collective-permute-done.refs_1_, bf16[4096,768]{1,0:T(8,128)(2,1)S(1)} %bitcast.15, bf16[4096,512]{1,0:T(8,128)(2,1)S(1)} %copy-done.2), custom_call_target="tpu_custom_call" | custom-call | flops 1000 | bytes 1000 | tf_op jit(solution)/shard_map/pallas_call | solution.py:331
  31.0 3.9 %shard_map.222 = (f32[256,768]{1,0:T(8,128)S(1)}, f32[256,512]{1,0:T(8,128)S(1)}, bf16[256,512]{1,0:T(8,128)(2,1)S(1)}) custom-call(bf16[64,4096]{1,0:T(8,128)(2,1)S(1)} %collective-permute-done.4.refs_0_, bf16[64,4096]{1,0:T(8,128)(2,1)} %collective-permute-done.1.refs_1_, bf16[64,4096]{1,0:T(8,128)(2,1)S(1)} %collective-permute-done.5.refs_2_, ...), custom_call_target="tpu_custom_call" | custom-call | flops 1000 | bytes 1000 | tf_op jit(solution)/shard_map/pallas_call | solution.py:331
  40.8 3.4 %collective-permute-start.13 = (bf16[384,512]{1,0:T(8,128)(2,1)S(1)}, bf16[384,512]{1,0:T(8,128)(2,1)S(1)}, u32[]{:S(2)}, u32[]{:S(2)}) collective-permute-start(bf16[384,512]{1,0:T(8,128)(2,1)S(1)} %pad_maximum_fusion.1), channel_id=1, source_target_pairs={{0,16},{1,17},{2,18},{3,19},{4,20},{5,21},{6,22},{7,23},{8,24},{9,... | collective-permute-start | bytes 1179656 | tf_op jit(solution)/shard_map/ppermute | solution.py:435
  44.3 2.9 %shard_map.224 = (f32[256,768]{1,0:T(8,128)S(1)}, f32[256,512]{1,0:T(8,128)S(1)}, bf16[256,512]{1,0:T(8,128)(2,1)S(1)}) custom-call(bf16[64,4096]{1,0:T(8,128)(2,1)S(1)} %collective-permute-done.9.refs_0_, bf16[64,4096]{1,0:T(8,128)(2,1)S(1)} %collective-permute-done.3.refs_1_, bf16[64,4096]{1,0:T(8,128)(2,1)S(1)} %collective-permute-done.10.refs_2_, ...), custom_call_target="tpu_custom_call" | custom-call | flops 1000 | bytes 1000 | tf_op jit(solution)/shard_map/pallas_call | solution.py:331
  48.7 3.6 %collective-permute-done.13 = bf16[384,512]{1,0:T(8,128)(2,1)S(1)} collective-permute-done((bf16[384,512]{1,0:T(8,128)(2,1)S(1)}, bf16[384,512]{1,0:T(8,128)(2,1)S(1)}, u32[]{:S(2)}, u32[]{:S(2)}) %collective-permute-start.13) | collective-permute-done | bytes 393248 | tf_op jit(solution)/shard_map/ppermute | solution.py:435
  53.9 4.6 %collective-permute-start.18 = (bf16[256,512]{1,0:T(8,128)(2,1)S(1)}, bf16[256,512]{1,0:T(8,128)(2,1)S(1)}, u32[]{:S(2)}, u32[]{:S(2)}) collective-permute-start(bf16[256,512]{1,0:T(8,128)(2,1)S(1)} %get-tuple-element.119), channel_id=1, source_target_pairs={{0,16},{1,17},{2,18},{3,19},{4,20},{5,21},{6,22},{7,23},{8,24},{9,... | collective-permute-start | bytes 786440 | tf_op jit(solution)/shard_map/ppermute | solution.py:435
  58.5 2.9 %shard_map.226 = (f32[256,768]{1,0:T(8,128)S(1)}, f32[256,512]{1,0:T(8,128)S(1)}, bf16[256,512]{1,0:T(8,128)(2,1)S(1)}) custom-call(bf16[64,4096]{1,0:T(8,128)(2,1)S(1)} %collective-permute-done.14.refs_0_, bf16[64,4096]{1,0:T(8,128)(2,1)S(1)} %collective-permute-done.8.refs_1_, bf16[64,4096]{1,0:T(8,128)(2,1)S(1)} %collective-permute-done.16.refs_2_, ...), custom_call_target="tpu_custom_call" | custom-call | flops 1000 | bytes 1000 | tf_op jit(solution)/shard_map/pallas_call | solution.py:331
  70.5 4.4 %collective-permute-start.23 = (bf16[384,512]{1,0:T(8,128)(2,1)S(1)}, bf16[384,512]{1,0:T(8,128)(2,1)S(1)}, u32[]{:S(2)}, u32[]{:S(2)}) collective-permute-start(bf16[384,512]{1,0:T(8,128)(2,1)S(1)} %pad_maximum_fusion.2), channel_id=1, source_target_pairs={{0,16},{1,17},{2,18},{3,19},{4,20},{5,21},{6,22},{7,23},{8,24},{9,... | collective-permute-start | bytes 1179656 | tf_op jit(solution)/shard_map/ppermute | solution.py:435
  76.6 2.7 %collective-permute-done.21 = bf16[32,1024]{1,0:T(8,128)(2,1)S(1)} collective-permute-done((bf16[32,1024]{1,0:T(8,128)(2,1)S(1)}, bf16[32,1024]{1,0:T(8,128)(2,1)S(1)}, u32[]{:S(2)}, u32[]{:S(2)}) %collective-permute-start.21) | collective-permute-done | bytes 65568 | tf_op jit(solution)/shard_map/ppermute | solution.py:348
  86.0 7.2 %shard_map.229 = (bf16[1024,256]{1,0:T(8,128)(2,1)S(1)}, bf16[1024,256]{1,0:T(8,128)(2,1)S(1)}, bf16[1024,256]{1,0:T(8,128)(2,1)S(1)}, bf16[1024,512]{1,0:T(8,128)(2,1)S(1)}, bf16[32,1024]{1,0:T(8,128)(2,1)S(1)}) custom-call(s32[26]{0:T(128)S(1)} %dynamic-slice_bitcast_fusion.info, f32[128,768]{1,0:T(8,128)S(1)} %get-tuple-element.95.refs_0_, ...), custom_call_target="tpu_custom_call" | custom-call | flops 1000 | bytes 1000 | tf_op jit(solution)/shard_map/pallas_call | solution.py:331
  96.0 7.0 %shard_map.231 = (bf16[1024,256]{1,0:T(8,128)(2,1)S(1)}, bf16[32,1024]{1,0:T(8,128)(2,1)S(1)}) custom-call(s32[26]{0:T(128)S(1)} %dynamic-slice_bitcast_fusion.info, bf16[1024,256]{1,0:T(8,128)(2,1)S(1)} %get-tuple-element.134.refs_0_, bf16[1024,256]{1,0:T(8,128)(2,1)S(1)} %get-tuple-element.135.refs_1_, bf16[1024,256]{1,0:T(8,128)(2,1)S(1)} %get-tuple-element.140.refs_2_, ...), custom_call_target="tpu_custom_call" | custom-call | flops 1000 | bytes 1000 | tf_op jit(solution)/shard_map/pallas_call | solution.py:331
  103.1 3.1 %shard_map.232 = (f32[192,4096]{1,0:T(8,128)S(1)}, bf16[64,4096]{1,0:T(8,128)(2,1)S(1)}) custom-call(bf16[1024,256]{1,0:T(8,128)(2,1)S(1)} %get-tuple-element.159.attended_ref, bf16[1024,512]{1,0:T(8,128)(2,1)S(1)} %get-tuple-element.146.hidden_ref, bf16[256,4096]{1,0:T(8,128)(2,1)S(1)} %bitcast.20, bf16[512,4096]{1,0:T(8,128)(2,1)S(1)} %copy-done.4), custom_call_target="tpu_custom_call" | custom-call | flops 1000 | bytes 1000 | tf_op jit(solution)/shard_map/pallas_call | solution.py:331
  109.0 3.1 %shard_map.233 = (f32[128,4096]{1,0:T(8,128)S(1)}, bf16[128,4096]{1,0:T(8,128)(2,1)S(1)}) custom-call(bf16[1024,256]{1,0:T(8,128)(2,1)S(1)} %get-tuple-element.159.attended_ref, bf16[1024,512]{1,0:T(8,128)(2,1)S(1)} %get-tuple-element.146.hidden_ref, bf16[256,4096]{1,0:T(8,128)(2,1)S(1)} %bitcast.21, bf16[512,4096]{1,0:T(8,128)(2,1)S(1)} %copy-done.4), custom_call_target="tpu_custom_call" | custom-call | flops 1000 | bytes 1000 | tf_op jit(solution)/shard_map/pallas_call | solution.py:331
  112.8 3.1 %shard_map.234 = (f32[128,4096]{1,0:T(8,128)S(1)}, bf16[128,4096]{1,0:T(8,128)(2,1)S(1)}) custom-call(bf16[1024,256]{1,0:T(8,128)(2,1)S(1)} %get-tuple-element.159.attended_ref, bf16[1024,512]{1,0:T(8,128)(2,1)S(1)} %get-tuple-element.146.hidden_ref, bf16[256,4096]{1,0:T(8,128)(2,1)S(1)} %bitcast.22, bf16[512,4096]{1,0:T(8,128)(2,1)S(1)} %copy-done.4), custom_call_target="tpu_custom_call" | custom-call | flops 1000 | bytes 1000 | tf_op jit(solution)/shard_map/pallas_call | solution.py:331
  119.5 3.1 %shard_map.235 = (f32[128,4096]{1,0:T(8,128)S(1)}, bf16[128,4096]{1,0:T(8,128)(2,1)S(1)}) custom-call(bf16[1024,256]{1,0:T(8,128)(2,1)S(1)} %get-tuple-element.159.attended_ref, bf16[1024,512]{1,0:T(8,128)(2,1)S(1)} %get-tuple-element.146.hidden_ref, bf16[256,4096]{1,0:T(8,128)(2,1)S(1)} %bitcast.23, bf16[512,4096]{1,0:T(8,128)(2,1)S(1)} %copy-done.4), custom_call_target="tpu_custom_call" | custom-call | flops 1000 | bytes 1000 | tf_op jit(solution)/shard_map/pallas_call | solution.py:331
  132.6 2.7 %collective-permute-done.32 = bf16[64,4096]{1,0:T(8,128)(2,1)S(1)} collective-permute-done((bf16[64,4096]{1,0:T(8,128)(2,1)S(1)}, bf16[64,4096]{1,0:T(8,128)(2,1)S(1)}, u32[]{:S(2)}, u32[]{:S(2)}) %collective-permute-start.32) | collective-permute-done | bytes 524320 | tf_op jit(solution)/shard_map/ppermute | solution.py:33
  135.7 5.1 %collective-permute-done.37 = bf16[64,4096]{1,0:T(8,128)(2,1)S(1)} collective-permute-done((bf16[64,4096]{1,0:T(8,128)(2,1)S(1)}, bf16[64,4096]{1,0:T(8,128)(2,1)S(1)}, u32[]{:S(2)}, u32[]{:S(2)}) %collective-permute-start.37) | collective-permute-done | bytes 524320 | tf_op jit(solution)/shard_map/ppermute | solution.py:33
  143.8 2.7 %collective-permute-done.33 = bf16[64,4096]{1,0:T(8,128)(2,1)S(1)} collective-permute-done((bf16[64,4096]{1,0:T(8,128)(2,1)S(1)}, bf16[64,4096]{1,0:T(8,128)(2,1)S(1)}, u32[]{:S(2)}, u32[]{:S(2)}) %collective-permute-start.33) | collective-permute-done | bytes 524320 | tf_op jit(solution)/shard_map/ppermute | solution.py:33
  147.0 5.1 %collective-permute-done.38 = bf16[64,4096]{1,0:T(8,128)(2,1)S(1)} collective-permute-done((bf16[64,4096]{1,0:T(8,128)(2,1)S(1)}, bf16[64,4096]{1,0:T(8,128)(2,1)S(1)}, u32[]{:S(2)}, u32[]{:S(2)}) %collective-permute-start.38) | collective-permute-done | bytes 524320 | tf_op jit(solution)/shard_map/ppermute | solution.py:33
  152.6 5.1 %collective-permute-done.34 = bf16[64,4096]{1,0:T(8,128)(2,1)S(1)} collective-permute-done((bf16[64,4096]{1,0:T(8,128)(2,1)S(1)}, bf16[64,4096]{1,0:T(8,128)(2,1)S(1)}, u32[]{:S(2)}, u32[]{:S(2)}) %collective-permute-start.34) | collective-permute-done | bytes 524320 | tf_op jit(solution)/shard_map/ppermute | solution.py:33
  158.2 5.1 %collective-permute-done.39 = bf16[64,4096]{1,0:T(8,128)(2,1)S(1)} collective-permute-done((bf16[64,4096]{1,0:T(8,128)(2,1)S(1)}, bf16[64,4096]{1,0:T(8,128)(2,1)S(1)}, u32[]{:S(2)}, u32[]{:S(2)}) %collective-permute-start.39) | collective-permute-done | bytes 524320 | tf_op jit(solution)/shard_map/ppermute | solution.py:33
  163.5 5.4 %collective-permute-done.36.arrived_ref = bf16[64,4096]{1,0:T(8,128)(2,1)S(1)} collective-permute-done((bf16[64,4096]{1,0:T(8,128)(2,1)S(1)}, bf16[64,4096]{1,0:T(8,128)(2,1)S(1)}, u32[]{:S(2)}, u32[]{:S(2)}) %collective-permute-start.36) | collective-permute-done | bytes 524320 | tf_op jit(solution)/shard_map/ppermute | solution.py:33
  (159 shorter events, 76.8 us)
Async XLA Ops:
  0.0 23.5 %collective-permute-start.2 = (bf16[4096,128]{1,0:T(8,128)(2,1)}, bf16[4096,128]{1,0:T(8,128)(2,1)}, u32[]{:S(2)}, u32[]{:S(2)}) collective-permute-start(bf16[4096,128]{1,0:T(8,128)(2,1)} %param.32), channel_id=1, source_target_pairs={{0,1},{1,0},{2,3},{3,2},{4,5},{5,4},{6,7},{7,6},{8,9},{9,8},{10,11... | collective-permute-start | bytes 3145736 | tf_op jit(solution)/shard_map/ppermute | solution.py:29
  3.6 10.1 %collective-permute-start.4 = (bf16[64,4096]{1,0:T(8,128)(2,1)S(1)}, bf16[64,4096]{1,0:T(8,128)(2,1)S(1)}, u32[]{:S(2)}, u32[]{:S(2)}) collective-permute-start(bf16[64,4096]{1,0:T(8,128)(2,1)S(1)} %shard_map.217.refs_0_), channel_id=1, source_target_pairs={{0,4},{4,8},{8,12},{12,14},{14,10},{10,6},{6,2},{2,0},{1,3},{5,1},... | collective-permute-start | bytes 1572872 | tf_op jit(solution)/shard_map/ppermute | solution.py:33
  7.3 17.9 %collective-permute-start.1 = (bf16[64,4096]{1,0:T(8,128)(2,1)}, bf16[64,4096]{1,0:T(8,128)(2,1)}, u32[]{:S(2)}, u32[]{:S(2)}) collective-permute-start(bf16[64,4096]{1,0:T(8,128)(2,1)} %collective-permute-done.refs_1_), channel_id=1, source_target_pairs={{0,4},{4,8},{8,12},{12,14},{14,10},{10,6},{6,2},{2,0},{1,3},{5,1},... | collective-permute-start | bytes 1572872 | tf_op jit(solution)/shard_map/ppermute | solution.py:33
  13.7 13.9 %collective-permute-start.9 = (bf16[64,4096]{1,0:T(8,128)(2,1)S(1)}, bf16[64,4096]{1,0:T(8,128)(2,1)S(1)}, u32[]{:S(2)}, u32[]{:S(2)}) collective-permute-start(bf16[64,4096]{1,0:T(8,128)(2,1)S(1)} %collective-permute-done.4.refs_0_), channel_id=1, source_target_pairs={{0,4},{4,8},{8,12},{12,14},{14,10},{10,6},{6,2},{2,0},{1,3},{5,1},... | collective-permute-start | bytes 1572872 | tf_op jit(solution)/shard_map/ppermute | solution.py:33
  15.8 15.1 %collective-permute-start.6 = (bf16[64,4096]{1,0:T(8,128)(2,1)S(1)}, bf16[64,4096]{1,0:T(8,128)(2,1)S(1)}, u32[]{:S(2)}, u32[]{:S(2)}) collective-permute-start(bf16[64,4096]{1,0:T(8,128)(2,1)S(1)} %collective-permute-done.4.refs_0_), channel_id=1, source_target_pairs={{0,1},{1,0},{2,3},{3,2},{4,5},{5,4},{6,7},{7,6},{8,9},{9,8},{10,11... | collective-permute-start | bytes 1572872 | tf_op jit(solution)/shard_map/ppermute | solution.py:29
  25.8 11.1 %collective-permute-start.3 = (bf16[64,4096]{1,0:T(8,128)(2,1)}, bf16[64,4096]{1,0:T(8,128)(2,1)S(1)}, u32[]{:S(2)}, u32[]{:S(2)}) collective-permute-start(bf16[64,4096]{1,0:T(8,128)(2,1)} %collective-permute-done.1.refs_1_), channel_id=1, source_target_pairs={{0,4},{4,8},{8,12},{12,14},{14,10},{10,6},{6,2},{2,0},{1,3},{5,1},... | collective-permute-start | bytes 1572872 | tf_op jit(solution)/shard_map/ppermute | solution.py:33
  27.4 21.3 %collective-permute-start.12 = (bf16[128,4096]{1,0:T(8,128)(2,1)S(1)}, bf16[128,4096]{1,0:T(8,128)(2,1)S(1)}, u32[]{:S(2)}, u32[]{:S(2)}) collective-permute-start(bf16[128,4096]{1,0:T(8,128)(2,1)S(1)} %copy-done.19), channel_id=1, source_target_pairs={{0,1},{1,0},{2,3},{3,2},{4,5},{5,4},{6,7},{7,6},{8,9},{9,8},{10,11... | collective-permute-start | bytes 3145736 | tf_op jit(solution)/shard_map/ppermute | solution.py:29
  27.6 13.2 %collective-permute-start.14 = (bf16[64,4096]{1,0:T(8,128)(2,1)S(1)}, bf16[64,4096]{1,0:T(8,128)(2,1)S(1)}, u32[]{:S(2)}, u32[]{:S(2)}) collective-permute-start(bf16[64,4096]{1,0:T(8,128)(2,1)S(1)} %collective-permute-done.9.refs_0_), channel_id=1, source_target_pairs={{0,4},{4,8},{8,12},{12,14},{14,10},{10,6},{6,2},{2,0},{1,3},{5,1},... | collective-permute-start | bytes 1572872 | tf_op jit(solution)/shard_map/ppermute | solution.py:33
  30.9 13.3 %collective-permute-start.11 = (bf16[64,4096]{1,0:T(8,128)(2,1)S(1)}, bf16[64,4096]{1,0:T(8,128)(2,1)S(1)}, u32[]{:S(2)}, u32[]{:S(2)}) collective-permute-start(bf16[64,4096]{1,0:T(8,128)(2,1)S(1)} %collective-permute-done.9.refs_0_), channel_id=1, source_target_pairs={{0,1},{1,0},{2,3},{3,2},{4,5},{5,4},{6,7},{7,6},{8,9},{9,8},{10,11... | collective-permute-start | bytes 1572872 | tf_op jit(solution)/shard_map/ppermute | solution.py:29
  37.5 14.9 %collective-permute-start.8 = (bf16[64,4096]{1,0:T(8,128)(2,1)S(1)}, bf16[64,4096]{1,0:T(8,128)(2,1)S(1)}, u32[]{:S(2)}, u32[]{:S(2)}) collective-permute-start(bf16[64,4096]{1,0:T(8,128)(2,1)S(1)} %collective-permute-done.3.refs_1_), channel_id=1, source_target_pairs={{0,4},{4,8},{8,12},{12,14},{14,10},{10,6},{6,2},{2,0},{1,3},{5,1},... | collective-permute-start | bytes 1572872 | tf_op jit(solution)/shard_map/ppermute | solution.py:33
  40.8 11.5 %collective-permute-start.13 = (bf16[384,512]{1,0:T(8,128)(2,1)S(1)}, bf16[384,512]{1,0:T(8,128)(2,1)S(1)}, u32[]{:S(2)}, u32[]{:S(2)}) collective-permute-start(bf16[384,512]{1,0:T(8,128)(2,1)S(1)} %pad_maximum_fusion.1), channel_id=1, source_target_pairs={{0,16},{1,17},{2,18},{3,19},{4,20},{5,21},{6,22},{7,23},{8,24},{9,... | collective-permute-start | bytes 1179656 | tf_op jit(solution)/shard_map/ppermute | solution.py:435
  44.2 14.2 %collective-permute-start.17 = (bf16[64,4096]{1,0:T(8,128)(2,1)S(1)}, bf16[64,4096]{1,0:T(8,128)(2,1)S(1)}, u32[]{:S(2)}, u32[]{:S(2)}) collective-permute-start(bf16[64,4096]{1,0:T(8,128)(2,1)S(1)} %collective-permute-done.14.refs_0_), channel_id=1, source_target_pairs={{0,1},{1,0},{2,3},{3,2},{4,5},{5,4},{6,7},{7,6},{8,9},{9,8},{10,11... | collective-permute-start | bytes 1572872 | tf_op jit(solution)/shard_map/ppermute | solution.py:29
  52.3 10.5 %collective-permute-start.15 = (bf16[64,4096]{1,0:T(8,128)(2,1)S(1)}, bf16[64,4096]{1,0:T(8,128)(2,1)S(1)}, u32[]{:S(2)}, u32[]{:S(2)}) collective-permute-start(bf16[64,4096]{1,0:T(8,128)(2,1)S(1)} %collective-permute-done.14.refs_0_), channel_id=1, source_target_pairs={{0,4},{4,8},{8,12},{12,14},{14,10},{10,6},{6,2},{2,0},{1,3},{5,1},... | collective-permute-start | bytes 1572872 | tf_op jit(solution)/shard_map/ppermute | solution.py:33
  53.9 9.2 %collective-permute-start.18 = (bf16[256,512]{1,0:T(8,128)(2,1)S(1)}, bf16[256,512]{1,0:T(8,128)(2,1)S(1)}, u32[]{:S(2)}, u32[]{:S(2)}) collective-permute-start(bf16[256,512]{1,0:T(8,128)(2,1)S(1)} %get-tuple-element.119), channel_id=1, source_target_pairs={{0,16},{1,17},{2,18},{3,19},{4,20},{5,21},{6,22},{7,23},{8,24},{9,... | collective-permute-start | bytes 786440 | tf_op jit(solution)/shard_map/ppermute | solution.py:435
  70.5 22.7 %collective-permute-start.23 = (bf16[384,512]{1,0:T(8,128)(2,1)S(1)}, bf16[384,512]{1,0:T(8,128)(2,1)S(1)}, u32[]{:S(2)}, u32[]{:S(2)}) collective-permute-start(bf16[384,512]{1,0:T(8,128)(2,1)S(1)} %pad_maximum_fusion.2), channel_id=1, source_target_pairs={{0,16},{1,17},{2,18},{3,19},{4,20},{5,21},{6,22},{7,23},{8,24},{9,... | collective-permute-start | bytes 1179656 | tf_op jit(solution)/shard_map/ppermute | solution.py:435
  84.6 8.8 %collective-permute-start.24 = (bf16[32,1024]{1,0:T(8,128)(2,1)S(1)}, bf16[32,1024]{1,0:T(8,128)(2,1)S(1)}, u32[]{:S(2)}, u32[]{:S(2)}) collective-permute-start(bf16[32,1024]{1,0:T(8,128)(2,1)S(1)} %add.63.refs_10_), channel_id=1, source_target_pairs={{0,16},{1,17},{2,18},{3,19},{4,20},{5,21},{6,22},{7,23},{8,24},{9,... | collective-permute-start | bytes 196616 | tf_op jit(solution)/shard_map/ppermute | solution.py:435
  126.0 9.2 %collective-permute-start.32 = (bf16[64,4096]{1,0:T(8,128)(2,1)S(1)}, bf16[64,4096]{1,0:T(8,128)(2,1)S(1)}, u32[]{:S(2)}, u32[]{:S(2)}) collective-permute-start(bf16[64,4096]{1,0:T(8,128)(2,1)S(1)} %shard_map.236), channel_id=1, source_target_pairs={{0,4},{4,8},{8,12},{12,14},{14,10},{10,6},{6,2},{2,0},{1,3},{5,1},... | collective-permute-start | bytes 1572872 | tf_op jit(solution)/shard_map/ppermute | solution.py:33
  126.4 14.9 %collective-permute-start.35 = (bf16[128,4096]{1,0:T(8,128)(2,1)S(1)}, bf16[128,4096]{1,0:T(8,128)(2,1)S(1)}, u32[]{:S(2)}, u32[]{:S(2)}) collective-permute-start(bf16[128,4096]{1,0:T(8,128)(2,1)S(1)} %get-tuple-element.174), channel_id=1, source_target_pairs={{0,1},{1,0},{2,3},{3,2},{4,5},{5,4},{6,7},{7,6},{8,9},{9,8},{10,11... | collective-permute-start | bytes 3145736 | tf_op jit(solution)/shard_map/ppermute | solution.py:29
  129.3 11.6 %collective-permute-start.37 = (bf16[64,4096]{1,0:T(8,128)(2,1)S(1)}, bf16[64,4096]{1,0:T(8,128)(2,1)S(1)}, u32[]{:S(2)}, u32[]{:S(2)}) collective-permute-start(bf16[64,4096]{1,0:T(8,128)(2,1)S(1)} %convert_element_type.78), channel_id=1, source_target_pairs={{0,4},{4,8},{8,12},{12,14},{14,10},{10,6},{6,2},{2,0},{1,3},{5,1},... | collective-permute-start | bytes 1572872 | tf_op jit(solution)/shard_map/ppermute | solution.py:33
  135.4 11.1 %collective-permute-start.33 = (bf16[64,4096]{1,0:T(8,128)(2,1)S(1)}, bf16[64,4096]{1,0:T(8,128)(2,1)S(1)}, u32[]{:S(2)}, u32[]{:S(2)}) collective-permute-start(bf16[64,4096]{1,0:T(8,128)(2,1)S(1)} %add_convert_fusion.6), channel_id=1, source_target_pairs={{0,4},{4,8},{8,12},{12,14},{14,10},{10,6},{6,2},{2,0},{1,3},{5,1},... | collective-permute-start | bytes 1572872 | tf_op jit(solution)/shard_map/ppermute | solution.py:33
  141.0 11.1 %collective-permute-start.38 = (bf16[64,4096]{1,0:T(8,128)(2,1)S(1)}, bf16[64,4096]{1,0:T(8,128)(2,1)S(1)}, u32[]{:S(2)}, u32[]{:S(2)}) collective-permute-start(bf16[64,4096]{1,0:T(8,128)(2,1)S(1)} %add_convert_fusion.3), channel_id=1, source_target_pairs={{0,4},{4,8},{8,12},{12,14},{14,10},{10,6},{6,2},{2,0},{1,3},{5,1},... | collective-permute-start | bytes 1572872 | tf_op jit(solution)/shard_map/ppermute | solution.py:33
  146.6 11.1 %collective-permute-start.34 = (bf16[64,4096]{1,0:T(8,128)(2,1)S(1)}, bf16[64,4096]{1,0:T(8,128)(2,1)S(1)}, u32[]{:S(2)}, u32[]{:S(2)}) collective-permute-start(bf16[64,4096]{1,0:T(8,128)(2,1)S(1)} %add_convert_fusion.5), channel_id=1, source_target_pairs={{0,4},{4,8},{8,12},{12,14},{14,10},{10,6},{6,2},{2,0},{1,3},{5,1},... | collective-permute-start | bytes 1572872 | tf_op jit(solution)/shard_map/ppermute | solution.py:33
  152.2 11.1 %collective-permute-start.39 = (bf16[64,4096]{1,0:T(8,128)(2,1)S(1)}, bf16[64,4096]{1,0:T(8,128)(2,1)S(1)}, u32[]{:S(2)}, u32[]{:S(2)}) collective-permute-start(bf16[64,4096]{1,0:T(8,128)(2,1)S(1)} %add_convert_fusion.2), channel_id=1, source_target_pairs={{0,4},{4,8},{8,12},{12,14},{14,10},{10,6},{6,2},{2,0},{1,3},{5,1},... | collective-permute-start | bytes 1572872 | tf_op jit(solution)/shard_map/ppermute | solution.py:33
  157.8 11.1 %collective-permute-start.36 = (bf16[64,4096]{1,0:T(8,128)(2,1)S(1)}, bf16[64,4096]{1,0:T(8,128)(2,1)S(1)}, u32[]{:S(2)}, u32[]{:S(2)}) collective-permute-start(bf16[64,4096]{1,0:T(8,128)(2,1)S(1)} %add_convert_fusion.4), channel_id=1, source_target_pairs={{0,4},{4,8},{8,12},{12,14},{14,10},{10,6},{6,2},{2,0},{1,3},{5,1},... | collective-permute-start | bytes 1572872 | tf_op jit(solution)/shard_map/ppermute | solution.py:33
  (39 other events, 262.2 us)
where the time goes:
time: 173 us; the launch traced here: 172 us
  Pallas kernels  65.5 us (38%)
  waiting for transfers between devices  47.4 us (27%)
  starting transfers between devices  44.4 us (26%)
  local copies, waits for them, and re-layouts  9.4 us (5%)
  other arithmetic  4.73 us (3%)
    pallas_call x24, Pallas kernels, call(): pl.pallas_call(kernel, in_specs=specs, out_specs=[vmem] * len(outs), out_...  65.5 us
    ppermute x14, waiting for transfers between devices, along_ring(): return lax.ppermute(value, 'mlp', RING_PERM)  33.2 us
    ppermute x14, starting transfers between devices, along_ring(): return lax.ppermute(value, 'mlp', RING_PERM)  16.2 us
    ppermute x4, starting transfers between devices, to_group(): lax.ppermute(value, 'req', [(g, g + d) for g in range(req_count - d)])  13.7 us
    unnamed x46, local copies, waits for them, and re-layouts  8.3 us
    ppermute x4, starting transfers between devices, per_device(): moved = lax.ppermute(rank_out, 'mlp', [(i, i ^ bit) for i in range(16)])  5.46 us
    ppermute x2, waiting for transfers between devices, sum_over_mlp(): lax.ppermute(value, 'mlp', [(i, i ^ bit) for i in range(16)])  5.27 us
    ppermute x2, starting transfers between devices, sum_over_mlp(): lax.ppermute(value, 'mlp', [(i, i ^ bit) for i in range(16)])  4.29 us
  transfers between devices with their start and end apart: 41, of which 16 were waited for; matrix products, arithmetic and copies ran while one was open for 3% of the time, Pallas kernels for 30%

commit v1 on v0

--- a/solution.py
+++ b/solution.py
@@ -62,11 +62,11 @@
     return pl.ds(pl.multiple_of(info[PAIRS + slot] * rows, rows), rows)
 
 
-def store_lanes(info, out_ref, lanes, slot):
+def store_lanes(info, out_ref, lanes, slots):
     width = out_ref.shape[1] // SLOTS
-    for k in range(lanes.shape[1] // width):
+    for k, slot in enumerate(slots):
         part = lanes[:, k * width : (k + 1) * width]
-        out_ref[:, pair_at(info, slot + k, width)] = swap_halves(info, part).astype(out_ref.dtype)
+        out_ref[:, pair_at(info, slot, width)] = swap_halves(info, part).astype(out_ref.dtype)
 
 
 def rank_rows(info, rank_ref, slot, count):
@@ -136,14 +136,14 @@
     lax.fori_loop(0, meta_ref.shape[0] // rows, one, 0)
 
 
-def rank_kernel(count, first_slot, info, *refs):
+def rank_kernel(count, slots, info, *refs):
     x = jnp.concatenate([ref[...] for ref in refs[:count]], axis=0)
     left_ref, meta_ref, slot_ref, fold_ref, held_ref, out_ref = refs[count:]
     products = rank_product(x, left_ref[...])
-    adapter = meta_ref[first_slot * 128 : first_slot * 128 + x.shape[0], 64:65]
+    adapter = jnp.concatenate([meta_ref[k * 128 : (k + 1) * 128, 64:65] for k in slots], axis=0)
     chosen = jnp.where(slot_ref[...] == adapter, products, 0.0).astype(jnp.bfloat16)
     out_ref[...] = held_ref[...]
-    store_lanes(info, out_ref, across(fold_ref[...], chosen), first_slot)
+    store_lanes(info, out_ref, across(fold_ref[...], chosen), slots)
 
 
 def base_kernel(count, *refs):
@@ -168,15 +168,17 @@
 
 
 def block_rows_of(refs, block):
-    if block:
-        return refs[block][...]
-    return jnp.concatenate([refs[0][...], refs[4][...]], axis=0)
+    if block == 0:
+        return jnp.concatenate([refs[0][:128], refs[3][128:]], axis=0)
+    if block == 3:
+        return jnp.concatenate([refs[2][...], refs[3][:128]], axis=0)
+    return refs[0][128:] if block == 1 else refs[1][...]
 
 
 def inner_kernel(info, *refs):
-    base_refs, up_refs, (rank_ref, meta_ref, turn_ref, first_ref, last_ref) = refs[:5], refs[5:10], refs[10:15]
-    qkv_right_ref, up_right_ref, bias_ref, left_ref = refs[15:19]
-    q_ref, k_ref, v_ref, hidden_ref, out_ref = refs[19:]
+    base_refs, up_refs, (rank_ref, meta_ref, turn_ref, first_ref, last_ref) = refs[:4], refs[4:8], refs[8:13]
+    qkv_right_ref, up_right_ref, bias_ref, left_ref = refs[13:17]
+    q_ref, k_ref, v_ref, hidden_ref, out_ref = refs[17:]
     rows = 256
     column_id = lane_ids((rows, first_ref.shape[1]), ADAPTER_RANK)
     for block in range(BLOCKS):
@@ -196,11 +198,11 @@
         hidden = (0.5 * x * (1.0 + jnp.tanh(inner))).astype(jnp.bfloat16)
         hidden_ref[at, :] = hidden
         chosen = jnp.where(own, rank_product(hidden, left_ref[...]), 0.0).astype(jnp.bfloat16)
-        store_lanes(info, out_ref, across(last_ref[...], chosen), 2 * block)
+        store_lanes(info, out_ref, across(last_ref[...], chosen), (2 * block, 2 * block + 1))
 
 
 def far_kernel(first_row, info, *refs):
-    shared_refs, (rank_ref, meta_ref, turn_ref, spread_ref, right_ref, k_ref, v_ref) = refs[:5], refs[5:]
+    shared_refs, (rank_ref, meta_ref, turn_ref, spread_ref, right_ref, k_ref, v_ref) = refs[:4], refs[4:]
     rows = 256
     column_id = lane_ids((rows, spread_ref.shape[1]), ADAPTER_RANK)
     for block in range(BLOCKS):
@@ -268,7 +270,9 @@
         attended = (acc_ref[...] / twice(sum_ref[...])).astype(jnp.bfloat16)
         attended_ref[at, :] = attended
         chosen = jnp.where(column_id == meta_ref[at, 64:65], rank_product(attended, left_ref[...]), 0.0)
-        store_lanes(info, fold_ref, across(spread_ref[...], chosen.astype(jnp.bfloat16)), 2 * block)
+        store_lanes(
+            info, fold_ref, across(spread_ref[...], chosen.astype(jnp.bfloat16)), (2 * block, 2 * block + 1)
+        )
         return 0
 
     lax.fori_loop(0, BLOCKS, one, 0)
@@ -323,7 +327,7 @@
     lax.fori_loop(0, right_ref.shape[1] // width, one, 0)
 
 
-def call(kernel, operands, outs, info=None, scratch=(), mib=24):
+def call(kernel, operands, outs, info=None, scratch=(), mib=24, flops=1000):
     vmem = pl.BlockSpec(memory_space=pltpu.VMEM)
     specs = [vmem] * len(operands)
     if info is not None:
@@ -335,7 +339,7 @@
         out_shape=outs,
         scratch_shapes=scratch,
         compiler_params=pltpu.CompilerParams(vmem_limit_bytes=mib * 1024 * 1024),
-        cost_estimate=pl.CostEstimate(flops=1000, bytes_accessed=1000, transcendentals=0),
+        cost_estimate=pl.CostEstimate(flops=flops, bytes_accessed=1000, transcendentals=0),
     )(*operands)
 
 
@@ -436,15 +440,15 @@
 
     held = functools.partial(pltpu.VMEM, dtype=jnp.float32)
 
-    def add_ranks(part, first_slot, so_far):
+    def add_ranks(part, slots, so_far):
         return call(
-            functools.partial(rank_kernel, len(part), first_slot),
+            functools.partial(rank_kernel, len(part), slots),
             list(part) + [pair_left, meta, slot_columns, spread_own, so_far],
             [shape(32, group_rows)],
             info,
         )[0]
 
-    def products_of(part):
+    def products_of(part, flops=1000):
         rows = len(part) * block
         return call(
             functools.partial(base_kernel, len(part)),
@@ -454,6 +458,7 @@
                 shape(rows, hidden_width, jnp.float32),
                 shape(rows, 2 * HEAD_SIZE),
             ],
+            flops=flops,
         )
 
     def to_groups(value):
@@ -464,36 +469,35 @@
 
     tie = lax.optimization_barrier
     own_part = (own, other)
-    ring_a, meta, turns = tie((ring_a, meta, turns))
-    zeroth = products_of(own_part)
-    ring_b, zeroth, pair_left = tie((ring_b, zeroth, pair_left))
+    ring_a, meta, turns, pair_left = tie((ring_a, meta, turns, pair_left))
+    ranks = add_ranks(own_part, (0,), jnp.zeros((32, group_rows), jnp.bfloat16))
+    ring_b, ranks = tie((ring_b, ranks))
     part = arrivals(ring_a, ring_b)
     ring_a, ring_b = along_ring(ring_a), along_ring(ring_b)
-    ranks = add_ranks(own_part, 0, jnp.zeros((32, group_rows), jnp.bfloat16))
-    ranks = add_ranks(part, 2, ranks)
-    first = products_of(part)
+    ranks = add_ranks(part, (2, 3), ranks)
+    first = products_of(own_part + part)
     ring_b, ranks, first = tie((ring_b, ranks, first))
     part = arrivals(ring_a, ring_b)
     ring_a, ring_b = along_ring(ring_a), along_ring(ring_b)
     far_right = to_partner(near_right)
-    far_early = to_groups(jnp.concatenate([zeroth[2], first[2]], axis=0))
-    ranks = add_ranks(part, 4, ranks)
+    far_early = to_groups(first[2])
+    ranks = add_ranks(part, (4, 5), ranks)
     second = products_of(part)
-    ring_b, ranks, second, far_right, far_early = tie((ring_b, ranks, second, far_right, far_early))
-    far_middle = to_groups(second[2])
+    ring_b, ranks, second, far_right = tie((ring_b, ranks, second, far_right))
     part = arrivals(ring_a, ring_b)
     ring_a = along_ring(ring_a)
-    ranks = add_ranks(part, 6, ranks)
-    third = products_of(part)
-    ring_a, ranks, third, far_middle = tie((ring_a, ranks, third, far_middle))
-    part = (ring_a, to_partner(ring_a))
-    ranks = add_ranks(part, 1, ranks)
+    third = products_of(part[:2], 2000000000)
+    ranks = add_ranks(part[:2], (6,), ranks)
+    ring_a, ranks, third = tie((ring_a, ranks, third))
+    part = part[2:] + (ring_a, to_partner(ring_a))
+    ranks = add_ranks(part, (7, 1), ranks)
     moved = lax.ppermute(ranks, "mlp", [(i, i ^ 2) for i in range(16)])
     fourth = products_of(part)
-    ranks, fourth = tie((ranks + moved, fourth))
+    ranks, fourth, far_early = tie((ranks + moved, fourth, far_early))
+    far_middle = to_groups(second[2])
     far_late = to_groups(jnp.concatenate([third[2], fourth[2]], axis=0))
     rank_in = sum_over_mlp(ranks, (4, 8))
-    products = (zeroth, first, second, third, fourth)
+    products = (first, second, third, fourth)
 
     bias_row = input_bias.reshape(1, -1)
     far_rank = to_groups(rank_in)
@@ -509,8 +513,7 @@
     keys, values = [own_keys], [own_values]
     for d in range(1, req_count):
         early, late = far_early[d - 1], far_late[d - 1]
-        shared = [early[:pair_rows], early[pair_rows:], far_middle[d - 1]]
-        shared += [late[:block_rows], late[block_rows:]]
+        shared = [early, far_middle[d - 1], late[:pair_rows], late[pair_rows:]]
         far_keys, far_values = call(
             functools.partial(far_kernel, d * group_rows),
             shared + [far_rank[d - 1], meta, turns, spread_first, qkv_right],
@@ -543,15 +546,17 @@
             [shape(block_rows - sent, model_width, jnp.float32), shape(sent, model_width)],
         )
 
-    kept, arrived, before = {}, {}, None
+    kept, arrived, sent = {}, {}, {}
     for bit, k in zip((1, 2, 4, 8), (0, 3, 2, 1)):
         moved = lax.ppermute(rank_out, "mlp", [(i, i ^ bit) for i in range(16)])
-        kept[k], sent = main(k, attended, hidden)
-        rank_out, attended, sent = tie((rank_out + moved, attended, sent))
-        if before is not None:
-            rank_out, arrived[before] = tie((rank_out, arrived[before]))
-        arrived[k], before = to_partner(sent), k
-
+        kept[k], sent[k] = main(k, attended, hidden)
+        rank_out, attended, kept[k], sent[k] = tie((rank_out + moved, attended, kept[k], sent[k]))
+        if k == 0:
+            arrived[k] = to_partner(sent[k])
+        if bit == 4:
+            arrived[3] = to_partner(sent[3])
+            rank_out, arrived[0] = tie((rank_out, arrived[0]))
+    rank_out, arrived[3] = tie((rank_out, arrived[3]))
     pair_right = jnp.concatenate([near_right, far_right], axis=0)
 
     def adapt(slot, half, kept, first, arrived):
@@ -570,15 +575,18 @@
     chain_b = None
     for s in (3, 2, 1):
         add_a, add_b = adapt(2 * s + 1, False, kept[s], 0, arrived[s])
+        if s > 1:
+            arrived[s - 1] = to_partner(sent[s - 1])
         if chain_b is None:
             chain_b = along_ring(narrow(add_b))
             chain_a = along_ring(narrow(wide(chain_a) + add_a))
         else:
             chain_a = along_ring(narrow(wide(chain_a) + add_a))
             chain_b = along_ring(narrow(wide(chain_b) + add_b))
-    arrived = to_partner(narrow(wide(chain_b) + kept[0][block : 2 * block]))
-    total = adapt(0, True, kept[0], 0, chain_a)[0] + wide(arrived)
-    return narrow(total + wide(tokens) + output_bias)
+    own_sum = adapt(0, True, kept[0], 0, tokens)[0]
+    chain_a, own_sum = tie((chain_a, own_sum))
+    arrived_last = to_partner(narrow(wide(chain_b) + kept[0][block : 2 * block]))
+    return narrow(wide(chain_a) + wide(arrived_last) + own_sum + output_bias)
 
 
 def solution(mesh):

time: 173 us -> 169 us (0.977)
  starting transfers between devices: 44.4 us -> 37.4 us
  waiting for transfers between devices: 47.4 us -> 50.1 us
  Pallas kernels: 65.5 us -> 67.8 us
  local copies, waits for them, and re-layouts: 9.4 us -> 7.23 us
    ppermute x14, waiting for transfers between devices: 33.2 us -> 38 us  [along_ring(): return lax.ppermute(value, 'mlp', RING_PERM)]
    ppermute x4, starting transfers between devices: 13.7 us -> 10.6 us  [to_group(): lax.ppermute(value, 'req', [(g, g + d) for g in range(req_count - d)])]
    pallas_call x24 -> x23, Pallas kernels: 65.5 us -> 67.8 us  [call(): pl.pallas_call(kernel, in_specs=specs, out_specs=[vmem] * len(outs), out_...]
    unnamed x46 -> x50, local copies, waits for them, and re-layouts: 8.3 us -> 6.14 us
    ppermute x14, starting transfers between devices: 16.2 us -> 14.3 us  [along_ring(): return lax.ppermute(value, 'mlp', RING_PERM)]
  transfers between devices with their start and end apart: 41 -> 41, of which waited for: 16 -> 18; matrix products, arithmetic and copies ran while one was open for 3% -> 3% of each run, Pallas kernels for 30% -> 35%
where the time goes in v1:
time: 169 us; the launch traced here: 167 us
  Pallas kernels  67.8 us (40%)
  waiting for transfers between devices  50.1 us (30%)
  starting transfers between devices  37.4 us (22%)
  local copies, waits for them, and re-layouts  7.23 us (4%)
  other arithmetic  4.19 us (2%)
    pallas_call x23, Pallas kernels, call(): pl.pallas_call(kernel, in_specs=specs, out_specs=[vmem] * len(outs), out_...  67.8 us
    ppermute x14, waiting for transfers between devices, along_ring(): return lax.ppermute(value, 'mlp', RING_PERM)  38 us
    ppermute x14, starting transfers between devices, along_ring(): return lax.ppermute(value, 'mlp', RING_PERM)  14.3 us
    ppermute x4, starting transfers between devices, to_group(): lax.ppermute(value, 'req', [(g, g + d) for g in range(req_count - d)])  10.6 us
    unnamed x50, local copies, waits for them, and re-layouts  6.14 us
    ppermute x2, waiting for transfers between devices, sum_over_mlp(): lax.ppermute(value, 'mlp', [(i, i ^ bit) for i in range(16)])  5.32 us
    ppermute x4, starting transfers between devices, per_device(): moved = lax.ppermute(rank_out, 'mlp', [(i, i ^ bit) for i in range(16)])  4.87 us
    ppermute x2, starting transfers between devices, sum_over_mlp(): lax.ppermute(value, 'mlp', [(i, i ^ bit) for i in range(16)])  4.24 us
  transfers between devices with their start and end apart: 41, of which 18 were waited for; matrix products, arithmetic and copies ran while one was open for 3% of the time, Pallas kernels for 35%

profile of v1, /device:TPU:0, one launch (start us, length us, event | category | flops | bytes accessed | tf_op | source)
XLA Modules:
  0.0 167.5 jit_solution(18356752398332037955)
XLA Ops:
  4.3 3.0 %collective-permute-start.2 = (bf16[64,4096]{1,0:T(8,128)(2,1)}, bf16[64,4096]{1,0:T(8,128)(2,1)}, u32[]{:S(2)}, u32[]{:S(2)}) collective-permute-start(bf16[64,4096]{1,0:T(8,128)(2,1)} %shard_map.217.refs_0_), channel_id=1, source_target_pairs={{0,4},{4,8},{8,12},{12,14},{14,10},{10,6},{6,2},{2,0},{1,3},{5,1},... | collective-permute-start | bytes 1572872 | tf_op jit(solution)/shard_map/ppermute | solution.py:33
  23.7 3.5 %collective-permute-done.9.refs_0_ = bf16[64,4096]{1,0:T(8,128)(2,1)} collective-permute-done((bf16[64,4096]{1,0:T(8,128)(2,1)}, bf16[64,4096]{1,0:T(8,128)(2,1)}, u32[]{:S(2)}, u32[]{:S(2)}) %collective-permute-start.9) | collective-permute-done | bytes 524320 | tf_op jit(solution)/shard_map/ppermute | solution.py:33
  31.0 2.8 %copy-done = bf16[4096,1,768]{2,0,1:T(8,128)(2,1)S(1)} copy-done((bf16[4096,1,768]{2,0,1:T(8,128)(2,1)S(1)}, bf16[4096,1,768]{2,0,1:T(8,128)(2,1)}, u32[]{:S(2)}) %copy-start) | copy-done | bytes 6291480
  33.8 6.0 %shard_map.221 = (f32[384,768]{1,0:T(8,128)S(1)}, f32[384,512]{1,0:T(8,128)S(1)}, bf16[384,512]{1,0:T(8,128)(2,1)S(1)}) custom-call(bf16[64,4096]{1,0:T(8,128)(2,1)} %shard_map.217.refs_0_, bf16[64,4096]{1,0:T(8,128)(2,1)} %collective-permute-done.refs_1_, bf16[64,4096]{1,0:T(8,128)(2,1)} %collective-permute-done.2.refs_0_.refs_2_, ...), custom_call_target="tpu_custom_call" | custom-call | flops 1000 | bytes 1000 | tf_op jit(solution)/shard_map/pallas_call | solution.py:335
  43.5 3.9 %shard_map.223 = (f32[256,768]{1,0:T(8,128)S(1)}, f32[256,512]{1,0:T(8,128)S(1)}, bf16[256,512]{1,0:T(8,128)(2,1)S(1)}) custom-call(bf16[64,4096]{1,0:T(8,128)(2,1)} %collective-permute-done.9.refs_0_, bf16[64,4096]{1,0:T(8,128)(2,1)S(1)} %collective-permute-done.5.refs_1_, bf16[64,4096]{1,0:T(8,128)(2,1)S(1)} %collective-permute-done.10.refs_2_, ...), custom_call_target="tpu_custom_call" | custom-call | flops 1000 | bytes 1000 | tf_op jit(solution)/shard_map/pallas_call | solution.py:335
  55.2 3.6 %collective-permute-start.19 = (bf16[384,512]{1,0:T(8,128)(2,1)S(1)}, bf16[384,512]{1,0:T(8,128)(2,1)S(1)}, u32[]{:S(2)}, u32[]{:S(2)}) collective-permute-start(bf16[384,512]{1,0:T(8,128)(2,1)S(1)} %get-tuple-element.118), channel_id=1, source_target_pairs={{0,16},{1,17},{2,18},{3,19},{4,20},{5,21},{6,22},{7,23},{8,24},{9,... | collective-permute-start | bytes 1179656 | tf_op jit(solution)/shard_map/ppermute | solution.py:439
  60.8 2.9 %shard_map.227 = (f32[256,768]{1,0:T(8,128)S(1)}, f32[256,512]{1,0:T(8,128)S(1)}, bf16[256,512]{1,0:T(8,128)(2,1)S(1)}) custom-call(bf16[64,4096]{1,0:T(8,128)(2,1)S(1)} %collective-permute-done.15.refs_0_, bf16[64,4096]{1,0:T(8,128)(2,1)S(1)} %collective-permute-done.16.refs_1_, bf16[64,4096]{1,0:T(8,128)(2,1)S(1)} %collective-permute-done.14.refs_2_, ...), custom_call_target="tpu_custom_call" | custom-call | flops 1000 | bytes 1000 | tf_op jit(solution)/shard_map/pallas_call | solution.py:335
  64.6 2.9 %collective-permute-done.19.refs_0_ = bf16[384,512]{1,0:T(8,128)(2,1)S(1)} collective-permute-done((bf16[384,512]{1,0:T(8,128)(2,1)S(1)}, bf16[384,512]{1,0:T(8,128)(2,1)S(1)}, u32[]{:S(2)}, u32[]{:S(2)}) %collective-permute-start.19) | collective-permute-done | bytes 393248 | tf_op jit(solution)/shard_map/ppermute | solution.py:439
  67.6 4.4 %collective-permute-start.23 = (bf16[384,512]{1,0:T(8,128)(2,1)S(1)}, bf16[384,512]{1,0:T(8,128)(2,1)S(1)}, u32[]{:S(2)}, u32[]{:S(2)}) collective-permute-start(bf16[384,512]{1,0:T(8,128)(2,1)S(1)} %pad_maximum_fusion.1), channel_id=1, source_target_pairs={{0,16},{1,17},{2,18},{3,19},{4,20},{5,21},{6,22},{7,23},{8,24},{9,... | collective-permute-start | bytes 1179656 | tf_op jit(solution)/shard_map/ppermute | solution.py:439
  75.0 2.7 %collective-permute-done.20 = bf16[32,1024]{1,0:T(8,128)(2,1)S(1)} collective-permute-done((bf16[32,1024]{1,0:T(8,128)(2,1)S(1)}, bf16[32,1024]{1,0:T(8,128)(2,1)S(1)}, u32[]{:S(2)}, u32[]{:S(2)}) %collective-permute-start.20) | collective-permute-done | bytes 65568 | tf_op jit(solution)/shard_map/ppermute | solution.py:352
  84.3 7.3 %shard_map.228 = (bf16[1024,256]{1,0:T(8,128)(2,1)S(1)}, bf16[1024,256]{1,0:T(8,128)(2,1)S(1)}, bf16[1024,256]{1,0:T(8,128)(2,1)S(1)}, bf16[1024,512]{1,0:T(8,128)(2,1)S(1)}, bf16[32,1024]{1,0:T(8,128)(2,1)S(1)}) custom-call(s32[26]{0:T(128)S(1)} %dynamic-slice_bitcast_fusion.info, f32[384,768]{1,0:T(8,128)S(1)} %get-tuple-element.100.refs_0_, ...), custom_call_target="tpu_custom_call" | custom-call | flops 1000 | bytes 1000 | tf_op jit(solution)/shard_map/pallas_call | solution.py:335
  91.7 2.7 %shard_map.229 = (bf16[1024,256]{1,0:T(8,128)(2,1)S(1)}, bf16[1024,256]{1,0:T(8,128)(2,1)S(1)}) custom-call(s32[26]{0:T(128)S(1)} %dynamic-slice_bitcast_fusion.info, bf16[384,512]{1,0:T(8,128)(2,1)S(1)} %collective-permute-done.19.refs_0_, bf16[256,512]{1,0:T(8,128)(2,1)S(1)} %collective-permute-done.22.refs_1_, bf16[128,512]{1,0:T(8,128)(2,1)S(1)} %slice.12.refs_2_, ...), custom_call_target="tpu_custom_call" | custom-call | flops 1000 | bytes 1000 | tf_op jit(solution)/shard_map/pallas_call | solution.py:335
  94.4 7.1 %shard_map.230 = (bf16[1024,256]{1,0:T(8,128)(2,1)S(1)}, bf16[32,1024]{1,0:T(8,128)(2,1)S(1)}) custom-call(s32[26]{0:T(128)S(1)} %dynamic-slice_bitcast_fusion.info, bf16[1024,256]{1,0:T(8,128)(2,1)S(1)} %get-tuple-element.126.refs_0_, bf16[1024,256]{1,0:T(8,128)(2,1)S(1)} %get-tuple-element.127.refs_1_, bf16[1024,256]{1,0:T(8,128)(2,1)S(1)} %get-tuple-element.132.refs_2_, ...), custom_call_target="tpu_custom_call" | custom-call | flops 1000 | bytes 1000 | tf_op jit(solution)/shard_map/pallas_call | solution.py:335
  101.6 3.0 %shard_map.231 = (f32[192,4096]{1,0:T(8,128)S(1)}, bf16[64,4096]{1,0:T(8,128)(2,1)S(1)}) custom-call(bf16[1024,256]{1,0:T(8,128)(2,1)S(1)} %get-tuple-element.152.attended_ref, bf16[1024,512]{1,0:T(8,128)(2,1)S(1)} %get-tuple-element.138.hidden_ref, bf16[256,4096]{1,0:T(8,128)(2,1)S(1)} %bitcast.21, bf16[512,4096]{1,0:T(8,128)(2,1)S(1)} %copy-done.2), custom_call_target="tpu_custom_call" | custom-call | flops 1000 | bytes 1000 | tf_op jit(solution)/shard_map/pallas_call | solution.py:335
  105.9 3.0 %shard_map.232 = (f32[128,4096]{1,0:T(8,128)S(1)}, bf16[128,4096]{1,0:T(8,128)(2,1)S(1)}) custom-call(bf16[1024,256]{1,0:T(8,128)(2,1)S(1)} %get-tuple-element.152.attended_ref, bf16[1024,512]{1,0:T(8,128)(2,1)S(1)} %get-tuple-element.138.hidden_ref, bf16[256,4096]{1,0:T(8,128)(2,1)S(1)} %bitcast.22, bf16[512,4096]{1,0:T(8,128)(2,1)S(1)} %copy-done.2), custom_call_target="tpu_custom_call" | custom-call | flops 1000 | bytes 1000 | tf_op jit(solution)/shard_map/pallas_call | solution.py:335
  111.1 3.0 %shard_map.233 = (f32[128,4096]{1,0:T(8,128)S(1)}, bf16[128,4096]{1,0:T(8,128)(2,1)S(1)}) custom-call(bf16[1024,256]{1,0:T(8,128)(2,1)S(1)} %get-tuple-element.152.attended_ref, bf16[1024,512]{1,0:T(8,128)(2,1)S(1)} %get-tuple-element.138.hidden_ref, bf16[256,4096]{1,0:T(8,128)(2,1)S(1)} %bitcast.23, bf16[512,4096]{1,0:T(8,128)(2,1)S(1)} %copy-done.2), custom_call_target="tpu_custom_call" | custom-call | flops 1000 | bytes 1000 | tf_op jit(solution)/shard_map/pallas_call | solution.py:335
  116.8 3.0 %shard_map.234 = (f32[128,4096]{1,0:T(8,128)S(1)}, bf16[128,4096]{1,0:T(8,128)(2,1)S(1)}) custom-call(bf16[1024,256]{1,0:T(8,128)(2,1)S(1)} %get-tuple-element.152.attended_ref, bf16[1024,512]{1,0:T(8,128)(2,1)S(1)} %get-tuple-element.138.hidden_ref, bf16[256,4096]{1,0:T(8,128)(2,1)S(1)} %bitcast.24, bf16[512,4096]{1,0:T(8,128)(2,1)S(1)} %copy-done.2), custom_call_target="tpu_custom_call" | custom-call | flops 1000 | bytes 1000 | tf_op jit(solution)/shard_map/pallas_call | solution.py:335
  130.0 2.8 %collective-permute-done.31 = bf16[64,4096]{1,0:T(8,128)(2,1)S(1)} collective-permute-done((bf16[64,4096]{1,0:T(8,128)(2,1)S(1)}, bf16[64,4096]{1,0:T(8,128)(2,1)S(1)}, u32[]{:S(2)}, u32[]{:S(2)}) %collective-permute-start.31) | collective-permute-done | bytes 524320 | tf_op jit(solution)/shard_map/ppermute | solution.py:33
  132.9 5.5 %collective-permute-done.37 = bf16[64,4096]{1,0:T(8,128)(2,1)S(1)} collective-permute-done((bf16[64,4096]{1,0:T(8,128)(2,1)S(1)}, bf16[64,4096]{1,0:T(8,128)(2,1)S(1)}, u32[]{:S(2)}, u32[]{:S(2)}) %collective-permute-start.37) | collective-permute-done | bytes 524320 | tf_op jit(solution)/shard_map/ppermute | solution.py:33
  141.0 3.0 %collective-permute-done.32 = bf16[64,4096]{1,0:T(8,128)(2,1)S(1)} collective-permute-done((bf16[64,4096]{1,0:T(8,128)(2,1)S(1)}, bf16[64,4096]{1,0:T(8,128)(2,1)S(1)}, u32[]{:S(2)}, u32[]{:S(2)}) %collective-permute-start.32) | collective-permute-done | bytes 524320 | tf_op jit(solution)/shard_map/ppermute | solution.py:33
  144.2 5.5 %collective-permute-done.38 = bf16[64,4096]{1,0:T(8,128)(2,1)S(1)} collective-permute-done((bf16[64,4096]{1,0:T(8,128)(2,1)S(1)}, bf16[64,4096]{1,0:T(8,128)(2,1)S(1)}, u32[]{:S(2)}, u32[]{:S(2)}) %collective-permute-start.38) | collective-permute-done | bytes 524320 | tf_op jit(solution)/shard_map/ppermute | solution.py:33
  149.8 5.5 %collective-permute-done.34 = bf16[64,4096]{1,0:T(8,128)(2,1)S(1)} collective-permute-done((bf16[64,4096]{1,0:T(8,128)(2,1)S(1)}, bf16[64,4096]{1,0:T(8,128)(2,1)S(1)}, u32[]{:S(2)}, u32[]{:S(2)}) %collective-permute-start.34) | collective-permute-done | bytes 524320 | tf_op jit(solution)/shard_map/ppermute | solution.py:33
  155.4 5.5 %collective-permute-done.39 = bf16[64,4096]{1,0:T(8,128)(2,1)S(1)} collective-permute-done((bf16[64,4096]{1,0:T(8,128)(2,1)S(1)}, bf16[64,4096]{1,0:T(8,128)(2,1)S(1)}, u32[]{:S(2)}, u32[]{:S(2)}) %collective-permute-start.39) | collective-permute-done | bytes 524320 | tf_op jit(solution)/shard_map/ppermute | solution.py:33
  163.3 3.2 %collective-permute-done.36 = bf16[64,4096]{1,0:T(8,128)(2,1)S(1)} collective-permute-done((bf16[64,4096]{1,0:T(8,128)(2,1)S(1)}, bf16[64,4096]{1,0:T(8,128)(2,1)S(1)}, u32[]{:S(2)}, u32[]{:S(2)}) %collective-permute-start.36) | collective-permute-done | bytes 524320 | tf_op jit(solution)/shard_map/ppermute | solution.py:33
  (160 shorter events, 71.0 us)
Async XLA Ops:
  0.0 13.7 %collective-permute-start.3 = (bf16[4096,128]{1,0:T(8,128)(2,1)}, bf16[4096,128]{1,0:T(8,128)(2,1)}, u32[]{:S(2)}, u32[]{:S(2)}) collective-permute-start(bf16[4096,128]{1,0:T(8,128)(2,1)} %param.32), channel_id=1, source_target_pairs={{0,1},{1,0},{2,3},{3,2},{4,5},{5,4},{6,7},{7,6},{8,9},{9,8},{10,11... | collective-permute-start | bytes 3145736 | tf_op jit(solution)/shard_map/ppermute | solution.py:29
  4.3 11.2 %collective-permute-start.2 = (bf16[64,4096]{1,0:T(8,128)(2,1)}, bf16[64,4096]{1,0:T(8,128)(2,1)}, u32[]{:S(2)}, u32[]{:S(2)}) collective-permute-start(bf16[64,4096]{1,0:T(8,128)(2,1)} %shard_map.217.refs_0_), channel_id=1, source_target_pairs={{0,4},{4,8},{8,12},{12,14},{14,10},{10,6},{6,2},{2,0},{1,3},{5,1},... | collective-permute-start | bytes 1572872 | tf_op jit(solution)/shard_map/ppermute | solution.py:33
  12.1 9.5 %collective-permute-start.1 = (bf16[64,4096]{1,0:T(8,128)(2,1)}, bf16[64,4096]{1,0:T(8,128)(2,1)}, u32[]{:S(2)}, u32[]{:S(2)}) collective-permute-start(bf16[64,4096]{1,0:T(8,128)(2,1)} %collective-permute-done.refs_1_), channel_id=1, source_target_pairs={{0,4},{4,8},{8,12},{12,14},{14,10},{10,6},{6,2},{2,0},{1,3},{5,1},... | collective-permute-start | bytes 1572872 | tf_op jit(solution)/shard_map/ppermute | solution.py:33
  15.5 11.7 %collective-permute-start.9 = (bf16[64,4096]{1,0:T(8,128)(2,1)}, bf16[64,4096]{1,0:T(8,128)(2,1)}, u32[]{:S(2)}, u32[]{:S(2)}) collective-permute-start(bf16[64,4096]{1,0:T(8,128)(2,1)} %collective-permute-done.2.refs_0_.refs_2_), channel_id=1, source_target_pairs={{0,4},{4,8},{8,12},{12,14},{14,10},{10,6},{6,2},{2,0},{1,3},{5,1},... | collective-permute-start | bytes 1572872 | tf_op jit(solution)/shard_map/ppermute | solution.py:33
  22.2 17.6 %collective-permute-start.5 = (bf16[64,4096]{1,0:T(8,128)(2,1)}, bf16[64,4096]{1,0:T(8,128)(2,1)S(1)}, u32[]{:S(2)}, u32[]{:S(2)}) collective-permute-start(bf16[64,4096]{1,0:T(8,128)(2,1)} %collective-permute-done.1.refs_1_.refs_3_), channel_id=1, source_target_pairs={{0,4},{4,8},{8,12},{12,14},{14,10},{10,6},{6,2},{2,0},{1,3},{5,1},... | collective-permute-start | bytes 1572872 | tf_op jit(solution)/shard_map/ppermute | solution.py:33
  23.7 25.7 %collective-permute-start.12 = (bf16[128,4096]{1,0:T(8,128)(2,1)S(1)}, bf16[128,4096]{1,0:T(8,128)(2,1)S(1)}, u32[]{:S(2)}, u32[]{:S(2)}) collective-permute-start(bf16[128,4096]{1,0:T(8,128)(2,1)S(1)} %copy-done.19), channel_id=1, source_target_pairs={{0,1},{1,0},{2,3},{3,2},{4,5},{5,4},{6,7},{7,6},{8,9},{9,8},{10,11... | collective-permute-start | bytes 3145736 | tf_op jit(solution)/shard_map/ppermute | solution.py:29
  27.3 14.7 %collective-permute-start.13 = (bf16[64,4096]{1,0:T(8,128)(2,1)}, bf16[64,4096]{1,0:T(8,128)(2,1)S(1)}, u32[]{:S(2)}, u32[]{:S(2)}) collective-permute-start(bf16[64,4096]{1,0:T(8,128)(2,1)} %collective-permute-done.9.refs_0_), channel_id=1, source_target_pairs={{0,4},{4,8},{8,12},{12,14},{14,10},{10,6},{6,2},{2,0},{1,3},{5,1},... | collective-permute-start | bytes 1572872 | tf_op jit(solution)/shard_map/ppermute | solution.py:33
  40.4 9.2 %collective-permute-start.8 = (bf16[64,4096]{1,0:T(8,128)(2,1)S(1)}, bf16[64,4096]{1,0:T(8,128)(2,1)S(1)}, u32[]{:S(2)}, u32[]{:S(2)}) collective-permute-start(bf16[64,4096]{1,0:T(8,128)(2,1)S(1)} %collective-permute-done.5.refs_1_), channel_id=1, source_target_pairs={{0,4},{4,8},{8,12},{12,14},{14,10},{10,6},{6,2},{2,0},{1,3},{5,1},... | collective-permute-start | bytes 1572872 | tf_op jit(solution)/shard_map/ppermute | solution.py:33
  41.9 13.2 %collective-permute-start.14 = (bf16[64,4096]{1,0:T(8,128)(2,1)S(1)}, bf16[64,4096]{1,0:T(8,128)(2,1)S(1)}, u32[]{:S(2)}, u32[]{:S(2)}) collective-permute-start(bf16[64,4096]{1,0:T(8,128)(2,1)S(1)} %collective-permute-done.13.refs_0_), channel_id=1, source_target_pairs={{0,4},{4,8},{8,12},{12,14},{14,10},{10,6},{6,2},{2,0},{1,3},{5,1},... | collective-permute-start | bytes 1572872 | tf_op jit(solution)/shard_map/ppermute | solution.py:33
  49.5 9.2 %collective-permute-start.15 = (bf16[64,4096]{1,0:T(8,128)(2,1)S(1)}, bf16[64,4096]{1,0:T(8,128)(2,1)S(1)}, u32[]{:S(2)}, u32[]{:S(2)}) collective-permute-start(bf16[64,4096]{1,0:T(8,128)(2,1)S(1)} %collective-permute-done.8.refs_1_), channel_id=1, source_target_pairs={{0,1},{1,0},{2,3},{3,2},{4,5},{5,4},{6,7},{7,6},{8,9},{9,8},{10,11... | collective-permute-start | bytes 1572872 | tf_op jit(solution)/shard_map/ppermute | solution.py:29
  49.6 9.2 %collective-permute-start.16 = (bf16[64,4096]{1,0:T(8,128)(2,1)S(1)}, bf16[64,4096]{1,0:T(8,128)(2,1)S(1)}, u32[]{:S(2)}, u32[]{:S(2)}) collective-permute-start(bf16[64,4096]{1,0:T(8,128)(2,1)S(1)} %collective-permute-done.13.refs_0_), channel_id=1, source_target_pairs={{0,1},{1,0},{2,3},{3,2},{4,5},{5,4},{6,7},{7,6},{8,9},{9,8},{10,11... | collective-permute-start | bytes 1572872 | tf_op jit(solution)/shard_map/ppermute | solution.py:29
  55.2 12.4 %collective-permute-start.19 = (bf16[384,512]{1,0:T(8,128)(2,1)S(1)}, bf16[384,512]{1,0:T(8,128)(2,1)S(1)}, u32[]{:S(2)}, u32[]{:S(2)}) collective-permute-start(bf16[384,512]{1,0:T(8,128)(2,1)S(1)} %get-tuple-element.118), channel_id=1, source_target_pairs={{0,16},{1,17},{2,18},{3,19},{4,20},{5,21},{6,22},{7,23},{8,24},{9,... | collective-permute-start | bytes 1179656 | tf_op jit(solution)/shard_map/ppermute | solution.py:439
  67.6 24.0 %collective-permute-start.23 = (bf16[384,512]{1,0:T(8,128)(2,1)S(1)}, bf16[384,512]{1,0:T(8,128)(2,1)S(1)}, u32[]{:S(2)}, u32[]{:S(2)}) collective-permute-start(bf16[384,512]{1,0:T(8,128)(2,1)S(1)} %pad_maximum_fusion.1), channel_id=1, source_target_pairs={{0,16},{1,17},{2,18},{3,19},{4,20},{5,21},{6,22},{7,23},{8,24},{9,... | collective-permute-start | bytes 1179656 | tf_op jit(solution)/shard_map/ppermute | solution.py:439
  72.0 19.7 %collective-permute-start.22 = (bf16[256,512]{1,0:T(8,128)(2,1)S(1)}, bf16[256,512]{1,0:T(8,128)(2,1)S(1)}, u32[]{:S(2)}, u32[]{:S(2)}) collective-permute-start(bf16[256,512]{1,0:T(8,128)(2,1)S(1)} %get-tuple-element.129), channel_id=1, source_target_pairs={{0,16},{1,17},{2,18},{3,19},{4,20},{5,21},{6,22},{7,23},{8,24},{9,... | collective-permute-start | bytes 786440 | tf_op jit(solution)/shard_map/ppermute | solution.py:439
  109.3 12.0 %collective-permute-start.30 = (bf16[128,4096]{1,0:T(8,128)(2,1)S(1)}, bf16[128,4096]{1,0:T(8,128)(2,1)S(1)}, u32[]{:S(2)}, u32[]{:S(2)}) collective-permute-start(bf16[128,4096]{1,0:T(8,128)(2,1)S(1)} %get-tuple-element.156), channel_id=1, source_target_pairs={{0,1},{1,0},{2,3},{3,2},{4,5},{5,4},{6,7},{7,6},{8,9},{9,8},{10,11... | collective-permute-start | bytes 3145736 | tf_op jit(solution)/shard_map/ppermute | solution.py:29
  114.2 13.4 %collective-permute-start.33 = (bf16[128,4096]{1,0:T(8,128)(2,1)S(1)}, bf16[128,4096]{1,0:T(8,128)(2,1)S(1)}, u32[]{:S(2)}, u32[]{:S(2)}) collective-permute-start(bf16[128,4096]{1,0:T(8,128)(2,1)S(1)} %get-tuple-element.165), channel_id=1, source_target_pairs={{0,1},{1,0},{2,3},{3,2},{4,5},{5,4},{6,7},{7,6},{8,9},{9,8},{10,11... | collective-permute-start | bytes 3145736 | tf_op jit(solution)/shard_map/ppermute | solution.py:29
  123.5 9.2 %collective-permute-start.31 = (bf16[64,4096]{1,0:T(8,128)(2,1)S(1)}, bf16[64,4096]{1,0:T(8,128)(2,1)S(1)}, u32[]{:S(2)}, u32[]{:S(2)}) collective-permute-start(bf16[64,4096]{1,0:T(8,128)(2,1)S(1)} %shard_map.235), channel_id=1, source_target_pairs={{0,4},{4,8},{8,12},{12,14},{14,10},{10,6},{6,2},{2,0},{1,3},{5,1},... | collective-permute-start | bytes 1572872 | tf_op jit(solution)/shard_map/ppermute | solution.py:33
  123.6 14.9 %collective-permute-start.35 = (bf16[128,4096]{1,0:T(8,128)(2,1)S(1)}, bf16[128,4096]{1,0:T(8,128)(2,1)S(1)}, u32[]{:S(2)}, u32[]{:S(2)}) collective-permute-start(bf16[128,4096]{1,0:T(8,128)(2,1)S(1)} %get-tuple-element.168), channel_id=1, source_target_pairs={{0,1},{1,0},{2,3},{3,2},{4,5},{5,4},{6,7},{7,6},{8,9},{9,8},{10,11... | collective-permute-start | bytes 3145736 | tf_op jit(solution)/shard_map/ppermute | solution.py:29
  126.2 12.2 %collective-permute-start.37 = (bf16[64,4096]{1,0:T(8,128)(2,1)S(1)}, bf16[64,4096]{1,0:T(8,128)(2,1)S(1)}, u32[]{:S(2)}, u32[]{:S(2)}) collective-permute-start(bf16[64,4096]{1,0:T(8,128)(2,1)S(1)} %convert_element_type.79), channel_id=1, source_target_pairs={{0,4},{4,8},{8,12},{12,14},{14,10},{10,6},{6,2},{2,0},{1,3},{5,1},... | collective-permute-start | bytes 1572872 | tf_op jit(solution)/shard_map/ppermute | solution.py:33
  132.9 11.1 %collective-permute-start.32 = (bf16[64,4096]{1,0:T(8,128)(2,1)S(1)}, bf16[64,4096]{1,0:T(8,128)(2,1)S(1)}, u32[]{:S(2)}, u32[]{:S(2)}) collective-permute-start(bf16[64,4096]{1,0:T(8,128)(2,1)S(1)} %add_convert_fusion.6), channel_id=1, source_target_pairs={{0,4},{4,8},{8,12},{12,14},{14,10},{10,6},{6,2},{2,0},{1,3},{5,1},... | collective-permute-start | bytes 1572872 | tf_op jit(solution)/shard_map/ppermute | solution.py:33
  138.5 11.1 %collective-permute-start.38 = (bf16[64,4096]{1,0:T(8,128)(2,1)S(1)}, bf16[64,4096]{1,0:T(8,128)(2,1)S(1)}, u32[]{:S(2)}, u32[]{:S(2)}) collective-permute-start(bf16[64,4096]{1,0:T(8,128)(2,1)S(1)} %add_convert_fusion.3), channel_id=1, source_target_pairs={{0,4},{4,8},{8,12},{12,14},{14,10},{10,6},{6,2},{2,0},{1,3},{5,1},... | collective-permute-start | bytes 1572872 | tf_op jit(solution)/shard_map/ppermute | solution.py:33
  144.1 11.1 %collective-permute-start.34 = (bf16[64,4096]{1,0:T(8,128)(2,1)S(1)}, bf16[64,4096]{1,0:T(8,128)(2,1)S(1)}, u32[]{:S(2)}, u32[]{:S(2)}) collective-permute-start(bf16[64,4096]{1,0:T(8,128)(2,1)S(1)} %add_convert_fusion.5), channel_id=1, source_target_pairs={{0,4},{4,8},{8,12},{12,14},{14,10},{10,6},{6,2},{2,0},{1,3},{5,1},... | collective-permute-start | bytes 1572872 | tf_op jit(solution)/shard_map/ppermute | solution.py:33
  149.7 11.1 %collective-permute-start.39 = (bf16[64,4096]{1,0:T(8,128)(2,1)S(1)}, bf16[64,4096]{1,0:T(8,128)(2,1)S(1)}, u32[]{:S(2)}, u32[]{:S(2)}) collective-permute-start(bf16[64,4096]{1,0:T(8,128)(2,1)S(1)} %add_convert_fusion.2), channel_id=1, source_target_pairs={{0,4},{4,8},{8,12},{12,14},{14,10},{10,6},{6,2},{2,0},{1,3},{5,1},... | collective-permute-start | bytes 1572872 | tf_op jit(solution)/shard_map/ppermute | solution.py:33
  155.3 11.1 %collective-permute-start.36 = (bf16[64,4096]{1,0:T(8,128)(2,1)S(1)}, bf16[64,4096]{1,0:T(8,128)(2,1)S(1)}, u32[]{:S(2)}, u32[]{:S(2)}) collective-permute-start(bf16[64,4096]{1,0:T(8,128)(2,1)S(1)} %add_convert_fusion.4), channel_id=1, source_target_pairs={{0,4},{4,8},{8,12},{12,14},{14,10},{10,6},{6,2},{2,0},{1,3},{5,1},... | collective-permute-start | bytes 1572872 | tf_op jit(solution)/shard_map/ppermute | solution.py:33
  (41 other events, 350.8 us)

commit v2 on v1

--- a/solution.py
+++ b/solution.py
@@ -22,7 +22,7 @@
 ]
 SLOTS = 8
 BLOCKS = 4
-CORE, MLP, PAIRS, BASES = 0, 1, 2, 2 + SLOTS
+CORE, MLP, PAIRS, PLACES, BASES = 0, 1, 2, 2 + SLOTS, 2 + 2 * SLOTS
 
 
 def to_partner(value):
@@ -79,8 +79,27 @@
     return jnp.transpose(lanes).astype(jnp.bfloat16)
 
 
-def widened(rows, spread_ref, own):
-    return jnp.where(own, rank_product(rows, spread_ref[...]), 0.0).astype(jnp.bfloat16)
+def widened(rows, spread_ref, adapter, columns):
+    tile = rank_product(rows, spread_ref[...]).astype(jnp.bfloat16)
+    group = lax.broadcasted_iota(jnp.int32, tile.shape, 1) // ADAPTER_RANK
+    apart = (adapter - group.astype(jnp.float32)).astype(jnp.bfloat16)
+    step = tile.shape[1] // ADAPTER_RANK
+    zero = jnp.zeros_like(tile)
+    return jnp.concatenate(
+        [jnp.where(apart == first, tile, zero) for first in range(0, columns // ADAPTER_RANK, step)], axis=1
+    )
+
+
+def folded(products, adapter, spread_ref):
+    width = spread_ref.shape[1]
+    group = lax.broadcasted_iota(jnp.int32, (products.shape[0], width), 1) // ADAPTER_RANK
+    apart = adapter - group.astype(jnp.float32)
+    total = None
+    for first in range(0, products.shape[1], width):
+        part = products[:, first : first + width]
+        part = jnp.where(apart == float(first // ADAPTER_RANK), part, 0.0)
+        total = part if total is None else total + part
+    return across(spread_ref[...], total.astype(jnp.bfloat16))
 
 
 def cosine(angle):
@@ -138,7 +157,8 @@
 
 def rank_kernel(count, slots, info, *refs):
     x = jnp.concatenate([ref[...] for ref in refs[:count]], axis=0)
-    left_ref, meta_ref, slot_ref, fold_ref, held_ref, out_ref = refs[count:]
+    left_ref, meta_ref, slot_ref, fold_ref, held_ref = refs[count : count + 5]
+    out_ref = refs[-1]
     products = rank_product(x, left_ref[...])
     adapter = jnp.concatenate([meta_ref[k * 128 : (k + 1) * 128, 64:65] for k in slots], axis=0)
     chosen = jnp.where(slot_ref[...] == adapter, products, 0.0).astype(jnp.bfloat16)
@@ -180,36 +200,35 @@
     qkv_right_ref, up_right_ref, bias_ref, left_ref = refs[13:17]
     q_ref, k_ref, v_ref, hidden_ref, out_ref = refs[17:]
     rows = 256
-    column_id = lane_ids((rows, first_ref.shape[1]), ADAPTER_RANK)
+    columns = qkv_right_ref.shape[0]
     for block in range(BLOCKS):
         at = slice(block * rows, (block + 1) * rows)
-        own = column_id == meta_ref[at, 64:65]
+        adapter = meta_ref[at, 64:65]
         ranks = rank_rows(info, rank_ref, 2 * block, 2)
         total = block_rows_of(base_refs, block) + rank_product(
-            widened(ranks, first_ref, own), qkv_right_ref[...]
+            widened(ranks, first_ref, adapter, columns), qkv_right_ref[...]
         )
         table = turn_ref[at, :]
         q_ref[at, :] = (turn(total[:, :HEAD_SIZE], table) * HEAD_SIZE ** (-0.5)).astype(jnp.bfloat16)
         k_ref[at, :] = turn(total[:, HEAD_SIZE : 2 * HEAD_SIZE], table).astype(jnp.bfloat16)
         v_ref[at, :] = total[:, 2 * HEAD_SIZE :].astype(jnp.bfloat16)
-        x = block_rows_of(up_refs, block) + rank_product(widened(ranks, last_ref, own), up_right_ref[...])
-        x = x + bias_ref[...]
+        wide = widened(ranks, last_ref, adapter, columns)
+        x = block_rows_of(up_refs, block) + rank_product(wide, up_right_ref[...]) + bias_ref[...]
         inner = math.sqrt(2.0 / math.pi) * (x + 0.044715 * (x * x * x))
         hidden = (0.5 * x * (1.0 + jnp.tanh(inner))).astype(jnp.bfloat16)
         hidden_ref[at, :] = hidden
-        chosen = jnp.where(own, rank_product(hidden, left_ref[...]), 0.0).astype(jnp.bfloat16)
-        store_lanes(info, out_ref, across(last_ref[...], chosen), (2 * block, 2 * block + 1))
+        lanes = folded(rank_product(hidden, left_ref[...]), adapter, last_ref)
+        store_lanes(info, out_ref, lanes, (2 * block, 2 * block + 1))
 
 
 def far_kernel(first_row, info, *refs):
     shared_refs, (rank_ref, meta_ref, turn_ref, spread_ref, right_ref, k_ref, v_ref) = refs[:4], refs[4:]
     rows = 256
-    column_id = lane_ids((rows, spread_ref.shape[1]), ADAPTER_RANK)
     for block in range(BLOCKS):
         at = slice(block * rows, (block + 1) * rows)
         far_at = slice(first_row + block * rows, first_row + (block + 1) * rows)
-        own = column_id == meta_ref[far_at, 64:65]
-        wide = widened(rank_rows(info, rank_ref, 2 * block, 2), spread_ref, own)
+        ranks = rank_rows(info, rank_ref, 2 * block, 2)
+        wide = widened(ranks, spread_ref, meta_ref[far_at, 64:65], right_ref.shape[0])
         total = block_rows_of(shared_refs, block).astype(jnp.float32)
         total = total + rank_product(wide, right_ref[:, HEAD_SIZE:])
         k_ref[at, :] = turn(total[:, :HEAD_SIZE], turn_ref[far_at, :]).astype(jnp.bfloat16)
@@ -220,59 +239,75 @@
     q_ref, refs = refs[0], refs[1:]
     key_refs, value_refs, refs = refs[:req_count], refs[req_count : 2 * req_count], refs[2 * req_count :]
     meta_ref, spread_ref, left_ref, hidden_rank_ref, attended_ref, out_ref = refs[:6]
-    top_ref, sum_ref, acc_ref, fold_ref = refs[6:]
+    keys_ref, values_ref, top_ref, sum_ref, acc_ref, fold_ref = refs[6:]
     rows = 256
     pair = rows // 2
-    column_id = lane_ids((rows, left_ref.shape[1]), ADAPTER_RANK)
+    group_rows = q_ref.shape[0]
 
     def twice(lanes):
         return jnp.concatenate([lanes] * (HEAD_SIZE // lanes.shape[1]), axis=1)
 
+    def slot_rows(slot):
+        return pl.ds(pl.multiple_of(slot * pair, pair), pair)
+
+    for d in range(req_count):
+        for k in range(SLOTS):
+            at = slice((req_count - 1 - d) * group_rows + k * pair, (req_count - 1 - d) * group_rows + (k + 1) * pair)
+            slot = slot_rows(info[PLACES + k])
+            keys_ref[at, :] = key_refs[d][slot, :]
+            values_ref[at, :] = value_refs[d][slot, :]
+    first_token = info[BASES + info[PLACES]] - (req_count - 1) * group_rows
+
+    def places(shape, dim):
+        at = lax.broadcasted_iota(jnp.int32, shape, dim)
+        second = at >= pair
+        at = jnp.where(second, at - pair, at) + info[CORE] * (pair // 2)
+        at = jnp.where(at >= pair, at - pair, at)
+        return (at + jnp.where(second, pair, 0)).astype(jnp.float32)
+
+    key_place = places((1, rows), 1)
+    query_place = places((rows, 1), 0)
+
     def one(block, _):
-        at = pl.ds(pl.multiple_of(block * rows, rows), rows)
-        start = meta_ref[at, 0:1]
-        query = local_tokens(info, 2 * block, (rows, 1), 0)
-        q = q_ref[at, :]
-
-        def scores_of(d):
-            scores = across(q, key_refs[d][...])
-            key = jnp.concatenate(
-                [local_tokens(info, d * SLOTS + k, (1, rows), 1) for k in range(0, SLOTS, 2)], axis=1
+        slots = [slot_rows(info[PLACES + 2 * block + k]) for k in (0, 1)]
+
+        def both(ref):
+            return jnp.concatenate([ref[at, :] for at in slots], axis=0)
+
+        meta = both(meta_ref)
+        start = meta[:, 0:1]
+        number = (req_count - 1) * BLOCKS + block
+        query = query_place + (first_token + number * rows).astype(jnp.float32)
+        q = both(q_ref)
+        lowest = jnp.min(start).astype(jnp.int32) - first_token
+        top_ref[...] = jnp.full_like(top_ref, NEGATIVE_FILL)
+        sum_ref[...] = jnp.zeros_like(sum_ref)
+        acc_ref[...] = jnp.zeros_like(acc_ref)
+
+        def chunk(j, _):
+            at = pl.ds(pl.multiple_of(j * rows, rows), rows)
+            scores = across(q, keys_ref[at, :])
+            key = key_place + (first_token + j * rows).astype(jnp.float32)
+            allowed = jnp.logical_and(key <= query, key >= start)
+            scores = jnp.where(allowed, scores, NEGATIVE_FILL)
+            top = top_ref[...]
+            new_top = jnp.maximum(top, jnp.max(scores, axis=1, keepdims=True))
+            weights = jnp.where(allowed, jnp.exp(scores - twice(new_top)), 0.0)
+            scale = jnp.exp(top - new_top)
+            top_ref[...] = new_top
+            sum_ref[...] = sum_ref[...] * scale + jnp.sum(weights, axis=1, keepdims=True)
+            acc_ref[...] = acc_ref[...] * twice(scale) + rank_product(
+                weights.astype(jnp.bfloat16), values_ref[at, :]
             )
-            allowed = jnp.logical_and(key <= query, key >= start)
-            return jnp.where(allowed, scores, NEGATIVE_FILL), allowed
-
-        scores, _ = scores_of(0)
-        top = jnp.max(scores, axis=1, keepdims=True)
-        weights = jnp.exp(scores - top)
-        top_ref[...] = jnp.broadcast_to(top, top_ref.shape)
-        sum_ref[...] = jnp.broadcast_to(jnp.sum(weights, axis=1, keepdims=True), sum_ref.shape)
-        acc_ref[...] = rank_product(weights.astype(jnp.bfloat16), value_refs[0][...])
-        lowest = jnp.min(start)
-        for d in range(1, req_count):
-            highest = info[BASES + d * SLOTS] + pair
-            for k in range(1, SLOTS):
-                highest = jnp.maximum(highest, info[BASES + d * SLOTS + k] + pair)
-
-            @pl.when(highest.astype(jnp.float32) > lowest)
-            def _(d=d):
-                scores, allowed = scores_of(d)
-                top = top_ref[...]
-                new_top = jnp.maximum(top, jnp.max(scores, axis=1, keepdims=True))
-                weights = jnp.where(allowed, jnp.exp(scores - new_top[:, 0:1]), 0.0)
-                scale = jnp.exp(top - new_top)
-                top_ref[...] = new_top
-                sum_ref[...] = sum_ref[...] * scale + jnp.sum(weights, axis=1, keepdims=True)
-                acc_ref[...] = acc_ref[...] * twice(scale) + rank_product(
-                    weights.astype(jnp.bfloat16), value_refs[d][...]
-                )
-
+            return 0
+
+        lax.fori_loop(lowest // rows, number + 1, chunk, 0)
         attended = (acc_ref[...] / twice(sum_ref[...])).astype(jnp.bfloat16)
-        attended_ref[at, :] = attended
-        chosen = jnp.where(column_id == meta_ref[at, 64:65], rank_product(attended, left_ref[...]), 0.0)
-        store_lanes(
-            info, fold_ref, across(spread_ref[...], chosen.astype(jnp.bfloat16)), (2 * block, 2 * block + 1)
-        )
+        lanes = folded(rank_product(attended, left_ref[...]), meta[:, 64:65], spread_ref)
+        for k in (0, 1):
+            attended_ref[slots[k], :] = attended[k * pair : (k + 1) * pair]
+            at = pl.ds(pl.multiple_of((2 * block + k) * pair, pair), pair)
+            fold_ref[:, at] = swap_halves(info, lanes[:, k * pair : (k + 1) * pair])
         return 0
 
     lax.fori_loop(0, BLOCKS, one, 0)
@@ -309,7 +344,8 @@
     partner = info[MLP] + 1 - 2 * info[CORE]
     column_id = column_id + jnp.where(column_id < count, info[MLP] * count, (partner - 1) * count)
     own = column_id.astype(jnp.float32) == meta_ref[slot * pair : (slot + 1) * pair, 64:65]
-    wide = widened(rank_rows(info, rank_ref, slot, 1), spread_ref, own)
+    spread = rank_product(rank_rows(info, rank_ref, slot, 1), spread_ref[...])
+    wide = jnp.where(own, spread, 0.0).astype(jnp.bfloat16)
     width = 512
 
     def one(step, _):
@@ -389,14 +425,14 @@
     group = lax.axis_index("req")
     me = lax.axis_index("mlp")
     block_rows = 2 * pair_rows
-    table = np.zeros((req_count, 16, 2 + SLOTS * (1 + req_count)), np.int32)
+    table = np.zeros((req_count, 16, 2 + SLOTS * (2 + req_count)), np.int32)
     for g in range(req_count):
         for m in range(16):
             side = 2 * (m % 2) - 1
             steps = [0, 4] + [t for s in (1, 2, 3) for t in (side * s, -side * s)]
             pairs = [RING[(PLACE[m // 2] + t) % 8] for t in steps]
             firsts = [(g - d) * group_rows + p * pair_rows for d in range(req_count) for p in pairs]
-            table[g, m] = [m % 2, m] + pairs + firsts
+            table[g, m] = [m % 2, m] + pairs + [pairs.index(p) for p in range(SLOTS)] + firsts
     info = lax.dynamic_slice(jnp.asarray(table), (group, me, 0), (1, 1, table.shape[2])).reshape(-1)
 
     own = call(
@@ -426,8 +462,8 @@
     qkv_rows = query_key_weight.reshape(model_width, 3 * HEAD_SIZE)
     adapter_columns = query_key_value_right.shape[0]
     qkv_right = query_key_value_right.reshape(adapter_columns, 3 * HEAD_SIZE)
-    spread_first = spread_table(ADAPTER_RANK, 0, adapter_columns)
-    spread_last = spread_table(ADAPTER_RANK, ADAPTER_RANK, adapter_columns)
+    spread_first = spread_table(ADAPTER_RANK, 0, 128)
+    spread_last = spread_table(ADAPTER_RANK, ADAPTER_RANK, 128)
     near_right = output_adapter_right
     slot_columns = wide(jnp.repeat(slot_adapter, 2 * ADAPTER_RANK))[None, :]
     slot_columns = jnp.concatenate([slot_columns, to_partner(slot_columns)], axis=1)
@@ -440,10 +476,10 @@
 
     held = functools.partial(pltpu.VMEM, dtype=jnp.float32)
 
-    def add_ranks(part, slots, so_far):
+    def add_ranks(part, slots, so_far, ahead=()):
         return call(
             functools.partial(rank_kernel, len(part), slots),
-            list(part) + [pair_left, meta, slot_columns, spread_own, so_far],
+            list(part) + [pair_left, meta, slot_columns, spread_own, so_far, *ahead],
             [shape(32, group_rows)],
             info,
         )[0]
@@ -470,7 +506,7 @@
     tie = lax.optimization_barrier
     own_part = (own, other)
     ring_a, meta, turns, pair_left = tie((ring_a, meta, turns, pair_left))
-    ranks = add_ranks(own_part, (0,), jnp.zeros((32, group_rows), jnp.bfloat16))
+    ranks = add_ranks(own_part, (0,), jnp.zeros((32, group_rows), jnp.bfloat16), (qkv_rows, up_weight))
     ring_b, ranks = tie((ring_b, ranks))
     part = arrivals(ring_a, ring_b)
     ring_a, ring_b = along_ring(ring_a), along_ring(ring_b)
@@ -483,7 +519,7 @@
     far_early = to_groups(first[2])
     ranks = add_ranks(part, (4, 5), ranks)
     second = products_of(part)
-    ring_b, ranks, second, far_right = tie((ring_b, ranks, second, far_right))
+    ring_b, ranks, second, far_right, far_early = tie((ring_b, ranks, second, far_right, far_early))
     part = arrivals(ring_a, ring_b)
     ring_a = along_ring(ring_a)
     third = products_of(part[:2], 2000000000)
@@ -493,7 +529,7 @@
     ranks = add_ranks(part, (7, 1), ranks)
     moved = lax.ppermute(ranks, "mlp", [(i, i ^ 2) for i in range(16)])
     fourth = products_of(part)
-    ranks, fourth, far_early = tie((ranks + moved, fourth, far_early))
+    ranks, fourth = tie((ranks + moved, fourth))
     far_middle = to_groups(second[2])
     far_late = to_groups(jnp.concatenate([third[2], fourth[2]], axis=0))
     rank_in = sum_over_mlp(ranks, (4, 8))
@@ -530,6 +566,8 @@
         [shape(group_rows, HEAD_SIZE), shape(32, group_rows)],
         info,
         [
+            pltpu.VMEM((req_count * group_rows, HEAD_SIZE), jnp.bfloat16),
+            pltpu.VMEM((req_count * group_rows, HEAD_SIZE), jnp.bfloat16),
             held((block_rows, 128)),
             held((block_rows, 128)),
             held((block_rows, HEAD_SIZE)),

time: 169 us -> 163 us (0.964)
  waiting for transfers between devices: 50.1 us -> 40.9 us
  starting transfers between devices: 37.4 us -> 41.9 us
  Pallas kernels: 67.8 us -> 65.1 us
  local copies, waits for them, and re-layouts: 7.23 us -> 9.4 us
    ppermute x14, waiting for transfers between devices: 38 us -> 30.3 us  [along_ring(): return lax.ppermute(value, 'mlp', RING_PERM)]
    ppermute x14, starting transfers between devices: 14.3 us -> 17.3 us  [along_ring(): return lax.ppermute(value, 'mlp', RING_PERM)]
    pallas_call x23, Pallas kernels: 67.8 us -> 65.1 us  [call(): pl.pallas_call(kernel, in_specs=specs, out_specs=[vmem] * len(outs), out_...]
    unnamed x50 -> x46, local copies, waits for them, and re-layouts: 6.14 us -> 8.31 us
  transfers between devices with their start and end apart: 41 -> 41, of which waited for: 18 -> 16; matrix products, arithmetic and copies ran while one was open for 3% -> 3% of each run, Pallas kernels for 35% -> 32%
where the time goes in v2:
time: 163 us
  Pallas kernels  65.1 us (40%)
  starting transfers between devices  41.9 us (26%)
  waiting for transfers between devices  40.9 us (25%)
  local copies, waits for them, and re-layouts  9.4 us (6%)
  other arithmetic  4.92 us (3%)
    pallas_call x23, Pallas kernels, call(): pl.pallas_call(kernel, in_specs=specs, out_specs=[vmem] * len(outs), out_...  65.1 us
    ppermute x14, waiting for transfers between devices, along_ring(): return lax.ppermute(value, 'mlp', RING_PERM)  30.3 us
    ppermute x14, starting transfers between devices, along_ring(): return lax.ppermute(value, 'mlp', RING_PERM)  17.3 us
    ppermute x4, starting transfers between devices, to_group(): lax.ppermute(value, 'req', [(g, g + d) for g in range(req_count - d)])  10.6 us
    unnamed x46, local copies, waits for them, and re-layouts  8.31 us
    ppermute x4, starting transfers between devices, per_device(): moved = lax.ppermute(rank_out, 'mlp', [(i, i ^ bit) for i in range(16)])  5.93 us
    ppermute x2, waiting for transfers between devices, sum_over_mlp(): lax.ppermute(value, 'mlp', [(i, i ^ bit) for i in range(16)])  5.31 us
    ppermute x2, starting transfers between devices, sum_over_mlp(): lax.ppermute(value, 'mlp', [(i, i ^ bit) for i in range(16)])  4.25 us
  transfers between devices with their start and end apart: 41, of which 16 were waited for; matrix products, arithmetic and copies ran while one was open for 3% of the time, Pallas kernels for 32%

profile of v2, /device:TPU:0, one launch (start us, length us, event | category | flops | bytes accessed | tf_op | source)
XLA Modules:
  0.0 162.9 jit_solution(9617107590563908593)
XLA Ops:
  3.6 3.0 %collective-permute-start.2 = (bf16[64,4096]{1,0:T(8,128)(2,1)S(1)}, bf16[64,4096]{1,0:T(8,128)(2,1)}, u32[]{:S(2)}, u32[]{:S(2)}) collective-permute-start(bf16[64,4096]{1,0:T(8,128)(2,1)S(1)} %shard_map.217.refs_0_), channel_id=1, source_target_pairs={{0,4},{4,8},{8,12},{12,14},{14,10},{10,6},{6,2},{2,0},{1,3},{5,1},... | collective-permute-start | bytes 1572872 | tf_op jit(solution)/shard_map/ppermute | solution.py:33
  17.3 2.8 %copy-done = bf16[4096,1,768]{2,0,1:T(8,128)(2,1)S(1)} copy-done((bf16[4096,1,768]{2,0,1:T(8,128)(2,1)S(1)}, bf16[4096,1,768]{2,0,1:T(8,128)(2,1)}, u32[]{:S(2)}) %copy-start) | copy-done | bytes 6291480
  28.6 5.3 %shard_map.221 = (f32[384,768]{1,0:T(8,128)S(1)}, f32[384,512]{1,0:T(8,128)S(1)}, bf16[384,512]{1,0:T(8,128)(2,1)S(1)}) custom-call(bf16[64,4096]{1,0:T(8,128)(2,1)S(1)} %shard_map.217.refs_0_, bf16[64,4096]{1,0:T(8,128)(2,1)S(1)} %collective-permute-done.refs_1_, bf16[64,4096]{1,0:T(8,128)(2,1)} %collective-permute-done.2.refs_0_.refs_2_, ...), custom_call_target="tpu_custom_call" | custom-call | flops 1000 | bytes 1000 | tf_op jit(solution)/shard_map/pallas_call | solution.py:371
  38.7 3.4 %collective-permute-start.13 = (bf16[384,512]{1,0:T(8,128)(2,1)S(1)}, bf16[384,512]{1,0:T(8,128)(2,1)S(1)}, u32[]{:S(2)}, u32[]{:S(2)}) collective-permute-start(bf16[384,512]{1,0:T(8,128)(2,1)S(1)} %get-tuple-element.106), channel_id=1, source_target_pairs={{0,16},{1,17},{2,18},{3,19},{4,20},{5,21},{6,22},{7,23},{8,24},{9,... | collective-permute-start | bytes 1179656 | tf_op jit(solution)/shard_map/ppermute | solution.py:475
  43.9 2.9 %shard_map.223 = (f32[256,768]{1,0:T(8,128)S(1)}, f32[256,512]{1,0:T(8,128)S(1)}, bf16[256,512]{1,0:T(8,128)(2,1)S(1)}) custom-call(bf16[64,4096]{1,0:T(8,128)(2,1)S(1)} %collective-permute-done.9.refs_0_, bf16[64,4096]{1,0:T(8,128)(2,1)S(1)} %collective-permute-done.5.refs_1_, bf16[64,4096]{1,0:T(8,128)(2,1)S(1)} %collective-permute-done.10.refs_2_, ...), custom_call_target="tpu_custom_call" | custom-call | flops 1000 | bytes 1000 | tf_op jit(solution)/shard_map/pallas_call | solution.py:371
  57.4 2.9 %shard_map.227 = (f32[256,768]{1,0:T(8,128)S(1)}, f32[256,512]{1,0:T(8,128)S(1)}, bf16[256,512]{1,0:T(8,128)(2,1)S(1)}) custom-call(bf16[64,4096]{1,0:T(8,128)(2,1)S(1)} %collective-permute-done.16.refs_0_, bf16[64,4096]{1,0:T(8,128)(2,1)S(1)} %collective-permute-done.17.refs_1_, bf16[64,4096]{1,0:T(8,128)(2,1)S(1)} %collective-permute-done.15.refs_2_, ...), custom_call_target="tpu_custom_call" | custom-call | flops 1000 | bytes 1000 | tf_op jit(solution)/shard_map/pallas_call | solution.py:371
  61.0 4.4 %collective-permute-start.23 = (bf16[384,512]{1,0:T(8,128)(2,1)S(1)}, bf16[384,512]{1,0:T(8,128)(2,1)S(1)}, u32[]{:S(2)}, u32[]{:S(2)}) collective-permute-start(bf16[384,512]{1,0:T(8,128)(2,1)S(1)} %pad_maximum_fusion.1), channel_id=1, source_target_pairs={{0,16},{1,17},{2,18},{3,19},{4,20},{5,21},{6,22},{7,23},{8,24},{9,... | collective-permute-start | bytes 1179656 | tf_op jit(solution)/shard_map/ppermute | solution.py:475
  68.3 2.7 %collective-permute-done.20 = bf16[32,1024]{1,0:T(8,128)(2,1)S(1)} collective-permute-done((bf16[32,1024]{1,0:T(8,128)(2,1)S(1)}, bf16[32,1024]{1,0:T(8,128)(2,1)S(1)}, u32[]{:S(2)}, u32[]{:S(2)}) %collective-permute-start.20) | collective-permute-done | bytes 65568 | tf_op jit(solution)/shard_map/ppermute | solution.py:388
  71.0 2.6 %collective-permute-start.21 = (bf16[32,1024]{1,0:T(8,128)(2,1)S(1)}, bf16[32,1024]{1,0:T(8,128)(2,1)S(1)}, u32[]{:S(2)}, u32[]{:S(2)}) collective-permute-start(bf16[32,1024]{1,0:T(8,128)(2,1)S(1)} %add.62), channel_id=1, source_target_pairs={{0,8},{1,9},{2,10},{3,11},{4,12},{5,13},{6,14},{7,15},{8,0},{9,1},... | collective-permute-start | bytes 196616 | tf_op jit(solution)/shard_map/ppermute | solution.py:388
  73.7 2.6 %collective-permute-done.21 = bf16[32,1024]{1,0:T(8,128)(2,1)S(1)} collective-permute-done((bf16[32,1024]{1,0:T(8,128)(2,1)S(1)}, bf16[32,1024]{1,0:T(8,128)(2,1)S(1)}, u32[]{:S(2)}, u32[]{:S(2)}) %collective-permute-start.21) | collective-permute-done | bytes 65568 | tf_op jit(solution)/shard_map/ppermute | solution.py:388
  77.9 7.3 %shard_map.228 = (bf16[1024,256]{1,0:T(8,128)(2,1)S(1)}, bf16[1024,256]{1,0:T(8,128)(2,1)S(1)}, bf16[1024,256]{1,0:T(8,128)(2,1)S(1)}, bf16[1024,512]{1,0:T(8,128)(2,1)S(1)}, bf16[32,1024]{1,0:T(8,128)(2,1)S(1)}) custom-call(s32[34]{0:T(128)S(1)} %dynamic-slice_bitcast_fusion.info, f32[384,768]{1,0:T(8,128)S(1)} %get-tuple-element.100.refs_0_, ...), custom_call_target="tpu_custom_call" | custom-call | flops 1000 | bytes 1000 | tf_op jit(solution)/shard_map/pallas_call | solution.py:371
  85.3 2.6 %shard_map.229 = (bf16[1024,256]{1,0:T(8,128)(2,1)S(1)}, bf16[1024,256]{1,0:T(8,128)(2,1)S(1)}) custom-call(s32[34]{0:T(128)S(1)} %dynamic-slice_bitcast_fusion.info, bf16[384,512]{1,0:T(8,128)(2,1)S(1)} %collective-permute-done.13.refs_0_, bf16[256,512]{1,0:T(8,128)(2,1)S(1)} %collective-permute-done.22.refs_1_, bf16[128,512]{1,0:T(8,128)(2,1)S(1)} %slice.12.refs_2_, ...), custom_call_target="tpu_custom_call" | custom-call | flops 1000 | bytes 1000 | tf_op jit(solution)/shard_map/pallas_call | solution.py:371
  87.9 8.4 %shard_map.230 = (bf16[1024,256]{1,0:T(8,128)(2,1)S(1)}, bf16[32,1024]{1,0:T(8,128)(2,1)S(1)}) custom-call(s32[34]{0:T(128)S(1)} %dynamic-slice_bitcast_fusion.info, bf16[1024,256]{1,0:T(8,128)(2,1)S(1)} %get-tuple-element.126.refs_0_, bf16[1024,256]{1,0:T(8,128)(2,1)S(1)} %get-tuple-element.127.refs_1_, bf16[1024,256]{1,0:T(8,128)(2,1)S(1)} %get-tuple-element.132.refs_2_, ...), custom_call_target="tpu_custom_call" | custom-call | flops 1000 | bytes 1000 | tf_op jit(solution)/shard_map/pallas_call | solution.py:371
  96.4 3.1 %shard_map.231 = (f32[192,4096]{1,0:T(8,128)S(1)}, bf16[64,4096]{1,0:T(8,128)(2,1)S(1)}) custom-call(bf16[1024,256]{1,0:T(8,128)(2,1)S(1)} %get-tuple-element.152.attended_ref, bf16[1024,512]{1,0:T(8,128)(2,1)S(1)} %get-tuple-element.138.hidden_ref, bf16[256,4096]{1,0:T(8,128)(2,1)S(1)} %bitcast.22, bf16[512,4096]{1,0:T(8,128)(2,1)S(1)} %copy-done.3), custom_call_target="tpu_custom_call" | custom-call | flops 1000 | bytes 1000 | tf_op jit(solution)/shard_map/pallas_call | solution.py:371
  100.5 3.0 %shard_map.232 = (f32[128,4096]{1,0:T(8,128)S(1)}, bf16[128,4096]{1,0:T(8,128)(2,1)S(1)}) custom-call(bf16[1024,256]{1,0:T(8,128)(2,1)S(1)} %get-tuple-element.152.attended_ref, bf16[1024,512]{1,0:T(8,128)(2,1)S(1)} %get-tuple-element.138.hidden_ref, bf16[256,4096]{1,0:T(8,128)(2,1)S(1)} %bitcast.23, bf16[512,4096]{1,0:T(8,128)(2,1)S(1)} %copy-done.3), custom_call_target="tpu_custom_call" | custom-call | flops 1000 | bytes 1000 | tf_op jit(solution)/shard_map/pallas_call | solution.py:371
  106.0 3.0 %shard_map.233 = (f32[128,4096]{1,0:T(8,128)S(1)}, bf16[128,4096]{1,0:T(8,128)(2,1)S(1)}) custom-call(bf16[1024,256]{1,0:T(8,128)(2,1)S(1)} %get-tuple-element.152.attended_ref, bf16[1024,512]{1,0:T(8,128)(2,1)S(1)} %get-tuple-element.138.hidden_ref, bf16[256,4096]{1,0:T(8,128)(2,1)S(1)} %bitcast.24, bf16[512,4096]{1,0:T(8,128)(2,1)S(1)} %copy-done.3), custom_call_target="tpu_custom_call" | custom-call | flops 1000 | bytes 1000 | tf_op jit(solution)/shard_map/pallas_call | solution.py:371
  109.6 3.3 %collective-permute-start.29 = (bf16[32,1024]{1,0:T(8,128)(2,1)S(1)}, bf16[32,1024]{1,0:T(8,128)(2,1)S(1)}, u32[]{:S(2)}, u32[]{:S(2)}) collective-permute-start(bf16[32,1024]{1,0:T(8,128)(2,1)S(1)} %add.66), channel_id=1, source_target_pairs={{0,8},{1,9},{2,10},{3,11},{4,12},{5,13},{6,14},{7,15},{8,0},{9,1},... | collective-permute-start | bytes 196616 | tf_op jit(solution)/shard_map/ppermute | solution.py:589
  112.9 3.1 %shard_map.234 = (f32[128,4096]{1,0:T(8,128)S(1)}, bf16[128,4096]{1,0:T(8,128)(2,1)S(1)}) custom-call(bf16[1024,256]{1,0:T(8,128)(2,1)S(1)} %get-tuple-element.152.attended_ref, bf16[1024,512]{1,0:T(8,128)(2,1)S(1)} %get-tuple-element.138.hidden_ref, bf16[256,4096]{1,0:T(8,128)(2,1)S(1)} %bitcast.25, bf16[512,4096]{1,0:T(8,128)(2,1)S(1)} %copy-done.3), custom_call_target="tpu_custom_call" | custom-call | flops 1000 | bytes 1000 | tf_op jit(solution)/shard_map/pallas_call | solution.py:371
  128.8 5.0 %collective-permute-done.37 = bf16[64,4096]{1,0:T(8,128)(2,1)S(1)} collective-permute-done((bf16[64,4096]{1,0:T(8,128)(2,1)S(1)}, bf16[64,4096]{1,0:T(8,128)(2,1)S(1)}, u32[]{:S(2)}, u32[]{:S(2)}) %collective-permute-start.37) | collective-permute-done | bytes 524320 | tf_op jit(solution)/shard_map/ppermute | solution.py:33
  136.8 2.6 %collective-permute-done.32 = bf16[64,4096]{1,0:T(8,128)(2,1)S(1)} collective-permute-done((bf16[64,4096]{1,0:T(8,128)(2,1)S(1)}, bf16[64,4096]{1,0:T(8,128)(2,1)S(1)}, u32[]{:S(2)}, u32[]{:S(2)}) %collective-permute-start.32) | collective-permute-done | bytes 524320 | tf_op jit(solution)/shard_map/ppermute | solution.py:33
  140.0 5.0 %collective-permute-done.38 = bf16[64,4096]{1,0:T(8,128)(2,1)S(1)} collective-permute-done((bf16[64,4096]{1,0:T(8,128)(2,1)S(1)}, bf16[64,4096]{1,0:T(8,128)(2,1)S(1)}, u32[]{:S(2)}, u32[]{:S(2)}) %collective-permute-start.38) | collective-permute-done | bytes 524320 | tf_op jit(solution)/shard_map/ppermute | solution.py:33
  145.6 5.0 %collective-permute-done.34 = bf16[64,4096]{1,0:T(8,128)(2,1)S(1)} collective-permute-done((bf16[64,4096]{1,0:T(8,128)(2,1)S(1)}, bf16[64,4096]{1,0:T(8,128)(2,1)S(1)}, u32[]{:S(2)}, u32[]{:S(2)}) %collective-permute-start.34) | collective-permute-done | bytes 524320 | tf_op jit(solution)/shard_map/ppermute | solution.py:33
  151.2 5.0 %collective-permute-done.39 = bf16[64,4096]{1,0:T(8,128)(2,1)S(1)} collective-permute-done((bf16[64,4096]{1,0:T(8,128)(2,1)S(1)}, bf16[64,4096]{1,0:T(8,128)(2,1)S(1)}, u32[]{:S(2)}, u32[]{:S(2)}) %collective-permute-start.39) | collective-permute-done | bytes 524320 | tf_op jit(solution)/shard_map/ppermute | solution.py:33
  158.7 3.2 %collective-permute-done.36 = bf16[64,4096]{1,0:T(8,128)(2,1)S(1)} collective-permute-done((bf16[64,4096]{1,0:T(8,128)(2,1)S(1)}, bf16[64,4096]{1,0:T(8,128)(2,1)S(1)}, u32[]{:S(2)}, u32[]{:S(2)}) %collective-permute-start.36) | collective-permute-done | bytes 524320 | tf_op jit(solution)/shard_map/ppermute | solution.py:33
  (156 shorter events, 70.1 us)
Async XLA Ops:
  0.0 13.8 %collective-permute-start.3 = (bf16[4096,128]{1,0:T(8,128)(2,1)}, bf16[4096,128]{1,0:T(8,128)(2,1)}, u32[]{:S(2)}, u32[]{:S(2)}) collective-permute-start(bf16[4096,128]{1,0:T(8,128)(2,1)} %param.32), channel_id=1, source_target_pairs={{0,1},{1,0},{2,3},{3,2},{4,5},{5,4},{6,7},{7,6},{8,9},{9,8},{10,11... | collective-permute-start | bytes 3145736 | tf_op jit(solution)/shard_map/ppermute | solution.py:29
  3.6 12.0 %collective-permute-start.2 = (bf16[64,4096]{1,0:T(8,128)(2,1)S(1)}, bf16[64,4096]{1,0:T(8,128)(2,1)}, u32[]{:S(2)}, u32[]{:S(2)}) collective-permute-start(bf16[64,4096]{1,0:T(8,128)(2,1)S(1)} %shard_map.217.refs_0_), channel_id=1, source_target_pairs={{0,4},{4,8},{8,12},{12,14},{14,10},{10,6},{6,2},{2,0},{1,3},{5,1},... | collective-permute-start | bytes 1572872 | tf_op jit(solution)/shard_map/ppermute | solution.py:33
  7.4 9.8 %collective-permute-start.4 = (f32[1,128]{1,0:T(1,128)S(1)}, f32[1,128]{1,0:T(1,128)S(1)}, u32[]{:S(2)}, u32[]{:S(2)}) collective-permute-start(f32[1,128]{1,0:T(1,128)S(1)} %convert_element_type.71), channel_id=1, source_target_pairs={{0,1},{1,0},{2,3},{3,2},{4,5},{5,4},{6,7},{7,6},{8,9},{9,8},{10,11... | collective-permute-start | bytes 1544 | tf_op jit(solution)/shard_map/ppermute | solution.py:29
  12.2 11.2 %collective-permute-start.1 = (bf16[64,4096]{1,0:T(8,128)(2,1)S(1)}, bf16[64,4096]{1,0:T(8,128)(2,1)S(1)}, u32[]{:S(2)}, u32[]{:S(2)}) collective-permute-start(bf16[64,4096]{1,0:T(8,128)(2,1)S(1)} %collective-permute-done.refs_1_), channel_id=1, source_target_pairs={{0,4},{4,8},{8,12},{12,14},{14,10},{10,6},{6,2},{2,0},{1,3},{5,1},... | collective-permute-start | bytes 1572872 | tf_op jit(solution)/shard_map/ppermute | solution.py:33
  15.6 11.4 %collective-permute-start.9 = (bf16[64,4096]{1,0:T(8,128)(2,1)}, bf16[64,4096]{1,0:T(8,128)(2,1)S(1)}, u32[]{:S(2)}, u32[]{:S(2)}) collective-permute-start(bf16[64,4096]{1,0:T(8,128)(2,1)} %collective-permute-done.2.refs_0_.refs_2_), channel_id=1, source_target_pairs={{0,4},{4,8},{8,12},{12,14},{14,10},{10,6},{6,2},{2,0},{1,3},{5,1},... | collective-permute-start | bytes 1572872 | tf_op jit(solution)/shard_map/ppermute | solution.py:33
  23.9 12.1 %collective-permute-start.5 = (bf16[64,4096]{1,0:T(8,128)(2,1)S(1)}, bf16[64,4096]{1,0:T(8,128)(2,1)S(1)}, u32[]{:S(2)}, u32[]{:S(2)}) collective-permute-start(bf16[64,4096]{1,0:T(8,128)(2,1)S(1)} %collective-permute-done.1.refs_1_.refs_3_), channel_id=1, source_target_pairs={{0,4},{4,8},{8,12},{12,14},{14,10},{10,6},{6,2},{2,0},{1,3},{5,1},... | collective-permute-start | bytes 1572872 | tf_op jit(solution)/shard_map/ppermute | solution.py:33
  25.4 22.8 %collective-permute-start.12 = (bf16[128,4096]{1,0:T(8,128)(2,1)S(1)}, bf16[128,4096]{1,0:T(8,128)(2,1)S(1)}, u32[]{:S(2)}, u32[]{:S(2)}) collective-permute-start(bf16[128,4096]{1,0:T(8,128)(2,1)S(1)} %copy-done.18), channel_id=1, source_target_pairs={{0,1},{1,0},{2,3},{3,2},{4,5},{5,4},{6,7},{7,6},{8,9},{9,8},{10,11... | collective-permute-start | bytes 3145736 | tf_op jit(solution)/shard_map/ppermute | solution.py:29
  27.0 11.7 %collective-permute-start.14 = (bf16[64,4096]{1,0:T(8,128)(2,1)S(1)}, bf16[64,4096]{1,0:T(8,128)(2,1)S(1)}, u32[]{:S(2)}, u32[]{:S(2)}) collective-permute-start(bf16[64,4096]{1,0:T(8,128)(2,1)S(1)} %collective-permute-done.9.refs_0_), channel_id=1, source_target_pairs={{0,4},{4,8},{8,12},{12,14},{14,10},{10,6},{6,2},{2,0},{1,3},{5,1},... | collective-permute-start | bytes 1572872 | tf_op jit(solution)/shard_map/ppermute | solution.py:33
  28.6 13.5 %collective-permute-start.11 = (bf16[64,4096]{1,0:T(8,128)(2,1)S(1)}, bf16[64,4096]{1,0:T(8,128)(2,1)S(1)}, u32[]{:S(2)}, u32[]{:S(2)}) collective-permute-start(bf16[64,4096]{1,0:T(8,128)(2,1)S(1)} %collective-permute-done.9.refs_0_), channel_id=1, source_target_pairs={{0,1},{1,0},{2,3},{3,2},{4,5},{5,4},{6,7},{7,6},{8,9},{9,8},{10,11... | collective-permute-start | bytes 1572872 | tf_op jit(solution)/shard_map/ppermute | solution.py:29
  36.6 13.3 %collective-permute-start.8 = (bf16[64,4096]{1,0:T(8,128)(2,1)S(1)}, bf16[64,4096]{1,0:T(8,128)(2,1)S(1)}, u32[]{:S(2)}, u32[]{:S(2)}) collective-permute-start(bf16[64,4096]{1,0:T(8,128)(2,1)S(1)} %collective-permute-done.5.refs_1_), channel_id=1, source_target_pairs={{0,4},{4,8},{8,12},{12,14},{14,10},{10,6},{6,2},{2,0},{1,3},{5,1},... | collective-permute-start | bytes 1572872 | tf_op jit(solution)/shard_map/ppermute | solution.py:33
  38.7 11.1 %collective-permute-start.13 = (bf16[384,512]{1,0:T(8,128)(2,1)S(1)}, bf16[384,512]{1,0:T(8,128)(2,1)S(1)}, u32[]{:S(2)}, u32[]{:S(2)}) collective-permute-start(bf16[384,512]{1,0:T(8,128)(2,1)S(1)} %get-tuple-element.106), channel_id=1, source_target_pairs={{0,16},{1,17},{2,18},{3,19},{4,20},{5,21},{6,22},{7,23},{8,24},{9,... | collective-permute-start | bytes 1179656 | tf_op jit(solution)/shard_map/ppermute | solution.py:475
  42.1 11.0 %collective-permute-start.15 = (bf16[64,4096]{1,0:T(8,128)(2,1)S(1)}, bf16[64,4096]{1,0:T(8,128)(2,1)S(1)}, u32[]{:S(2)}, u32[]{:S(2)}) collective-permute-start(bf16[64,4096]{1,0:T(8,128)(2,1)S(1)} %collective-permute-done.14.refs_0_), channel_id=1, source_target_pairs={{0,4},{4,8},{8,12},{12,14},{14,10},{10,6},{6,2},{2,0},{1,3},{5,1},... | collective-permute-start | bytes 1572872 | tf_op jit(solution)/shard_map/ppermute | solution.py:33
  61.0 24.2 %collective-permute-start.23 = (bf16[384,512]{1,0:T(8,128)(2,1)S(1)}, bf16[384,512]{1,0:T(8,128)(2,1)S(1)}, u32[]{:S(2)}, u32[]{:S(2)}) collective-permute-start(bf16[384,512]{1,0:T(8,128)(2,1)S(1)} %pad_maximum_fusion.1), channel_id=1, source_target_pairs={{0,16},{1,17},{2,18},{3,19},{4,20},{5,21},{6,22},{7,23},{8,24},{9,... | collective-permute-start | bytes 1179656 | tf_op jit(solution)/shard_map/ppermute | solution.py:475
  65.4 19.9 %collective-permute-start.22 = (bf16[256,512]{1,0:T(8,128)(2,1)S(1)}, bf16[256,512]{1,0:T(8,128)(2,1)S(1)}, u32[]{:S(2)}, u32[]{:S(2)}) collective-permute-start(bf16[256,512]{1,0:T(8,128)(2,1)S(1)} %get-tuple-element.129), channel_id=1, source_target_pairs={{0,16},{1,17},{2,18},{3,19},{4,20},{5,21},{6,22},{7,23},{8,24},{9,... | collective-permute-start | bytes 786440 | tf_op jit(solution)/shard_map/ppermute | solution.py:475
  104.1 12.6 %collective-permute-start.30 = (bf16[128,4096]{1,0:T(8,128)(2,1)S(1)}, bf16[128,4096]{1,0:T(8,128)(2,1)S(1)}, u32[]{:S(2)}, u32[]{:S(2)}) collective-permute-start(bf16[128,4096]{1,0:T(8,128)(2,1)S(1)} %get-tuple-element.156), channel_id=1, source_target_pairs={{0,1},{1,0},{2,3},{3,2},{4,5},{5,4},{6,7},{7,6},{8,9},{9,8},{10,11... | collective-permute-start | bytes 3145736 | tf_op jit(solution)/shard_map/ppermute | solution.py:29
  109.0 14.3 %collective-permute-start.33 = (bf16[128,4096]{1,0:T(8,128)(2,1)S(1)}, bf16[128,4096]{1,0:T(8,128)(2,1)S(1)}, u32[]{:S(2)}, u32[]{:S(2)}) collective-permute-start(bf16[128,4096]{1,0:T(8,128)(2,1)S(1)} %get-tuple-element.165), channel_id=1, source_target_pairs={{0,1},{1,0},{2,3},{3,2},{4,5},{5,4},{6,7},{7,6},{8,9},{9,8},{10,11... | collective-permute-start | bytes 3145736 | tf_op jit(solution)/shard_map/ppermute | solution.py:29
  118.9 9.2 %collective-permute-start.31 = (bf16[64,4096]{1,0:T(8,128)(2,1)S(1)}, bf16[64,4096]{1,0:T(8,128)(2,1)S(1)}, u32[]{:S(2)}, u32[]{:S(2)}) collective-permute-start(bf16[64,4096]{1,0:T(8,128)(2,1)S(1)} %shard_map.235), channel_id=1, source_target_pairs={{0,4},{4,8},{8,12},{12,14},{14,10},{10,6},{6,2},{2,0},{1,3},{5,1},... | collective-permute-start | bytes 1572872 | tf_op jit(solution)/shard_map/ppermute | solution.py:33
  119.4 14.9 %collective-permute-start.35 = (bf16[128,4096]{1,0:T(8,128)(2,1)S(1)}, bf16[128,4096]{1,0:T(8,128)(2,1)S(1)}, u32[]{:S(2)}, u32[]{:S(2)}) collective-permute-start(bf16[128,4096]{1,0:T(8,128)(2,1)S(1)} %get-tuple-element.168), channel_id=1, source_target_pairs={{0,1},{1,0},{2,3},{3,2},{4,5},{5,4},{6,7},{7,6},{8,9},{9,8},{10,11... | collective-permute-start | bytes 3145736 | tf_op jit(solution)/shard_map/ppermute | solution.py:29
  121.9 11.9 %collective-permute-start.37 = (bf16[64,4096]{1,0:T(8,128)(2,1)S(1)}, bf16[64,4096]{1,0:T(8,128)(2,1)S(1)}, u32[]{:S(2)}, u32[]{:S(2)}) collective-permute-start(bf16[64,4096]{1,0:T(8,128)(2,1)S(1)} %convert_element_type.79), channel_id=1, source_target_pairs={{0,4},{4,8},{8,12},{12,14},{14,10},{10,6},{6,2},{2,0},{1,3},{5,1},... | collective-permute-start | bytes 1572872 | tf_op jit(solution)/shard_map/ppermute | solution.py:33
  128.3 11.1 %collective-permute-start.32 = (bf16[64,4096]{1,0:T(8,128)(2,1)S(1)}, bf16[64,4096]{1,0:T(8,128)(2,1)S(1)}, u32[]{:S(2)}, u32[]{:S(2)}) collective-permute-start(bf16[64,4096]{1,0:T(8,128)(2,1)S(1)} %add_convert_fusion.6), channel_id=1, source_target_pairs={{0,4},{4,8},{8,12},{12,14},{14,10},{10,6},{6,2},{2,0},{1,3},{5,1},... | collective-permute-start | bytes 1572872 | tf_op jit(solution)/shard_map/ppermute | solution.py:33
  133.9 11.1 %collective-permute-start.38 = (bf16[64,4096]{1,0:T(8,128)(2,1)S(1)}, bf16[64,4096]{1,0:T(8,128)(2,1)S(1)}, u32[]{:S(2)}, u32[]{:S(2)}) collective-permute-start(bf16[64,4096]{1,0:T(8,128)(2,1)S(1)} %add_convert_fusion.3), channel_id=1, source_target_pairs={{0,4},{4,8},{8,12},{12,14},{14,10},{10,6},{6,2},{2,0},{1,3},{5,1},... | collective-permute-start | bytes 1572872 | tf_op jit(solution)/shard_map/ppermute | solution.py:33
  139.5 11.1 %collective-permute-start.34 = (bf16[64,4096]{1,0:T(8,128)(2,1)S(1)}, bf16[64,4096]{1,0:T(8,128)(2,1)S(1)}, u32[]{:S(2)}, u32[]{:S(2)}) collective-permute-start(bf16[64,4096]{1,0:T(8,128)(2,1)S(1)} %add_convert_fusion.5), channel_id=1, source_target_pairs={{0,4},{4,8},{8,12},{12,14},{14,10},{10,6},{6,2},{2,0},{1,3},{5,1},... | collective-permute-start | bytes 1572872 | tf_op jit(solution)/shard_map/ppermute | solution.py:33
  145.1 11.1 %collective-permute-start.39 = (bf16[64,4096]{1,0:T(8,128)(2,1)S(1)}, bf16[64,4096]{1,0:T(8,128)(2,1)S(1)}, u32[]{:S(2)}, u32[]{:S(2)}) collective-permute-start(bf16[64,4096]{1,0:T(8,128)(2,1)S(1)} %add_convert_fusion.2), channel_id=1, source_target_pairs={{0,4},{4,8},{8,12},{12,14},{14,10},{10,6},{6,2},{2,0},{1,3},{5,1},... | collective-permute-start | bytes 1572872 | tf_op jit(solution)/shard_map/ppermute | solution.py:33
  150.7 11.1 %collective-permute-start.36 = (bf16[64,4096]{1,0:T(8,128)(2,1)S(1)}, bf16[64,4096]{1,0:T(8,128)(2,1)S(1)}, u32[]{:S(2)}, u32[]{:S(2)}) collective-permute-start(bf16[64,4096]{1,0:T(8,128)(2,1)S(1)} %add_convert_fusion.4), channel_id=1, source_target_pairs={{0,4},{4,8},{8,12},{12,14},{14,10},{10,6},{6,2},{2,0},{1,3},{5,1},... | collective-permute-start | bytes 1572872 | tf_op jit(solution)/shard_map/ppermute | solution.py:33
  (39 other events, 301.9 us)

commit v3 on v2

--- a/solution.py
+++ b/solution.py
@@ -195,17 +195,21 @@
     return refs[0][128:] if block == 1 else refs[1][...]
 
 
+def two_blocks(refs, index):
+    return jnp.concatenate([block_rows_of(refs, 2 * index + k) for k in (0, 1)], axis=0)
+
+
 def inner_kernel(info, *refs):
     base_refs, up_refs, (rank_ref, meta_ref, turn_ref, first_ref, last_ref) = refs[:4], refs[4:8], refs[8:13]
     qkv_right_ref, up_right_ref, bias_ref, left_ref = refs[13:17]
     q_ref, k_ref, v_ref, hidden_ref, out_ref = refs[17:]
-    rows = 256
+    rows = 512
     columns = qkv_right_ref.shape[0]
-    for block in range(BLOCKS):
+    for block in range(BLOCKS // 2):
         at = slice(block * rows, (block + 1) * rows)
         adapter = meta_ref[at, 64:65]
-        ranks = rank_rows(info, rank_ref, 2 * block, 2)
-        total = block_rows_of(base_refs, block) + rank_product(
+        ranks = rank_rows(info, rank_ref, 4 * block, 4)
+        total = two_blocks(base_refs, block) + rank_product(
             widened(ranks, first_ref, adapter, columns), qkv_right_ref[...]
         )
         table = turn_ref[at, :]
@@ -213,23 +217,23 @@
         k_ref[at, :] = turn(total[:, HEAD_SIZE : 2 * HEAD_SIZE], table).astype(jnp.bfloat16)
         v_ref[at, :] = total[:, 2 * HEAD_SIZE :].astype(jnp.bfloat16)
         wide = widened(ranks, last_ref, adapter, columns)
-        x = block_rows_of(up_refs, block) + rank_product(wide, up_right_ref[...]) + bias_ref[...]
+        x = two_blocks(up_refs, block) + rank_product(wide, up_right_ref[...]) + bias_ref[...]
         inner = math.sqrt(2.0 / math.pi) * (x + 0.044715 * (x * x * x))
         hidden = (0.5 * x * (1.0 + jnp.tanh(inner))).astype(jnp.bfloat16)
         hidden_ref[at, :] = hidden
         lanes = folded(rank_product(hidden, left_ref[...]), adapter, last_ref)
-        store_lanes(info, out_ref, lanes, (2 * block, 2 * block + 1))
+        store_lanes(info, out_ref, lanes, range(4 * block, 4 * block + 4))
 
 
 def far_kernel(first_row, info, *refs):
     shared_refs, (rank_ref, meta_ref, turn_ref, spread_ref, right_ref, k_ref, v_ref) = refs[:4], refs[4:]
-    rows = 256
-    for block in range(BLOCKS):
+    rows = 512
+    for block in range(BLOCKS // 2):
         at = slice(block * rows, (block + 1) * rows)
         far_at = slice(first_row + block * rows, first_row + (block + 1) * rows)
-        ranks = rank_rows(info, rank_ref, 2 * block, 2)
+        ranks = rank_rows(info, rank_ref, 4 * block, 4)
         wide = widened(ranks, spread_ref, meta_ref[far_at, 64:65], right_ref.shape[0])
-        total = block_rows_of(shared_refs, block).astype(jnp.float32)
+        total = two_blocks(shared_refs, block).astype(jnp.float32)
         total = total + rank_product(wide, right_ref[:, HEAD_SIZE:])
         k_ref[at, :] = turn(total[:, :HEAD_SIZE], turn_ref[far_at, :]).astype(jnp.bfloat16)
         v_ref[at, :] = total[:, HEAD_SIZE:].astype(jnp.bfloat16)
@@ -239,13 +243,10 @@
     q_ref, refs = refs[0], refs[1:]
     key_refs, value_refs, refs = refs[:req_count], refs[req_count : 2 * req_count], refs[2 * req_count :]
     meta_ref, spread_ref, left_ref, hidden_rank_ref, attended_ref, out_ref = refs[:6]
-    keys_ref, values_ref, top_ref, sum_ref, acc_ref, fold_ref = refs[6:]
+    keys_ref, values_ref, scores_ref, top_ref, sum_ref, acc_ref, fold_ref = refs[6:]
     rows = 256
     pair = rows // 2
     group_rows = q_ref.shape[0]
-
-    def twice(lanes):
-        return jnp.concatenate([lanes] * (HEAD_SIZE // lanes.shape[1]), axis=1)
 
     def slot_rows(slot):
         return pl.ds(pl.multiple_of(slot * pair, pair), pair)
@@ -284,25 +285,29 @@
         sum_ref[...] = jnp.zeros_like(sum_ref)
         acc_ref[...] = jnp.zeros_like(acc_ref)
 
-        def chunk(j, _):
+        def score(j, _):
             at = pl.ds(pl.multiple_of(j * rows, rows), rows)
             scores = across(q, keys_ref[at, :])
             key = key_place + (first_token + j * rows).astype(jnp.float32)
             allowed = jnp.logical_and(key <= query, key >= start)
             scores = jnp.where(allowed, scores, NEGATIVE_FILL)
-            top = top_ref[...]
-            new_top = jnp.maximum(top, jnp.max(scores, axis=1, keepdims=True))
-            weights = jnp.where(allowed, jnp.exp(scores - twice(new_top)), 0.0)
-            scale = jnp.exp(top - new_top)
-            top_ref[...] = new_top
-            sum_ref[...] = sum_ref[...] * scale + jnp.sum(weights, axis=1, keepdims=True)
-            acc_ref[...] = acc_ref[...] * twice(scale) + rank_product(
-                weights.astype(jnp.bfloat16), values_ref[at, :]
-            )
+            scores_ref[:, at] = scores
+            top_ref[...] = jnp.maximum(top_ref[...], jnp.maximum(scores[:, :pair], scores[:, pair:]))
             return 0
 
-        lax.fori_loop(lowest // rows, number + 1, chunk, 0)
-        attended = (acc_ref[...] / twice(sum_ref[...])).astype(jnp.bfloat16)
+        lax.fori_loop(lowest // rows, number + 1, score, 0)
+        top = jnp.max(top_ref[...], axis=1, keepdims=True)
+
+        def weigh(j, _):
+            at = pl.ds(pl.multiple_of(j * rows, rows), rows)
+            weights = jnp.exp(scores_ref[:, at] - top)
+            sum_ref[...] = sum_ref[...] + (weights[:, :pair] + weights[:, pair:])
+            acc_ref[...] = acc_ref[...] + rank_product(weights.astype(jnp.bfloat16), values_ref[at, :])
+            return 0
+
+        lax.fori_loop(lowest // rows, number + 1, weigh, 0)
+        total = jnp.sum(sum_ref[...], axis=1, keepdims=True)
+        attended = (acc_ref[...] / total).astype(jnp.bfloat16)
         lanes = folded(rank_product(attended, left_ref[...]), meta[:, 64:65], spread_ref)
         for k in (0, 1):
             attended_ref[slots[k], :] = attended[k * pair : (k + 1) * pair]
@@ -321,8 +326,8 @@
     attended = attended_ref[block * rows : (block + 1) * rows, :]
     hidden = hidden_ref[block * rows : (block + 1) * rows, :]
 
-    def one(step, _):
-        at = pl.ds(pl.multiple_of(step * width, width), width)
+    for step in range(output_ref.shape[1] // width):
+        at = slice(step * width, (step + 1) * width)
         total = rank_product(attended, output_ref[:, at]) + rank_product(hidden, down_ref[:, at])
         if block:
             sent_ref[:, at] = total[:sent].astype(sent_ref.dtype)
@@ -330,9 +335,6 @@
         else:
             kept_ref[:, at] = total[: rows - sent]
             sent_ref[:, at] = total[rows - sent :].astype(sent_ref.dtype)
-        return 0
-
-    lax.fori_loop(0, output_ref.shape[1] // width, one, 0)
 
 
 def adapt_kernel(slot, first, info, rank_ref, meta_ref, spread_ref, right_ref, kept_ref, arrived_ref, *out_refs):
@@ -348,8 +350,8 @@
     wide = jnp.where(own, spread, 0.0).astype(jnp.bfloat16)
     width = 512
 
-    def one(step, _):
-        at = pl.ds(pl.multiple_of(step * width, width), width)
+    for step in range(right_ref.shape[1] // width):
+        at = slice(step * width, (step + 1) * width)
         if len(out_refs) == 1:
             total = rank_product(wide[:half], right_ref[:, at]) + kept_ref[first : first + half, at]
             total = total + arrived_ref[:, at].astype(jnp.float32)
@@ -358,9 +360,6 @@
             total = rank_product(wide, right_ref[:, at]) + kept_ref[:, at]
             out_refs[0][:, at] = total[:half] + arrived_ref[half:, at].astype(jnp.float32)
             out_refs[1][:, at] = total[half:] + arrived_ref[:half, at].astype(jnp.float32)
-        return 0
-
-    lax.fori_loop(0, right_ref.shape[1] // width, one, 0)
 
 
 def call(kernel, operands, outs, info=None, scratch=(), mib=24, flops=1000):
@@ -519,11 +518,12 @@
     far_early = to_groups(first[2])
     ranks = add_ranks(part, (4, 5), ranks)
     second = products_of(part)
-    ring_b, ranks, second, far_right, far_early = tie((ring_b, ranks, second, far_right, far_early))
+    ring_b, ranks, second, far_right = tie((ring_b, ranks, second, far_right))
     part = arrivals(ring_a, ring_b)
     ring_a = along_ring(ring_a)
-    third = products_of(part[:2], 2000000000)
-    ranks = add_ranks(part[:2], (6,), ranks)
+    held_rows, far_early = tie((part[:2], far_early))
+    third = products_of(held_rows, 2000000000)
+    ranks = add_ranks(held_rows, (6,), ranks)
     ring_a, ranks, third = tie((ring_a, ranks, third))
     part = part[2:] + (ring_a, to_partner(ring_a))
     ranks = add_ranks(part, (7, 1), ranks)
@@ -568,6 +568,7 @@
         [
             pltpu.VMEM((req_count * group_rows, HEAD_SIZE), jnp.bfloat16),
             pltpu.VMEM((req_count * group_rows, HEAD_SIZE), jnp.bfloat16),
+            held((block_rows, req_count * group_rows)),
             held((block_rows, 128)),
             held((block_rows, 128)),
             held((block_rows, HEAD_SIZE)),

time: 163 us -> 158 us (0.969)
  Pallas kernels: 65.1 us -> 53 us
  waiting for transfers between devices: 40.9 us -> 47.3 us
    pallas_call x23, Pallas kernels: 65.1 us -> 53 us  [call(): pl.pallas_call(kernel, in_specs=specs, out_specs=[vmem] * len(outs), out_...]
    ppermute x4, waiting for transfers between devices: 1.18 us -> 4.96 us  [per_device(): moved = lax.ppermute(rank_out, 'mlp', [(i, i ^ bit) for i in range(16)])]
    ppermute x14, waiting for transfers between devices: 30.3 us -> 33.3 us  [along_ring(): return lax.ppermute(value, 'mlp', RING_PERM)]
  transfers between devices with their start and end apart: 41 -> 41, of which waited for: 16 -> 17; matrix products, arithmetic and copies ran while one was open for 3% -> 3% of each run, Pallas kernels for 32% -> 26%
where the time goes in v3:
time: 158 us
  Pallas kernels  53 us (34%)
  waiting for transfers between devices  47.3 us (30%)
  starting transfers between devices  42.8 us (27%)
  local copies, waits for them, and re-layouts  9.4 us (6%)
  other arithmetic  4.92 us (3%)
    pallas_call x23, Pallas kernels, call(): pl.pallas_call(kernel, in_specs=specs, out_specs=[vmem] * len(outs), out_...  53 us
    ppermute x14, waiting for transfers between devices, along_ring(): return lax.ppermute(value, 'mlp', RING_PERM)  33.3 us
    ppermute x14, starting transfers between devices, along_ring(): return lax.ppermute(value, 'mlp', RING_PERM)  18.7 us
    ppermute x4, starting transfers between devices, to_group(): lax.ppermute(value, 'req', [(g, g + d) for g in range(req_count - d)])  10.6 us
    unnamed x46, local copies, waits for them, and re-layouts  8.31 us
    ppermute x4, starting transfers between devices, per_device(): moved = lax.ppermute(rank_out, 'mlp', [(i, i ^ bit) for i in range(16)])  5.65 us
    ppermute x2, waiting for transfers between devices, sum_over_mlp(): lax.ppermute(value, 'mlp', [(i, i ^ bit) for i in range(16)])  5.31 us
    ppermute x4, waiting for transfers between devices, per_device(): moved = lax.ppermute(rank_out, 'mlp', [(i, i ^ bit) for i in range(16)])  4.96 us
  transfers between devices with their start and end apart: 41, of which 17 were waited for; matrix products, arithmetic and copies ran while one was open for 3% of the time, Pallas kernels for 26%

profile of v3, /device:TPU:0, one launch (start us, length us, event | category | flops | bytes accessed | tf_op | source)
XLA Modules:
  0.0 158.1 jit_solution(2273785594567038630)
XLA Ops:
  3.6 3.0 %collective-permute-start.2 = (bf16[64,4096]{1,0:T(8,128)(2,1)S(1)}, bf16[64,4096]{1,0:T(8,128)(2,1)}, u32[]{:S(2)}, u32[]{:S(2)}) collective-permute-start(bf16[64,4096]{1,0:T(8,128)(2,1)S(1)} %shard_map.217.refs_0_), channel_id=1, source_target_pairs={{0,4},{4,8},{8,12},{12,14},{14,10},{10,6},{6,2},{2,0},{1,3},{5,1},... | collective-permute-start | bytes 1572872 | tf_op jit(solution)/shard_map/ppermute | solution.py:33
  9.6 2.5 %shard_map.218 = (f32[2048,128]{1,0:T(8,128)S(1)}, f32[2048,128]{1,0:T(8,128)S(1)}) custom-call(s32[34]{0:T(128)S(1)} %dynamic-slice_bitcast_fusion.info, f32[65,1]{1,0:T(8,128)S(1)} %copy.24.column_ref, f32[1,65]{1,0:T(1,128)S(1)} %get-tuple-element.179.row_ref, f32[1,65]{1,0:T(1,128)S(1)} %get-tuple-element.181.ids_ref, f32[8,128]{1,0:T(8,128)S(1)} %copy-done.16), custom_call_target="tpu_custom_call" | custom-call | flops 1000 | bytes 1000 | tf_op jit(solution)/shard_map/pallas_call | solution.py:370
  17.3 2.8 %copy-done = bf16[4096,1,768]{2,0,1:T(8,128)(2,1)S(1)} copy-done((bf16[4096,1,768]{2,0,1:T(8,128)(2,1)S(1)}, bf16[4096,1,768]{2,0,1:T(8,128)(2,1)}, u32[]{:S(2)}) %copy-start) | copy-done | bytes 6291480
  20.0 2.2 %copy-done.1 = bf16[4096,512]{1,0:T(8,128)(2,1)S(1)} copy-done((bf16[4096,512]{1,0:T(8,128)(2,1)S(1)}, bf16[4096,512]{1,0:T(8,128)(2,1)}, u32[]{:S(2)}) %copy-start.1) | copy-done | bytes 4194328
  28.6 5.3 %shard_map.221 = (f32[384,768]{1,0:T(8,128)S(1)}, f32[384,512]{1,0:T(8,128)S(1)}, bf16[384,512]{1,0:T(8,128)(2,1)S(1)}) custom-call(bf16[64,4096]{1,0:T(8,128)(2,1)S(1)} %shard_map.217.refs_0_, bf16[64,4096]{1,0:T(8,128)(2,1)S(1)} %collective-permute-done.refs_1_, bf16[64,4096]{1,0:T(8,128)(2,1)} %collective-permute-done.2.refs_0_.refs_2_, ...), custom_call_target="tpu_custom_call" | custom-call | flops 1000 | bytes 1000 | tf_op jit(solution)/shard_map/pallas_call | solution.py:370
  38.7 3.4 %collective-permute-start.15 = (bf16[384,512]{1,0:T(8,128)(2,1)S(1)}, bf16[384,512]{1,0:T(8,128)(2,1)S(1)}, u32[]{:S(2)}, u32[]{:S(2)}) collective-permute-start(bf16[384,512]{1,0:T(8,128)(2,1)S(1)} %get-tuple-element.110), channel_id=1, source_target_pairs={{0,16},{1,17},{2,18},{3,19},{4,20},{5,21},{6,22},{7,23},{8,24},{9,... | collective-permute-start | bytes 1179656 | tf_op jit(solution)/shard_map/ppermute | solution.py:474
  43.9 2.9 %shard_map.223 = (f32[256,768]{1,0:T(8,128)S(1)}, f32[256,512]{1,0:T(8,128)S(1)}, bf16[256,512]{1,0:T(8,128)(2,1)S(1)}) custom-call(bf16[64,4096]{1,0:T(8,128)(2,1)S(1)} %collective-permute-done.9.refs_0_, bf16[64,4096]{1,0:T(8,128)(2,1)S(1)} %collective-permute-done.5.refs_1_, bf16[64,4096]{1,0:T(8,128)(2,1)S(1)} %collective-permute-done.10.refs_2_, ...), custom_call_target="tpu_custom_call" | custom-call | flops 1000 | bytes 1000 | tf_op jit(solution)/shard_map/pallas_call | solution.py:370
  57.0 2.9 %shard_map.227 = (f32[256,768]{1,0:T(8,128)S(1)}, f32[256,512]{1,0:T(8,128)S(1)}, bf16[256,512]{1,0:T(8,128)(2,1)S(1)}) custom-call(bf16[64,4096]{1,0:T(8,128)(2,1)S(1)} %collective-permute-done.16.refs_0_, bf16[64,4096]{1,0:T(8,128)(2,1)S(1)} %collective-permute-done.17.refs_1_, bf16[64,4096]{1,0:T(8,128)(2,1)S(1)} %collective-permute-done.14.refs_2_, ...), custom_call_target="tpu_custom_call" | custom-call | flops 1000 | bytes 1000 | tf_op jit(solution)/shard_map/pallas_call | solution.py:370
  60.7 4.4 %collective-permute-start.23 = (bf16[384,512]{1,0:T(8,128)(2,1)S(1)}, bf16[384,512]{1,0:T(8,128)(2,1)S(1)}, u32[]{:S(2)}, u32[]{:S(2)}) collective-permute-start(bf16[384,512]{1,0:T(8,128)(2,1)S(1)} %pad_maximum_fusion.1), channel_id=1, source_target_pairs={{0,16},{1,17},{2,18},{3,19},{4,20},{5,21},{6,22},{7,23},{8,24},{9,... | collective-permute-start | bytes 1179656 | tf_op jit(solution)/shard_map/ppermute | solution.py:474
  68.0 2.7 %collective-permute-done.20 = bf16[32,1024]{1,0:T(8,128)(2,1)S(1)} collective-permute-done((bf16[32,1024]{1,0:T(8,128)(2,1)S(1)}, bf16[32,1024]{1,0:T(8,128)(2,1)S(1)}, u32[]{:S(2)}, u32[]{:S(2)}) %collective-permute-start.20) | collective-permute-done | bytes 65568 | tf_op jit(solution)/shard_map/ppermute | solution.py:387
  70.8 2.6 %collective-permute-start.21 = (bf16[32,1024]{1,0:T(8,128)(2,1)S(1)}, bf16[32,1024]{1,0:T(8,128)(2,1)S(1)}, u32[]{:S(2)}, u32[]{:S(2)}) collective-permute-start(bf16[32,1024]{1,0:T(8,128)(2,1)S(1)} %add.62), channel_id=1, source_target_pairs={{0,8},{1,9},{2,10},{3,11},{4,12},{5,13},{6,14},{7,15},{8,0},{9,1},... | collective-permute-start | bytes 196616 | tf_op jit(solution)/shard_map/ppermute | solution.py:387
  73.4 2.6 %collective-permute-done.21 = bf16[32,1024]{1,0:T(8,128)(2,1)S(1)} collective-permute-done((bf16[32,1024]{1,0:T(8,128)(2,1)S(1)}, bf16[32,1024]{1,0:T(8,128)(2,1)S(1)}, u32[]{:S(2)}, u32[]{:S(2)}) %collective-permute-start.21) | collective-permute-done | bytes 65568 | tf_op jit(solution)/shard_map/ppermute | solution.py:387
  77.6 6.5 %shard_map.228 = (bf16[1024,256]{1,0:T(8,128)(2,1)S(1)}, bf16[1024,256]{1,0:T(8,128)(2,1)S(1)}, bf16[1024,256]{1,0:T(8,128)(2,1)S(1)}, bf16[1024,512]{1,0:T(8,128)(2,1)S(1)}, bf16[32,1024]{1,0:T(8,128)(2,1)S(1)}) custom-call(s32[34]{0:T(128)S(1)} %dynamic-slice_bitcast_fusion.info, f32[384,768]{1,0:T(8,128)S(1)} %get-tuple-element.102.refs_0_, ...), custom_call_target="tpu_custom_call" | custom-call | flops 1000 | bytes 1000 | tf_op jit(solution)/shard_map/pallas_call | solution.py:370
  84.2 2.3 %shard_map.229 = (bf16[1024,256]{1,0:T(8,128)(2,1)S(1)}, bf16[1024,256]{1,0:T(8,128)(2,1)S(1)}) custom-call(s32[34]{0:T(128)S(1)} %dynamic-slice_bitcast_fusion.info, bf16[384,512]{1,0:T(8,128)(2,1)S(1)} %collective-permute-done.15.refs_0_, bf16[256,512]{1,0:T(8,128)(2,1)S(1)} %collective-permute-done.22.refs_1_, bf16[128,512]{1,0:T(8,128)(2,1)S(1)} %slice.12.refs_2_, ...), custom_call_target="tpu_custom_call" | custom-call | flops 1000 | bytes 1000 | tf_op jit(solution)/shard_map/pallas_call | solution.py:370
  86.5 7.8 %shard_map.230 = (bf16[1024,256]{1,0:T(8,128)(2,1)S(1)}, bf16[32,1024]{1,0:T(8,128)(2,1)S(1)}) custom-call(s32[34]{0:T(128)S(1)} %dynamic-slice_bitcast_fusion.info, bf16[1024,256]{1,0:T(8,128)(2,1)S(1)} %get-tuple-element.130.refs_0_, bf16[1024,256]{1,0:T(8,128)(2,1)S(1)} %get-tuple-element.131.refs_1_, bf16[1024,256]{1,0:T(8,128)(2,1)S(1)} %get-tuple-element.136.refs_2_, ...), custom_call_target="tpu_custom_call" | custom-call | flops 1000 | bytes 1000 | tf_op jit(solution)/shard_map/pallas_call | solution.py:370
  105.6 3.0 %collective-permute-start.29 = (bf16[32,1024]{1,0:T(8,128)(2,1)S(1)}, bf16[32,1024]{1,0:T(8,128)(2,1)S(1)}, u32[]{:S(2)}, u32[]{:S(2)}) collective-permute-start(bf16[32,1024]{1,0:T(8,128)(2,1)S(1)} %add.66), channel_id=1, source_target_pairs={{0,8},{1,9},{2,10},{3,11},{4,12},{5,13},{6,14},{7,15},{8,0},{9,1},... | collective-permute-start | bytes 196616 | tf_op jit(solution)/shard_map/ppermute | solution.py:590
  110.6 2.2 %collective-permute-done.29 = bf16[32,1024]{1,0:T(8,128)(2,1)S(1)} collective-permute-done((bf16[32,1024]{1,0:T(8,128)(2,1)S(1)}, bf16[32,1024]{1,0:T(8,128)(2,1)S(1)}, u32[]{:S(2)}, u32[]{:S(2)}) %collective-permute-start.29) | collective-permute-done | bytes 65568 | tf_op jit(solution)/shard_map/ppermute | solution.py:590
  118.7 4.6 %collective-permute-done.31 = bf16[64,4096]{1,0:T(8,128)(2,1)S(1)} collective-permute-done((bf16[64,4096]{1,0:T(8,128)(2,1)S(1)}, bf16[64,4096]{1,0:T(8,128)(2,1)S(1)}, u32[]{:S(2)}, u32[]{:S(2)}) %collective-permute-start.31) | collective-permute-done | bytes 524320 | tf_op jit(solution)/shard_map/ppermute | solution.py:33
  124.3 4.7 %collective-permute-done.37 = bf16[64,4096]{1,0:T(8,128)(2,1)S(1)} collective-permute-done((bf16[64,4096]{1,0:T(8,128)(2,1)S(1)}, bf16[64,4096]{1,0:T(8,128)(2,1)S(1)}, u32[]{:S(2)}, u32[]{:S(2)}) %collective-permute-start.37) | collective-permute-done | bytes 524320 | tf_op jit(solution)/shard_map/ppermute | solution.py:33
  131.1 3.5 %collective-permute-done.32 = bf16[64,4096]{1,0:T(8,128)(2,1)S(1)} collective-permute-done((bf16[64,4096]{1,0:T(8,128)(2,1)S(1)}, bf16[64,4096]{1,0:T(8,128)(2,1)S(1)}, u32[]{:S(2)}, u32[]{:S(2)}) %collective-permute-start.32) | collective-permute-done | bytes 524320 | tf_op jit(solution)/shard_map/ppermute | solution.py:33
  135.5 4.7 %collective-permute-done.38 = bf16[64,4096]{1,0:T(8,128)(2,1)S(1)} collective-permute-done((bf16[64,4096]{1,0:T(8,128)(2,1)S(1)}, bf16[64,4096]{1,0:T(8,128)(2,1)S(1)}, u32[]{:S(2)}, u32[]{:S(2)}) %collective-permute-start.38) | collective-permute-done | bytes 524320 | tf_op jit(solution)/shard_map/ppermute | solution.py:33
  141.1 4.7 %collective-permute-done.34 = bf16[64,4096]{1,0:T(8,128)(2,1)S(1)} collective-permute-done((bf16[64,4096]{1,0:T(8,128)(2,1)S(1)}, bf16[64,4096]{1,0:T(8,128)(2,1)S(1)}, u32[]{:S(2)}, u32[]{:S(2)}) %collective-permute-start.34) | collective-permute-done | bytes 524320 | tf_op jit(solution)/shard_map/ppermute | solution.py:33
  146.7 4.7 %collective-permute-done.39 = bf16[64,4096]{1,0:T(8,128)(2,1)S(1)} collective-permute-done((bf16[64,4096]{1,0:T(8,128)(2,1)S(1)}, bf16[64,4096]{1,0:T(8,128)(2,1)S(1)}, u32[]{:S(2)}, u32[]{:S(2)}) %collective-permute-start.39) | collective-permute-done | bytes 524320 | tf_op jit(solution)/shard_map/ppermute | solution.py:33
  152.9 4.2 %collective-permute-done.36 = bf16[64,4096]{1,0:T(8,128)(2,1)S(1)} collective-permute-done((bf16[64,4096]{1,0:T(8,128)(2,1)S(1)}, bf16[64,4096]{1,0:T(8,128)(2,1)S(1)}, u32[]{:S(2)}, u32[]{:S(2)}) %collective-permute-start.36) | collective-permute-done | bytes 524320 | tf_op jit(solution)/shard_map/ppermute | solution.py:33
  (156 shorter events, 67.2 us)
Async XLA Ops:
  0.0 13.8 %collective-permute-start.3 = (bf16[4096,128]{1,0:T(8,128)(2,1)}, bf16[4096,128]{1,0:T(8,128)(2,1)}, u32[]{:S(2)}, u32[]{:S(2)}) collective-permute-start(bf16[4096,128]{1,0:T(8,128)(2,1)} %param.32), channel_id=1, source_target_pairs={{0,1},{1,0},{2,3},{3,2},{4,5},{5,4},{6,7},{7,6},{8,9},{9,8},{10,11... | collective-permute-start | bytes 3145736 | tf_op jit(solution)/shard_map/ppermute | solution.py:29
  3.6 12.0 %collective-permute-start.2 = (bf16[64,4096]{1,0:T(8,128)(2,1)S(1)}, bf16[64,4096]{1,0:T(8,128)(2,1)}, u32[]{:S(2)}, u32[]{:S(2)}) collective-permute-start(bf16[64,4096]{1,0:T(8,128)(2,1)S(1)} %shard_map.217.refs_0_), channel_id=1, source_target_pairs={{0,4},{4,8},{8,12},{12,14},{14,10},{10,6},{6,2},{2,0},{1,3},{5,1},... | collective-permute-start | bytes 1572872 | tf_op jit(solution)/shard_map/ppermute | solution.py:33
  7.4 9.8 %collective-permute-start.4 = (f32[1,128]{1,0:T(1,128)S(1)}, f32[1,128]{1,0:T(1,128)S(1)}, u32[]{:S(2)}, u32[]{:S(2)}) collective-permute-start(f32[1,128]{1,0:T(1,128)S(1)} %convert_element_type.71), channel_id=1, source_target_pairs={{0,1},{1,0},{2,3},{3,2},{4,5},{5,4},{6,7},{7,6},{8,9},{9,8},{10,11... | collective-permute-start | bytes 1544 | tf_op jit(solution)/shard_map/ppermute | solution.py:29
  12.2 11.2 %collective-permute-start.1 = (bf16[64,4096]{1,0:T(8,128)(2,1)S(1)}, bf16[64,4096]{1,0:T(8,128)(2,1)S(1)}, u32[]{:S(2)}, u32[]{:S(2)}) collective-permute-start(bf16[64,4096]{1,0:T(8,128)(2,1)S(1)} %collective-permute-done.refs_1_), channel_id=1, source_target_pairs={{0,4},{4,8},{8,12},{12,14},{14,10},{10,6},{6,2},{2,0},{1,3},{5,1},... | collective-permute-start | bytes 1572872 | tf_op jit(solution)/shard_map/ppermute | solution.py:33
  15.6 11.4 %collective-permute-start.9 = (bf16[64,4096]{1,0:T(8,128)(2,1)}, bf16[64,4096]{1,0:T(8,128)(2,1)S(1)}, u32[]{:S(2)}, u32[]{:S(2)}) collective-permute-start(bf16[64,4096]{1,0:T(8,128)(2,1)} %collective-permute-done.2.refs_0_.refs_2_), channel_id=1, source_target_pairs={{0,4},{4,8},{8,12},{12,14},{14,10},{10,6},{6,2},{2,0},{1,3},{5,1},... | collective-permute-start | bytes 1572872 | tf_op jit(solution)/shard_map/ppermute | solution.py:33
  23.9 12.1 %collective-permute-start.5 = (bf16[64,4096]{1,0:T(8,128)(2,1)S(1)}, bf16[64,4096]{1,0:T(8,128)(2,1)S(1)}, u32[]{:S(2)}, u32[]{:S(2)}) collective-permute-start(bf16[64,4096]{1,0:T(8,128)(2,1)S(1)} %collective-permute-done.1.refs_1_.refs_3_), channel_id=1, source_target_pairs={{0,4},{4,8},{8,12},{12,14},{14,10},{10,6},{6,2},{2,0},{1,3},{5,1},... | collective-permute-start | bytes 1572872 | tf_op jit(solution)/shard_map/ppermute | solution.py:33
  25.4 22.8 %collective-permute-start.12 = (bf16[128,4096]{1,0:T(8,128)(2,1)S(1)}, bf16[128,4096]{1,0:T(8,128)(2,1)S(1)}, u32[]{:S(2)}, u32[]{:S(2)}) collective-permute-start(bf16[128,4096]{1,0:T(8,128)(2,1)S(1)} %copy-done.18), channel_id=1, source_target_pairs={{0,1},{1,0},{2,3},{3,2},{4,5},{5,4},{6,7},{7,6},{8,9},{9,8},{10,11... | collective-permute-start | bytes 3145736 | tf_op jit(solution)/shard_map/ppermute | solution.py:29
  27.0 11.7 %collective-permute-start.13 = (bf16[64,4096]{1,0:T(8,128)(2,1)S(1)}, bf16[64,4096]{1,0:T(8,128)(2,1)S(1)}, u32[]{:S(2)}, u32[]{:S(2)}) collective-permute-start(bf16[64,4096]{1,0:T(8,128)(2,1)S(1)} %collective-permute-done.9.refs_0_), channel_id=1, source_target_pairs={{0,4},{4,8},{8,12},{12,14},{14,10},{10,6},{6,2},{2,0},{1,3},{5,1},... | collective-permute-start | bytes 1572872 | tf_op jit(solution)/shard_map/ppermute | solution.py:33
  28.6 13.5 %collective-permute-start.11 = (bf16[64,4096]{1,0:T(8,128)(2,1)S(1)}, bf16[64,4096]{1,0:T(8,128)(2,1)S(1)}, u32[]{:S(2)}, u32[]{:S(2)}) collective-permute-start(bf16[64,4096]{1,0:T(8,128)(2,1)S(1)} %collective-permute-done.9.refs_0_), channel_id=1, source_target_pairs={{0,1},{1,0},{2,3},{3,2},{4,5},{5,4},{6,7},{7,6},{8,9},{9,8},{10,11... | collective-permute-start | bytes 1572872 | tf_op jit(solution)/shard_map/ppermute | solution.py:29
  36.6 11.7 %collective-permute-start.8 = (bf16[64,4096]{1,0:T(8,128)(2,1)S(1)}, bf16[64,4096]{1,0:T(8,128)(2,1)S(1)}, u32[]{:S(2)}, u32[]{:S(2)}) collective-permute-start(bf16[64,4096]{1,0:T(8,128)(2,1)S(1)} %collective-permute-done.5.refs_1_), channel_id=1, source_target_pairs={{0,4},{4,8},{8,12},{12,14},{14,10},{10,6},{6,2},{2,0},{1,3},{5,1},... | collective-permute-start | bytes 1572872 | tf_op jit(solution)/shard_map/ppermute | solution.py:33
  38.7 11.1 %collective-permute-start.15 = (bf16[384,512]{1,0:T(8,128)(2,1)S(1)}, bf16[384,512]{1,0:T(8,128)(2,1)S(1)}, u32[]{:S(2)}, u32[]{:S(2)}) collective-permute-start(bf16[384,512]{1,0:T(8,128)(2,1)S(1)} %get-tuple-element.110), channel_id=1, source_target_pairs={{0,16},{1,17},{2,18},{3,19},{4,20},{5,21},{6,22},{7,23},{8,24},{9,... | collective-permute-start | bytes 1179656 | tf_op jit(solution)/shard_map/ppermute | solution.py:474
  42.1 10.5 %collective-permute-start.14 = (bf16[64,4096]{1,0:T(8,128)(2,1)S(1)}, bf16[64,4096]{1,0:T(8,128)(2,1)S(1)}, u32[]{:S(2)}, u32[]{:S(2)}) collective-permute-start(bf16[64,4096]{1,0:T(8,128)(2,1)S(1)} %collective-permute-done.13.refs_0_), channel_id=1, source_target_pairs={{0,4},{4,8},{8,12},{12,14},{14,10},{10,6},{6,2},{2,0},{1,3},{5,1},... | collective-permute-start | bytes 1572872 | tf_op jit(solution)/shard_map/ppermute | solution.py:33
  60.7 23.4 %collective-permute-start.23 = (bf16[384,512]{1,0:T(8,128)(2,1)S(1)}, bf16[384,512]{1,0:T(8,128)(2,1)S(1)}, u32[]{:S(2)}, u32[]{:S(2)}) collective-permute-start(bf16[384,512]{1,0:T(8,128)(2,1)S(1)} %pad_maximum_fusion.1), channel_id=1, source_target_pairs={{0,16},{1,17},{2,18},{3,19},{4,20},{5,21},{6,22},{7,23},{8,24},{9,... | collective-permute-start | bytes 1179656 | tf_op jit(solution)/shard_map/ppermute | solution.py:474
  65.1 19.0 %collective-permute-start.22 = (bf16[256,512]{1,0:T(8,128)(2,1)S(1)}, bf16[256,512]{1,0:T(8,128)(2,1)S(1)}, u32[]{:S(2)}, u32[]{:S(2)}) collective-permute-start(bf16[256,512]{1,0:T(8,128)(2,1)S(1)} %get-tuple-element.133), channel_id=1, source_target_pairs={{0,16},{1,17},{2,18},{3,19},{4,20},{5,21},{6,22},{7,23},{8,24},{9,... | collective-permute-start | bytes 786440 | tf_op jit(solution)/shard_map/ppermute | solution.py:474
  100.8 12.0 %collective-permute-start.30 = (bf16[128,4096]{1,0:T(8,128)(2,1)S(1)}, bf16[128,4096]{1,0:T(8,128)(2,1)S(1)}, u32[]{:S(2)}, u32[]{:S(2)}) collective-permute-start(bf16[128,4096]{1,0:T(8,128)(2,1)S(1)} %get-tuple-element.160), channel_id=1, source_target_pairs={{0,1},{1,0},{2,3},{3,2},{4,5},{5,4},{6,7},{7,6},{8,9},{9,8},{10,11... | collective-permute-start | bytes 3145736 | tf_op jit(solution)/shard_map/ppermute | solution.py:29
  105.4 12.0 %collective-permute-start.33 = (bf16[128,4096]{1,0:T(8,128)(2,1)S(1)}, bf16[128,4096]{1,0:T(8,128)(2,1)S(1)}, u32[]{:S(2)}, u32[]{:S(2)}) collective-permute-start(bf16[128,4096]{1,0:T(8,128)(2,1)S(1)} %get-tuple-element.169), channel_id=1, source_target_pairs={{0,1},{1,0},{2,3},{3,2},{4,5},{5,4},{6,7},{7,6},{8,9},{9,8},{10,11... | collective-permute-start | bytes 3145736 | tf_op jit(solution)/shard_map/ppermute | solution.py:29
  114.1 9.2 %collective-permute-start.31 = (bf16[64,4096]{1,0:T(8,128)(2,1)S(1)}, bf16[64,4096]{1,0:T(8,128)(2,1)S(1)}, u32[]{:S(2)}, u32[]{:S(2)}) collective-permute-start(bf16[64,4096]{1,0:T(8,128)(2,1)S(1)} %shard_map.235), channel_id=1, source_target_pairs={{0,4},{4,8},{8,12},{12,14},{14,10},{10,6},{6,2},{2,0},{1,3},{5,1},... | collective-permute-start | bytes 1572872 | tf_op jit(solution)/shard_map/ppermute | solution.py:33
  114.9 14.9 %collective-permute-start.35 = (bf16[128,4096]{1,0:T(8,128)(2,1)S(1)}, bf16[128,4096]{1,0:T(8,128)(2,1)S(1)}, u32[]{:S(2)}, u32[]{:S(2)}) collective-permute-start(bf16[128,4096]{1,0:T(8,128)(2,1)S(1)} %get-tuple-element.172), channel_id=1, source_target_pairs={{0,1},{1,0},{2,3},{3,2},{4,5},{5,4},{6,7},{7,6},{8,9},{9,8},{10,11... | collective-permute-start | bytes 3145736 | tf_op jit(solution)/shard_map/ppermute | solution.py:29
  116.2 12.7 %collective-permute-start.37 = (bf16[64,4096]{1,0:T(8,128)(2,1)S(1)}, bf16[64,4096]{1,0:T(8,128)(2,1)S(1)}, u32[]{:S(2)}, u32[]{:S(2)}) collective-permute-start(bf16[64,4096]{1,0:T(8,128)(2,1)S(1)} %convert_element_type.79), channel_id=1, source_target_pairs={{0,4},{4,8},{8,12},{12,14},{14,10},{10,6},{6,2},{2,0},{1,3},{5,1},... | collective-permute-start | bytes 1572872 | tf_op jit(solution)/shard_map/ppermute | solution.py:33
  123.5 11.1 %collective-permute-start.32 = (bf16[64,4096]{1,0:T(8,128)(2,1)S(1)}, bf16[64,4096]{1,0:T(8,128)(2,1)S(1)}, u32[]{:S(2)}, u32[]{:S(2)}) collective-permute-start(bf16[64,4096]{1,0:T(8,128)(2,1)S(1)} %add_convert_fusion.6), channel_id=1, source_target_pairs={{0,4},{4,8},{8,12},{12,14},{14,10},{10,6},{6,2},{2,0},{1,3},{5,1},... | collective-permute-start | bytes 1572872 | tf_op jit(solution)/shard_map/ppermute | solution.py:33
  129.1 11.1 %collective-permute-start.38 = (bf16[64,4096]{1,0:T(8,128)(2,1)S(1)}, bf16[64,4096]{1,0:T(8,128)(2,1)S(1)}, u32[]{:S(2)}, u32[]{:S(2)}) collective-permute-start(bf16[64,4096]{1,0:T(8,128)(2,1)S(1)} %add_convert_fusion.3), channel_id=1, source_target_pairs={{0,4},{4,8},{8,12},{12,14},{14,10},{10,6},{6,2},{2,0},{1,3},{5,1},... | collective-permute-start | bytes 1572872 | tf_op jit(solution)/shard_map/ppermute | solution.py:33
  134.7 11.1 %collective-permute-start.34 = (bf16[64,4096]{1,0:T(8,128)(2,1)S(1)}, bf16[64,4096]{1,0:T(8,128)(2,1)S(1)}, u32[]{:S(2)}, u32[]{:S(2)}) collective-permute-start(bf16[64,4096]{1,0:T(8,128)(2,1)S(1)} %add_convert_fusion.5), channel_id=1, source_target_pairs={{0,4},{4,8},{8,12},{12,14},{14,10},{10,6},{6,2},{2,0},{1,3},{5,1},... | collective-permute-start | bytes 1572872 | tf_op jit(solution)/shard_map/ppermute | solution.py:33
  140.3 11.1 %collective-permute-start.39 = (bf16[64,4096]{1,0:T(8,128)(2,1)S(1)}, bf16[64,4096]{1,0:T(8,128)(2,1)S(1)}, u32[]{:S(2)}, u32[]{:S(2)}) collective-permute-start(bf16[64,4096]{1,0:T(8,128)(2,1)S(1)} %add_convert_fusion.2), channel_id=1, source_target_pairs={{0,4},{4,8},{8,12},{12,14},{14,10},{10,6},{6,2},{2,0},{1,3},{5,1},... | collective-permute-start | bytes 1572872 | tf_op jit(solution)/shard_map/ppermute | solution.py:33
  145.9 11.1 %collective-permute-start.36 = (bf16[64,4096]{1,0:T(8,128)(2,1)S(1)}, bf16[64,4096]{1,0:T(8,128)(2,1)S(1)}, u32[]{:S(2)}, u32[]{:S(2)}) collective-permute-start(bf16[64,4096]{1,0:T(8,128)(2,1)S(1)} %add_convert_fusion.4), channel_id=1, source_target_pairs={{0,4},{4,8},{8,12},{12,14},{14,10},{10,6},{6,2},{2,0},{1,3},{5,1},... | collective-permute-start | bytes 1572872 | tf_op jit(solution)/shard_map/ppermute | solution.py:33
  (39 other events, 298.4 us)

commit v4 on v3

--- a/solution.py
+++ b/solution.py
@@ -113,11 +113,18 @@
     return value * (1.0 - 2.0 * odd)
 
 
-def norm_kernel(x_ref, gain_ref, bias_ref, out_ref):
+def norm_kernel(x_hbm, gain_hbm, bias_hbm, out_ref, x_ref, gain_ref, bias_ref, sems):
+    pairs = ((x_hbm, x_ref), (gain_hbm, gain_ref), (bias_hbm, bias_ref))
+    copies = [pltpu.make_async_copy(a, b, sems.at[k]) for k, (a, b) in enumerate(pairs)]
+    for copy in copies:
+        copy.start()
+    copies[0].wait()
     values = x_ref[...].astype(jnp.float32)
     center = values - jnp.mean(values, axis=1, keepdims=True)
     spread = jnp.mean(center * center, axis=1, keepdims=True)
     scaled = center * lax.rsqrt(spread + EPSILON)
+    copies[1].wait()
+    copies[2].wait()
     out_ref[...] = (scaled * gain_ref[...] + bias_ref[...]).astype(out_ref.dtype)
 
 
@@ -244,8 +251,9 @@
     key_refs, value_refs, refs = refs[:req_count], refs[req_count : 2 * req_count], refs[2 * req_count :]
     meta_ref, spread_ref, left_ref, hidden_rank_ref, attended_ref, out_ref = refs[:6]
     keys_ref, values_ref, scores_ref, top_ref, sum_ref, acc_ref, fold_ref = refs[6:]
-    rows = 256
-    pair = rows // 2
+    span = 256
+    rows = 2 * span
+    pair = span // 2
     group_rows = q_ref.shape[0]
 
     def slot_rows(slot):
@@ -261,24 +269,23 @@
 
     def places(shape, dim):
         at = lax.broadcasted_iota(jnp.int32, shape, dim)
-        second = at >= pair
-        at = jnp.where(second, at - pair, at) + info[CORE] * (pair // 2)
-        at = jnp.where(at >= pair, at - pair, at)
-        return (at + jnp.where(second, pair, 0)).astype(jnp.float32)
-
-    key_place = places((1, rows), 1)
+        before = at // pair * pair
+        at = at - before + info[CORE] * (pair // 2)
+        return (before + jnp.where(at >= pair, at - pair, at)).astype(jnp.float32)
+
+    key_place = places((1, span), 1)
     query_place = places((rows, 1), 0)
 
     def one(block, _):
-        slots = [slot_rows(info[PLACES + 2 * block + k]) for k in (0, 1)]
+        slots = [slot_rows(info[PLACES + 4 * block + k]) for k in range(4)]
 
         def both(ref):
             return jnp.concatenate([ref[at, :] for at in slots], axis=0)
 
         meta = both(meta_ref)
         start = meta[:, 0:1]
-        number = (req_count - 1) * BLOCKS + block
-        query = query_place + (first_token + number * rows).astype(jnp.float32)
+        number = (req_count - 1) * BLOCKS + 2 * block
+        query = query_place + (first_token + number * span).astype(jnp.float32)
         q = both(q_ref)
         lowest = jnp.min(start).astype(jnp.int32) - first_token
         top_ref[...] = jnp.full_like(top_ref, NEGATIVE_FILL)
@@ -286,36 +293,36 @@
         acc_ref[...] = jnp.zeros_like(acc_ref)
 
         def score(j, _):
-            at = pl.ds(pl.multiple_of(j * rows, rows), rows)
+            at = pl.ds(pl.multiple_of(j * span, span), span)
             scores = across(q, keys_ref[at, :])
-            key = key_place + (first_token + j * rows).astype(jnp.float32)
+            key = key_place + (first_token + j * span).astype(jnp.float32)
             allowed = jnp.logical_and(key <= query, key >= start)
             scores = jnp.where(allowed, scores, NEGATIVE_FILL)
             scores_ref[:, at] = scores
             top_ref[...] = jnp.maximum(top_ref[...], jnp.maximum(scores[:, :pair], scores[:, pair:]))
             return 0
 
-        lax.fori_loop(lowest // rows, number + 1, score, 0)
+        lax.fori_loop(lowest // span, number + 2, score, 0)
         top = jnp.max(top_ref[...], axis=1, keepdims=True)
 
         def weigh(j, _):
-            at = pl.ds(pl.multiple_of(j * rows, rows), rows)
+            at = pl.ds(pl.multiple_of(j * span, span), span)
             weights = jnp.exp(scores_ref[:, at] - top)
             sum_ref[...] = sum_ref[...] + (weights[:, :pair] + weights[:, pair:])
             acc_ref[...] = acc_ref[...] + rank_product(weights.astype(jnp.bfloat16), values_ref[at, :])
             return 0
 
-        lax.fori_loop(lowest // rows, number + 1, weigh, 0)
+        lax.fori_loop(lowest // span, number + 2, weigh, 0)
         total = jnp.sum(sum_ref[...], axis=1, keepdims=True)
         attended = (acc_ref[...] / total).astype(jnp.bfloat16)
         lanes = folded(rank_product(attended, left_ref[...]), meta[:, 64:65], spread_ref)
-        for k in (0, 1):
+        for k in range(4):
             attended_ref[slots[k], :] = attended[k * pair : (k + 1) * pair]
-            at = pl.ds(pl.multiple_of((2 * block + k) * pair, pair), pair)
+            at = pl.ds(pl.multiple_of((4 * block + k) * pair, pair), pair)
             fold_ref[:, at] = swap_halves(info, lanes[:, k * pair : (k + 1) * pair])
         return 0
 
-    lax.fori_loop(0, BLOCKS, one, 0)
+    lax.fori_loop(0, BLOCKS // 2, one, 0)
     out_ref[...] = (fold_ref[...] + hidden_rank_ref[...].astype(jnp.float32)).astype(out_ref.dtype)
 
 
@@ -362,9 +369,9 @@
             out_refs[1][:, at] = total[half:] + arrived_ref[:half, at].astype(jnp.float32)
 
 
-def call(kernel, operands, outs, info=None, scratch=(), mib=24, flops=1000):
+def call(kernel, operands, outs, info=None, scratch=(), mib=24, flops=1000, space=pltpu.VMEM):
     vmem = pl.BlockSpec(memory_space=pltpu.VMEM)
-    specs = [vmem] * len(operands)
+    specs = [pl.BlockSpec(memory_space=space)] * len(operands)
     if info is not None:
         operands, specs = [info] + operands, [pl.BlockSpec(memory_space=pltpu.SMEM)] + specs
     return pl.pallas_call(
@@ -434,10 +441,13 @@
             table[g, m] = [m % 2, m] + pairs + [pairs.index(p) for p in range(SLOTS)] + firsts
     info = lax.dynamic_slice(jnp.asarray(table), (group, me, 0), (1, 1, table.shape[2])).reshape(-1)
 
+    norm_args = [tokens, layer_norm_gain.reshape(1, -1), layer_norm_bias.reshape(1, -1)]
     own = call(
         norm_kernel,
-        [tokens, layer_norm_gain.reshape(1, -1), layer_norm_bias.reshape(1, -1)],
+        norm_args,
         [shape(block, model_width)],
+        scratch=[pltpu.VMEM(x.shape, x.dtype) for x in norm_args] + [pltpu.SemaphoreType.DMA((3,))],
+        space=pl.ANY,
     )[0]
     other = to_partner(own)
     ring_a, ring_b = along_ring(own), along_ring(other)
@@ -521,17 +531,16 @@
     ring_b, ranks, second, far_right = tie((ring_b, ranks, second, far_right))
     part = arrivals(ring_a, ring_b)
     ring_a = along_ring(ring_a)
-    held_rows, far_early = tie((part[:2], far_early))
+    held_rows = part[:2]
     third = products_of(held_rows, 2000000000)
     ranks = add_ranks(held_rows, (6,), ranks)
-    ring_a, ranks, third = tie((ring_a, ranks, third))
+    ring_a, ranks, third, far_early = tie((ring_a, ranks, third, far_early))
     part = part[2:] + (ring_a, to_partner(ring_a))
     ranks = add_ranks(part, (7, 1), ranks)
     moved = lax.ppermute(ranks, "mlp", [(i, i ^ 2) for i in range(16)])
     fourth = products_of(part)
     ranks, fourth = tie((ranks + moved, fourth))
-    far_middle = to_groups(second[2])
-    far_late = to_groups(jnp.concatenate([third[2], fourth[2]], axis=0))
+    far_late = to_groups(jnp.concatenate([second[2], third[2], fourth[2]], axis=0))
     rank_in = sum_over_mlp(ranks, (4, 8))
     products = (first, second, third, fourth)
 
@@ -549,7 +558,8 @@
     keys, values = [own_keys], [own_values]
     for d in range(1, req_count):
         early, late = far_early[d - 1], far_late[d - 1]
-        shared = [early, far_middle[d - 1], late[:pair_rows], late[pair_rows:]]
+        ends = (0, block_rows, block_rows + pair_rows, 2 * block_rows + pair_rows)
+        shared = [early] + [late[ends[k] : ends[k + 1]] for k in range(3)]
         far_keys, far_values = call(
             functools.partial(far_kernel, d * group_rows),
             shared + [far_rank[d - 1], meta, turns, spread_first, qkv_right],
@@ -568,12 +578,13 @@
         [
             pltpu.VMEM((req_count * group_rows, HEAD_SIZE), jnp.bfloat16),
             pltpu.VMEM((req_count * group_rows, HEAD_SIZE), jnp.bfloat16),
-            held((block_rows, req_count * group_rows)),
-            held((block_rows, 128)),
-            held((block_rows, 128)),
-            held((block_rows, HEAD_SIZE)),
+            held((2 * block_rows, req_count * group_rows)),
+            held((2 * block_rows, 128)),
+            held((2 * block_rows, 128)),
+            held((2 * block_rows, HEAD_SIZE)),
             held((32, group_rows)),
         ],
+        mib=24 + 3 * req_count,
     )
     output_rows = output_weight.reshape(HEAD_SIZE, model_width)
 

time: 158 us -> 153 us (0.968)
  starting transfers between devices: 42.8 us -> 40.3 us
  Pallas kernels: 53 us -> 51 us
    pallas_call x23, Pallas kernels: 53 us -> 51 us  [call(): pl.pallas_call(kernel, in_specs=specs, out_specs=[vmem] * len(outs), out_...]
    ppermute x4 -> x3, starting transfers between devices: 10.6 us -> 8.62 us  [to_group(): lax.ppermute(value, 'req', [(g, g + d) for g in range(req_count - d)])]
  transfers between devices with their start and end apart: 41 -> 40, of which waited for: 17 -> 16; matrix products, arithmetic and copies ran while one was open for 3% -> 3% of each run, Pallas kernels for 26% -> 27%
where the time goes in v4:
time: 153 us; the launch traced here: 152 us
  Pallas kernels  51 us (33%)
  waiting for transfers between devices  46 us (30%)
  starting transfers between devices  40.3 us (26%)
  local copies, waits for them, and re-layouts  9.39 us (6%)
  other arithmetic  4.99 us (3%)
    pallas_call x23, Pallas kernels, call(): pl.pallas_call(kernel, in_specs=specs, out_specs=[vmem] * len(outs), out_...  51 us
    ppermute x14, waiting for transfers between devices, along_ring(): return lax.ppermute(value, 'mlp', RING_PERM)  33.2 us
    ppermute x14, starting transfers between devices, along_ring(): return lax.ppermute(value, 'mlp', RING_PERM)  18.5 us
    ppermute x3, starting transfers between devices, to_group(): lax.ppermute(value, 'req', [(g, g + d) for g in range(req_count - d)])  8.62 us
    unnamed x46, local copies, waits for them, and re-layouts  8.31 us
    ppermute x4, starting transfers between devices, per_device(): moved = lax.ppermute(rank_out, 'mlp', [(i, i ^ bit) for i in range(16)])  5.77 us
    ppermute x2, waiting for transfers between devices, sum_over_mlp(): lax.ppermute(value, 'mlp', [(i, i ^ bit) for i in range(16)])  5.47 us
    ppermute x4, waiting for transfers between devices, per_device(): moved = lax.ppermute(rank_out, 'mlp', [(i, i ^ bit) for i in range(16)])  4.6 us
  transfers between devices with their start and end apart: 40, of which 16 were waited for; matrix products, arithmetic and copies ran while one was open for 3% of the time, Pallas kernels for 27%

profile of v4, /device:TPU:0, one launch (start us, length us, event | category | flops | bytes accessed | tf_op | source)
XLA Modules:
  0.0 152.3 jit_solution(11935784490117142366)
XLA Ops:
  3.6 3.0 %collective-permute-start.2 = (bf16[64,4096]{1,0:T(8,128)(2,1)S(1)}, bf16[64,4096]{1,0:T(8,128)(2,1)}, u32[]{:S(2)}, u32[]{:S(2)}) collective-permute-start(bf16[64,4096]{1,0:T(8,128)(2,1)S(1)} %shard_map.217.refs_0_), channel_id=1, source_target_pairs={{0,4},{4,8},{8,12},{12,14},{14,10},{10,6},{6,2},{2,0},{1,3},{5,1},... | collective-permute-start | bytes 1572872 | tf_op jit(solution)/shard_map/ppermute | solution.py:33
  9.6 2.5 %shard_map.218 = (f32[2048,128]{1,0:T(8,128)S(1)}, f32[2048,128]{1,0:T(8,128)S(1)}) custom-call(s32[34]{0:T(128)S(1)} %dynamic-slice_bitcast_fusion.info, f32[65,1]{1,0:T(8,128)S(1)} %copy.24.column_ref, f32[1,65]{1,0:T(1,128)S(1)} %get-tuple-element.177.row_ref, f32[1,65]{1,0:T(1,128)S(1)} %get-tuple-element.179.ids_ref, f32[8,128]{1,0:T(8,128)S(1)} %copy-done.16), custom_call_target="tpu_custom_call" | custom-call | flops 1000 | bytes 1000 | tf_op jit(solution)/shard_map/pallas_call | solution.py:377
  17.3 2.8 %copy-done = bf16[4096,1,768]{2,0,1:T(8,128)(2,1)S(1)} copy-done((bf16[4096,1,768]{2,0,1:T(8,128)(2,1)S(1)}, bf16[4096,1,768]{2,0,1:T(8,128)(2,1)}, u32[]{:S(2)}) %copy-start) | copy-done | bytes 6291480
  20.1 2.2 %copy-done.1 = bf16[4096,512]{1,0:T(8,128)(2,1)S(1)} copy-done((bf16[4096,512]{1,0:T(8,128)(2,1)S(1)}, bf16[4096,512]{1,0:T(8,128)(2,1)}, u32[]{:S(2)}) %copy-start.1) | copy-done | bytes 4194328
  28.7 5.2 %shard_map.221 = (f32[384,768]{1,0:T(8,128)S(1)}, f32[384,512]{1,0:T(8,128)S(1)}, bf16[384,512]{1,0:T(8,128)(2,1)S(1)}) custom-call(bf16[64,4096]{1,0:T(8,128)(2,1)S(1)} %shard_map.217.refs_0_, bf16[64,4096]{1,0:T(8,128)(2,1)S(1)} %collective-permute-done.refs_1_, bf16[64,4096]{1,0:T(8,128)(2,1)} %collective-permute-done.2.refs_0_.refs_2_, ...), custom_call_target="tpu_custom_call" | custom-call | flops 1000 | bytes 1000 | tf_op jit(solution)/shard_map/pallas_call | solution.py:377
  40.3 3.6 %collective-permute-start.15 = (bf16[384,512]{1,0:T(8,128)(2,1)S(1)}, bf16[384,512]{1,0:T(8,128)(2,1)S(1)}, u32[]{:S(2)}, u32[]{:S(2)}) collective-permute-start(bf16[384,512]{1,0:T(8,128)(2,1)S(1)} %get-tuple-element.112), channel_id=1, source_target_pairs={{0,16},{1,17},{2,18},{3,19},{4,20},{5,21},{6,22},{7,23},{8,24},{9,... | collective-permute-start | bytes 1179656 | tf_op jit(solution)/shard_map/ppermute | solution.py:484
  43.9 2.9 %shard_map.223 = (f32[256,768]{1,0:T(8,128)S(1)}, f32[256,512]{1,0:T(8,128)S(1)}, bf16[256,512]{1,0:T(8,128)(2,1)S(1)}) custom-call(bf16[64,4096]{1,0:T(8,128)(2,1)S(1)} %collective-permute-done.9.refs_0_, bf16[64,4096]{1,0:T(8,128)(2,1)S(1)} %collective-permute-done.5.refs_1_, bf16[64,4096]{1,0:T(8,128)(2,1)S(1)} %collective-permute-done.10.refs_2_, ...), custom_call_target="tpu_custom_call" | custom-call | flops 1000 | bytes 1000 | tf_op jit(solution)/shard_map/pallas_call | solution.py:377
  55.6 2.9 %shard_map.227 = (f32[256,768]{1,0:T(8,128)S(1)}, f32[256,512]{1,0:T(8,128)S(1)}, bf16[256,512]{1,0:T(8,128)(2,1)S(1)}) custom-call(bf16[64,4096]{1,0:T(8,128)(2,1)S(1)} %collective-permute-done.16.refs_0_, bf16[64,4096]{1,0:T(8,128)(2,1)S(1)} %collective-permute-done.17.refs_1_, bf16[64,4096]{1,0:T(8,128)(2,1)S(1)} %collective-permute-done.14.refs_2_, ...), custom_call_target="tpu_custom_call" | custom-call | flops 1000 | bytes 1000 | tf_op jit(solution)/shard_map/pallas_call | solution.py:377
  59.4 3.5 %collective-permute-start.22 = (bf16[640,512]{1,0:T(8,128)(2,1)S(1)}, bf16[640,512]{1,0:T(8,128)(2,1)S(1)}, u32[]{:S(2)}, u32[]{:S(2)}) collective-permute-start(bf16[640,512]{1,0:T(8,128)(2,1)S(1)} %pad_maximum_fusion.1), channel_id=1, source_target_pairs={{0,16},{1,17},{2,18},{3,19},{4,20},{5,21},{6,22},{7,23},{8,24},{9,... | collective-permute-start | bytes 1966088 | tf_op jit(solution)/shard_map/ppermute | solution.py:484
  64.6 2.7 %collective-permute-done.20 = bf16[32,1024]{1,0:T(8,128)(2,1)S(1)} collective-permute-done((bf16[32,1024]{1,0:T(8,128)(2,1)S(1)}, bf16[32,1024]{1,0:T(8,128)(2,1)S(1)}, u32[]{:S(2)}, u32[]{:S(2)}) %collective-permute-start.20) | collective-permute-done | bytes 65568 | tf_op jit(solution)/shard_map/ppermute | solution.py:394
  67.3 2.5 %collective-permute-start.21 = (bf16[32,1024]{1,0:T(8,128)(2,1)S(1)}, bf16[32,1024]{1,0:T(8,128)(2,1)S(1)}, u32[]{:S(2)}, u32[]{:S(2)}) collective-permute-start(bf16[32,1024]{1,0:T(8,128)(2,1)S(1)} %add.62), channel_id=1, source_target_pairs={{0,8},{1,9},{2,10},{3,11},{4,12},{5,13},{6,14},{7,15},{8,0},{9,1},... | collective-permute-start | bytes 196616 | tf_op jit(solution)/shard_map/ppermute | solution.py:394
  69.8 2.8 %collective-permute-done.21 = bf16[32,1024]{1,0:T(8,128)(2,1)S(1)} collective-permute-done((bf16[32,1024]{1,0:T(8,128)(2,1)S(1)}, bf16[32,1024]{1,0:T(8,128)(2,1)S(1)}, u32[]{:S(2)}, u32[]{:S(2)}) %collective-permute-start.21) | collective-permute-done | bytes 65568 | tf_op jit(solution)/shard_map/ppermute | solution.py:394
  74.1 6.4 %shard_map.228 = (bf16[1024,256]{1,0:T(8,128)(2,1)S(1)}, bf16[1024,256]{1,0:T(8,128)(2,1)S(1)}, bf16[1024,256]{1,0:T(8,128)(2,1)S(1)}, bf16[1024,512]{1,0:T(8,128)(2,1)S(1)}, bf16[32,1024]{1,0:T(8,128)(2,1)S(1)}) custom-call(s32[34]{0:T(128)S(1)} %dynamic-slice_bitcast_fusion.info, f32[384,768]{1,0:T(8,128)S(1)} %get-tuple-element.100.refs_0_, ...), custom_call_target="tpu_custom_call" | custom-call | flops 1000 | bytes 1000 | tf_op jit(solution)/shard_map/pallas_call | solution.py:377
  80.7 2.3 %shard_map.229 = (bf16[1024,256]{1,0:T(8,128)(2,1)S(1)}, bf16[1024,256]{1,0:T(8,128)(2,1)S(1)}) custom-call(s32[34]{0:T(128)S(1)} %dynamic-slice_bitcast_fusion.info, bf16[384,512]{1,0:T(8,128)(2,1)S(1)} %collective-permute-done.15.refs_0_, bf16[256,512]{1,0:T(8,128)(2,1)S(1)} %get-tuple-element.176.refs_1_, bf16[128,512]{1,0:T(8,128)(2,1)S(1)} %slice.17.refs_2_, ...), custom_call_target="tpu_custom_call" | custom-call | flops 1000 | bytes 1000 | tf_op jit(solution)/shard_map/pallas_call | solution.py:377
  83.0 5.8 %shard_map.230 = (bf16[1024,256]{1,0:T(8,128)(2,1)S(1)}, bf16[32,1024]{1,0:T(8,128)(2,1)S(1)}) custom-call(s32[34]{0:T(128)S(1)} %dynamic-slice_bitcast_fusion.info, bf16[1024,256]{1,0:T(8,128)(2,1)S(1)} %get-tuple-element.126.refs_0_, bf16[1024,256]{1,0:T(8,128)(2,1)S(1)} %get-tuple-element.127.refs_1_, bf16[1024,256]{1,0:T(8,128)(2,1)S(1)} %get-tuple-element.132.refs_2_, ...), custom_call_target="tpu_custom_call" | custom-call | flops 1000 | bytes 1000 | tf_op jit(solution)/shard_map/pallas_call | solution.py:377
  100.1 2.8 %collective-permute-start.28 = (bf16[32,1024]{1,0:T(8,128)(2,1)S(1)}, bf16[32,1024]{1,0:T(8,128)(2,1)S(1)}, u32[]{:S(2)}, u32[]{:S(2)}) collective-permute-start(bf16[32,1024]{1,0:T(8,128)(2,1)S(1)} %add.66), channel_id=1, source_target_pairs={{0,8},{1,9},{2,10},{3,11},{4,12},{5,13},{6,14},{7,15},{8,0},{9,1},... | collective-permute-start | bytes 196616 | tf_op jit(solution)/shard_map/ppermute | solution.py:601
  104.8 2.3 %collective-permute-done.28 = bf16[32,1024]{1,0:T(8,128)(2,1)S(1)} collective-permute-done((bf16[32,1024]{1,0:T(8,128)(2,1)S(1)}, bf16[32,1024]{1,0:T(8,128)(2,1)S(1)}, u32[]{:S(2)}, u32[]{:S(2)}) %collective-permute-start.28) | collective-permute-done | bytes 65568 | tf_op jit(solution)/shard_map/ppermute | solution.py:601
  112.9 4.6 %collective-permute-done.30 = bf16[64,4096]{1,0:T(8,128)(2,1)S(1)} collective-permute-done((bf16[64,4096]{1,0:T(8,128)(2,1)S(1)}, bf16[64,4096]{1,0:T(8,128)(2,1)S(1)}, u32[]{:S(2)}, u32[]{:S(2)}) %collective-permute-start.30) | collective-permute-done | bytes 524320 | tf_op jit(solution)/shard_map/ppermute | solution.py:33
  118.5 4.7 %collective-permute-done.36 = bf16[64,4096]{1,0:T(8,128)(2,1)S(1)} collective-permute-done((bf16[64,4096]{1,0:T(8,128)(2,1)S(1)}, bf16[64,4096]{1,0:T(8,128)(2,1)S(1)}, u32[]{:S(2)}, u32[]{:S(2)}) %collective-permute-start.36) | collective-permute-done | bytes 524320 | tf_op jit(solution)/shard_map/ppermute | solution.py:33
  125.4 3.5 %collective-permute-done.31 = bf16[64,4096]{1,0:T(8,128)(2,1)S(1)} collective-permute-done((bf16[64,4096]{1,0:T(8,128)(2,1)S(1)}, bf16[64,4096]{1,0:T(8,128)(2,1)S(1)}, u32[]{:S(2)}, u32[]{:S(2)}) %collective-permute-start.31) | collective-permute-done | bytes 524320 | tf_op jit(solution)/shard_map/ppermute | solution.py:33
  129.7 4.7 %collective-permute-done.37 = bf16[64,4096]{1,0:T(8,128)(2,1)S(1)} collective-permute-done((bf16[64,4096]{1,0:T(8,128)(2,1)S(1)}, bf16[64,4096]{1,0:T(8,128)(2,1)S(1)}, u32[]{:S(2)}, u32[]{:S(2)}) %collective-permute-start.37) | collective-permute-done | bytes 524320 | tf_op jit(solution)/shard_map/ppermute | solution.py:33
  135.3 4.7 %collective-permute-done.33 = bf16[64,4096]{1,0:T(8,128)(2,1)S(1)} collective-permute-done((bf16[64,4096]{1,0:T(8,128)(2,1)S(1)}, bf16[64,4096]{1,0:T(8,128)(2,1)S(1)}, u32[]{:S(2)}, u32[]{:S(2)}) %collective-permute-start.33) | collective-permute-done | bytes 524320 | tf_op jit(solution)/shard_map/ppermute | solution.py:33
  140.9 4.7 %collective-permute-done.38 = bf16[64,4096]{1,0:T(8,128)(2,1)S(1)} collective-permute-done((bf16[64,4096]{1,0:T(8,128)(2,1)S(1)}, bf16[64,4096]{1,0:T(8,128)(2,1)S(1)}, u32[]{:S(2)}, u32[]{:S(2)}) %collective-permute-start.38) | collective-permute-done | bytes 524320 | tf_op jit(solution)/shard_map/ppermute | solution.py:33
  147.1 4.2 %collective-permute-done.35 = bf16[64,4096]{1,0:T(8,128)(2,1)S(1)} collective-permute-done((bf16[64,4096]{1,0:T(8,128)(2,1)S(1)}, bf16[64,4096]{1,0:T(8,128)(2,1)S(1)}, u32[]{:S(2)}, u32[]{:S(2)}) %collective-permute-start.35) | collective-permute-done | bytes 524320 | tf_op jit(solution)/shard_map/ppermute | solution.py:33
  (154 shorter events, 64.5 us)
Async XLA Ops:
  0.0 13.8 %collective-permute-start.3 = (bf16[4096,128]{1,0:T(8,128)(2,1)}, bf16[4096,128]{1,0:T(8,128)(2,1)}, u32[]{:S(2)}, u32[]{:S(2)}) collective-permute-start(bf16[4096,128]{1,0:T(8,128)(2,1)} %param.32), channel_id=1, source_target_pairs={{0,1},{1,0},{2,3},{3,2},{4,5},{5,4},{6,7},{7,6},{8,9},{9,8},{10,11... | collective-permute-start | bytes 3145736 | tf_op jit(solution)/shard_map/ppermute | solution.py:29
  3.5 8.7 %collective-permute-start = (bf16[64,4096]{1,0:T(8,128)(2,1)S(1)}, bf16[64,4096]{1,0:T(8,128)(2,1)S(1)}, u32[]{:S(2)}, u32[]{:S(2)}) collective-permute-start(bf16[64,4096]{1,0:T(8,128)(2,1)S(1)} %shard_map.217.refs_0_), channel_id=1, source_target_pairs={{0,1},{1,0},{2,3},{3,2},{4,5},{5,4},{6,7},{7,6},{8,9},{9,8},{10,11... | collective-permute-start | bytes 1572872 | tf_op jit(solution)/shard_map/ppermute | solution.py:29
  3.6 12.0 %collective-permute-start.2 = (bf16[64,4096]{1,0:T(8,128)(2,1)S(1)}, bf16[64,4096]{1,0:T(8,128)(2,1)}, u32[]{:S(2)}, u32[]{:S(2)}) collective-permute-start(bf16[64,4096]{1,0:T(8,128)(2,1)S(1)} %shard_map.217.refs_0_), channel_id=1, source_target_pairs={{0,4},{4,8},{8,12},{12,14},{14,10},{10,6},{6,2},{2,0},{1,3},{5,1},... | collective-permute-start | bytes 1572872 | tf_op jit(solution)/shard_map/ppermute | solution.py:33
  7.5 9.8 %collective-permute-start.4 = (f32[1,128]{1,0:T(1,128)S(1)}, f32[1,128]{1,0:T(1,128)S(1)}, u32[]{:S(2)}, u32[]{:S(2)}) collective-permute-start(f32[1,128]{1,0:T(1,128)S(1)} %convert_element_type.71), channel_id=1, source_target_pairs={{0,1},{1,0},{2,3},{3,2},{4,5},{5,4},{6,7},{7,6},{8,9},{9,8},{10,11... | collective-permute-start | bytes 1544 | tf_op jit(solution)/shard_map/ppermute | solution.py:29
  12.2 11.2 %collective-permute-start.1 = (bf16[64,4096]{1,0:T(8,128)(2,1)S(1)}, bf16[64,4096]{1,0:T(8,128)(2,1)S(1)}, u32[]{:S(2)}, u32[]{:S(2)}) collective-permute-start(bf16[64,4096]{1,0:T(8,128)(2,1)S(1)} %collective-permute-done.refs_1_), channel_id=1, source_target_pairs={{0,4},{4,8},{8,12},{12,14},{14,10},{10,6},{6,2},{2,0},{1,3},{5,1},... | collective-permute-start | bytes 1572872 | tf_op jit(solution)/shard_map/ppermute | solution.py:33
  15.6 11.4 %collective-permute-start.9 = (bf16[64,4096]{1,0:T(8,128)(2,1)}, bf16[64,4096]{1,0:T(8,128)(2,1)S(1)}, u32[]{:S(2)}, u32[]{:S(2)}) collective-permute-start(bf16[64,4096]{1,0:T(8,128)(2,1)} %collective-permute-done.2.refs_0_.refs_2_), channel_id=1, source_target_pairs={{0,4},{4,8},{8,12},{12,14},{14,10},{10,6},{6,2},{2,0},{1,3},{5,1},... | collective-permute-start | bytes 1572872 | tf_op jit(solution)/shard_map/ppermute | solution.py:33
  24.0 12.1 %collective-permute-start.5 = (bf16[64,4096]{1,0:T(8,128)(2,1)S(1)}, bf16[64,4096]{1,0:T(8,128)(2,1)S(1)}, u32[]{:S(2)}, u32[]{:S(2)}) collective-permute-start(bf16[64,4096]{1,0:T(8,128)(2,1)S(1)} %collective-permute-done.1.refs_1_.refs_3_), channel_id=1, source_target_pairs={{0,4},{4,8},{8,12},{12,14},{14,10},{10,6},{6,2},{2,0},{1,3},{5,1},... | collective-permute-start | bytes 1572872 | tf_op jit(solution)/shard_map/ppermute | solution.py:33
  25.5 22.7 %collective-permute-start.12 = (bf16[128,4096]{1,0:T(8,128)(2,1)S(1)}, bf16[128,4096]{1,0:T(8,128)(2,1)S(1)}, u32[]{:S(2)}, u32[]{:S(2)}) collective-permute-start(bf16[128,4096]{1,0:T(8,128)(2,1)S(1)} %copy-done.18), channel_id=1, source_target_pairs={{0,1},{1,0},{2,3},{3,2},{4,5},{5,4},{6,7},{7,6},{8,9},{9,8},{10,11... | collective-permute-start | bytes 3145736 | tf_op jit(solution)/shard_map/ppermute | solution.py:29
  27.1 11.7 %collective-permute-start.13 = (bf16[64,4096]{1,0:T(8,128)(2,1)S(1)}, bf16[64,4096]{1,0:T(8,128)(2,1)S(1)}, u32[]{:S(2)}, u32[]{:S(2)}) collective-permute-start(bf16[64,4096]{1,0:T(8,128)(2,1)S(1)} %collective-permute-done.9.refs_0_), channel_id=1, source_target_pairs={{0,4},{4,8},{8,12},{12,14},{14,10},{10,6},{6,2},{2,0},{1,3},{5,1},... | collective-permute-start | bytes 1572872 | tf_op jit(solution)/shard_map/ppermute | solution.py:33
  28.6 11.6 %collective-permute-start.11 = (bf16[64,4096]{1,0:T(8,128)(2,1)S(1)}, bf16[64,4096]{1,0:T(8,128)(2,1)S(1)}, u32[]{:S(2)}, u32[]{:S(2)}) collective-permute-start(bf16[64,4096]{1,0:T(8,128)(2,1)S(1)} %collective-permute-done.9.refs_0_), channel_id=1, source_target_pairs={{0,1},{1,0},{2,3},{3,2},{4,5},{5,4},{6,7},{7,6},{8,9},{9,8},{10,11... | collective-permute-start | bytes 1572872 | tf_op jit(solution)/shard_map/ppermute | solution.py:29
  36.6 11.6 %collective-permute-start.8 = (bf16[64,4096]{1,0:T(8,128)(2,1)S(1)}, bf16[64,4096]{1,0:T(8,128)(2,1)S(1)}, u32[]{:S(2)}, u32[]{:S(2)}) collective-permute-start(bf16[64,4096]{1,0:T(8,128)(2,1)S(1)} %collective-permute-done.5.refs_1_), channel_id=1, source_target_pairs={{0,4},{4,8},{8,12},{12,14},{14,10},{10,6},{6,2},{2,0},{1,3},{5,1},... | collective-permute-start | bytes 1572872 | tf_op jit(solution)/shard_map/ppermute | solution.py:33
  38.8 12.8 %collective-permute-start.14 = (bf16[64,4096]{1,0:T(8,128)(2,1)S(1)}, bf16[64,4096]{1,0:T(8,128)(2,1)S(1)}, u32[]{:S(2)}, u32[]{:S(2)}) collective-permute-start(bf16[64,4096]{1,0:T(8,128)(2,1)S(1)} %collective-permute-done.13.refs_0_), channel_id=1, source_target_pairs={{0,4},{4,8},{8,12},{12,14},{14,10},{10,6},{6,2},{2,0},{1,3},{5,1},... | collective-permute-start | bytes 1572872 | tf_op jit(solution)/shard_map/ppermute | solution.py:33
  40.3 11.3 %collective-permute-start.15 = (bf16[384,512]{1,0:T(8,128)(2,1)S(1)}, bf16[384,512]{1,0:T(8,128)(2,1)S(1)}, u32[]{:S(2)}, u32[]{:S(2)}) collective-permute-start(bf16[384,512]{1,0:T(8,128)(2,1)S(1)} %get-tuple-element.112), channel_id=1, source_target_pairs={{0,16},{1,17},{2,18},{3,19},{4,20},{5,21},{6,22},{7,23},{8,24},{9,... | collective-permute-start | bytes 1179656 | tf_op jit(solution)/shard_map/ppermute | solution.py:484
  59.4 21.2 %collective-permute-start.22 = (bf16[640,512]{1,0:T(8,128)(2,1)S(1)}, bf16[640,512]{1,0:T(8,128)(2,1)S(1)}, u32[]{:S(2)}, u32[]{:S(2)}) collective-permute-start(bf16[640,512]{1,0:T(8,128)(2,1)S(1)} %pad_maximum_fusion.1), channel_id=1, source_target_pairs={{0,16},{1,17},{2,18},{3,19},{4,20},{5,21},{6,22},{7,23},{8,24},{9,... | collective-permute-start | bytes 1966088 | tf_op jit(solution)/shard_map/ppermute | solution.py:484
  95.3 11.7 %collective-permute-start.29 = (bf16[128,4096]{1,0:T(8,128)(2,1)S(1)}, bf16[128,4096]{1,0:T(8,128)(2,1)S(1)}, u32[]{:S(2)}, u32[]{:S(2)}) collective-permute-start(bf16[128,4096]{1,0:T(8,128)(2,1)S(1)} %get-tuple-element.156), channel_id=1, source_target_pairs={{0,1},{1,0},{2,3},{3,2},{4,5},{5,4},{6,7},{7,6},{8,9},{9,8},{10,11... | collective-permute-start | bytes 3145736 | tf_op jit(solution)/shard_map/ppermute | solution.py:29
  99.9 11.7 %collective-permute-start.32 = (bf16[128,4096]{1,0:T(8,128)(2,1)S(1)}, bf16[128,4096]{1,0:T(8,128)(2,1)S(1)}, u32[]{:S(2)}, u32[]{:S(2)}) collective-permute-start(bf16[128,4096]{1,0:T(8,128)(2,1)S(1)} %get-tuple-element.165), channel_id=1, source_target_pairs={{0,1},{1,0},{2,3},{3,2},{4,5},{5,4},{6,7},{7,6},{8,9},{9,8},{10,11... | collective-permute-start | bytes 3145736 | tf_op jit(solution)/shard_map/ppermute | solution.py:29
  108.3 9.2 %collective-permute-start.30 = (bf16[64,4096]{1,0:T(8,128)(2,1)S(1)}, bf16[64,4096]{1,0:T(8,128)(2,1)S(1)}, u32[]{:S(2)}, u32[]{:S(2)}) collective-permute-start(bf16[64,4096]{1,0:T(8,128)(2,1)S(1)} %shard_map.235), channel_id=1, source_target_pairs={{0,4},{4,8},{8,12},{12,14},{14,10},{10,6},{6,2},{2,0},{1,3},{5,1},... | collective-permute-start | bytes 1572872 | tf_op jit(solution)/shard_map/ppermute | solution.py:33
  109.1 15.0 %collective-permute-start.34 = (bf16[128,4096]{1,0:T(8,128)(2,1)S(1)}, bf16[128,4096]{1,0:T(8,128)(2,1)S(1)}, u32[]{:S(2)}, u32[]{:S(2)}) collective-permute-start(bf16[128,4096]{1,0:T(8,128)(2,1)S(1)} %get-tuple-element.168), channel_id=1, source_target_pairs={{0,1},{1,0},{2,3},{3,2},{4,5},{5,4},{6,7},{7,6},{8,9},{9,8},{10,11... | collective-permute-start | bytes 3145736 | tf_op jit(solution)/shard_map/ppermute | solution.py:29
  110.5 12.7 %collective-permute-start.36 = (bf16[64,4096]{1,0:T(8,128)(2,1)S(1)}, bf16[64,4096]{1,0:T(8,128)(2,1)S(1)}, u32[]{:S(2)}, u32[]{:S(2)}) collective-permute-start(bf16[64,4096]{1,0:T(8,128)(2,1)S(1)} %convert_element_type.79), channel_id=1, source_target_pairs={{0,4},{4,8},{8,12},{12,14},{14,10},{10,6},{6,2},{2,0},{1,3},{5,1},... | collective-permute-start | bytes 1572872 | tf_op jit(solution)/shard_map/ppermute | solution.py:33
  117.7 11.1 %collective-permute-start.31 = (bf16[64,4096]{1,0:T(8,128)(2,1)S(1)}, bf16[64,4096]{1,0:T(8,128)(2,1)S(1)}, u32[]{:S(2)}, u32[]{:S(2)}) collective-permute-start(bf16[64,4096]{1,0:T(8,128)(2,1)S(1)} %add_convert_fusion.6), channel_id=1, source_target_pairs={{0,4},{4,8},{8,12},{12,14},{14,10},{10,6},{6,2},{2,0},{1,3},{5,1},... | collective-permute-start | bytes 1572872 | tf_op jit(solution)/shard_map/ppermute | solution.py:33
  123.3 11.1 %collective-permute-start.37 = (bf16[64,4096]{1,0:T(8,128)(2,1)S(1)}, bf16[64,4096]{1,0:T(8,128)(2,1)S(1)}, u32[]{:S(2)}, u32[]{:S(2)}) collective-permute-start(bf16[64,4096]{1,0:T(8,128)(2,1)S(1)} %add_convert_fusion.3), channel_id=1, source_target_pairs={{0,4},{4,8},{8,12},{12,14},{14,10},{10,6},{6,2},{2,0},{1,3},{5,1},... | collective-permute-start | bytes 1572872 | tf_op jit(solution)/shard_map/ppermute | solution.py:33
  128.9 11.1 %collective-permute-start.33 = (bf16[64,4096]{1,0:T(8,128)(2,1)S(1)}, bf16[64,4096]{1,0:T(8,128)(2,1)S(1)}, u32[]{:S(2)}, u32[]{:S(2)}) collective-permute-start(bf16[64,4096]{1,0:T(8,128)(2,1)S(1)} %add_convert_fusion.5), channel_id=1, source_target_pairs={{0,4},{4,8},{8,12},{12,14},{14,10},{10,6},{6,2},{2,0},{1,3},{5,1},... | collective-permute-start | bytes 1572872 | tf_op jit(solution)/shard_map/ppermute | solution.py:33
  134.5 11.1 %collective-permute-start.38 = (bf16[64,4096]{1,0:T(8,128)(2,1)S(1)}, bf16[64,4096]{1,0:T(8,128)(2,1)S(1)}, u32[]{:S(2)}, u32[]{:S(2)}) collective-permute-start(bf16[64,4096]{1,0:T(8,128)(2,1)S(1)} %add_convert_fusion.2), channel_id=1, source_target_pairs={{0,4},{4,8},{8,12},{12,14},{14,10},{10,6},{6,2},{2,0},{1,3},{5,1},... | collective-permute-start | bytes 1572872 | tf_op jit(solution)/shard_map/ppermute | solution.py:33
  140.1 11.1 %collective-permute-start.35 = (bf16[64,4096]{1,0:T(8,128)(2,1)S(1)}, bf16[64,4096]{1,0:T(8,128)(2,1)S(1)}, u32[]{:S(2)}, u32[]{:S(2)}) collective-permute-start(bf16[64,4096]{1,0:T(8,128)(2,1)S(1)} %add_convert_fusion.4), channel_id=1, source_target_pairs={{0,4},{4,8},{8,12},{12,14},{14,10},{10,6},{6,2},{2,0},{1,3},{5,1},... | collective-permute-start | bytes 1572872 | tf_op jit(solution)/shard_map/ppermute | solution.py:33
  (38 other events, 271.8 us)

commit v5 on v4

--- a/solution.py
+++ b/solution.py
@@ -137,7 +137,13 @@
     return (at + jnp.where(second, info[BASES + slot + 1], info[BASES + slot])).astype(jnp.float32)
 
 
-def token_kernel(info, column_ref, row_ref, ids_ref, table_ref, meta_ref, turn_ref):
+def token_kernel(info, column_ref, row_ref, ids_ref, table_ref, *refs):
+    count = (len(refs) - 3) // 2
+    meta_ref, turn_ref = refs[count : count + 2]
+    pairs = zip(refs[:count], refs[count + 2 : -1])
+    copies = [pltpu.make_async_copy(a, b, refs[-1].at[k]) for k, (a, b) in enumerate(pairs)]
+    for copy in copies:
+        copy.start()
     rows = 2 * 128
     count = row_ref.shape[1]
     earlier = lax.broadcasted_iota(jnp.int32, (count, count), 0) < lax.broadcasted_iota(
@@ -160,6 +166,8 @@
         return 0
 
     lax.fori_loop(0, meta_ref.shape[0] // rows, one, 0)
+    for copy in copies:
+        copy.wait()
 
 
 def rank_kernel(count, slots, info, *refs):
@@ -369,9 +377,10 @@
             out_refs[1][:, at] = total[half:] + arrived_ref[:half, at].astype(jnp.float32)
 
 
-def call(kernel, operands, outs, info=None, scratch=(), mib=24, flops=1000, space=pltpu.VMEM):
+def call(kernel, operands, outs, info=None, scratch=(), mib=24, flops=1000, space=pltpu.VMEM, in_hbm=0):
     vmem = pl.BlockSpec(memory_space=pltpu.VMEM)
-    specs = [pl.BlockSpec(memory_space=space)] * len(operands)
+    specs = [pl.BlockSpec(memory_space=space)] * (len(operands) - in_hbm)
+    specs += [pl.BlockSpec(memory_space=pltpu.HBM)] * in_hbm
     if info is not None:
         operands, specs = [info] + operands, [pl.BlockSpec(memory_space=pltpu.SMEM)] + specs
     return pl.pallas_call(
@@ -442,12 +451,13 @@
     info = lax.dynamic_slice(jnp.asarray(table), (group, me, 0), (1, 1, table.shape[2])).reshape(-1)
 
     norm_args = [tokens, layer_norm_gain.reshape(1, -1), layer_norm_bias.reshape(1, -1)]
+    norm_args = [pltpu.with_memory_space_constraint(x, pltpu.HBM) for x in norm_args]
     own = call(
         norm_kernel,
         norm_args,
         [shape(block, model_width)],
         scratch=[pltpu.VMEM(x.shape, x.dtype) for x in norm_args] + [pltpu.SemaphoreType.DMA((3,))],
-        space=pl.ANY,
+        space=pltpu.HBM,
     )[0]
     other = to_partner(own)
     ring_a, ring_b = along_ring(own), along_ring(other)
@@ -466,9 +476,17 @@
         wide(request_adapter)[None, :],
         jnp.asarray(turn_rows),
     ]
-    meta, turns = call(token_kernel, token_args, [shape(token_rows, 128, jnp.float32)] * 2, info)
-
-    qkv_rows = query_key_weight.reshape(model_width, 3 * HEAD_SIZE)
+    weights = [query_key_weight.reshape(model_width, 3 * HEAD_SIZE), up_weight]
+    weights = [pltpu.with_memory_space_constraint(x, pltpu.HBM) for x in weights]
+    meta, turns, qkv_rows, up_rows = call(
+        token_kernel,
+        token_args + weights,
+        [shape(token_rows, 128, jnp.float32)] * 2 + [shape(*x.shape) for x in weights],
+        info,
+        [pltpu.SemaphoreType.DMA((2,))],
+        in_hbm=2,
+    )
+
     adapter_columns = query_key_value_right.shape[0]
     qkv_right = query_key_value_right.reshape(adapter_columns, 3 * HEAD_SIZE)
     spread_first = spread_table(ADAPTER_RANK, 0, 128)
@@ -485,10 +503,10 @@
 
     held = functools.partial(pltpu.VMEM, dtype=jnp.float32)
 
-    def add_ranks(part, slots, so_far, ahead=()):
+    def add_ranks(part, slots, so_far):
         return call(
             functools.partial(rank_kernel, len(part), slots),
-            list(part) + [pair_left, meta, slot_columns, spread_own, so_far, *ahead],
+            list(part) + [pair_left, meta, slot_columns, spread_own, so_far],
             [shape(32, group_rows)],
             info,
         )[0]
@@ -497,7 +515,7 @@
         rows = len(part) * block
         return call(
             functools.partial(base_kernel, len(part)),
-            list(part) + [qkv_rows, up_weight],
+            list(part) + [qkv_rows, up_rows],
             [
                 shape(rows, 3 * HEAD_SIZE, jnp.float32),
                 shape(rows, hidden_width, jnp.float32),
@@ -515,7 +533,7 @@
     tie = lax.optimization_barrier
     own_part = (own, other)
     ring_a, meta, turns, pair_left = tie((ring_a, meta, turns, pair_left))
-    ranks = add_ranks(own_part, (0,), jnp.zeros((32, group_rows), jnp.bfloat16), (qkv_rows, up_weight))
+    ranks = add_ranks(own_part, (0,), jnp.zeros((32, group_rows), jnp.bfloat16))
     ring_b, ranks = tie((ring_b, ranks))
     part = arrivals(ring_a, ring_b)
     ring_a, ring_b = along_ring(ring_a), along_ring(ring_b)

time: 153 us -> 153 us (level)
  waiting for transfers between devices: 46 us -> 54.1 us
  local copies, waits for them, and re-layouts: 9.39 us -> 1.92 us
  other arithmetic: 4.99 us -> 3.4 us
    ppermute x14, waiting for transfers between devices: 33.2 us -> 41.2 us  [along_ring(): return lax.ppermute(value, 'mlp', RING_PERM)]
    unnamed x46 -> x32, local copies, waits for them, and re-layouts: 8.31 us -> 0.84 us
    concatenate x1, other arithmetic: 1.77 us -> 0.23 us  [per_device(): jnp.concatenate([input_adapter_left, to_partner(input_adapter_left)], axi...]
  transfers between devices with their start and end apart: 40 -> 40, of which waited for: 16 -> 17; matrix products, arithmetic and copies ran while one was open for 3% -> 2% of each run, Pallas kernels for 27% -> 28%
where the time goes in v5:
time: 153 us
  waiting for transfers between devices  54.1 us (35%)
  Pallas kernels  52.4 us (34%)
  starting transfers between devices  40.4 us (26%)
  other arithmetic  3.4 us (2%)
  local copies, waits for them, and re-layouts  1.92 us (1%)
    pallas_call x23, Pallas kernels, call(): pl.pallas_call(kernel, in_specs=specs, out_specs=[vmem] * len(outs), out_...  52.4 us
    ppermute x14, waiting for transfers between devices, along_ring(): return lax.ppermute(value, 'mlp', RING_PERM)  41.2 us
    ppermute x14, starting transfers between devices, along_ring(): return lax.ppermute(value, 'mlp', RING_PERM)  18.3 us
    ppermute x3, starting transfers between devices, to_group(): lax.ppermute(value, 'req', [(g, g + d) for g in range(req_count - d)])  8.98 us
    ppermute x2, waiting for transfers between devices, sum_over_mlp(): lax.ppermute(value, 'mlp', [(i, i ^ bit) for i in range(16)])  5.67 us
    ppermute x4, starting transfers between devices, per_device(): moved = lax.ppermute(rank_out, 'mlp', [(i, i ^ bit) for i in range(16)])  5.67 us
    ppermute x4, waiting for transfers between devices, per_device(): moved = lax.ppermute(rank_out, 'mlp', [(i, i ^ bit) for i in range(16)])  4.64 us
    ppermute x2, starting transfers between devices, sum_over_mlp(): lax.ppermute(value, 'mlp', [(i, i ^ bit) for i in range(16)])  3.89 us
  transfers between devices with their start and end apart: 40, of which 17 were waited for; matrix products, arithmetic and copies ran while one was open for 2% of the time, Pallas kernels for 28%

profile of v5, /device:TPU:0, one launch (start us, length us, event | category | flops | bytes accessed | tf_op | source)
XLA Modules:
  0.0 152.7 jit_solution(12887321936966389287)
XLA Ops:
  2.1 3.0 %collective-permute-start.2 = (bf16[64,4096]{1,0:T(8,128)(2,1)S(1)}, bf16[64,4096]{1,0:T(8,128)(2,1)S(1)}, u32[]{:S(2)}, u32[]{:S(2)}) collective-permute-start(bf16[64,4096]{1,0:T(8,128)(2,1)S(1)} %shard_map.217.refs_0_), channel_id=1, source_target_pairs={{0,4},{4,8},{8,12},{12,14},{14,10},{10,6},{6,2},{2,0},{1,3},{5,1},... | collective-permute-start | bytes 1572872 | tf_op jit(solution)/shard_map/ppermute | solution.py:33
  8.1 4.6 %shard_map.218 = (f32[2048,128]{1,0:T(8,128)S(1)}, f32[2048,128]{1,0:T(8,128)S(1)}, bf16[4096,768]{1,0:T(8,128)(2,1)S(1)}, bf16[4096,512]{1,0:T(8,128)(2,1)S(1)}) custom-call(s32[34]{0:T(128)S(1)} %dynamic-slice_bitcast_fusion.info, f32[65,1]{1,0:T(8,128)S(1)} %copy.24.column_ref, f32[1,65]{1,0:T(1,128)S(1)} %get-tuple-element.181.row_ref, ...), custom_call_target="tpu_custom_call" | custom-call | flops 1000 | bytes 1000 | tf_op jit(solution)/shard_map/pallas_call | solution.py:386
  17.4 4.5 %collective-permute-done.1.refs_1_.refs_3_ = bf16[64,4096]{1,0:T(8,128)(2,1)S(1)} collective-permute-done((bf16[64,4096]{1,0:T(8,128)(2,1)S(1)}, bf16[64,4096]{1,0:T(8,128)(2,1)S(1)}, u32[]{:S(2)}, u32[]{:S(2)}) %collective-permute-start.1) | collective-permute-done | bytes 524320 | tf_op jit(solution)/shard_map/ppermute | solution.py:33
  24.0 3.5 %collective-permute-done.9.refs_0_ = bf16[64,4096]{1,0:T(8,128)(2,1)S(1)} collective-permute-done((bf16[64,4096]{1,0:T(8,128)(2,1)S(1)}, bf16[64,4096]{1,0:T(8,128)(2,1)S(1)}, u32[]{:S(2)}, u32[]{:S(2)}) %collective-permute-start.9) | collective-permute-done | bytes 524320 | tf_op jit(solution)/shard_map/ppermute | solution.py:33
  30.6 4.2 %shard_map.221 = (f32[384,768]{1,0:T(8,128)S(1)}, f32[384,512]{1,0:T(8,128)S(1)}, bf16[384,512]{1,0:T(8,128)(2,1)S(1)}) custom-call(bf16[64,4096]{1,0:T(8,128)(2,1)S(1)} %shard_map.217.refs_0_, bf16[64,4096]{1,0:T(8,128)(2,1)S(1)} %collective-permute-done.refs_1_, bf16[64,4096]{1,0:T(8,128)(2,1)S(1)} %collective-permute-done.2.refs_0_.refs_2_, ...), custom_call_target="tpu_custom_call" | custom-call | flops 1000 | bytes 1000 | tf_op jit(solution)/shard_map/pallas_call | solution.py:386
  40.4 3.6 %collective-permute-start.15 = (bf16[384,512]{1,0:T(8,128)(2,1)S(1)}, bf16[384,512]{1,0:T(8,128)(2,1)S(1)}, u32[]{:S(2)}, u32[]{:S(2)}) collective-permute-start(bf16[384,512]{1,0:T(8,128)(2,1)S(1)} %get-tuple-element.116), channel_id=1, source_target_pairs={{0,16},{1,17},{2,18},{3,19},{4,20},{5,21},{6,22},{7,23},{8,24},{9,... | collective-permute-start | bytes 1179656 | tf_op jit(solution)/shard_map/ppermute | solution.py:502
  44.0 2.9 %shard_map.223 = (f32[256,768]{1,0:T(8,128)S(1)}, f32[256,512]{1,0:T(8,128)S(1)}, bf16[256,512]{1,0:T(8,128)(2,1)S(1)}) custom-call(bf16[64,4096]{1,0:T(8,128)(2,1)S(1)} %collective-permute-done.9.refs_0_, bf16[64,4096]{1,0:T(8,128)(2,1)S(1)} %collective-permute-done.5.refs_1_, bf16[64,4096]{1,0:T(8,128)(2,1)S(1)} %collective-permute-done.10.refs_2_, ...), custom_call_target="tpu_custom_call" | custom-call | flops 1000 | bytes 1000 | tf_op jit(solution)/shard_map/pallas_call | solution.py:386
  55.9 2.9 %shard_map.227 = (f32[256,768]{1,0:T(8,128)S(1)}, f32[256,512]{1,0:T(8,128)S(1)}, bf16[256,512]{1,0:T(8,128)(2,1)S(1)}) custom-call(bf16[64,4096]{1,0:T(8,128)(2,1)S(1)} %collective-permute-done.16.refs_0_, bf16[64,4096]{1,0:T(8,128)(2,1)S(1)} %collective-permute-done.17.refs_1_, bf16[64,4096]{1,0:T(8,128)(2,1)S(1)} %collective-permute-done.14.refs_2_, ...), custom_call_target="tpu_custom_call" | custom-call | flops 1000 | bytes 1000 | tf_op jit(solution)/shard_map/pallas_call | solution.py:386
  59.6 3.9 %collective-permute-start.22 = (bf16[640,512]{1,0:T(8,128)(2,1)S(1)}, bf16[640,512]{1,0:T(8,128)(2,1)S(1)}, u32[]{:S(2)}, u32[]{:S(2)}) collective-permute-start(bf16[640,512]{1,0:T(8,128)(2,1)S(1)} %pad_maximum_fusion.1), channel_id=1, source_target_pairs={{0,16},{1,17},{2,18},{3,19},{4,20},{5,21},{6,22},{7,23},{8,24},{9,... | collective-permute-start | bytes 1966088 | tf_op jit(solution)/shard_map/ppermute | solution.py:502
  65.1 2.7 %collective-permute-done.20 = bf16[32,1024]{1,0:T(8,128)(2,1)S(1)} collective-permute-done((bf16[32,1024]{1,0:T(8,128)(2,1)S(1)}, bf16[32,1024]{1,0:T(8,128)(2,1)S(1)}, u32[]{:S(2)}, u32[]{:S(2)}) %collective-permute-start.20) | collective-permute-done | bytes 65568 | tf_op jit(solution)/shard_map/ppermute | solution.py:403
  67.8 2.2 %collective-permute-start.21 = (bf16[32,1024]{1,0:T(8,128)(2,1)S(1)}, bf16[32,1024]{1,0:T(8,128)(2,1)S(1)}, u32[]{:S(2)}, u32[]{:S(2)}) collective-permute-start(bf16[32,1024]{1,0:T(8,128)(2,1)S(1)} %add.62), channel_id=1, source_target_pairs={{0,8},{1,9},{2,10},{3,11},{4,12},{5,13},{6,14},{7,15},{8,0},{9,1},... | collective-permute-start | bytes 196616 | tf_op jit(solution)/shard_map/ppermute | solution.py:403
  70.1 3.0 %collective-permute-done.21 = bf16[32,1024]{1,0:T(8,128)(2,1)S(1)} collective-permute-done((bf16[32,1024]{1,0:T(8,128)(2,1)S(1)}, bf16[32,1024]{1,0:T(8,128)(2,1)S(1)}, u32[]{:S(2)}, u32[]{:S(2)}) %collective-permute-start.21) | collective-permute-done | bytes 65568 | tf_op jit(solution)/shard_map/ppermute | solution.py:403
  74.7 6.4 %shard_map.228 = (bf16[1024,256]{1,0:T(8,128)(2,1)S(1)}, bf16[1024,256]{1,0:T(8,128)(2,1)S(1)}, bf16[1024,256]{1,0:T(8,128)(2,1)S(1)}, bf16[1024,512]{1,0:T(8,128)(2,1)S(1)}, bf16[32,1024]{1,0:T(8,128)(2,1)S(1)}) custom-call(s32[34]{0:T(128)S(1)} %dynamic-slice_bitcast_fusion.info, f32[384,768]{1,0:T(8,128)S(1)} %get-tuple-element.104.refs_0_, ...), custom_call_target="tpu_custom_call" | custom-call | flops 1000 | bytes 1000 | tf_op jit(solution)/shard_map/pallas_call | solution.py:386
  81.2 2.3 %shard_map.229 = (bf16[1024,256]{1,0:T(8,128)(2,1)S(1)}, bf16[1024,256]{1,0:T(8,128)(2,1)S(1)}) custom-call(s32[34]{0:T(128)S(1)} %dynamic-slice_bitcast_fusion.info, bf16[384,512]{1,0:T(8,128)(2,1)S(1)} %collective-permute-done.15.refs_0_, bf16[256,512]{1,0:T(8,128)(2,1)S(1)} %get-tuple-element.180.refs_1_, bf16[128,512]{1,0:T(8,128)(2,1)S(1)} %slice.17.refs_2_, ...), custom_call_target="tpu_custom_call" | custom-call | flops 1000 | bytes 1000 | tf_op jit(solution)/shard_map/pallas_call | solution.py:386
  83.6 5.8 %shard_map.230 = (bf16[1024,256]{1,0:T(8,128)(2,1)S(1)}, bf16[32,1024]{1,0:T(8,128)(2,1)S(1)}) custom-call(s32[34]{0:T(128)S(1)} %dynamic-slice_bitcast_fusion.info, bf16[1024,256]{1,0:T(8,128)(2,1)S(1)} %get-tuple-element.130.refs_0_, bf16[1024,256]{1,0:T(8,128)(2,1)S(1)} %get-tuple-element.131.refs_1_, bf16[1024,256]{1,0:T(8,128)(2,1)S(1)} %get-tuple-element.136.refs_2_, ...), custom_call_target="tpu_custom_call" | custom-call | flops 1000 | bytes 1000 | tf_op jit(solution)/shard_map/pallas_call | solution.py:386
  100.6 2.7 %collective-permute-start.28 = (bf16[32,1024]{1,0:T(8,128)(2,1)S(1)}, bf16[32,1024]{1,0:T(8,128)(2,1)S(1)}, u32[]{:S(2)}, u32[]{:S(2)}) collective-permute-start(bf16[32,1024]{1,0:T(8,128)(2,1)S(1)} %add.66), channel_id=1, source_target_pairs={{0,8},{1,9},{2,10},{3,11},{4,12},{5,13},{6,14},{7,15},{8,0},{9,1},... | collective-permute-start | bytes 196616 | tf_op jit(solution)/shard_map/ppermute | solution.py:619
  105.2 2.3 %collective-permute-done.28 = bf16[32,1024]{1,0:T(8,128)(2,1)S(1)} collective-permute-done((bf16[32,1024]{1,0:T(8,128)(2,1)S(1)}, bf16[32,1024]{1,0:T(8,128)(2,1)S(1)}, u32[]{:S(2)}, u32[]{:S(2)}) %collective-permute-start.28) | collective-permute-done | bytes 65568 | tf_op jit(solution)/shard_map/ppermute | solution.py:619
  113.4 4.7 %collective-permute-done.30 = bf16[64,4096]{1,0:T(8,128)(2,1)S(1)} collective-permute-done((bf16[64,4096]{1,0:T(8,128)(2,1)S(1)}, bf16[64,4096]{1,0:T(8,128)(2,1)S(1)}, u32[]{:S(2)}, u32[]{:S(2)}) %collective-permute-start.30) | collective-permute-done | bytes 524320 | tf_op jit(solution)/shard_map/ppermute | solution.py:33
  118.9 4.7 %collective-permute-done.36 = bf16[64,4096]{1,0:T(8,128)(2,1)S(1)} collective-permute-done((bf16[64,4096]{1,0:T(8,128)(2,1)S(1)}, bf16[64,4096]{1,0:T(8,128)(2,1)S(1)}, u32[]{:S(2)}, u32[]{:S(2)}) %collective-permute-start.36) | collective-permute-done | bytes 524320 | tf_op jit(solution)/shard_map/ppermute | solution.py:33
  125.8 3.5 %collective-permute-done.31 = bf16[64,4096]{1,0:T(8,128)(2,1)S(1)} collective-permute-done((bf16[64,4096]{1,0:T(8,128)(2,1)S(1)}, bf16[64,4096]{1,0:T(8,128)(2,1)S(1)}, u32[]{:S(2)}, u32[]{:S(2)}) %collective-permute-start.31) | collective-permute-done | bytes 524320 | tf_op jit(solution)/shard_map/ppermute | solution.py:33
  130.1 4.8 %collective-permute-done.37 = bf16[64,4096]{1,0:T(8,128)(2,1)S(1)} collective-permute-done((bf16[64,4096]{1,0:T(8,128)(2,1)S(1)}, bf16[64,4096]{1,0:T(8,128)(2,1)S(1)}, u32[]{:S(2)}, u32[]{:S(2)}) %collective-permute-start.37) | collective-permute-done | bytes 524320 | tf_op jit(solution)/shard_map/ppermute | solution.py:33
  135.7 4.8 %collective-permute-done.33 = bf16[64,4096]{1,0:T(8,128)(2,1)S(1)} collective-permute-done((bf16[64,4096]{1,0:T(8,128)(2,1)S(1)}, bf16[64,4096]{1,0:T(8,128)(2,1)S(1)}, u32[]{:S(2)}, u32[]{:S(2)}) %collective-permute-start.33) | collective-permute-done | bytes 524320 | tf_op jit(solution)/shard_map/ppermute | solution.py:33
  141.3 4.8 %collective-permute-done.38 = bf16[64,4096]{1,0:T(8,128)(2,1)S(1)} collective-permute-done((bf16[64,4096]{1,0:T(8,128)(2,1)S(1)}, bf16[64,4096]{1,0:T(8,128)(2,1)S(1)}, u32[]{:S(2)}, u32[]{:S(2)}) %collective-permute-start.38) | collective-permute-done | bytes 524320 | tf_op jit(solution)/shard_map/ppermute | solution.py:33
  147.6 4.2 %collective-permute-done.35 = bf16[64,4096]{1,0:T(8,128)(2,1)S(1)} collective-permute-done((bf16[64,4096]{1,0:T(8,128)(2,1)S(1)}, bf16[64,4096]{1,0:T(8,128)(2,1)S(1)}, u32[]{:S(2)}, u32[]{:S(2)}) %collective-permute-start.35) | collective-permute-done | bytes 524320 | tf_op jit(solution)/shard_map/ppermute | solution.py:33
  (139 shorter events, 60.3 us)
Async XLA Ops:
  0.0 14.3 %collective-permute-start.3 = (bf16[4096,128]{1,0:T(8,128)(2,1)}, bf16[4096,128]{1,0:T(8,128)(2,1)S(1)}, u32[]{:S(2)}, u32[]{:S(2)}) collective-permute-start(bf16[4096,128]{1,0:T(8,128)(2,1)} %param.32), channel_id=1, source_target_pairs={{0,1},{1,0},{2,3},{3,2},{4,5},{5,4},{6,7},{7,6},{8,9},{9,8},{10,11... | collective-permute-start | bytes 3145736 | tf_op jit(solution)/shard_map/ppermute | solution.py:29
  2.0 10.7 %collective-permute-start = (bf16[64,4096]{1,0:T(8,128)(2,1)S(1)}, bf16[64,4096]{1,0:T(8,128)(2,1)S(1)}, u32[]{:S(2)}, u32[]{:S(2)}) collective-permute-start(bf16[64,4096]{1,0:T(8,128)(2,1)S(1)} %shard_map.217.refs_0_), channel_id=1, source_target_pairs={{0,1},{1,0},{2,3},{3,2},{4,5},{5,4},{6,7},{7,6},{8,9},{9,8},{10,11... | collective-permute-start | bytes 1572872 | tf_op jit(solution)/shard_map/ppermute | solution.py:29
  2.1 12.5 %collective-permute-start.2 = (bf16[64,4096]{1,0:T(8,128)(2,1)S(1)}, bf16[64,4096]{1,0:T(8,128)(2,1)S(1)}, u32[]{:S(2)}, u32[]{:S(2)}) collective-permute-start(bf16[64,4096]{1,0:T(8,128)(2,1)S(1)} %shard_map.217.refs_0_), channel_id=1, source_target_pairs={{0,4},{4,8},{8,12},{12,14},{14,10},{10,6},{6,2},{2,0},{1,3},{5,1},... | collective-permute-start | bytes 1572872 | tf_op jit(solution)/shard_map/ppermute | solution.py:33
  6.0 10.3 %collective-permute-start.4 = (f32[1,128]{1,0:T(1,128)S(1)}, f32[1,128]{1,0:T(1,128)S(1)}, u32[]{:S(2)}, u32[]{:S(2)}) collective-permute-start(f32[1,128]{1,0:T(1,128)S(1)} %convert_element_type.71), channel_id=1, source_target_pairs={{0,1},{1,0},{2,3},{3,2},{4,5},{5,4},{6,7},{7,6},{8,9},{9,8},{10,11... | collective-permute-start | bytes 1544 | tf_op jit(solution)/shard_map/ppermute | solution.py:29
  12.7 9.2 %collective-permute-start.1 = (bf16[64,4096]{1,0:T(8,128)(2,1)S(1)}, bf16[64,4096]{1,0:T(8,128)(2,1)S(1)}, u32[]{:S(2)}, u32[]{:S(2)}) collective-permute-start(bf16[64,4096]{1,0:T(8,128)(2,1)S(1)} %collective-permute-done.refs_1_), channel_id=1, source_target_pairs={{0,4},{4,8},{8,12},{12,14},{14,10},{10,6},{6,2},{2,0},{1,3},{5,1},... | collective-permute-start | bytes 1572872 | tf_op jit(solution)/shard_map/ppermute | solution.py:33
  14.6 13.0 %collective-permute-start.9 = (bf16[64,4096]{1,0:T(8,128)(2,1)S(1)}, bf16[64,4096]{1,0:T(8,128)(2,1)S(1)}, u32[]{:S(2)}, u32[]{:S(2)}) collective-permute-start(bf16[64,4096]{1,0:T(8,128)(2,1)S(1)} %collective-permute-done.2.refs_0_.refs_2_), channel_id=1, source_target_pairs={{0,4},{4,8},{8,12},{12,14},{14,10},{10,6},{6,2},{2,0},{1,3},{5,1},... | collective-permute-start | bytes 1572872 | tf_op jit(solution)/shard_map/ppermute | solution.py:33
  22.5 12.4 %collective-permute-start.5 = (bf16[64,4096]{1,0:T(8,128)(2,1)S(1)}, bf16[64,4096]{1,0:T(8,128)(2,1)S(1)}, u32[]{:S(2)}, u32[]{:S(2)}) collective-permute-start(bf16[64,4096]{1,0:T(8,128)(2,1)S(1)} %collective-permute-done.1.refs_1_.refs_3_), channel_id=1, source_target_pairs={{0,4},{4,8},{8,12},{12,14},{14,10},{10,6},{6,2},{2,0},{1,3},{5,1},... | collective-permute-start | bytes 1572872 | tf_op jit(solution)/shard_map/ppermute | solution.py:33
  24.0 24.3 %collective-permute-start.12 = (bf16[128,4096]{1,0:T(8,128)(2,1)S(1)}, bf16[128,4096]{1,0:T(8,128)(2,1)S(1)}, u32[]{:S(2)}, u32[]{:S(2)}) collective-permute-start(bf16[128,4096]{1,0:T(8,128)(2,1)S(1)} %copy-done.12), channel_id=1, source_target_pairs={{0,1},{1,0},{2,3},{3,2},{4,5},{5,4},{6,7},{7,6},{8,9},{9,8},{10,11... | collective-permute-start | bytes 3145736 | tf_op jit(solution)/shard_map/ppermute | solution.py:29
  27.6 11.2 %collective-permute-start.13 = (bf16[64,4096]{1,0:T(8,128)(2,1)S(1)}, bf16[64,4096]{1,0:T(8,128)(2,1)S(1)}, u32[]{:S(2)}, u32[]{:S(2)}) collective-permute-start(bf16[64,4096]{1,0:T(8,128)(2,1)S(1)} %collective-permute-done.9.refs_0_), channel_id=1, source_target_pairs={{0,4},{4,8},{8,12},{12,14},{14,10},{10,6},{6,2},{2,0},{1,3},{5,1},... | collective-permute-start | bytes 1572872 | tf_op jit(solution)/shard_map/ppermute | solution.py:33
  34.9 9.1 %collective-permute-start.11 = (bf16[64,4096]{1,0:T(8,128)(2,1)S(1)}, bf16[64,4096]{1,0:T(8,128)(2,1)S(1)}, u32[]{:S(2)}, u32[]{:S(2)}) collective-permute-start(bf16[64,4096]{1,0:T(8,128)(2,1)S(1)} %collective-permute-done.9.refs_0_), channel_id=1, source_target_pairs={{0,1},{1,0},{2,3},{3,2},{4,5},{5,4},{6,7},{7,6},{8,9},{9,8},{10,11... | collective-permute-start | bytes 1572872 | tf_op jit(solution)/shard_map/ppermute | solution.py:29
  35.4 12.9 %collective-permute-start.8 = (bf16[64,4096]{1,0:T(8,128)(2,1)S(1)}, bf16[64,4096]{1,0:T(8,128)(2,1)S(1)}, u32[]{:S(2)}, u32[]{:S(2)}) collective-permute-start(bf16[64,4096]{1,0:T(8,128)(2,1)S(1)} %collective-permute-done.5.refs_1_), channel_id=1, source_target_pairs={{0,4},{4,8},{8,12},{12,14},{14,10},{10,6},{6,2},{2,0},{1,3},{5,1},... | collective-permute-start | bytes 1572872 | tf_op jit(solution)/shard_map/ppermute | solution.py:33
  38.8 12.9 %collective-permute-start.14 = (bf16[64,4096]{1,0:T(8,128)(2,1)S(1)}, bf16[64,4096]{1,0:T(8,128)(2,1)S(1)}, u32[]{:S(2)}, u32[]{:S(2)}) collective-permute-start(bf16[64,4096]{1,0:T(8,128)(2,1)S(1)} %collective-permute-done.13.refs_0_), channel_id=1, source_target_pairs={{0,4},{4,8},{8,12},{12,14},{14,10},{10,6},{6,2},{2,0},{1,3},{5,1},... | collective-permute-start | bytes 1572872 | tf_op jit(solution)/shard_map/ppermute | solution.py:33
  40.4 11.3 %collective-permute-start.15 = (bf16[384,512]{1,0:T(8,128)(2,1)S(1)}, bf16[384,512]{1,0:T(8,128)(2,1)S(1)}, u32[]{:S(2)}, u32[]{:S(2)}) collective-permute-start(bf16[384,512]{1,0:T(8,128)(2,1)S(1)} %get-tuple-element.116), channel_id=1, source_target_pairs={{0,16},{1,17},{2,18},{3,19},{4,20},{5,21},{6,22},{7,23},{8,24},{9,... | collective-permute-start | bytes 1179656 | tf_op jit(solution)/shard_map/ppermute | solution.py:502
  59.6 21.5 %collective-permute-start.22 = (bf16[640,512]{1,0:T(8,128)(2,1)S(1)}, bf16[640,512]{1,0:T(8,128)(2,1)S(1)}, u32[]{:S(2)}, u32[]{:S(2)}) collective-permute-start(bf16[640,512]{1,0:T(8,128)(2,1)S(1)} %pad_maximum_fusion.1), channel_id=1, source_target_pairs={{0,16},{1,17},{2,18},{3,19},{4,20},{5,21},{6,22},{7,23},{8,24},{9,... | collective-permute-start | bytes 1966088 | tf_op jit(solution)/shard_map/ppermute | solution.py:502
  95.9 11.7 %collective-permute-start.29 = (bf16[128,4096]{1,0:T(8,128)(2,1)S(1)}, bf16[128,4096]{1,0:T(8,128)(2,1)S(1)}, u32[]{:S(2)}, u32[]{:S(2)}) collective-permute-start(bf16[128,4096]{1,0:T(8,128)(2,1)S(1)} %get-tuple-element.160), channel_id=1, source_target_pairs={{0,1},{1,0},{2,3},{3,2},{4,5},{5,4},{6,7},{7,6},{8,9},{9,8},{10,11... | collective-permute-start | bytes 3145736 | tf_op jit(solution)/shard_map/ppermute | solution.py:29
  100.5 11.6 %collective-permute-start.32 = (bf16[128,4096]{1,0:T(8,128)(2,1)S(1)}, bf16[128,4096]{1,0:T(8,128)(2,1)S(1)}, u32[]{:S(2)}, u32[]{:S(2)}) collective-permute-start(bf16[128,4096]{1,0:T(8,128)(2,1)S(1)} %get-tuple-element.169), channel_id=1, source_target_pairs={{0,1},{1,0},{2,3},{3,2},{4,5},{5,4},{6,7},{7,6},{8,9},{9,8},{10,11... | collective-permute-start | bytes 3145736 | tf_op jit(solution)/shard_map/ppermute | solution.py:29
  108.8 9.2 %collective-permute-start.30 = (bf16[64,4096]{1,0:T(8,128)(2,1)S(1)}, bf16[64,4096]{1,0:T(8,128)(2,1)S(1)}, u32[]{:S(2)}, u32[]{:S(2)}) collective-permute-start(bf16[64,4096]{1,0:T(8,128)(2,1)S(1)} %shard_map.235), channel_id=1, source_target_pairs={{0,4},{4,8},{8,12},{12,14},{14,10},{10,6},{6,2},{2,0},{1,3},{5,1},... | collective-permute-start | bytes 1572872 | tf_op jit(solution)/shard_map/ppermute | solution.py:33
  109.5 15.0 %collective-permute-start.34 = (bf16[128,4096]{1,0:T(8,128)(2,1)S(1)}, bf16[128,4096]{1,0:T(8,128)(2,1)S(1)}, u32[]{:S(2)}, u32[]{:S(2)}) collective-permute-start(bf16[128,4096]{1,0:T(8,128)(2,1)S(1)} %get-tuple-element.172), channel_id=1, source_target_pairs={{0,1},{1,0},{2,3},{3,2},{4,5},{5,4},{6,7},{7,6},{8,9},{9,8},{10,11... | collective-permute-start | bytes 3145736 | tf_op jit(solution)/shard_map/ppermute | solution.py:29
  110.9 12.8 %collective-permute-start.36 = (bf16[64,4096]{1,0:T(8,128)(2,1)S(1)}, bf16[64,4096]{1,0:T(8,128)(2,1)S(1)}, u32[]{:S(2)}, u32[]{:S(2)}) collective-permute-start(bf16[64,4096]{1,0:T(8,128)(2,1)S(1)} %convert_element_type.79), channel_id=1, source_target_pairs={{0,4},{4,8},{8,12},{12,14},{14,10},{10,6},{6,2},{2,0},{1,3},{5,1},... | collective-permute-start | bytes 1572872 | tf_op jit(solution)/shard_map/ppermute | solution.py:33
  118.2 11.1 %collective-permute-start.31 = (bf16[64,4096]{1,0:T(8,128)(2,1)S(1)}, bf16[64,4096]{1,0:T(8,128)(2,1)S(1)}, u32[]{:S(2)}, u32[]{:S(2)}) collective-permute-start(bf16[64,4096]{1,0:T(8,128)(2,1)S(1)} %add_convert_fusion.6), channel_id=1, source_target_pairs={{0,4},{4,8},{8,12},{12,14},{14,10},{10,6},{6,2},{2,0},{1,3},{5,1},... | collective-permute-start | bytes 1572872 | tf_op jit(solution)/shard_map/ppermute | solution.py:33
  123.8 11.1 %collective-permute-start.37 = (bf16[64,4096]{1,0:T(8,128)(2,1)S(1)}, bf16[64,4096]{1,0:T(8,128)(2,1)S(1)}, u32[]{:S(2)}, u32[]{:S(2)}) collective-permute-start(bf16[64,4096]{1,0:T(8,128)(2,1)S(1)} %add_convert_fusion.3), channel_id=1, source_target_pairs={{0,4},{4,8},{8,12},{12,14},{14,10},{10,6},{6,2},{2,0},{1,3},{5,1},... | collective-permute-start | bytes 1572872 | tf_op jit(solution)/shard_map/ppermute | solution.py:33
  129.4 11.1 %collective-permute-start.33 = (bf16[64,4096]{1,0:T(8,128)(2,1)S(1)}, bf16[64,4096]{1,0:T(8,128)(2,1)S(1)}, u32[]{:S(2)}, u32[]{:S(2)}) collective-permute-start(bf16[64,4096]{1,0:T(8,128)(2,1)S(1)} %add_convert_fusion.5), channel_id=1, source_target_pairs={{0,4},{4,8},{8,12},{12,14},{14,10},{10,6},{6,2},{2,0},{1,3},{5,1},... | collective-permute-start | bytes 1572872 | tf_op jit(solution)/shard_map/ppermute | solution.py:33
  135.0 11.1 %collective-permute-start.38 = (bf16[64,4096]{1,0:T(8,128)(2,1)S(1)}, bf16[64,4096]{1,0:T(8,128)(2,1)S(1)}, u32[]{:S(2)}, u32[]{:S(2)}) collective-permute-start(bf16[64,4096]{1,0:T(8,128)(2,1)S(1)} %add_convert_fusion.2), channel_id=1, source_target_pairs={{0,4},{4,8},{8,12},{12,14},{14,10},{10,6},{6,2},{2,0},{1,3},{5,1},... | collective-permute-start | bytes 1572872 | tf_op jit(solution)/shard_map/ppermute | solution.py:33
  140.6 11.1 %collective-permute-start.35 = (bf16[64,4096]{1,0:T(8,128)(2,1)S(1)}, bf16[64,4096]{1,0:T(8,128)(2,1)S(1)}, u32[]{:S(2)}, u32[]{:S(2)}) collective-permute-start(bf16[64,4096]{1,0:T(8,128)(2,1)S(1)} %add_convert_fusion.4), channel_id=1, source_target_pairs={{0,4},{4,8},{8,12},{12,14},{14,10},{10,6},{6,2},{2,0},{1,3},{5,1},... | collective-permute-start | bytes 1572872 | tf_op jit(solution)/shard_map/ppermute | solution.py:33
  (31 other events, 234.9 us)

commit v6 on v5

--- a/solution.py
+++ b/solution.py
@@ -461,7 +461,7 @@
     )[0]
     other = to_partner(own)
     ring_a, ring_b = along_ring(own), along_ring(other)
-    pair_left = jnp.concatenate([input_adapter_left, to_partner(input_adapter_left)], axis=1)
+    near_left, far_left = input_adapter_left, to_partner(input_adapter_left)
 
     float_lengths = wide(lengths)
     lane = np.arange(128)
@@ -532,12 +532,12 @@
 
     tie = lax.optimization_barrier
     own_part = (own, other)
-    ring_a, meta, turns, pair_left = tie((ring_a, meta, turns, pair_left))
-    ranks = add_ranks(own_part, (0,), jnp.zeros((32, group_rows), jnp.bfloat16))
-    ring_b, ranks = tie((ring_b, ranks))
+    ring_a, meta, turns, qkv_rows, up_rows = tie((ring_a, meta, turns, qkv_rows, up_rows))
+    ring_b, near_left, far_left = tie((ring_b, near_left, far_left))
+    pair_left = jnp.concatenate([near_left, far_left], axis=1)
     part = arrivals(ring_a, ring_b)
     ring_a, ring_b = along_ring(ring_a), along_ring(ring_b)
-    ranks = add_ranks(part, (2, 3), ranks)
+    ranks = add_ranks(own_part + part, (0, 2, 3), jnp.zeros((32, group_rows), jnp.bfloat16))
     first = products_of(own_part + part)
     ring_b, ranks, first = tie((ring_b, ranks, first))
     part = arrivals(ring_a, ring_b)

time: 153 us -> 150 us (0.980)
  starting transfers between devices: 40.4 us -> 36.7 us
  local copies, waits for them, and re-layouts: 1.92 us -> 3.6 us
    ppermute x14, starting transfers between devices: 18.3 us -> 14.3 us  [along_ring(): return lax.ppermute(value, 'mlp', RING_PERM)]
    pallas_call x23 -> x22, Pallas kernels: 52.4 us -> 51.5 us  [call(): pl.pallas_call(kernel, in_specs=specs, out_specs=[vmem] * len(outs), out_...]
  transfers between devices with their start and end apart: 40 -> 40, of which waited for: 17 -> 16; matrix products, arithmetic and copies ran while one was open for 2% -> 3% of each run, Pallas kernels for 28% -> 27%
where the time goes in v6:
time: 150 us
  waiting for transfers between devices  54.1 us (36%)
  Pallas kernels  51.5 us (34%)
  starting transfers between devices  36.7 us (24%)
  local copies, waits for them, and re-layouts  3.6 us (2%)
  other arithmetic  3.22 us (2%)
    pallas_call x22, Pallas kernels, call(): pl.pallas_call(kernel, in_specs=specs, out_specs=[vmem] * len(outs), out_...  51.5 us
    ppermute x14, waiting for transfers between devices, along_ring(): return lax.ppermute(value, 'mlp', RING_PERM)  40.9 us
    ppermute x14, starting transfers between devices, along_ring(): return lax.ppermute(value, 'mlp', RING_PERM)  14.3 us
    ppermute x3, starting transfers between devices, to_group(): lax.ppermute(value, 'req', [(g, g + d) for g in range(req_count - d)])  9.44 us
    ppermute x2, waiting for transfers between devices, sum_over_mlp(): lax.ppermute(value, 'mlp', [(i, i ^ bit) for i in range(16)])  5.98 us
    ppermute x4, waiting for transfers between devices, per_device(): moved = lax.ppermute(rank_out, 'mlp', [(i, i ^ bit) for i in range(16)])  5.26 us
    ppermute x4, starting transfers between devices, per_device(): moved = lax.ppermute(rank_out, 'mlp', [(i, i ^ bit) for i in range(16)])  5.02 us
    ppermute x2, starting transfers between devices, sum_over_mlp(): lax.ppermute(value, 'mlp', [(i, i ^ bit) for i in range(16)])  3.59 us
  transfers between devices with their start and end apart: 40, of which 16 were waited for; matrix products, arithmetic and copies ran while one was open for 3% of the time, Pallas kernels for 27%

profile of v6, /device:TPU:0, one launch (start us, length us, event | category | flops | bytes accessed | tf_op | source)
XLA Modules:
  0.0 149.8 jit_solution(3548713457710947970)
XLA Ops:
  2.1 3.0 %collective-permute-start.4 = (bf16[64,4096]{1,0:T(8,128)(2,1)S(1)}, bf16[64,4096]{1,0:T(8,128)(2,1)S(1)}, u32[]{:S(2)}, u32[]{:S(2)}) collective-permute-start(bf16[64,4096]{1,0:T(8,128)(2,1)S(1)} %shard_map.217.refs_0_), channel_id=1, source_target_pairs={{0,4},{4,8},{8,12},{12,14},{14,10},{10,6},{6,2},{2,0},{1,3},{5,1},... | collective-permute-start | bytes 1572872 | tf_op jit(solution)/shard_map/ppermute | solution.py:33
  10.2 4.6 %shard_map.218 = (f32[2048,128]{1,0:T(8,128)S(1)}, f32[2048,128]{1,0:T(8,128)S(1)}, bf16[4096,768]{1,0:T(8,128)(2,1)S(1)}, bf16[4096,512]{1,0:T(8,128)(2,1)S(1)}) custom-call(s32[34]{0:T(128)S(1)} %dynamic-slice_bitcast_fusion.info, f32[65,1]{1,0:T(8,128)S(1)} %copy.24.column_ref, f32[1,65]{1,0:T(1,128)S(1)} %get-tuple-element.185.row_ref, ...), custom_call_target="tpu_custom_call" | custom-call | flops 1000 | bytes 1000 | tf_op jit(solution)/shard_map/pallas_call | solution.py:386
  17.9 2.1 %collective-permute-start.3 = (bf16[64,4096]{1,0:T(8,128)(2,1)S(1)}, bf16[64,4096]{1,0:T(8,128)(2,1)S(1)}, u32[]{:S(2)}, u32[]{:S(2)}) collective-permute-start(bf16[64,4096]{1,0:T(8,128)(2,1)S(1)} %collective-permute-done.1.refs_3_), channel_id=1, source_target_pairs={{0,4},{4,8},{8,12},{12,14},{14,10},{10,6},{6,2},{2,0},{1,3},{5,1},... | collective-permute-start | bytes 1572872 | tf_op jit(solution)/shard_map/ppermute | solution.py:33
  20.1 4.0 %collective-permute-done.9.refs_0_ = bf16[64,4096]{1,0:T(8,128)(2,1)S(1)} collective-permute-done((bf16[64,4096]{1,0:T(8,128)(2,1)S(1)}, bf16[64,4096]{1,0:T(8,128)(2,1)S(1)}, u32[]{:S(2)}, u32[]{:S(2)}) %collective-permute-start.9) | collective-permute-done | bytes 524320 | tf_op jit(solution)/shard_map/ppermute | solution.py:33
  27.2 4.2 %shard_map.220 = (f32[384,768]{1,0:T(8,128)S(1)}, f32[384,512]{1,0:T(8,128)S(1)}, bf16[384,512]{1,0:T(8,128)(2,1)S(1)}) custom-call(bf16[64,4096]{1,0:T(8,128)(2,1)S(1)} %shard_map.217.refs_0_, bf16[64,4096]{1,0:T(8,128)(2,1)S(1)} %collective-permute-done.refs_1_, bf16[64,4096]{1,0:T(8,128)(2,1)S(1)} %collective-permute-done.4.refs_2_, ...), custom_call_target="tpu_custom_call" | custom-call | flops 1000 | bytes 1000 | tf_op jit(solution)/shard_map/pallas_call | solution.py:386
  36.9 3.6 %collective-permute-start.15 = (bf16[384,512]{1,0:T(8,128)(2,1)S(1)}, bf16[384,512]{1,0:T(8,128)(2,1)S(1)}, u32[]{:S(2)}, u32[]{:S(2)}) collective-permute-start(bf16[384,512]{1,0:T(8,128)(2,1)S(1)} %get-tuple-element.120), channel_id=1, source_target_pairs={{0,16},{1,17},{2,18},{3,19},{4,20},{5,21},{6,22},{7,23},{8,24},{9,... | collective-permute-start | bytes 1179656 | tf_op jit(solution)/shard_map/ppermute | solution.py:502
  40.6 2.9 %shard_map.222 = (f32[256,768]{1,0:T(8,128)S(1)}, f32[256,512]{1,0:T(8,128)S(1)}, bf16[256,512]{1,0:T(8,128)(2,1)S(1)}) custom-call(bf16[64,4096]{1,0:T(8,128)(2,1)S(1)} %collective-permute-done.9.refs_0_, bf16[64,4096]{1,0:T(8,128)(2,1)S(1)} %collective-permute-done.3.refs_1_, bf16[64,4096]{1,0:T(8,128)(2,1)S(1)} %collective-permute-done.10.refs_2_, ...), custom_call_target="tpu_custom_call" | custom-call | flops 1000 | bytes 1000 | tf_op jit(solution)/shard_map/pallas_call | solution.py:386
  53.2 2.9 %shard_map.226 = (f32[256,768]{1,0:T(8,128)S(1)}, f32[256,512]{1,0:T(8,128)S(1)}, bf16[256,512]{1,0:T(8,128)(2,1)S(1)}) custom-call(bf16[64,4096]{1,0:T(8,128)(2,1)S(1)} %collective-permute-done.16.refs_0_, bf16[64,4096]{1,0:T(8,128)(2,1)S(1)} %collective-permute-done.17.refs_1_, bf16[64,4096]{1,0:T(8,128)(2,1)S(1)} %collective-permute-done.14.refs_2_, ...), custom_call_target="tpu_custom_call" | custom-call | flops 1000 | bytes 1000 | tf_op jit(solution)/shard_map/pallas_call | solution.py:386
  56.2 4.3 %collective-permute-start.22 = (bf16[640,512]{1,0:T(8,128)(2,1)S(1)}, bf16[640,512]{1,0:T(8,128)(2,1)S(1)}, u32[]{:S(2)}, u32[]{:S(2)}) collective-permute-start(bf16[640,512]{1,0:T(8,128)(2,1)S(1)} %pad_maximum_fusion), channel_id=1, source_target_pairs={{0,16},{1,17},{2,18},{3,19},{4,20},{5,21},{6,22},{7,23},{8,24},{9,... | collective-permute-start | bytes 1966088 | tf_op jit(solution)/shard_map/ppermute | solution.py:502
  61.8 3.0 %collective-permute-done.20 = bf16[32,1024]{1,0:T(8,128)(2,1)S(1)} collective-permute-done((bf16[32,1024]{1,0:T(8,128)(2,1)S(1)}, bf16[32,1024]{1,0:T(8,128)(2,1)S(1)}, u32[]{:S(2)}, u32[]{:S(2)}) %collective-permute-start.20) | collective-permute-done | bytes 65568 | tf_op jit(solution)/shard_map/ppermute | solution.py:403
  64.9 2.3 %collective-permute-start.21 = (bf16[32,1024]{1,0:T(8,128)(2,1)S(1)}, bf16[32,1024]{1,0:T(8,128)(2,1)S(1)}, u32[]{:S(2)}, u32[]{:S(2)}) collective-permute-start(bf16[32,1024]{1,0:T(8,128)(2,1)S(1)} %add.62), channel_id=1, source_target_pairs={{0,8},{1,9},{2,10},{3,11},{4,12},{5,13},{6,14},{7,15},{8,0},{9,1},... | collective-permute-start | bytes 196616 | tf_op jit(solution)/shard_map/ppermute | solution.py:403
  67.2 2.9 %collective-permute-done.21 = bf16[32,1024]{1,0:T(8,128)(2,1)S(1)} collective-permute-done((bf16[32,1024]{1,0:T(8,128)(2,1)S(1)}, bf16[32,1024]{1,0:T(8,128)(2,1)S(1)}, u32[]{:S(2)}, u32[]{:S(2)}) %collective-permute-start.21) | collective-permute-done | bytes 65568 | tf_op jit(solution)/shard_map/ppermute | solution.py:403
  71.7 6.5 %shard_map.227 = (bf16[1024,256]{1,0:T(8,128)(2,1)S(1)}, bf16[1024,256]{1,0:T(8,128)(2,1)S(1)}, bf16[1024,256]{1,0:T(8,128)(2,1)S(1)}, bf16[1024,512]{1,0:T(8,128)(2,1)S(1)}, bf16[32,1024]{1,0:T(8,128)(2,1)S(1)}) custom-call(s32[34]{0:T(128)S(1)} %dynamic-slice_bitcast_fusion.info, f32[384,768]{1,0:T(8,128)S(1)} %get-tuple-element.108.refs_0_, ...), custom_call_target="tpu_custom_call" | custom-call | flops 1000 | bytes 1000 | tf_op jit(solution)/shard_map/pallas_call | solution.py:386
  78.3 2.3 %shard_map.228 = (bf16[1024,256]{1,0:T(8,128)(2,1)S(1)}, bf16[1024,256]{1,0:T(8,128)(2,1)S(1)}) custom-call(s32[34]{0:T(128)S(1)} %dynamic-slice_bitcast_fusion.info, bf16[384,512]{1,0:T(8,128)(2,1)S(1)} %collective-permute-done.15.refs_0_, bf16[256,512]{1,0:T(8,128)(2,1)S(1)} %get-tuple-element.184.refs_1_, bf16[128,512]{1,0:T(8,128)(2,1)S(1)} %slice.17.refs_2_, ...), custom_call_target="tpu_custom_call" | custom-call | flops 1000 | bytes 1000 | tf_op jit(solution)/shard_map/pallas_call | solution.py:386
  80.6 5.8 %shard_map.229 = (bf16[1024,256]{1,0:T(8,128)(2,1)S(1)}, bf16[32,1024]{1,0:T(8,128)(2,1)S(1)}) custom-call(s32[34]{0:T(128)S(1)} %dynamic-slice_bitcast_fusion.info, bf16[1024,256]{1,0:T(8,128)(2,1)S(1)} %get-tuple-element.134.refs_0_, bf16[1024,256]{1,0:T(8,128)(2,1)S(1)} %get-tuple-element.135.refs_1_, bf16[1024,256]{1,0:T(8,128)(2,1)S(1)} %get-tuple-element.140.refs_2_, ...), custom_call_target="tpu_custom_call" | custom-call | flops 1000 | bytes 1000 | tf_op jit(solution)/shard_map/pallas_call | solution.py:386
  97.7 2.3 %collective-permute-start.28 = (bf16[32,1024]{1,0:T(8,128)(2,1)S(1)}, bf16[32,1024]{1,0:T(8,128)(2,1)S(1)}, u32[]{:S(2)}, u32[]{:S(2)}) collective-permute-start(bf16[32,1024]{1,0:T(8,128)(2,1)S(1)} %add.66), channel_id=1, source_target_pairs={{0,8},{1,9},{2,10},{3,11},{4,12},{5,13},{6,14},{7,15},{8,0},{9,1},... | collective-permute-start | bytes 196616 | tf_op jit(solution)/shard_map/ppermute | solution.py:619
  102.0 2.6 %collective-permute-done.28 = bf16[32,1024]{1,0:T(8,128)(2,1)S(1)} collective-permute-done((bf16[32,1024]{1,0:T(8,128)(2,1)S(1)}, bf16[32,1024]{1,0:T(8,128)(2,1)S(1)}, u32[]{:S(2)}, u32[]{:S(2)}) %collective-permute-start.28) | collective-permute-done | bytes 65568 | tf_op jit(solution)/shard_map/ppermute | solution.py:619
  110.1 5.0 %collective-permute-done.30 = bf16[64,4096]{1,0:T(8,128)(2,1)S(1)} collective-permute-done((bf16[64,4096]{1,0:T(8,128)(2,1)S(1)}, bf16[64,4096]{1,0:T(8,128)(2,1)S(1)}, u32[]{:S(2)}, u32[]{:S(2)}) %collective-permute-start.30) | collective-permute-done | bytes 524320 | tf_op jit(solution)/shard_map/ppermute | solution.py:33
  115.3 5.4 %collective-permute-done.36 = bf16[64,4096]{1,0:T(8,128)(2,1)S(1)} collective-permute-done((bf16[64,4096]{1,0:T(8,128)(2,1)S(1)}, bf16[64,4096]{1,0:T(8,128)(2,1)S(1)}, u32[]{:S(2)}, u32[]{:S(2)}) %collective-permute-start.36) | collective-permute-done | bytes 524320 | tf_op jit(solution)/shard_map/ppermute | solution.py:33
  122.2 4.2 %collective-permute-done.31 = bf16[64,4096]{1,0:T(8,128)(2,1)S(1)} collective-permute-done((bf16[64,4096]{1,0:T(8,128)(2,1)S(1)}, bf16[64,4096]{1,0:T(8,128)(2,1)S(1)}, u32[]{:S(2)}, u32[]{:S(2)}) %collective-permute-start.31) | collective-permute-done | bytes 524320 | tf_op jit(solution)/shard_map/ppermute | solution.py:33
  126.5 5.4 %collective-permute-done.37 = bf16[64,4096]{1,0:T(8,128)(2,1)S(1)} collective-permute-done((bf16[64,4096]{1,0:T(8,128)(2,1)S(1)}, bf16[64,4096]{1,0:T(8,128)(2,1)S(1)}, u32[]{:S(2)}, u32[]{:S(2)}) %collective-permute-start.37) | collective-permute-done | bytes 524320 | tf_op jit(solution)/shard_map/ppermute | solution.py:33
  132.1 5.5 %collective-permute-done.33 = bf16[64,4096]{1,0:T(8,128)(2,1)S(1)} collective-permute-done((bf16[64,4096]{1,0:T(8,128)(2,1)S(1)}, bf16[64,4096]{1,0:T(8,128)(2,1)S(1)}, u32[]{:S(2)}, u32[]{:S(2)}) %collective-permute-start.33) | collective-permute-done | bytes 524320 | tf_op jit(solution)/shard_map/ppermute | solution.py:33
  137.8 5.5 %collective-permute-done.38 = bf16[64,4096]{1,0:T(8,128)(2,1)S(1)} collective-permute-done((bf16[64,4096]{1,0:T(8,128)(2,1)S(1)}, bf16[64,4096]{1,0:T(8,128)(2,1)S(1)}, u32[]{:S(2)}, u32[]{:S(2)}) %collective-permute-start.38) | collective-permute-done | bytes 524320 | tf_op jit(solution)/shard_map/ppermute | solution.py:33
  144.7 4.2 %collective-permute-done.35 = bf16[64,4096]{1,0:T(8,128)(2,1)S(1)} collective-permute-done((bf16[64,4096]{1,0:T(8,128)(2,1)S(1)}, bf16[64,4096]{1,0:T(8,128)(2,1)S(1)}, u32[]{:S(2)}, u32[]{:S(2)}) %collective-permute-start.35) | collective-permute-done | bytes 524320 | tf_op jit(solution)/shard_map/ppermute | solution.py:33
  (139 shorter events, 54.7 us)
Async XLA Ops:
  2.1 15.8 %collective-permute-start.2 = (bf16[4096,128]{1,0:T(8,128)(2,1)}, bf16[4096,128]{1,0:T(8,128)(2,1)}, u32[]{:S(2)}, u32[]{:S(2)}) collective-permute-start(bf16[4096,128]{1,0:T(8,128)(2,1)} %param.32), channel_id=1, source_target_pairs={{0,1},{1,0},{2,3},{3,2},{4,5},{5,4},{6,7},{7,6},{8,9},{9,8},{10,11... | collective-permute-start | bytes 3145736 | tf_op jit(solution)/shard_map/ppermute | solution.py:29
  2.1 12.7 %collective-permute-start.4 = (bf16[64,4096]{1,0:T(8,128)(2,1)S(1)}, bf16[64,4096]{1,0:T(8,128)(2,1)S(1)}, u32[]{:S(2)}, u32[]{:S(2)}) collective-permute-start(bf16[64,4096]{1,0:T(8,128)(2,1)S(1)} %shard_map.217.refs_0_), channel_id=1, source_target_pairs={{0,4},{4,8},{8,12},{12,14},{14,10},{10,6},{6,2},{2,0},{1,3},{5,1},... | collective-permute-start | bytes 1572872 | tf_op jit(solution)/shard_map/ppermute | solution.py:33
  6.0 8.9 %collective-permute-start.7 = (f32[1,128]{1,0:T(1,128)S(1)}, f32[1,128]{1,0:T(1,128)S(1)}, u32[]{:S(2)}, u32[]{:S(2)}) collective-permute-start(f32[1,128]{1,0:T(1,128)S(1)} %convert_element_type.71), channel_id=1, source_target_pairs={{0,1},{1,0},{2,3},{3,2},{4,5},{5,4},{6,7},{7,6},{8,9},{9,8},{10,11... | collective-permute-start | bytes 1544 | tf_op jit(solution)/shard_map/ppermute | solution.py:29
  6.0 39.0 %collective-permute-start.12 = (bf16[128,4096]{1,0:T(8,128)(2,1)}, bf16[128,4096]{1,0:T(8,128)(2,1)S(1)}, u32[]{:S(2)}, u32[]{:S(2)}) collective-permute-start(bf16[128,4096]{1,0:T(8,128)(2,1)} %param.37), channel_id=1, source_target_pairs={{0,1},{1,0},{2,3},{3,2},{4,5},{5,4},{6,7},{7,6},{8,9},{9,8},{10,11... | collective-permute-start | bytes 3145736 | tf_op jit(solution)/shard_map/ppermute | solution.py:29
  6.5 11.4 %collective-permute-start.1 = (bf16[64,4096]{1,0:T(8,128)(2,1)S(1)}, bf16[64,4096]{1,0:T(8,128)(2,1)S(1)}, u32[]{:S(2)}, u32[]{:S(2)}) collective-permute-start(bf16[64,4096]{1,0:T(8,128)(2,1)S(1)} %collective-permute-done.refs_1_), channel_id=1, source_target_pairs={{0,4},{4,8},{8,12},{12,14},{14,10},{10,6},{6,2},{2,0},{1,3},{5,1},... | collective-permute-start | bytes 1572872 | tf_op jit(solution)/shard_map/ppermute | solution.py:33
  14.8 9.3 %collective-permute-start.6 = (bf16[64,4096]{1,0:T(8,128)(2,1)S(1)}, bf16[64,4096]{1,0:T(8,128)(2,1)S(1)}, u32[]{:S(2)}, u32[]{:S(2)}) collective-permute-start(bf16[64,4096]{1,0:T(8,128)(2,1)S(1)} %collective-permute-done.4.refs_2_), channel_id=1, source_target_pairs={{0,1},{1,0},{2,3},{3,2},{4,5},{5,4},{6,7},{7,6},{8,9},{9,8},{10,11... | collective-permute-start | bytes 1572872 | tf_op jit(solution)/shard_map/ppermute | solution.py:29
  14.9 9.2 %collective-permute-start.9 = (bf16[64,4096]{1,0:T(8,128)(2,1)S(1)}, bf16[64,4096]{1,0:T(8,128)(2,1)S(1)}, u32[]{:S(2)}, u32[]{:S(2)}) collective-permute-start(bf16[64,4096]{1,0:T(8,128)(2,1)S(1)} %collective-permute-done.4.refs_2_), channel_id=1, source_target_pairs={{0,4},{4,8},{8,12},{12,14},{14,10},{10,6},{6,2},{2,0},{1,3},{5,1},... | collective-permute-start | bytes 1572872 | tf_op jit(solution)/shard_map/ppermute | solution.py:33
  17.9 15.4 %collective-permute-start.3 = (bf16[64,4096]{1,0:T(8,128)(2,1)S(1)}, bf16[64,4096]{1,0:T(8,128)(2,1)S(1)}, u32[]{:S(2)}, u32[]{:S(2)}) collective-permute-start(bf16[64,4096]{1,0:T(8,128)(2,1)S(1)} %collective-permute-done.1.refs_3_), channel_id=1, source_target_pairs={{0,4},{4,8},{8,12},{12,14},{14,10},{10,6},{6,2},{2,0},{1,3},{5,1},... | collective-permute-start | bytes 1572872 | tf_op jit(solution)/shard_map/ppermute | solution.py:33
  24.1 12.8 %collective-permute-start.11 = (bf16[64,4096]{1,0:T(8,128)(2,1)S(1)}, bf16[64,4096]{1,0:T(8,128)(2,1)S(1)}, u32[]{:S(2)}, u32[]{:S(2)}) collective-permute-start(bf16[64,4096]{1,0:T(8,128)(2,1)S(1)} %collective-permute-done.9.refs_0_), channel_id=1, source_target_pairs={{0,1},{1,0},{2,3},{3,2},{4,5},{5,4},{6,7},{7,6},{8,9},{9,8},{10,11... | collective-permute-start | bytes 1572872 | tf_op jit(solution)/shard_map/ppermute | solution.py:29
  24.1 11.2 %collective-permute-start.13 = (bf16[64,4096]{1,0:T(8,128)(2,1)S(1)}, bf16[64,4096]{1,0:T(8,128)(2,1)S(1)}, u32[]{:S(2)}, u32[]{:S(2)}) collective-permute-start(bf16[64,4096]{1,0:T(8,128)(2,1)S(1)} %collective-permute-done.9.refs_0_), channel_id=1, source_target_pairs={{0,4},{4,8},{8,12},{12,14},{14,10},{10,6},{6,2},{2,0},{1,3},{5,1},... | collective-permute-start | bytes 1572872 | tf_op jit(solution)/shard_map/ppermute | solution.py:33
  33.4 11.6 %collective-permute-start.8 = (bf16[64,4096]{1,0:T(8,128)(2,1)S(1)}, bf16[64,4096]{1,0:T(8,128)(2,1)S(1)}, u32[]{:S(2)}, u32[]{:S(2)}) collective-permute-start(bf16[64,4096]{1,0:T(8,128)(2,1)S(1)} %collective-permute-done.3.refs_1_), channel_id=1, source_target_pairs={{0,4},{4,8},{8,12},{12,14},{14,10},{10,6},{6,2},{2,0},{1,3},{5,1},... | collective-permute-start | bytes 1572872 | tf_op jit(solution)/shard_map/ppermute | solution.py:33
  35.4 13.0 %collective-permute-start.14 = (bf16[64,4096]{1,0:T(8,128)(2,1)S(1)}, bf16[64,4096]{1,0:T(8,128)(2,1)S(1)}, u32[]{:S(2)}, u32[]{:S(2)}) collective-permute-start(bf16[64,4096]{1,0:T(8,128)(2,1)S(1)} %collective-permute-done.13.refs_0_), channel_id=1, source_target_pairs={{0,4},{4,8},{8,12},{12,14},{14,10},{10,6},{6,2},{2,0},{1,3},{5,1},... | collective-permute-start | bytes 1572872 | tf_op jit(solution)/shard_map/ppermute | solution.py:33
  36.9 11.4 %collective-permute-start.15 = (bf16[384,512]{1,0:T(8,128)(2,1)S(1)}, bf16[384,512]{1,0:T(8,128)(2,1)S(1)}, u32[]{:S(2)}, u32[]{:S(2)}) collective-permute-start(bf16[384,512]{1,0:T(8,128)(2,1)S(1)} %get-tuple-element.120), channel_id=1, source_target_pairs={{0,16},{1,17},{2,18},{3,19},{4,20},{5,21},{6,22},{7,23},{8,24},{9,... | collective-permute-start | bytes 1179656 | tf_op jit(solution)/shard_map/ppermute | solution.py:502
  56.2 22.0 %collective-permute-start.22 = (bf16[640,512]{1,0:T(8,128)(2,1)S(1)}, bf16[640,512]{1,0:T(8,128)(2,1)S(1)}, u32[]{:S(2)}, u32[]{:S(2)}) collective-permute-start(bf16[640,512]{1,0:T(8,128)(2,1)S(1)} %pad_maximum_fusion), channel_id=1, source_target_pairs={{0,16},{1,17},{2,18},{3,19},{4,20},{5,21},{6,22},{7,23},{8,24},{9,... | collective-permute-start | bytes 1966088 | tf_op jit(solution)/shard_map/ppermute | solution.py:502
  92.9 11.7 %collective-permute-start.29 = (bf16[128,4096]{1,0:T(8,128)(2,1)S(1)}, bf16[128,4096]{1,0:T(8,128)(2,1)S(1)}, u32[]{:S(2)}, u32[]{:S(2)}) collective-permute-start(bf16[128,4096]{1,0:T(8,128)(2,1)S(1)} %get-tuple-element.164), channel_id=1, source_target_pairs={{0,1},{1,0},{2,3},{3,2},{4,5},{5,4},{6,7},{7,6},{8,9},{9,8},{10,11... | collective-permute-start | bytes 3145736 | tf_op jit(solution)/shard_map/ppermute | solution.py:29
  97.6 11.3 %collective-permute-start.32 = (bf16[128,4096]{1,0:T(8,128)(2,1)S(1)}, bf16[128,4096]{1,0:T(8,128)(2,1)S(1)}, u32[]{:S(2)}, u32[]{:S(2)}) collective-permute-start(bf16[128,4096]{1,0:T(8,128)(2,1)S(1)} %get-tuple-element.173), channel_id=1, source_target_pairs={{0,1},{1,0},{2,3},{3,2},{4,5},{5,4},{6,7},{7,6},{8,9},{9,8},{10,11... | collective-permute-start | bytes 3145736 | tf_op jit(solution)/shard_map/ppermute | solution.py:29
  105.9 9.2 %collective-permute-start.30 = (bf16[64,4096]{1,0:T(8,128)(2,1)S(1)}, bf16[64,4096]{1,0:T(8,128)(2,1)S(1)}, u32[]{:S(2)}, u32[]{:S(2)}) collective-permute-start(bf16[64,4096]{1,0:T(8,128)(2,1)S(1)} %shard_map.234), channel_id=1, source_target_pairs={{0,4},{4,8},{8,12},{12,14},{14,10},{10,6},{6,2},{2,0},{1,3},{5,1},... | collective-permute-start | bytes 1572872 | tf_op jit(solution)/shard_map/ppermute | solution.py:33
  106.0 15.0 %collective-permute-start.34 = (bf16[128,4096]{1,0:T(8,128)(2,1)S(1)}, bf16[128,4096]{1,0:T(8,128)(2,1)S(1)}, u32[]{:S(2)}, u32[]{:S(2)}) collective-permute-start(bf16[128,4096]{1,0:T(8,128)(2,1)S(1)} %get-tuple-element.176), channel_id=1, source_target_pairs={{0,1},{1,0},{2,3},{3,2},{4,5},{5,4},{6,7},{7,6},{8,9},{9,8},{10,11... | collective-permute-start | bytes 3145736 | tf_op jit(solution)/shard_map/ppermute | solution.py:29
  107.9 12.8 %collective-permute-start.36 = (bf16[64,4096]{1,0:T(8,128)(2,1)S(1)}, bf16[64,4096]{1,0:T(8,128)(2,1)S(1)}, u32[]{:S(2)}, u32[]{:S(2)}) collective-permute-start(bf16[64,4096]{1,0:T(8,128)(2,1)S(1)} %convert_element_type.79), channel_id=1, source_target_pairs={{0,4},{4,8},{8,12},{12,14},{14,10},{10,6},{6,2},{2,0},{1,3},{5,1},... | collective-permute-start | bytes 1572872 | tf_op jit(solution)/shard_map/ppermute | solution.py:33
  115.2 11.1 %collective-permute-start.31 = (bf16[64,4096]{1,0:T(8,128)(2,1)S(1)}, bf16[64,4096]{1,0:T(8,128)(2,1)S(1)}, u32[]{:S(2)}, u32[]{:S(2)}) collective-permute-start(bf16[64,4096]{1,0:T(8,128)(2,1)S(1)} %add_convert_fusion.6), channel_id=1, source_target_pairs={{0,4},{4,8},{8,12},{12,14},{14,10},{10,6},{6,2},{2,0},{1,3},{5,1},... | collective-permute-start | bytes 1572872 | tf_op jit(solution)/shard_map/ppermute | solution.py:33
  120.9 11.1 %collective-permute-start.37 = (bf16[64,4096]{1,0:T(8,128)(2,1)S(1)}, bf16[64,4096]{1,0:T(8,128)(2,1)S(1)}, u32[]{:S(2)}, u32[]{:S(2)}) collective-permute-start(bf16[64,4096]{1,0:T(8,128)(2,1)S(1)} %add_convert_fusion.3), channel_id=1, source_target_pairs={{0,4},{4,8},{8,12},{12,14},{14,10},{10,6},{6,2},{2,0},{1,3},{5,1},... | collective-permute-start | bytes 1572872 | tf_op jit(solution)/shard_map/ppermute | solution.py:33
  126.5 11.1 %collective-permute-start.33 = (bf16[64,4096]{1,0:T(8,128)(2,1)S(1)}, bf16[64,4096]{1,0:T(8,128)(2,1)S(1)}, u32[]{:S(2)}, u32[]{:S(2)}) collective-permute-start(bf16[64,4096]{1,0:T(8,128)(2,1)S(1)} %add_convert_fusion.5), channel_id=1, source_target_pairs={{0,4},{4,8},{8,12},{12,14},{14,10},{10,6},{6,2},{2,0},{1,3},{5,1},... | collective-permute-start | bytes 1572872 | tf_op jit(solution)/shard_map/ppermute | solution.py:33
  132.1 11.1 %collective-permute-start.38 = (bf16[64,4096]{1,0:T(8,128)(2,1)S(1)}, bf16[64,4096]{1,0:T(8,128)(2,1)S(1)}, u32[]{:S(2)}, u32[]{:S(2)}) collective-permute-start(bf16[64,4096]{1,0:T(8,128)(2,1)S(1)} %add_convert_fusion.2), channel_id=1, source_target_pairs={{0,4},{4,8},{8,12},{12,14},{14,10},{10,6},{6,2},{2,0},{1,3},{5,1},... | collective-permute-start | bytes 1572872 | tf_op jit(solution)/shard_map/ppermute | solution.py:33
  137.7 11.1 %collective-permute-start.35 = (bf16[64,4096]{1,0:T(8,128)(2,1)S(1)}, bf16[64,4096]{1,0:T(8,128)(2,1)S(1)}, u32[]{:S(2)}, u32[]{:S(2)}) collective-permute-start(bf16[64,4096]{1,0:T(8,128)(2,1)S(1)} %add_convert_fusion.4), channel_id=1, source_target_pairs={{0,4},{4,8},{8,12},{12,14},{14,10},{10,6},{6,2},{2,0},{1,3},{5,1},... | collective-permute-start | bytes 1572872 | tf_op jit(solution)/shard_map/ppermute | solution.py:33
  (31 other events, 241.0 us)

commit v7 on v6

--- a/solution.py
+++ b/solution.py
@@ -204,10 +204,10 @@
 
 def block_rows_of(refs, block):
     if block == 0:
-        return jnp.concatenate([refs[0][:128], refs[3][128:]], axis=0)
+        return jnp.concatenate([refs[0][...], refs[4][128:]], axis=0)
     if block == 3:
-        return jnp.concatenate([refs[2][...], refs[3][:128]], axis=0)
-    return refs[0][128:] if block == 1 else refs[1][...]
+        return jnp.concatenate([refs[3][...], refs[4][:128]], axis=0)
+    return refs[block][...]
 
 
 def two_blocks(refs, index):
@@ -215,9 +215,9 @@
 
 
 def inner_kernel(info, *refs):
-    base_refs, up_refs, (rank_ref, meta_ref, turn_ref, first_ref, last_ref) = refs[:4], refs[4:8], refs[8:13]
-    qkv_right_ref, up_right_ref, bias_ref, left_ref = refs[13:17]
-    q_ref, k_ref, v_ref, hidden_ref, out_ref = refs[17:]
+    base_refs, up_refs, (rank_ref, meta_ref, turn_ref, first_ref, last_ref) = refs[:5], refs[5:10], refs[10:15]
+    qkv_right_ref, up_right_ref, bias_ref, left_ref = refs[15:19]
+    q_ref, k_ref, v_ref, hidden_ref, out_ref = refs[19:]
     rows = 512
     columns = qkv_right_ref.shape[0]
     for block in range(BLOCKS // 2):
@@ -241,7 +241,7 @@
 
 
 def far_kernel(first_row, info, *refs):
-    shared_refs, (rank_ref, meta_ref, turn_ref, spread_ref, right_ref, k_ref, v_ref) = refs[:4], refs[4:]
+    shared_refs, (rank_ref, meta_ref, turn_ref, spread_ref, right_ref, k_ref, v_ref) = refs[:5], refs[5:]
     rows = 512
     for block in range(BLOCKS // 2):
         at = slice(block * rows, (block + 1) * rows)
@@ -259,10 +259,12 @@
     key_refs, value_refs, refs = refs[:req_count], refs[req_count : 2 * req_count], refs[2 * req_count :]
     meta_ref, spread_ref, left_ref, hidden_rank_ref, attended_ref, out_ref = refs[:6]
     keys_ref, values_ref, scores_ref, top_ref, sum_ref, acc_ref, fold_ref = refs[6:]
-    span = 256
-    rows = 2 * span
-    pair = span // 2
+    span = rows = 512
+    pair = 128
     group_rows = q_ref.shape[0]
+
+    def lane_parts(value):
+        return [value[:, k * pair : (k + 1) * pair] for k in range(span // pair)]
 
     def slot_rows(slot):
         return pl.ds(pl.multiple_of(slot * pair, pair), pair)
@@ -292,7 +294,7 @@
 
         meta = both(meta_ref)
         start = meta[:, 0:1]
-        number = (req_count - 1) * BLOCKS + 2 * block
+        number = (req_count - 1) * (group_rows // span) + block
         query = query_place + (first_token + number * span).astype(jnp.float32)
         q = both(q_ref)
         lowest = jnp.min(start).astype(jnp.int32) - first_token
@@ -307,20 +309,20 @@
             allowed = jnp.logical_and(key <= query, key >= start)
             scores = jnp.where(allowed, scores, NEGATIVE_FILL)
             scores_ref[:, at] = scores
-            top_ref[...] = jnp.maximum(top_ref[...], jnp.maximum(scores[:, :pair], scores[:, pair:]))
+            top_ref[...] = functools.reduce(jnp.maximum, lane_parts(scores), top_ref[...])
             return 0
 
-        lax.fori_loop(lowest // span, number + 2, score, 0)
+        lax.fori_loop(lowest // span, number + 1, score, 0)
         top = jnp.max(top_ref[...], axis=1, keepdims=True)
 
         def weigh(j, _):
             at = pl.ds(pl.multiple_of(j * span, span), span)
             weights = jnp.exp(scores_ref[:, at] - top)
-            sum_ref[...] = sum_ref[...] + (weights[:, :pair] + weights[:, pair:])
+            sum_ref[...] = functools.reduce(jnp.add, lane_parts(weights), sum_ref[...])
             acc_ref[...] = acc_ref[...] + rank_product(weights.astype(jnp.bfloat16), values_ref[at, :])
             return 0
 
-        lax.fori_loop(lowest // span, number + 2, weigh, 0)
+        lax.fori_loop(lowest // span, number + 1, weigh, 0)
         total = jnp.sum(sum_ref[...], axis=1, keepdims=True)
         attended = (acc_ref[...] / total).astype(jnp.bfloat16)
         lanes = folded(rank_product(attended, left_ref[...]), meta[:, 64:65], spread_ref)
@@ -538,8 +540,11 @@
     part = arrivals(ring_a, ring_b)
     ring_a, ring_b = along_ring(ring_a), along_ring(ring_b)
     ranks = add_ranks(own_part + part, (0, 2, 3), jnp.zeros((32, group_rows), jnp.bfloat16))
-    first = products_of(own_part + part)
-    ring_b, ranks, first = tie((ring_b, ranks, first))
+    zeroth = products_of(own_part)
+    ring_a, zeroth = tie((ring_a, zeroth))
+    far_own = to_groups(zeroth[2])
+    first = products_of(part)
+    ring_b, ranks, first, far_own = tie((ring_b, ranks, first, far_own))
     part = arrivals(ring_a, ring_b)
     ring_a, ring_b = along_ring(ring_a), along_ring(ring_b)
     far_right = to_partner(near_right)
@@ -560,7 +565,7 @@
     ranks, fourth = tie((ranks + moved, fourth))
     far_late = to_groups(jnp.concatenate([second[2], third[2], fourth[2]], axis=0))
     rank_in = sum_over_mlp(ranks, (4, 8))
-    products = (first, second, third, fourth)
+    products = (zeroth, first, second, third, fourth)
 
     bias_row = input_bias.reshape(1, -1)
     far_rank = to_groups(rank_in)
@@ -577,7 +582,7 @@
     for d in range(1, req_count):
         early, late = far_early[d - 1], far_late[d - 1]
         ends = (0, block_rows, block_rows + pair_rows, 2 * block_rows + pair_rows)
-        shared = [early] + [late[ends[k] : ends[k + 1]] for k in range(3)]
+        shared = [far_own[d - 1], early] + [late[ends[k] : ends[k + 1]] for k in range(3)]
         far_keys, far_values = call(
             functools.partial(far_kernel, d * group_rows),
             shared + [far_rank[d - 1], meta, turns, spread_first, qkv_right],

time: 150 us -> 149 us (level)
  waiting for transfers between devices: 54.1 us -> 48.2 us
  starting transfers between devices: 36.7 us -> 41.8 us
    ppermute x14, starting transfers between devices: 14.3 us -> 19.1 us  [along_ring(): return lax.ppermute(value, 'mlp', RING_PERM)]
    ppermute x14, waiting for transfers between devices: 40.9 us -> 36.3 us  [along_ring(): return lax.ppermute(value, 'mlp', RING_PERM)]
    ppermute x3 -> x4, starting transfers between devices: 9.44 us -> 8.58 us  [to_group(): lax.ppermute(value, 'req', [(g, g + d) for g in range(req_count - d)])]
    pallas_call x22 -> x23, Pallas kernels: 51.5 us -> 51.2 us  [call(): pl.pallas_call(kernel, in_specs=specs, out_specs=[vmem] * len(outs), out_...]
  transfers between devices with their start and end apart: 40 -> 41, of which waited for: 16 -> 16; matrix products, arithmetic and copies ran while one was open for 3% -> 3% of each run, Pallas kernels for 27% -> 27%
where the time goes in v7:
time: 149 us
  Pallas kernels  51.2 us (34%)
  waiting for transfers between devices  48.2 us (32%)
  starting transfers between devices  41.8 us (28%)
  local copies, waits for them, and re-layouts  3.6 us (2%)
  other arithmetic  3.18 us (2%)
    pallas_call x23, Pallas kernels, call(): pl.pallas_call(kernel, in_specs=specs, out_specs=[vmem] * len(outs), out_...  51.2 us
    ppermute x14, waiting for transfers between devices, along_ring(): return lax.ppermute(value, 'mlp', RING_PERM)  36.3 us
    ppermute x14, starting transfers between devices, along_ring(): return lax.ppermute(value, 'mlp', RING_PERM)  19.1 us
    ppermute x4, starting transfers between devices, to_group(): lax.ppermute(value, 'req', [(g, g + d) for g in range(req_count - d)])  8.58 us
    ppermute x4, starting transfers between devices, per_device(): moved = lax.ppermute(rank_out, 'mlp', [(i, i ^ bit) for i in range(16)])  5.72 us
    ppermute x2, waiting for transfers between devices, sum_over_mlp(): lax.ppermute(value, 'mlp', [(i, i ^ bit) for i in range(16)])  5.26 us
    ppermute x4, waiting for transfers between devices, per_device(): moved = lax.ppermute(rank_out, 'mlp', [(i, i ^ bit) for i in range(16)])  4.67 us
    ppermute x2, starting transfers between devices, sum_over_mlp(): lax.ppermute(value, 'mlp', [(i, i ^ bit) for i in range(16)])  4.3 us
  transfers between devices with their start and end apart: 41, of which 16 were waited for; matrix products, arithmetic and copies ran while one was open for 3% of the time, Pallas kernels for 27%

profile of v7, /device:TPU:0, one launch (start us, length us, event | category | flops | bytes accessed | tf_op | source)
XLA Modules:
  0.0 148.6 jit_solution(11814667900369187380)
XLA Ops:
  2.1 3.0 %collective-permute-start = (bf16[64,4096]{1,0:T(8,128)(2,1)S(1)}, bf16[64,4096]{1,0:T(8,128)(2,1)S(1)}, u32[]{:S(2)}, u32[]{:S(2)}) collective-permute-start(bf16[64,4096]{1,0:T(8,128)(2,1)S(1)} %shard_map.217.refs_0_), channel_id=1, source_target_pairs={{0,4},{4,8},{8,12},{12,14},{14,10},{10,6},{6,2},{2,0},{1,3},{5,1},... | collective-permute-start | bytes 1572872 | tf_op jit(solution)/shard_map/ppermute | solution.py:33
  10.2 4.6 %shard_map.218 = (f32[2048,128]{1,0:T(8,128)S(1)}, f32[2048,128]{1,0:T(8,128)S(1)}, bf16[4096,768]{1,0:T(8,128)(2,1)S(1)}, bf16[4096,512]{1,0:T(8,128)(2,1)S(1)}) custom-call(s32[34]{0:T(128)S(1)} %dynamic-slice_bitcast_fusion.info, f32[65,1]{1,0:T(8,128)S(1)} %copy.24.column_ref, f32[1,65]{1,0:T(1,128)S(1)} %get-tuple-element.201.row_ref, ...), custom_call_target="tpu_custom_call" | custom-call | flops 1000 | bytes 1000 | tf_op jit(solution)/shard_map/pallas_call | solution.py:388
  19.9 2.1 %collective-permute-start.5 = (bf16[64,4096]{1,0:T(8,128)(2,1)S(1)}, bf16[64,4096]{1,0:T(8,128)(2,1)S(1)}, u32[]{:S(2)}, u32[]{:S(2)}) collective-permute-start(bf16[64,4096]{1,0:T(8,128)(2,1)S(1)} %collective-permute-done.3.refs_3_.refs_1_), channel_id=1, source_target_pairs={{0,4},{4,8},{8,12},{12,14},{14,10},{10,6},{6,2},{2,0},{1,3},{5,1},... | collective-permute-start | bytes 1572872 | tf_op jit(solution)/shard_map/ppermute | solution.py:33
  25.6 3.4 %collective-permute-start.9 = (bf16[128,512]{1,0:T(8,128)(2,1)S(1)}, bf16[128,512]{1,0:T(8,128)(2,1)S(1)}, u32[]{:S(2)}, u32[]{:S(2)}) collective-permute-start(bf16[128,512]{1,0:T(8,128)(2,1)S(1)} %get-tuple-element.120), channel_id=1, source_target_pairs={{0,16},{1,17},{2,18},{3,19},{4,20},{5,21},{6,22},{7,23},{8,24},{9,... | collective-permute-start | bytes 393224 | tf_op jit(solution)/shard_map/ppermute | solution.py:504
  30.5 2.9 %shard_map.221 = (f32[256,768]{1,0:T(8,128)S(1)}, f32[256,512]{1,0:T(8,128)S(1)}, bf16[256,512]{1,0:T(8,128)(2,1)S(1)}) custom-call(bf16[64,4096]{1,0:T(8,128)(2,1)S(1)} %collective-permute-done.refs_2_.refs_0_, bf16[64,4096]{1,0:T(8,128)(2,1)S(1)} %collective-permute-done.3.refs_3_.refs_1_, bf16[64,4096]{1,0:T(8,128)(2,1)S(1)} %collective-permute-done.6.refs_4_.refs_2_, ...), custom_call_target="tpu_custom_call" | custom-call | flops 1000 | bytes 1000 | tf_op jit(solution)/shard_map/pallas_call | solution.py:388
  38.5 1.9 %collective-permute-start.16 = (bf16[256,512]{1,0:T(8,128)(2,1)S(1)}, bf16[256,512]{1,0:T(8,128)(2,1)S(1)}, u32[]{:S(2)}, u32[]{:S(2)}) collective-permute-start(bf16[256,512]{1,0:T(8,128)(2,1)S(1)} %get-tuple-element.134), channel_id=1, source_target_pairs={{0,16},{1,17},{2,18},{3,19},{4,20},{5,21},{6,22},{7,23},{8,24},{9,... | collective-permute-start | bytes 786440 | tf_op jit(solution)/shard_map/ppermute | solution.py:504
  40.5 2.9 %shard_map.223 = (f32[256,768]{1,0:T(8,128)S(1)}, f32[256,512]{1,0:T(8,128)S(1)}, bf16[256,512]{1,0:T(8,128)(2,1)S(1)}) custom-call(bf16[64,4096]{1,0:T(8,128)(2,1)S(1)} %collective-permute-done.1.refs_0_, bf16[64,4096]{1,0:T(8,128)(2,1)S(1)} %collective-permute-done.5.refs_1_, bf16[64,4096]{1,0:T(8,128)(2,1)S(1)} %collective-permute-done.11.refs_2_, ...), custom_call_target="tpu_custom_call" | custom-call | flops 1000 | bytes 1000 | tf_op jit(solution)/shard_map/pallas_call | solution.py:388
  48.2 2.0 %collective-permute-done.15.refs_2_ = bf16[64,4096]{1,0:T(8,128)(2,1)S(1)} collective-permute-done((bf16[64,4096]{1,0:T(8,128)(2,1)S(1)}, bf16[64,4096]{1,0:T(8,128)(2,1)S(1)}, u32[]{:S(2)}, u32[]{:S(2)}) %collective-permute-start.15) | collective-permute-done | bytes 524320 | tf_op jit(solution)/shard_map/ppermute | solution.py:33
  55.0 2.9 %shard_map.227 = (f32[256,768]{1,0:T(8,128)S(1)}, f32[256,512]{1,0:T(8,128)S(1)}, bf16[256,512]{1,0:T(8,128)(2,1)S(1)}) custom-call(bf16[64,4096]{1,0:T(8,128)(2,1)S(1)} %collective-permute-done.17.refs_0_, bf16[64,4096]{1,0:T(8,128)(2,1)S(1)} %collective-permute-done.18.refs_1_, bf16[64,4096]{1,0:T(8,128)(2,1)S(1)} %collective-permute-done.15.refs_2_, ...), custom_call_target="tpu_custom_call" | custom-call | flops 1000 | bytes 1000 | tf_op jit(solution)/shard_map/pallas_call | solution.py:388
  61.4 2.7 %collective-permute-done.21 = bf16[32,1024]{1,0:T(8,128)(2,1)S(1)} collective-permute-done((bf16[32,1024]{1,0:T(8,128)(2,1)S(1)}, bf16[32,1024]{1,0:T(8,128)(2,1)S(1)}, u32[]{:S(2)}, u32[]{:S(2)}) %collective-permute-start.21) | collective-permute-done | bytes 65568 | tf_op jit(solution)/shard_map/ppermute | solution.py:405
  64.1 2.7 %collective-permute-start.22 = (bf16[32,1024]{1,0:T(8,128)(2,1)S(1)}, bf16[32,1024]{1,0:T(8,128)(2,1)S(1)}, u32[]{:S(2)}, u32[]{:S(2)}) collective-permute-start(bf16[32,1024]{1,0:T(8,128)(2,1)S(1)} %add.62), channel_id=1, source_target_pairs={{0,8},{1,9},{2,10},{3,11},{4,12},{5,13},{6,14},{7,15},{8,0},{9,1},... | collective-permute-start | bytes 196616 | tf_op jit(solution)/shard_map/ppermute | solution.py:405
  66.8 2.6 %collective-permute-done.22 = bf16[32,1024]{1,0:T(8,128)(2,1)S(1)} collective-permute-done((bf16[32,1024]{1,0:T(8,128)(2,1)S(1)}, bf16[32,1024]{1,0:T(8,128)(2,1)S(1)}, u32[]{:S(2)}, u32[]{:S(2)}) %collective-permute-start.22) | collective-permute-done | bytes 65568 | tf_op jit(solution)/shard_map/ppermute | solution.py:405
  70.9 6.5 %shard_map.228 = (bf16[1024,256]{1,0:T(8,128)(2,1)S(1)}, bf16[1024,256]{1,0:T(8,128)(2,1)S(1)}, bf16[1024,256]{1,0:T(8,128)(2,1)S(1)}, bf16[1024,512]{1,0:T(8,128)(2,1)S(1)}, bf16[32,1024]{1,0:T(8,128)(2,1)S(1)}) custom-call(s32[34]{0:T(128)S(1)} %dynamic-slice_bitcast_fusion.info, f32[128,768]{1,0:T(8,128)S(1)} %get-tuple-element.112.refs_0_, ...), custom_call_target="tpu_custom_call" | custom-call | flops 1000 | bytes 1000 | tf_op jit(solution)/shard_map/pallas_call | solution.py:388
  77.5 2.3 %shard_map.229 = (bf16[1024,256]{1,0:T(8,128)(2,1)S(1)}, bf16[1024,256]{1,0:T(8,128)(2,1)S(1)}) custom-call(s32[34]{0:T(128)S(1)} %dynamic-slice_bitcast_fusion.info, bf16[128,512]{1,0:T(8,128)(2,1)S(1)} %collective-permute-done.9.refs_0_, bf16[256,512]{1,0:T(8,128)(2,1)S(1)} %collective-permute-done.16.refs_1_, ...), custom_call_target="tpu_custom_call" | custom-call | flops 1000 | bytes 1000 | tf_op jit(solution)/shard_map/pallas_call | solution.py:388
  79.9 5.3 %shard_map.230 = (bf16[1024,256]{1,0:T(8,128)(2,1)S(1)}, bf16[32,1024]{1,0:T(8,128)(2,1)S(1)}) custom-call(s32[34]{0:T(128)S(1)} %dynamic-slice_bitcast_fusion.info, bf16[1024,256]{1,0:T(8,128)(2,1)S(1)} %get-tuple-element.149.refs_0_, bf16[1024,256]{1,0:T(8,128)(2,1)S(1)} %get-tuple-element.150.refs_1_, bf16[1024,256]{1,0:T(8,128)(2,1)S(1)} %get-tuple-element.156.refs_2_, ...), custom_call_target="tpu_custom_call" | custom-call | flops 1000 | bytes 1000 | tf_op jit(solution)/shard_map/pallas_call | solution.py:388
  96.4 2.8 %collective-permute-start.29 = (bf16[32,1024]{1,0:T(8,128)(2,1)S(1)}, bf16[32,1024]{1,0:T(8,128)(2,1)S(1)}, u32[]{:S(2)}, u32[]{:S(2)}) collective-permute-start(bf16[32,1024]{1,0:T(8,128)(2,1)S(1)} %add.66), channel_id=1, source_target_pairs={{0,8},{1,9},{2,10},{3,11},{4,12},{5,13},{6,14},{7,15},{8,0},{9,1},... | collective-permute-start | bytes 196616 | tf_op jit(solution)/shard_map/ppermute | solution.py:624
  101.1 2.3 %collective-permute-done.29 = bf16[32,1024]{1,0:T(8,128)(2,1)S(1)} collective-permute-done((bf16[32,1024]{1,0:T(8,128)(2,1)S(1)}, bf16[32,1024]{1,0:T(8,128)(2,1)S(1)}, u32[]{:S(2)}, u32[]{:S(2)}) %collective-permute-start.29) | collective-permute-done | bytes 65568 | tf_op jit(solution)/shard_map/ppermute | solution.py:624
  109.2 4.6 %collective-permute-done.31 = bf16[64,4096]{1,0:T(8,128)(2,1)S(1)} collective-permute-done((bf16[64,4096]{1,0:T(8,128)(2,1)S(1)}, bf16[64,4096]{1,0:T(8,128)(2,1)S(1)}, u32[]{:S(2)}, u32[]{:S(2)}) %collective-permute-start.31) | collective-permute-done | bytes 524320 | tf_op jit(solution)/shard_map/ppermute | solution.py:33
  114.8 4.7 %collective-permute-done.37 = bf16[64,4096]{1,0:T(8,128)(2,1)S(1)} collective-permute-done((bf16[64,4096]{1,0:T(8,128)(2,1)S(1)}, bf16[64,4096]{1,0:T(8,128)(2,1)S(1)}, u32[]{:S(2)}, u32[]{:S(2)}) %collective-permute-start.37) | collective-permute-done | bytes 524320 | tf_op jit(solution)/shard_map/ppermute | solution.py:33
  121.6 3.5 %collective-permute-done.32 = bf16[64,4096]{1,0:T(8,128)(2,1)S(1)} collective-permute-done((bf16[64,4096]{1,0:T(8,128)(2,1)S(1)}, bf16[64,4096]{1,0:T(8,128)(2,1)S(1)}, u32[]{:S(2)}, u32[]{:S(2)}) %collective-permute-start.32) | collective-permute-done | bytes 524320 | tf_op jit(solution)/shard_map/ppermute | solution.py:33
  126.0 4.7 %collective-permute-done.38 = bf16[64,4096]{1,0:T(8,128)(2,1)S(1)} collective-permute-done((bf16[64,4096]{1,0:T(8,128)(2,1)S(1)}, bf16[64,4096]{1,0:T(8,128)(2,1)S(1)}, u32[]{:S(2)}, u32[]{:S(2)}) %collective-permute-start.38) | collective-permute-done | bytes 524320 | tf_op jit(solution)/shard_map/ppermute | solution.py:33
  131.6 4.7 %collective-permute-done.34 = bf16[64,4096]{1,0:T(8,128)(2,1)S(1)} collective-permute-done((bf16[64,4096]{1,0:T(8,128)(2,1)S(1)}, bf16[64,4096]{1,0:T(8,128)(2,1)S(1)}, u32[]{:S(2)}, u32[]{:S(2)}) %collective-permute-start.34) | collective-permute-done | bytes 524320 | tf_op jit(solution)/shard_map/ppermute | solution.py:33
  137.2 4.7 %collective-permute-done.39 = bf16[64,4096]{1,0:T(8,128)(2,1)S(1)} collective-permute-done((bf16[64,4096]{1,0:T(8,128)(2,1)S(1)}, bf16[64,4096]{1,0:T(8,128)(2,1)S(1)}, u32[]{:S(2)}, u32[]{:S(2)}) %collective-permute-start.39) | collective-permute-done | bytes 524320 | tf_op jit(solution)/shard_map/ppermute | solution.py:33
  143.4 4.2 %collective-permute-done.36 = bf16[64,4096]{1,0:T(8,128)(2,1)S(1)} collective-permute-done((bf16[64,4096]{1,0:T(8,128)(2,1)S(1)}, bf16[64,4096]{1,0:T(8,128)(2,1)S(1)}, u32[]{:S(2)}, u32[]{:S(2)}) %collective-permute-start.36) | collective-permute-done | bytes 524320 | tf_op jit(solution)/shard_map/ppermute | solution.py:33
  (142 shorter events, 64.2 us)
Async XLA Ops:
  2.1 15.8 %collective-permute-start.4 = (bf16[4096,128]{1,0:T(8,128)(2,1)}, bf16[4096,128]{1,0:T(8,128)(2,1)}, u32[]{:S(2)}, u32[]{:S(2)}) collective-permute-start(bf16[4096,128]{1,0:T(8,128)(2,1)} %param.32), channel_id=1, source_target_pairs={{0,1},{1,0},{2,3},{3,2},{4,5},{5,4},{6,7},{7,6},{8,9},{9,8},{10,11... | collective-permute-start | bytes 3145736 | tf_op jit(solution)/shard_map/ppermute | solution.py:29
  2.1 12.7 %collective-permute-start = (bf16[64,4096]{1,0:T(8,128)(2,1)S(1)}, bf16[64,4096]{1,0:T(8,128)(2,1)S(1)}, u32[]{:S(2)}, u32[]{:S(2)}) collective-permute-start(bf16[64,4096]{1,0:T(8,128)(2,1)S(1)} %shard_map.217.refs_0_), channel_id=1, source_target_pairs={{0,4},{4,8},{8,12},{12,14},{14,10},{10,6},{6,2},{2,0},{1,3},{5,1},... | collective-permute-start | bytes 1572872 | tf_op jit(solution)/shard_map/ppermute | solution.py:33
  5.1 12.7 %collective-permute-start.3 = (bf16[64,4096]{1,0:T(8,128)(2,1)S(1)}, bf16[64,4096]{1,0:T(8,128)(2,1)S(1)}, u32[]{:S(2)}, u32[]{:S(2)}) collective-permute-start(bf16[64,4096]{1,0:T(8,128)(2,1)S(1)} %collective-permute-done.2.refs_1_), channel_id=1, source_target_pairs={{0,4},{4,8},{8,12},{12,14},{14,10},{10,6},{6,2},{2,0},{1,3},{5,1},... | collective-permute-start | bytes 1572872 | tf_op jit(solution)/shard_map/ppermute | solution.py:33
  7.5 10.8 %collective-permute-start.8 = (f32[1,128]{1,0:T(1,128)S(1)}, f32[1,128]{1,0:T(1,128)S(1)}, u32[]{:S(2)}, u32[]{:S(2)}) collective-permute-start(f32[1,128]{1,0:T(1,128)S(1)} %convert_element_type.71), channel_id=1, source_target_pairs={{0,1},{1,0},{2,3},{3,2},{4,5},{5,4},{6,7},{7,6},{8,9},{9,8},{10,11... | collective-permute-start | bytes 1544 | tf_op jit(solution)/shard_map/ppermute | solution.py:29
  7.5 37.4 %collective-permute-start.13 = (bf16[128,4096]{1,0:T(8,128)(2,1)}, bf16[128,4096]{1,0:T(8,128)(2,1)S(1)}, u32[]{:S(2)}, u32[]{:S(2)}) collective-permute-start(bf16[128,4096]{1,0:T(8,128)(2,1)} %param.37), channel_id=1, source_target_pairs={{0,1},{1,0},{2,3},{3,2},{4,5},{5,4},{6,7},{7,6},{8,9},{9,8},{10,11... | collective-permute-start | bytes 3145736 | tf_op jit(solution)/shard_map/ppermute | solution.py:29
  14.8 9.2 %collective-permute-start.1 = (bf16[64,4096]{1,0:T(8,128)(2,1)S(1)}, bf16[64,4096]{1,0:T(8,128)(2,1)S(1)}, u32[]{:S(2)}, u32[]{:S(2)}) collective-permute-start(bf16[64,4096]{1,0:T(8,128)(2,1)S(1)} %collective-permute-done.refs_2_.refs_0_), channel_id=1, source_target_pairs={{0,4},{4,8},{8,12},{12,14},{14,10},{10,6},{6,2},{2,0},{1,3},{5,1},... | collective-permute-start | bytes 1572872 | tf_op jit(solution)/shard_map/ppermute | solution.py:33
  19.9 15.3 %collective-permute-start.5 = (bf16[64,4096]{1,0:T(8,128)(2,1)S(1)}, bf16[64,4096]{1,0:T(8,128)(2,1)S(1)}, u32[]{:S(2)}, u32[]{:S(2)}) collective-permute-start(bf16[64,4096]{1,0:T(8,128)(2,1)S(1)} %collective-permute-done.3.refs_3_.refs_1_), channel_id=1, source_target_pairs={{0,4},{4,8},{8,12},{12,14},{14,10},{10,6},{6,2},{2,0},{1,3},{5,1},... | collective-permute-start | bytes 1572872 | tf_op jit(solution)/shard_map/ppermute | solution.py:33
  24.0 14.5 %collective-permute-start.12 = (bf16[64,4096]{1,0:T(8,128)(2,1)S(1)}, bf16[64,4096]{1,0:T(8,128)(2,1)S(1)}, u32[]{:S(2)}, u32[]{:S(2)}) collective-permute-start(bf16[64,4096]{1,0:T(8,128)(2,1)S(1)} %collective-permute-done.1.refs_0_), channel_id=1, source_target_pairs={{0,1},{1,0},{2,3},{3,2},{4,5},{5,4},{6,7},{7,6},{8,9},{9,8},{10,11... | collective-permute-start | bytes 1572872 | tf_op jit(solution)/shard_map/ppermute | solution.py:29
  24.0 12.9 %collective-permute-start.14 = (bf16[64,4096]{1,0:T(8,128)(2,1)S(1)}, bf16[64,4096]{1,0:T(8,128)(2,1)S(1)}, u32[]{:S(2)}, u32[]{:S(2)}) collective-permute-start(bf16[64,4096]{1,0:T(8,128)(2,1)S(1)} %collective-permute-done.1.refs_0_), channel_id=1, source_target_pairs={{0,4},{4,8},{8,12},{12,14},{14,10},{10,6},{6,2},{2,0},{1,3},{5,1},... | collective-permute-start | bytes 1572872 | tf_op jit(solution)/shard_map/ppermute | solution.py:33
  25.6 9.6 %collective-permute-start.9 = (bf16[128,512]{1,0:T(8,128)(2,1)S(1)}, bf16[128,512]{1,0:T(8,128)(2,1)S(1)}, u32[]{:S(2)}, u32[]{:S(2)}) collective-permute-start(bf16[128,512]{1,0:T(8,128)(2,1)S(1)} %get-tuple-element.120), channel_id=1, source_target_pairs={{0,16},{1,17},{2,18},{3,19},{4,20},{5,21},{6,22},{7,23},{8,24},{9,... | collective-permute-start | bytes 393224 | tf_op jit(solution)/shard_map/ppermute | solution.py:504
  35.3 9.6 %collective-permute-start.10 = (bf16[64,4096]{1,0:T(8,128)(2,1)S(1)}, bf16[64,4096]{1,0:T(8,128)(2,1)S(1)}, u32[]{:S(2)}, u32[]{:S(2)}) collective-permute-start(bf16[64,4096]{1,0:T(8,128)(2,1)S(1)} %collective-permute-done.5.refs_1_), channel_id=1, source_target_pairs={{0,4},{4,8},{8,12},{12,14},{14,10},{10,6},{6,2},{2,0},{1,3},{5,1},... | collective-permute-start | bytes 1572872 | tf_op jit(solution)/shard_map/ppermute | solution.py:33
  36.9 13.3 %collective-permute-start.15 = (bf16[64,4096]{1,0:T(8,128)(2,1)S(1)}, bf16[64,4096]{1,0:T(8,128)(2,1)S(1)}, u32[]{:S(2)}, u32[]{:S(2)}) collective-permute-start(bf16[64,4096]{1,0:T(8,128)(2,1)S(1)} %collective-permute-done.14.refs_0_), channel_id=1, source_target_pairs={{0,4},{4,8},{8,12},{12,14},{14,10},{10,6},{6,2},{2,0},{1,3},{5,1},... | collective-permute-start | bytes 1572872 | tf_op jit(solution)/shard_map/ppermute | solution.py:33
  38.5 9.7 %collective-permute-start.16 = (bf16[256,512]{1,0:T(8,128)(2,1)S(1)}, bf16[256,512]{1,0:T(8,128)(2,1)S(1)}, u32[]{:S(2)}, u32[]{:S(2)}) collective-permute-start(bf16[256,512]{1,0:T(8,128)(2,1)S(1)} %get-tuple-element.134), channel_id=1, source_target_pairs={{0,16},{1,17},{2,18},{3,19},{4,20},{5,21},{6,22},{7,23},{8,24},{9,... | collective-permute-start | bytes 786440 | tf_op jit(solution)/shard_map/ppermute | solution.py:504
  40.5 9.8 %collective-permute-start.18 = (bf16[64,4096]{1,0:T(8,128)(2,1)S(1)}, bf16[64,4096]{1,0:T(8,128)(2,1)S(1)}, u32[]{:S(2)}, u32[]{:S(2)}) collective-permute-start(bf16[64,4096]{1,0:T(8,128)(2,1)S(1)} %collective-permute-done.14.refs_0_), channel_id=1, source_target_pairs={{0,1},{1,0},{2,3},{3,2},{4,5},{5,4},{6,7},{7,6},{8,9},{9,8},{10,11... | collective-permute-start | bytes 1572872 | tf_op jit(solution)/shard_map/ppermute | solution.py:29
  58.0 19.4 %collective-permute-start.23 = (bf16[640,512]{1,0:T(8,128)(2,1)S(1)}, bf16[640,512]{1,0:T(8,128)(2,1)S(1)}, u32[]{:S(2)}, u32[]{:S(2)}) collective-permute-start(bf16[640,512]{1,0:T(8,128)(2,1)S(1)} %pad_maximum_fusion), channel_id=1, source_target_pairs={{0,16},{1,17},{2,18},{3,19},{4,20},{5,21},{6,22},{7,23},{8,24},{9,... | collective-permute-start | bytes 1966088 | tf_op jit(solution)/shard_map/ppermute | solution.py:504
  91.6 11.7 %collective-permute-start.30 = (bf16[128,4096]{1,0:T(8,128)(2,1)S(1)}, bf16[128,4096]{1,0:T(8,128)(2,1)S(1)}, u32[]{:S(2)}, u32[]{:S(2)}) collective-permute-start(bf16[128,4096]{1,0:T(8,128)(2,1)S(1)} %get-tuple-element.180), channel_id=1, source_target_pairs={{0,1},{1,0},{2,3},{3,2},{4,5},{5,4},{6,7},{7,6},{8,9},{9,8},{10,11... | collective-permute-start | bytes 3145736 | tf_op jit(solution)/shard_map/ppermute | solution.py:29
  96.2 11.7 %collective-permute-start.33 = (bf16[128,4096]{1,0:T(8,128)(2,1)S(1)}, bf16[128,4096]{1,0:T(8,128)(2,1)S(1)}, u32[]{:S(2)}, u32[]{:S(2)}) collective-permute-start(bf16[128,4096]{1,0:T(8,128)(2,1)S(1)} %get-tuple-element.189), channel_id=1, source_target_pairs={{0,1},{1,0},{2,3},{3,2},{4,5},{5,4},{6,7},{7,6},{8,9},{9,8},{10,11... | collective-permute-start | bytes 3145736 | tf_op jit(solution)/shard_map/ppermute | solution.py:29
  105.4 14.9 %collective-permute-start.35 = (bf16[128,4096]{1,0:T(8,128)(2,1)S(1)}, bf16[128,4096]{1,0:T(8,128)(2,1)S(1)}, u32[]{:S(2)}, u32[]{:S(2)}) collective-permute-start(bf16[128,4096]{1,0:T(8,128)(2,1)S(1)} %get-tuple-element.192), channel_id=1, source_target_pairs={{0,1},{1,0},{2,3},{3,2},{4,5},{5,4},{6,7},{7,6},{8,9},{9,8},{10,11... | collective-permute-start | bytes 3145736 | tf_op jit(solution)/shard_map/ppermute | solution.py:29
  106.8 12.7 %collective-permute-start.37 = (bf16[64,4096]{1,0:T(8,128)(2,1)S(1)}, bf16[64,4096]{1,0:T(8,128)(2,1)S(1)}, u32[]{:S(2)}, u32[]{:S(2)}) collective-permute-start(bf16[64,4096]{1,0:T(8,128)(2,1)S(1)} %convert_element_type.79), channel_id=1, source_target_pairs={{0,4},{4,8},{8,12},{12,14},{14,10},{10,6},{6,2},{2,0},{1,3},{5,1},... | collective-permute-start | bytes 1572872 | tf_op jit(solution)/shard_map/ppermute | solution.py:33
  114.0 11.1 %collective-permute-start.32 = (bf16[64,4096]{1,0:T(8,128)(2,1)S(1)}, bf16[64,4096]{1,0:T(8,128)(2,1)S(1)}, u32[]{:S(2)}, u32[]{:S(2)}) collective-permute-start(bf16[64,4096]{1,0:T(8,128)(2,1)S(1)} %add_convert_fusion.6), channel_id=1, source_target_pairs={{0,4},{4,8},{8,12},{12,14},{14,10},{10,6},{6,2},{2,0},{1,3},{5,1},... | collective-permute-start | bytes 1572872 | tf_op jit(solution)/shard_map/ppermute | solution.py:33
  119.6 11.1 %collective-permute-start.38 = (bf16[64,4096]{1,0:T(8,128)(2,1)S(1)}, bf16[64,4096]{1,0:T(8,128)(2,1)S(1)}, u32[]{:S(2)}, u32[]{:S(2)}) collective-permute-start(bf16[64,4096]{1,0:T(8,128)(2,1)S(1)} %add_convert_fusion.3), channel_id=1, source_target_pairs={{0,4},{4,8},{8,12},{12,14},{14,10},{10,6},{6,2},{2,0},{1,3},{5,1},... | collective-permute-start | bytes 1572872 | tf_op jit(solution)/shard_map/ppermute | solution.py:33
  125.2 11.1 %collective-permute-start.34 = (bf16[64,4096]{1,0:T(8,128)(2,1)S(1)}, bf16[64,4096]{1,0:T(8,128)(2,1)S(1)}, u32[]{:S(2)}, u32[]{:S(2)}) collective-permute-start(bf16[64,4096]{1,0:T(8,128)(2,1)S(1)} %add_convert_fusion.5), channel_id=1, source_target_pairs={{0,4},{4,8},{8,12},{12,14},{14,10},{10,6},{6,2},{2,0},{1,3},{5,1},... | collective-permute-start | bytes 1572872 | tf_op jit(solution)/shard_map/ppermute | solution.py:33
  130.8 11.1 %collective-permute-start.39 = (bf16[64,4096]{1,0:T(8,128)(2,1)S(1)}, bf16[64,4096]{1,0:T(8,128)(2,1)S(1)}, u32[]{:S(2)}, u32[]{:S(2)}) collective-permute-start(bf16[64,4096]{1,0:T(8,128)(2,1)S(1)} %add_convert_fusion.2), channel_id=1, source_target_pairs={{0,4},{4,8},{8,12},{12,14},{14,10},{10,6},{6,2},{2,0},{1,3},{5,1},... | collective-permute-start | bytes 1572872 | tf_op jit(solution)/shard_map/ppermute | solution.py:33
  136.4 11.1 %collective-permute-start.36 = (bf16[64,4096]{1,0:T(8,128)(2,1)S(1)}, bf16[64,4096]{1,0:T(8,128)(2,1)S(1)}, u32[]{:S(2)}, u32[]{:S(2)}) collective-permute-start(bf16[64,4096]{1,0:T(8,128)(2,1)S(1)} %add_convert_fusion.4), channel_id=1, source_target_pairs={{0,4},{4,8},{8,12},{12,14},{14,10},{10,6},{6,2},{2,0},{1,3},{5,1},... | collective-permute-start | bytes 1572872 | tf_op jit(solution)/shard_map/ppermute | solution.py:33
  (32 other events, 223.2 us)

commit v8 on v7

--- a/solution.py
+++ b/solution.py
@@ -210,21 +210,21 @@
     return refs[block][...]
 
 
-def two_blocks(refs, index):
-    return jnp.concatenate([block_rows_of(refs, 2 * index + k) for k in (0, 1)], axis=0)
+def four_blocks(refs, index):
+    return jnp.concatenate([block_rows_of(refs, 4 * index + k) for k in range(4)], axis=0)
 
 
 def inner_kernel(info, *refs):
     base_refs, up_refs, (rank_ref, meta_ref, turn_ref, first_ref, last_ref) = refs[:5], refs[5:10], refs[10:15]
     qkv_right_ref, up_right_ref, bias_ref, left_ref = refs[15:19]
     q_ref, k_ref, v_ref, hidden_ref, out_ref = refs[19:]
-    rows = 512
+    rows = 1024
     columns = qkv_right_ref.shape[0]
-    for block in range(BLOCKS // 2):
+    for block in range(BLOCKS // 4):
         at = slice(block * rows, (block + 1) * rows)
         adapter = meta_ref[at, 64:65]
-        ranks = rank_rows(info, rank_ref, 4 * block, 4)
-        total = two_blocks(base_refs, block) + rank_product(
+        ranks = rank_rows(info, rank_ref, 8 * block, 8)
+        total = four_blocks(base_refs, block) + rank_product(
             widened(ranks, first_ref, adapter, columns), qkv_right_ref[...]
         )
         table = turn_ref[at, :]
@@ -232,23 +232,23 @@
         k_ref[at, :] = turn(total[:, HEAD_SIZE : 2 * HEAD_SIZE], table).astype(jnp.bfloat16)
         v_ref[at, :] = total[:, 2 * HEAD_SIZE :].astype(jnp.bfloat16)
         wide = widened(ranks, last_ref, adapter, columns)
-        x = two_blocks(up_refs, block) + rank_product(wide, up_right_ref[...]) + bias_ref[...]
+        x = four_blocks(up_refs, block) + rank_product(wide, up_right_ref[...]) + bias_ref[...]
         inner = math.sqrt(2.0 / math.pi) * (x + 0.044715 * (x * x * x))
         hidden = (0.5 * x * (1.0 + jnp.tanh(inner))).astype(jnp.bfloat16)
         hidden_ref[at, :] = hidden
         lanes = folded(rank_product(hidden, left_ref[...]), adapter, last_ref)
-        store_lanes(info, out_ref, lanes, range(4 * block, 4 * block + 4))
+        store_lanes(info, out_ref, lanes, range(8 * block, 8 * block + 8))
 
 
 def far_kernel(first_row, info, *refs):
     shared_refs, (rank_ref, meta_ref, turn_ref, spread_ref, right_ref, k_ref, v_ref) = refs[:5], refs[5:]
-    rows = 512
-    for block in range(BLOCKS // 2):
+    rows = 1024
+    for block in range(BLOCKS // 4):
         at = slice(block * rows, (block + 1) * rows)
         far_at = slice(first_row + block * rows, first_row + (block + 1) * rows)
-        ranks = rank_rows(info, rank_ref, 4 * block, 4)
+        ranks = rank_rows(info, rank_ref, 8 * block, 8)
         wide = widened(ranks, spread_ref, meta_ref[far_at, 64:65], right_ref.shape[0])
-        total = two_blocks(shared_refs, block).astype(jnp.float32)
+        total = four_blocks(shared_refs, block).astype(jnp.float32)
         total = total + rank_product(wide, right_ref[:, HEAD_SIZE:])
         k_ref[at, :] = turn(total[:, :HEAD_SIZE], turn_ref[far_at, :]).astype(jnp.bfloat16)
         v_ref[at, :] = total[:, HEAD_SIZE:].astype(jnp.bfloat16)

time: 149 us -> 149 us (level)
  no operation moved by 1% of the time
where the time goes in v8:
time: 149 us; the launch traced here: 148 us
  Pallas kernels  50.8 us (34%)
  waiting for transfers between devices  48.2 us (32%)
  starting transfers between devices  41.8 us (28%)
  local copies, waits for them, and re-layouts  3.6 us (2%)
  other arithmetic  3.18 us (2%)
    pallas_call x23, Pallas kernels, call(): pl.pallas_call(kernel, in_specs=specs, out_specs=[vmem] * len(outs), out_...  50.8 us
    ppermute x14, waiting for transfers between devices, along_ring(): return lax.ppermute(value, 'mlp', RING_PERM)  36.3 us
    ppermute x14, starting transfers between devices, along_ring(): return lax.ppermute(value, 'mlp', RING_PERM)  19.1 us
    ppermute x4, starting transfers between devices, to_group(): lax.ppermute(value, 'req', [(g, g + d) for g in range(req_count - d)])  8.58 us
    ppermute x4, starting transfers between devices, per_device(): moved = lax.ppermute(rank_out, 'mlp', [(i, i ^ bit) for i in range(16)])  5.74 us
    ppermute x2, waiting for transfers between devices, sum_over_mlp(): lax.ppermute(value, 'mlp', [(i, i ^ bit) for i in range(16)])  5.26 us
    ppermute x4, waiting for transfers between devices, per_device(): moved = lax.ppermute(rank_out, 'mlp', [(i, i ^ bit) for i in range(16)])  4.64 us
    ppermute x2, starting transfers between devices, sum_over_mlp(): lax.ppermute(value, 'mlp', [(i, i ^ bit) for i in range(16)])  4.3 us
  transfers between devices with their start and end apart: 41, of which 16 were waited for; matrix products, arithmetic and copies ran while one was open for 3% of the time, Pallas kernels for 27%

profile of v8, /device:TPU:0, one launch (start us, length us, event | category | flops | bytes accessed | tf_op | source)
XLA Modules:
  0.0 148.2 jit_solution(14264305868267077449)
XLA Ops:
  2.1 3.0 %collective-permute-start = (bf16[64,4096]{1,0:T(8,128)(2,1)S(1)}, bf16[64,4096]{1,0:T(8,128)(2,1)S(1)}, u32[]{:S(2)}, u32[]{:S(2)}) collective-permute-start(bf16[64,4096]{1,0:T(8,128)(2,1)S(1)} %shard_map.217.refs_0_), channel_id=1, source_target_pairs={{0,4},{4,8},{8,12},{12,14},{14,10},{10,6},{6,2},{2,0},{1,3},{5,1},... | collective-permute-start | bytes 1572872 | tf_op jit(solution)/shard_map/ppermute | solution.py:33
  10.2 4.6 %shard_map.218 = (f32[2048,128]{1,0:T(8,128)S(1)}, f32[2048,128]{1,0:T(8,128)S(1)}, bf16[4096,768]{1,0:T(8,128)(2,1)S(1)}, bf16[4096,512]{1,0:T(8,128)(2,1)S(1)}) custom-call(s32[34]{0:T(128)S(1)} %dynamic-slice_bitcast_fusion.info, f32[65,1]{1,0:T(8,128)S(1)} %copy.24.column_ref, f32[1,65]{1,0:T(1,128)S(1)} %get-tuple-element.201.row_ref, ...), custom_call_target="tpu_custom_call" | custom-call | flops 1000 | bytes 1000 | tf_op jit(solution)/shard_map/pallas_call | solution.py:388
  19.9 2.1 %collective-permute-start.5 = (bf16[64,4096]{1,0:T(8,128)(2,1)S(1)}, bf16[64,4096]{1,0:T(8,128)(2,1)S(1)}, u32[]{:S(2)}, u32[]{:S(2)}) collective-permute-start(bf16[64,4096]{1,0:T(8,128)(2,1)S(1)} %collective-permute-done.3.refs_3_.refs_1_), channel_id=1, source_target_pairs={{0,4},{4,8},{8,12},{12,14},{14,10},{10,6},{6,2},{2,0},{1,3},{5,1},... | collective-permute-start | bytes 1572872 | tf_op jit(solution)/shard_map/ppermute | solution.py:33
  25.6 3.4 %collective-permute-start.9 = (bf16[128,512]{1,0:T(8,128)(2,1)S(1)}, bf16[128,512]{1,0:T(8,128)(2,1)S(1)}, u32[]{:S(2)}, u32[]{:S(2)}) collective-permute-start(bf16[128,512]{1,0:T(8,128)(2,1)S(1)} %get-tuple-element.120), channel_id=1, source_target_pairs={{0,16},{1,17},{2,18},{3,19},{4,20},{5,21},{6,22},{7,23},{8,24},{9,... | collective-permute-start | bytes 393224 | tf_op jit(solution)/shard_map/ppermute | solution.py:504
  30.5 2.9 %shard_map.221 = (f32[256,768]{1,0:T(8,128)S(1)}, f32[256,512]{1,0:T(8,128)S(1)}, bf16[256,512]{1,0:T(8,128)(2,1)S(1)}) custom-call(bf16[64,4096]{1,0:T(8,128)(2,1)S(1)} %collective-permute-done.refs_2_.refs_0_, bf16[64,4096]{1,0:T(8,128)(2,1)S(1)} %collective-permute-done.3.refs_3_.refs_1_, bf16[64,4096]{1,0:T(8,128)(2,1)S(1)} %collective-permute-done.6.refs_4_.refs_2_, ...), custom_call_target="tpu_custom_call" | custom-call | flops 1000 | bytes 1000 | tf_op jit(solution)/shard_map/pallas_call | solution.py:388
  38.5 1.9 %collective-permute-start.16 = (bf16[256,512]{1,0:T(8,128)(2,1)S(1)}, bf16[256,512]{1,0:T(8,128)(2,1)S(1)}, u32[]{:S(2)}, u32[]{:S(2)}) collective-permute-start(bf16[256,512]{1,0:T(8,128)(2,1)S(1)} %get-tuple-element.134), channel_id=1, source_target_pairs={{0,16},{1,17},{2,18},{3,19},{4,20},{5,21},{6,22},{7,23},{8,24},{9,... | collective-permute-start | bytes 786440 | tf_op jit(solution)/shard_map/ppermute | solution.py:504
  40.5 2.9 %shard_map.223 = (f32[256,768]{1,0:T(8,128)S(1)}, f32[256,512]{1,0:T(8,128)S(1)}, bf16[256,512]{1,0:T(8,128)(2,1)S(1)}) custom-call(bf16[64,4096]{1,0:T(8,128)(2,1)S(1)} %collective-permute-done.1.refs_0_, bf16[64,4096]{1,0:T(8,128)(2,1)S(1)} %collective-permute-done.5.refs_1_, bf16[64,4096]{1,0:T(8,128)(2,1)S(1)} %collective-permute-done.11.refs_2_, ...), custom_call_target="tpu_custom_call" | custom-call | flops 1000 | bytes 1000 | tf_op jit(solution)/shard_map/pallas_call | solution.py:388
  48.2 2.0 %collective-permute-done.15.refs_2_ = bf16[64,4096]{1,0:T(8,128)(2,1)S(1)} collective-permute-done((bf16[64,4096]{1,0:T(8,128)(2,1)S(1)}, bf16[64,4096]{1,0:T(8,128)(2,1)S(1)}, u32[]{:S(2)}, u32[]{:S(2)}) %collective-permute-start.15) | collective-permute-done | bytes 524320 | tf_op jit(solution)/shard_map/ppermute | solution.py:33
  55.0 2.9 %shard_map.227 = (f32[256,768]{1,0:T(8,128)S(1)}, f32[256,512]{1,0:T(8,128)S(1)}, bf16[256,512]{1,0:T(8,128)(2,1)S(1)}) custom-call(bf16[64,4096]{1,0:T(8,128)(2,1)S(1)} %collective-permute-done.17.refs_0_, bf16[64,4096]{1,0:T(8,128)(2,1)S(1)} %collective-permute-done.18.refs_1_, bf16[64,4096]{1,0:T(8,128)(2,1)S(1)} %collective-permute-done.15.refs_2_, ...), custom_call_target="tpu_custom_call" | custom-call | flops 1000 | bytes 1000 | tf_op jit(solution)/shard_map/pallas_call | solution.py:388
  61.4 2.7 %collective-permute-done.21 = bf16[32,1024]{1,0:T(8,128)(2,1)S(1)} collective-permute-done((bf16[32,1024]{1,0:T(8,128)(2,1)S(1)}, bf16[32,1024]{1,0:T(8,128)(2,1)S(1)}, u32[]{:S(2)}, u32[]{:S(2)}) %collective-permute-start.21) | collective-permute-done | bytes 65568 | tf_op jit(solution)/shard_map/ppermute | solution.py:405
  64.1 2.7 %collective-permute-start.22 = (bf16[32,1024]{1,0:T(8,128)(2,1)S(1)}, bf16[32,1024]{1,0:T(8,128)(2,1)S(1)}, u32[]{:S(2)}, u32[]{:S(2)}) collective-permute-start(bf16[32,1024]{1,0:T(8,128)(2,1)S(1)} %add.62), channel_id=1, source_target_pairs={{0,8},{1,9},{2,10},{3,11},{4,12},{5,13},{6,14},{7,15},{8,0},{9,1},... | collective-permute-start | bytes 196616 | tf_op jit(solution)/shard_map/ppermute | solution.py:405
  66.8 2.6 %collective-permute-done.22 = bf16[32,1024]{1,0:T(8,128)(2,1)S(1)} collective-permute-done((bf16[32,1024]{1,0:T(8,128)(2,1)S(1)}, bf16[32,1024]{1,0:T(8,128)(2,1)S(1)}, u32[]{:S(2)}, u32[]{:S(2)}) %collective-permute-start.22) | collective-permute-done | bytes 65568 | tf_op jit(solution)/shard_map/ppermute | solution.py:405
  70.9 6.2 %shard_map.228 = (bf16[1024,256]{1,0:T(8,128)(2,1)S(1)}, bf16[1024,256]{1,0:T(8,128)(2,1)S(1)}, bf16[1024,256]{1,0:T(8,128)(2,1)S(1)}, bf16[1024,512]{1,0:T(8,128)(2,1)S(1)}, bf16[32,1024]{1,0:T(8,128)(2,1)S(1)}) custom-call(s32[34]{0:T(128)S(1)} %dynamic-slice_bitcast_fusion.info, f32[128,768]{1,0:T(8,128)S(1)} %get-tuple-element.112.refs_0_, ...), custom_call_target="tpu_custom_call" | custom-call | flops 1000 | bytes 1000 | tf_op jit(solution)/shard_map/pallas_call | solution.py:388
  77.2 2.3 %shard_map.229 = (bf16[1024,256]{1,0:T(8,128)(2,1)S(1)}, bf16[1024,256]{1,0:T(8,128)(2,1)S(1)}) custom-call(s32[34]{0:T(128)S(1)} %dynamic-slice_bitcast_fusion.info, bf16[128,512]{1,0:T(8,128)(2,1)S(1)} %collective-permute-done.9.refs_0_, bf16[256,512]{1,0:T(8,128)(2,1)S(1)} %collective-permute-done.16.refs_1_, ...), custom_call_target="tpu_custom_call" | custom-call | flops 1000 | bytes 1000 | tf_op jit(solution)/shard_map/pallas_call | solution.py:388
  79.5 5.2 %shard_map.230 = (bf16[1024,256]{1,0:T(8,128)(2,1)S(1)}, bf16[32,1024]{1,0:T(8,128)(2,1)S(1)}) custom-call(s32[34]{0:T(128)S(1)} %dynamic-slice_bitcast_fusion.info, bf16[1024,256]{1,0:T(8,128)(2,1)S(1)} %get-tuple-element.149.refs_0_, bf16[1024,256]{1,0:T(8,128)(2,1)S(1)} %get-tuple-element.150.refs_1_, bf16[1024,256]{1,0:T(8,128)(2,1)S(1)} %get-tuple-element.156.refs_2_, ...), custom_call_target="tpu_custom_call" | custom-call | flops 1000 | bytes 1000 | tf_op jit(solution)/shard_map/pallas_call | solution.py:388
  96.1 2.8 %collective-permute-start.29 = (bf16[32,1024]{1,0:T(8,128)(2,1)S(1)}, bf16[32,1024]{1,0:T(8,128)(2,1)S(1)}, u32[]{:S(2)}, u32[]{:S(2)}) collective-permute-start(bf16[32,1024]{1,0:T(8,128)(2,1)S(1)} %add.66), channel_id=1, source_target_pairs={{0,8},{1,9},{2,10},{3,11},{4,12},{5,13},{6,14},{7,15},{8,0},{9,1},... | collective-permute-start | bytes 196616 | tf_op jit(solution)/shard_map/ppermute | solution.py:624
  100.7 2.3 %collective-permute-done.29 = bf16[32,1024]{1,0:T(8,128)(2,1)S(1)} collective-permute-done((bf16[32,1024]{1,0:T(8,128)(2,1)S(1)}, bf16[32,1024]{1,0:T(8,128)(2,1)S(1)}, u32[]{:S(2)}, u32[]{:S(2)}) %collective-permute-start.29) | collective-permute-done | bytes 65568 | tf_op jit(solution)/shard_map/ppermute | solution.py:624
  108.9 4.6 %collective-permute-done.31 = bf16[64,4096]{1,0:T(8,128)(2,1)S(1)} collective-permute-done((bf16[64,4096]{1,0:T(8,128)(2,1)S(1)}, bf16[64,4096]{1,0:T(8,128)(2,1)S(1)}, u32[]{:S(2)}, u32[]{:S(2)}) %collective-permute-start.31) | collective-permute-done | bytes 524320 | tf_op jit(solution)/shard_map/ppermute | solution.py:33
  114.4 4.7 %collective-permute-done.37 = bf16[64,4096]{1,0:T(8,128)(2,1)S(1)} collective-permute-done((bf16[64,4096]{1,0:T(8,128)(2,1)S(1)}, bf16[64,4096]{1,0:T(8,128)(2,1)S(1)}, u32[]{:S(2)}, u32[]{:S(2)}) %collective-permute-start.37) | collective-permute-done | bytes 524320 | tf_op jit(solution)/shard_map/ppermute | solution.py:33
  121.2 3.5 %collective-permute-done.32 = bf16[64,4096]{1,0:T(8,128)(2,1)S(1)} collective-permute-done((bf16[64,4096]{1,0:T(8,128)(2,1)S(1)}, bf16[64,4096]{1,0:T(8,128)(2,1)S(1)}, u32[]{:S(2)}, u32[]{:S(2)}) %collective-permute-start.32) | collective-permute-done | bytes 524320 | tf_op jit(solution)/shard_map/ppermute | solution.py:33
  125.7 4.7 %collective-permute-done.38 = bf16[64,4096]{1,0:T(8,128)(2,1)S(1)} collective-permute-done((bf16[64,4096]{1,0:T(8,128)(2,1)S(1)}, bf16[64,4096]{1,0:T(8,128)(2,1)S(1)}, u32[]{:S(2)}, u32[]{:S(2)}) %collective-permute-start.38) | collective-permute-done | bytes 524320 | tf_op jit(solution)/shard_map/ppermute | solution.py:33
  131.2 4.7 %collective-permute-done.34 = bf16[64,4096]{1,0:T(8,128)(2,1)S(1)} collective-permute-done((bf16[64,4096]{1,0:T(8,128)(2,1)S(1)}, bf16[64,4096]{1,0:T(8,128)(2,1)S(1)}, u32[]{:S(2)}, u32[]{:S(2)}) %collective-permute-start.34) | collective-permute-done | bytes 524320 | tf_op jit(solution)/shard_map/ppermute | solution.py:33
  136.9 4.7 %collective-permute-done.39 = bf16[64,4096]{1,0:T(8,128)(2,1)S(1)} collective-permute-done((bf16[64,4096]{1,0:T(8,128)(2,1)S(1)}, bf16[64,4096]{1,0:T(8,128)(2,1)S(1)}, u32[]{:S(2)}, u32[]{:S(2)}) %collective-permute-start.39) | collective-permute-done | bytes 524320 | tf_op jit(solution)/shard_map/ppermute | solution.py:33
  143.0 4.2 %collective-permute-done.36 = bf16[64,4096]{1,0:T(8,128)(2,1)S(1)} collective-permute-done((bf16[64,4096]{1,0:T(8,128)(2,1)S(1)}, bf16[64,4096]{1,0:T(8,128)(2,1)S(1)}, u32[]{:S(2)}, u32[]{:S(2)}) %collective-permute-start.36) | collective-permute-done | bytes 524320 | tf_op jit(solution)/shard_map/ppermute | solution.py:33
  (142 shorter events, 64.2 us)
Async XLA Ops:
  2.1 15.8 %collective-permute-start.4 = (bf16[4096,128]{1,0:T(8,128)(2,1)}, bf16[4096,128]{1,0:T(8,128)(2,1)}, u32[]{:S(2)}, u32[]{:S(2)}) collective-permute-start(bf16[4096,128]{1,0:T(8,128)(2,1)} %param.32), channel_id=1, source_target_pairs={{0,1},{1,0},{2,3},{3,2},{4,5},{5,4},{6,7},{7,6},{8,9},{9,8},{10,11... | collective-permute-start | bytes 3145736 | tf_op jit(solution)/shard_map/ppermute | solution.py:29
  2.1 12.7 %collective-permute-start = (bf16[64,4096]{1,0:T(8,128)(2,1)S(1)}, bf16[64,4096]{1,0:T(8,128)(2,1)S(1)}, u32[]{:S(2)}, u32[]{:S(2)}) collective-permute-start(bf16[64,4096]{1,0:T(8,128)(2,1)S(1)} %shard_map.217.refs_0_), channel_id=1, source_target_pairs={{0,4},{4,8},{8,12},{12,14},{14,10},{10,6},{6,2},{2,0},{1,3},{5,1},... | collective-permute-start | bytes 1572872 | tf_op jit(solution)/shard_map/ppermute | solution.py:33
  5.1 12.7 %collective-permute-start.3 = (bf16[64,4096]{1,0:T(8,128)(2,1)S(1)}, bf16[64,4096]{1,0:T(8,128)(2,1)S(1)}, u32[]{:S(2)}, u32[]{:S(2)}) collective-permute-start(bf16[64,4096]{1,0:T(8,128)(2,1)S(1)} %collective-permute-done.2.refs_1_), channel_id=1, source_target_pairs={{0,4},{4,8},{8,12},{12,14},{14,10},{10,6},{6,2},{2,0},{1,3},{5,1},... | collective-permute-start | bytes 1572872 | tf_op jit(solution)/shard_map/ppermute | solution.py:33
  7.5 10.8 %collective-permute-start.8 = (f32[1,128]{1,0:T(1,128)S(1)}, f32[1,128]{1,0:T(1,128)S(1)}, u32[]{:S(2)}, u32[]{:S(2)}) collective-permute-start(f32[1,128]{1,0:T(1,128)S(1)} %convert_element_type.71), channel_id=1, source_target_pairs={{0,1},{1,0},{2,3},{3,2},{4,5},{5,4},{6,7},{7,6},{8,9},{9,8},{10,11... | collective-permute-start | bytes 1544 | tf_op jit(solution)/shard_map/ppermute | solution.py:29
  7.5 37.4 %collective-permute-start.13 = (bf16[128,4096]{1,0:T(8,128)(2,1)}, bf16[128,4096]{1,0:T(8,128)(2,1)S(1)}, u32[]{:S(2)}, u32[]{:S(2)}) collective-permute-start(bf16[128,4096]{1,0:T(8,128)(2,1)} %param.37), channel_id=1, source_target_pairs={{0,1},{1,0},{2,3},{3,2},{4,5},{5,4},{6,7},{7,6},{8,9},{9,8},{10,11... | collective-permute-start | bytes 3145736 | tf_op jit(solution)/shard_map/ppermute | solution.py:29
  14.8 9.2 %collective-permute-start.1 = (bf16[64,4096]{1,0:T(8,128)(2,1)S(1)}, bf16[64,4096]{1,0:T(8,128)(2,1)S(1)}, u32[]{:S(2)}, u32[]{:S(2)}) collective-permute-start(bf16[64,4096]{1,0:T(8,128)(2,1)S(1)} %collective-permute-done.refs_2_.refs_0_), channel_id=1, source_target_pairs={{0,4},{4,8},{8,12},{12,14},{14,10},{10,6},{6,2},{2,0},{1,3},{5,1},... | collective-permute-start | bytes 1572872 | tf_op jit(solution)/shard_map/ppermute | solution.py:33
  19.9 15.3 %collective-permute-start.5 = (bf16[64,4096]{1,0:T(8,128)(2,1)S(1)}, bf16[64,4096]{1,0:T(8,128)(2,1)S(1)}, u32[]{:S(2)}, u32[]{:S(2)}) collective-permute-start(bf16[64,4096]{1,0:T(8,128)(2,1)S(1)} %collective-permute-done.3.refs_3_.refs_1_), channel_id=1, source_target_pairs={{0,4},{4,8},{8,12},{12,14},{14,10},{10,6},{6,2},{2,0},{1,3},{5,1},... | collective-permute-start | bytes 1572872 | tf_op jit(solution)/shard_map/ppermute | solution.py:33
  24.0 14.5 %collective-permute-start.12 = (bf16[64,4096]{1,0:T(8,128)(2,1)S(1)}, bf16[64,4096]{1,0:T(8,128)(2,1)S(1)}, u32[]{:S(2)}, u32[]{:S(2)}) collective-permute-start(bf16[64,4096]{1,0:T(8,128)(2,1)S(1)} %collective-permute-done.1.refs_0_), channel_id=1, source_target_pairs={{0,1},{1,0},{2,3},{3,2},{4,5},{5,4},{6,7},{7,6},{8,9},{9,8},{10,11... | collective-permute-start | bytes 1572872 | tf_op jit(solution)/shard_map/ppermute | solution.py:29
  24.0 12.9 %collective-permute-start.14 = (bf16[64,4096]{1,0:T(8,128)(2,1)S(1)}, bf16[64,4096]{1,0:T(8,128)(2,1)S(1)}, u32[]{:S(2)}, u32[]{:S(2)}) collective-permute-start(bf16[64,4096]{1,0:T(8,128)(2,1)S(1)} %collective-permute-done.1.refs_0_), channel_id=1, source_target_pairs={{0,4},{4,8},{8,12},{12,14},{14,10},{10,6},{6,2},{2,0},{1,3},{5,1},... | collective-permute-start | bytes 1572872 | tf_op jit(solution)/shard_map/ppermute | solution.py:33
  25.6 9.6 %collective-permute-start.9 = (bf16[128,512]{1,0:T(8,128)(2,1)S(1)}, bf16[128,512]{1,0:T(8,128)(2,1)S(1)}, u32[]{:S(2)}, u32[]{:S(2)}) collective-permute-start(bf16[128,512]{1,0:T(8,128)(2,1)S(1)} %get-tuple-element.120), channel_id=1, source_target_pairs={{0,16},{1,17},{2,18},{3,19},{4,20},{5,21},{6,22},{7,23},{8,24},{9,... | collective-permute-start | bytes 393224 | tf_op jit(solution)/shard_map/ppermute | solution.py:504
  35.3 9.6 %collective-permute-start.10 = (bf16[64,4096]{1,0:T(8,128)(2,1)S(1)}, bf16[64,4096]{1,0:T(8,128)(2,1)S(1)}, u32[]{:S(2)}, u32[]{:S(2)}) collective-permute-start(bf16[64,4096]{1,0:T(8,128)(2,1)S(1)} %collective-permute-done.5.refs_1_), channel_id=1, source_target_pairs={{0,4},{4,8},{8,12},{12,14},{14,10},{10,6},{6,2},{2,0},{1,3},{5,1},... | collective-permute-start | bytes 1572872 | tf_op jit(solution)/shard_map/ppermute | solution.py:33
  36.9 13.3 %collective-permute-start.15 = (bf16[64,4096]{1,0:T(8,128)(2,1)S(1)}, bf16[64,4096]{1,0:T(8,128)(2,1)S(1)}, u32[]{:S(2)}, u32[]{:S(2)}) collective-permute-start(bf16[64,4096]{1,0:T(8,128)(2,1)S(1)} %collective-permute-done.14.refs_0_), channel_id=1, source_target_pairs={{0,4},{4,8},{8,12},{12,14},{14,10},{10,6},{6,2},{2,0},{1,3},{5,1},... | collective-permute-start | bytes 1572872 | tf_op jit(solution)/shard_map/ppermute | solution.py:33
  38.5 9.7 %collective-permute-start.16 = (bf16[256,512]{1,0:T(8,128)(2,1)S(1)}, bf16[256,512]{1,0:T(8,128)(2,1)S(1)}, u32[]{:S(2)}, u32[]{:S(2)}) collective-permute-start(bf16[256,512]{1,0:T(8,128)(2,1)S(1)} %get-tuple-element.134), channel_id=1, source_target_pairs={{0,16},{1,17},{2,18},{3,19},{4,20},{5,21},{6,22},{7,23},{8,24},{9,... | collective-permute-start | bytes 786440 | tf_op jit(solution)/shard_map/ppermute | solution.py:504
  40.5 9.8 %collective-permute-start.18 = (bf16[64,4096]{1,0:T(8,128)(2,1)S(1)}, bf16[64,4096]{1,0:T(8,128)(2,1)S(1)}, u32[]{:S(2)}, u32[]{:S(2)}) collective-permute-start(bf16[64,4096]{1,0:T(8,128)(2,1)S(1)} %collective-permute-done.14.refs_0_), channel_id=1, source_target_pairs={{0,1},{1,0},{2,3},{3,2},{4,5},{5,4},{6,7},{7,6},{8,9},{9,8},{10,11... | collective-permute-start | bytes 1572872 | tf_op jit(solution)/shard_map/ppermute | solution.py:29
  58.0 19.1 %collective-permute-start.23 = (bf16[640,512]{1,0:T(8,128)(2,1)S(1)}, bf16[640,512]{1,0:T(8,128)(2,1)S(1)}, u32[]{:S(2)}, u32[]{:S(2)}) collective-permute-start(bf16[640,512]{1,0:T(8,128)(2,1)S(1)} %pad_maximum_fusion), channel_id=1, source_target_pairs={{0,16},{1,17},{2,18},{3,19},{4,20},{5,21},{6,22},{7,23},{8,24},{9,... | collective-permute-start | bytes 1966088 | tf_op jit(solution)/shard_map/ppermute | solution.py:504
  91.3 11.7 %collective-permute-start.30 = (bf16[128,4096]{1,0:T(8,128)(2,1)S(1)}, bf16[128,4096]{1,0:T(8,128)(2,1)S(1)}, u32[]{:S(2)}, u32[]{:S(2)}) collective-permute-start(bf16[128,4096]{1,0:T(8,128)(2,1)S(1)} %get-tuple-element.180), channel_id=1, source_target_pairs={{0,1},{1,0},{2,3},{3,2},{4,5},{5,4},{6,7},{7,6},{8,9},{9,8},{10,11... | collective-permute-start | bytes 3145736 | tf_op jit(solution)/shard_map/ppermute | solution.py:29
  95.9 11.7 %collective-permute-start.33 = (bf16[128,4096]{1,0:T(8,128)(2,1)S(1)}, bf16[128,4096]{1,0:T(8,128)(2,1)S(1)}, u32[]{:S(2)}, u32[]{:S(2)}) collective-permute-start(bf16[128,4096]{1,0:T(8,128)(2,1)S(1)} %get-tuple-element.189), channel_id=1, source_target_pairs={{0,1},{1,0},{2,3},{3,2},{4,5},{5,4},{6,7},{7,6},{8,9},{9,8},{10,11... | collective-permute-start | bytes 3145736 | tf_op jit(solution)/shard_map/ppermute | solution.py:29
  105.1 14.9 %collective-permute-start.35 = (bf16[128,4096]{1,0:T(8,128)(2,1)S(1)}, bf16[128,4096]{1,0:T(8,128)(2,1)S(1)}, u32[]{:S(2)}, u32[]{:S(2)}) collective-permute-start(bf16[128,4096]{1,0:T(8,128)(2,1)S(1)} %get-tuple-element.192), channel_id=1, source_target_pairs={{0,1},{1,0},{2,3},{3,2},{4,5},{5,4},{6,7},{7,6},{8,9},{9,8},{10,11... | collective-permute-start | bytes 3145736 | tf_op jit(solution)/shard_map/ppermute | solution.py:29
  106.4 12.7 %collective-permute-start.37 = (bf16[64,4096]{1,0:T(8,128)(2,1)S(1)}, bf16[64,4096]{1,0:T(8,128)(2,1)S(1)}, u32[]{:S(2)}, u32[]{:S(2)}) collective-permute-start(bf16[64,4096]{1,0:T(8,128)(2,1)S(1)} %convert_element_type.79), channel_id=1, source_target_pairs={{0,4},{4,8},{8,12},{12,14},{14,10},{10,6},{6,2},{2,0},{1,3},{5,1},... | collective-permute-start | bytes 1572872 | tf_op jit(solution)/shard_map/ppermute | solution.py:33
  113.6 11.1 %collective-permute-start.32 = (bf16[64,4096]{1,0:T(8,128)(2,1)S(1)}, bf16[64,4096]{1,0:T(8,128)(2,1)S(1)}, u32[]{:S(2)}, u32[]{:S(2)}) collective-permute-start(bf16[64,4096]{1,0:T(8,128)(2,1)S(1)} %add_convert_fusion.6), channel_id=1, source_target_pairs={{0,4},{4,8},{8,12},{12,14},{14,10},{10,6},{6,2},{2,0},{1,3},{5,1},... | collective-permute-start | bytes 1572872 | tf_op jit(solution)/shard_map/ppermute | solution.py:33
  119.2 11.1 %collective-permute-start.38 = (bf16[64,4096]{1,0:T(8,128)(2,1)S(1)}, bf16[64,4096]{1,0:T(8,128)(2,1)S(1)}, u32[]{:S(2)}, u32[]{:S(2)}) collective-permute-start(bf16[64,4096]{1,0:T(8,128)(2,1)S(1)} %add_convert_fusion.3), channel_id=1, source_target_pairs={{0,4},{4,8},{8,12},{12,14},{14,10},{10,6},{6,2},{2,0},{1,3},{5,1},... | collective-permute-start | bytes 1572872 | tf_op jit(solution)/shard_map/ppermute | solution.py:33
  124.9 11.1 %collective-permute-start.34 = (bf16[64,4096]{1,0:T(8,128)(2,1)S(1)}, bf16[64,4096]{1,0:T(8,128)(2,1)S(1)}, u32[]{:S(2)}, u32[]{:S(2)}) collective-permute-start(bf16[64,4096]{1,0:T(8,128)(2,1)S(1)} %add_convert_fusion.5), channel_id=1, source_target_pairs={{0,4},{4,8},{8,12},{12,14},{14,10},{10,6},{6,2},{2,0},{1,3},{5,1},... | collective-permute-start | bytes 1572872 | tf_op jit(solution)/shard_map/ppermute | solution.py:33
  130.4 11.1 %collective-permute-start.39 = (bf16[64,4096]{1,0:T(8,128)(2,1)S(1)}, bf16[64,4096]{1,0:T(8,128)(2,1)S(1)}, u32[]{:S(2)}, u32[]{:S(2)}) collective-permute-start(bf16[64,4096]{1,0:T(8,128)(2,1)S(1)} %add_convert_fusion.2), channel_id=1, source_target_pairs={{0,4},{4,8},{8,12},{12,14},{14,10},{10,6},{6,2},{2,0},{1,3},{5,1},... | collective-permute-start | bytes 1572872 | tf_op jit(solution)/shard_map/ppermute | solution.py:33
  136.1 11.1 %collective-permute-start.36 = (bf16[64,4096]{1,0:T(8,128)(2,1)S(1)}, bf16[64,4096]{1,0:T(8,128)(2,1)S(1)}, u32[]{:S(2)}, u32[]{:S(2)}) collective-permute-start(bf16[64,4096]{1,0:T(8,128)(2,1)S(1)} %add_convert_fusion.4), channel_id=1, source_target_pairs={{0,4},{4,8},{8,12},{12,14},{14,10},{10,6},{6,2},{2,0},{1,3},{5,1},... | collective-permute-start | bytes 1572872 | tf_op jit(solution)/shard_map/ppermute | solution.py:33
  (32 other events, 222.7 us)

commit v9 on v8

--- a/solution.py
+++ b/solution.py
@@ -140,8 +140,13 @@
 def token_kernel(info, column_ref, row_ref, ids_ref, table_ref, *refs):
     count = (len(refs) - 3) // 2
     meta_ref, turn_ref = refs[count : count + 2]
-    pairs = zip(refs[:count], refs[count + 2 : -1])
-    copies = [pltpu.make_async_copy(a, b, refs[-1].at[k]) for k, (a, b) in enumerate(pairs)]
+    pieces = 4
+    copies = []
+    for k, (a, b) in enumerate(zip(refs[:count], refs[count + 2 : -1])):
+        depth = a.shape[0] // pieces
+        for piece in range(pieces):
+            at = pl.ds(piece * depth, depth)
+            copies.append(pltpu.make_async_copy(a.at[at, :], b.at[at, :], refs[-1].at[k * pieces + piece]))
     for copy in copies:
         copy.start()
     rows = 2 * 128
@@ -485,7 +490,7 @@
         token_args + weights,
         [shape(token_rows, 128, jnp.float32)] * 2 + [shape(*x.shape) for x in weights],
         info,
-        [pltpu.SemaphoreType.DMA((2,))],
+        [pltpu.SemaphoreType.DMA((8,))],
         in_hbm=2,
     )
 

time: 149 us -> 149 us (level)
  no operation moved by 1% of the time
where the time goes in v9:
time: 149 us; the launch traced here: 148 us
  Pallas kernels  50.8 us (34%)
  waiting for transfers between devices  48.2 us (32%)
  starting transfers between devices  41.7 us (28%)
  local copies, waits for them, and re-layouts  3.6 us (2%)
  other arithmetic  3.18 us (2%)
    pallas_call x23, Pallas kernels, call(): pl.pallas_call(kernel, in_specs=specs, out_specs=[vmem] * len(outs), out_...  50.8 us
    ppermute x14, waiting for transfers between devices, along_ring(): return lax.ppermute(value, 'mlp', RING_PERM)  36.3 us
    ppermute x14, starting transfers between devices, along_ring(): return lax.ppermute(value, 'mlp', RING_PERM)  19 us
    ppermute x4, starting transfers between devices, to_group(): lax.ppermute(value, 'req', [(g, g + d) for g in range(req_count - d)])  8.59 us
    ppermute x4, starting transfers between devices, per_device(): moved = lax.ppermute(rank_out, 'mlp', [(i, i ^ bit) for i in range(16)])  5.74 us
    ppermute x2, waiting for transfers between devices, sum_over_mlp(): lax.ppermute(value, 'mlp', [(i, i ^ bit) for i in range(16)])  5.26 us
    ppermute x4, waiting for transfers between devices, per_device(): moved = lax.ppermute(rank_out, 'mlp', [(i, i ^ bit) for i in range(16)])  4.64 us
    ppermute x2, starting transfers between devices, sum_over_mlp(): lax.ppermute(value, 'mlp', [(i, i ^ bit) for i in range(16)])  4.3 us
  transfers between devices with their start and end apart: 41, of which 16 were waited for; matrix products, arithmetic and copies ran while one was open for 3% of the time, Pallas kernels for 27%

profile of v9, /device:TPU:0, one launch (start us, length us, event | category | flops | bytes accessed | tf_op | source)
XLA Modules:
  0.0 148.2 jit_solution(4335450310639113119)
XLA Ops:
  2.1 3.0 %collective-permute-start = (bf16[64,4096]{1,0:T(8,128)(2,1)S(1)}, bf16[64,4096]{1,0:T(8,128)(2,1)S(1)}, u32[]{:S(2)}, u32[]{:S(2)}) collective-permute-start(bf16[64,4096]{1,0:T(8,128)(2,1)S(1)} %shard_map.217.refs_0_), channel_id=1, source_target_pairs={{0,4},{4,8},{8,12},{12,14},{14,10},{10,6},{6,2},{2,0},{1,3},{5,1},... | collective-permute-start | bytes 1572872 | tf_op jit(solution)/shard_map/ppermute | solution.py:33
  10.2 4.6 %shard_map.218 = (f32[2048,128]{1,0:T(8,128)S(1)}, f32[2048,128]{1,0:T(8,128)S(1)}, bf16[4096,768]{1,0:T(8,128)(2,1)S(1)}, bf16[4096,512]{1,0:T(8,128)(2,1)S(1)}) custom-call(s32[34]{0:T(128)S(1)} %dynamic-slice_bitcast_fusion.info, f32[65,1]{1,0:T(8,128)S(1)} %copy.24.column_ref, f32[1,65]{1,0:T(1,128)S(1)} %get-tuple-element.201.row_ref, ...), custom_call_target="tpu_custom_call" | custom-call | flops 1000 | bytes 1000 | tf_op jit(solution)/shard_map/pallas_call | solution.py:393
  19.9 2.1 %collective-permute-start.5 = (bf16[64,4096]{1,0:T(8,128)(2,1)S(1)}, bf16[64,4096]{1,0:T(8,128)(2,1)S(1)}, u32[]{:S(2)}, u32[]{:S(2)}) collective-permute-start(bf16[64,4096]{1,0:T(8,128)(2,1)S(1)} %collective-permute-done.3.refs_3_.refs_1_), channel_id=1, source_target_pairs={{0,4},{4,8},{8,12},{12,14},{14,10},{10,6},{6,2},{2,0},{1,3},{5,1},... | collective-permute-start | bytes 1572872 | tf_op jit(solution)/shard_map/ppermute | solution.py:33
  25.7 3.4 %collective-permute-start.9 = (bf16[128,512]{1,0:T(8,128)(2,1)S(1)}, bf16[128,512]{1,0:T(8,128)(2,1)S(1)}, u32[]{:S(2)}, u32[]{:S(2)}) collective-permute-start(bf16[128,512]{1,0:T(8,128)(2,1)S(1)} %get-tuple-element.120), channel_id=1, source_target_pairs={{0,16},{1,17},{2,18},{3,19},{4,20},{5,21},{6,22},{7,23},{8,24},{9,... | collective-permute-start | bytes 393224 | tf_op jit(solution)/shard_map/ppermute | solution.py:509
  30.5 2.9 %shard_map.221 = (f32[256,768]{1,0:T(8,128)S(1)}, f32[256,512]{1,0:T(8,128)S(1)}, bf16[256,512]{1,0:T(8,128)(2,1)S(1)}) custom-call(bf16[64,4096]{1,0:T(8,128)(2,1)S(1)} %collective-permute-done.refs_2_.refs_0_, bf16[64,4096]{1,0:T(8,128)(2,1)S(1)} %collective-permute-done.3.refs_3_.refs_1_, bf16[64,4096]{1,0:T(8,128)(2,1)S(1)} %collective-permute-done.6.refs_4_.refs_2_, ...), custom_call_target="tpu_custom_call" | custom-call | flops 1000 | bytes 1000 | tf_op jit(solution)/shard_map/pallas_call | solution.py:393
  38.5 2.0 %collective-permute-start.16 = (bf16[256,512]{1,0:T(8,128)(2,1)S(1)}, bf16[256,512]{1,0:T(8,128)(2,1)S(1)}, u32[]{:S(2)}, u32[]{:S(2)}) collective-permute-start(bf16[256,512]{1,0:T(8,128)(2,1)S(1)} %get-tuple-element.134), channel_id=1, source_target_pairs={{0,16},{1,17},{2,18},{3,19},{4,20},{5,21},{6,22},{7,23},{8,24},{9,... | collective-permute-start | bytes 786440 | tf_op jit(solution)/shard_map/ppermute | solution.py:509
  40.6 2.9 %shard_map.223 = (f32[256,768]{1,0:T(8,128)S(1)}, f32[256,512]{1,0:T(8,128)S(1)}, bf16[256,512]{1,0:T(8,128)(2,1)S(1)}) custom-call(bf16[64,4096]{1,0:T(8,128)(2,1)S(1)} %collective-permute-done.1.refs_0_, bf16[64,4096]{1,0:T(8,128)(2,1)S(1)} %collective-permute-done.5.refs_1_, bf16[64,4096]{1,0:T(8,128)(2,1)S(1)} %collective-permute-done.11.refs_2_, ...), custom_call_target="tpu_custom_call" | custom-call | flops 1000 | bytes 1000 | tf_op jit(solution)/shard_map/pallas_call | solution.py:393
  48.3 2.0 %collective-permute-done.15.refs_2_ = bf16[64,4096]{1,0:T(8,128)(2,1)S(1)} collective-permute-done((bf16[64,4096]{1,0:T(8,128)(2,1)S(1)}, bf16[64,4096]{1,0:T(8,128)(2,1)S(1)}, u32[]{:S(2)}, u32[]{:S(2)}) %collective-permute-start.15) | collective-permute-done | bytes 524320 | tf_op jit(solution)/shard_map/ppermute | solution.py:33
  55.0 2.9 %shard_map.227 = (f32[256,768]{1,0:T(8,128)S(1)}, f32[256,512]{1,0:T(8,128)S(1)}, bf16[256,512]{1,0:T(8,128)(2,1)S(1)}) custom-call(bf16[64,4096]{1,0:T(8,128)(2,1)S(1)} %collective-permute-done.17.refs_0_, bf16[64,4096]{1,0:T(8,128)(2,1)S(1)} %collective-permute-done.18.refs_1_, bf16[64,4096]{1,0:T(8,128)(2,1)S(1)} %collective-permute-done.15.refs_2_, ...), custom_call_target="tpu_custom_call" | custom-call | flops 1000 | bytes 1000 | tf_op jit(solution)/shard_map/pallas_call | solution.py:393
  61.4 2.7 %collective-permute-done.21 = bf16[32,1024]{1,0:T(8,128)(2,1)S(1)} collective-permute-done((bf16[32,1024]{1,0:T(8,128)(2,1)S(1)}, bf16[32,1024]{1,0:T(8,128)(2,1)S(1)}, u32[]{:S(2)}, u32[]{:S(2)}) %collective-permute-start.21) | collective-permute-done | bytes 65568 | tf_op jit(solution)/shard_map/ppermute | solution.py:410
  64.1 2.7 %collective-permute-start.22 = (bf16[32,1024]{1,0:T(8,128)(2,1)S(1)}, bf16[32,1024]{1,0:T(8,128)(2,1)S(1)}, u32[]{:S(2)}, u32[]{:S(2)}) collective-permute-start(bf16[32,1024]{1,0:T(8,128)(2,1)S(1)} %add.62), channel_id=1, source_target_pairs={{0,8},{1,9},{2,10},{3,11},{4,12},{5,13},{6,14},{7,15},{8,0},{9,1},... | collective-permute-start | bytes 196616 | tf_op jit(solution)/shard_map/ppermute | solution.py:410
  66.8 2.6 %collective-permute-done.22 = bf16[32,1024]{1,0:T(8,128)(2,1)S(1)} collective-permute-done((bf16[32,1024]{1,0:T(8,128)(2,1)S(1)}, bf16[32,1024]{1,0:T(8,128)(2,1)S(1)}, u32[]{:S(2)}, u32[]{:S(2)}) %collective-permute-start.22) | collective-permute-done | bytes 65568 | tf_op jit(solution)/shard_map/ppermute | solution.py:410
  70.9 6.2 %shard_map.228 = (bf16[1024,256]{1,0:T(8,128)(2,1)S(1)}, bf16[1024,256]{1,0:T(8,128)(2,1)S(1)}, bf16[1024,256]{1,0:T(8,128)(2,1)S(1)}, bf16[1024,512]{1,0:T(8,128)(2,1)S(1)}, bf16[32,1024]{1,0:T(8,128)(2,1)S(1)}) custom-call(s32[34]{0:T(128)S(1)} %dynamic-slice_bitcast_fusion.info, f32[128,768]{1,0:T(8,128)S(1)} %get-tuple-element.112.refs_0_, ...), custom_call_target="tpu_custom_call" | custom-call | flops 1000 | bytes 1000 | tf_op jit(solution)/shard_map/pallas_call | solution.py:393
  77.2 2.3 %shard_map.229 = (bf16[1024,256]{1,0:T(8,128)(2,1)S(1)}, bf16[1024,256]{1,0:T(8,128)(2,1)S(1)}) custom-call(s32[34]{0:T(128)S(1)} %dynamic-slice_bitcast_fusion.info, bf16[128,512]{1,0:T(8,128)(2,1)S(1)} %collective-permute-done.9.refs_0_, bf16[256,512]{1,0:T(8,128)(2,1)S(1)} %collective-permute-done.16.refs_1_, ...), custom_call_target="tpu_custom_call" | custom-call | flops 1000 | bytes 1000 | tf_op jit(solution)/shard_map/pallas_call | solution.py:393
  79.5 5.2 %shard_map.230 = (bf16[1024,256]{1,0:T(8,128)(2,1)S(1)}, bf16[32,1024]{1,0:T(8,128)(2,1)S(1)}) custom-call(s32[34]{0:T(128)S(1)} %dynamic-slice_bitcast_fusion.info, bf16[1024,256]{1,0:T(8,128)(2,1)S(1)} %get-tuple-element.149.refs_0_, bf16[1024,256]{1,0:T(8,128)(2,1)S(1)} %get-tuple-element.150.refs_1_, bf16[1024,256]{1,0:T(8,128)(2,1)S(1)} %get-tuple-element.156.refs_2_, ...), custom_call_target="tpu_custom_call" | custom-call | flops 1000 | bytes 1000 | tf_op jit(solution)/shard_map/pallas_call | solution.py:393
  96.1 2.8 %collective-permute-start.29 = (bf16[32,1024]{1,0:T(8,128)(2,1)S(1)}, bf16[32,1024]{1,0:T(8,128)(2,1)S(1)}, u32[]{:S(2)}, u32[]{:S(2)}) collective-permute-start(bf16[32,1024]{1,0:T(8,128)(2,1)S(1)} %add.66), channel_id=1, source_target_pairs={{0,8},{1,9},{2,10},{3,11},{4,12},{5,13},{6,14},{7,15},{8,0},{9,1},... | collective-permute-start | bytes 196616 | tf_op jit(solution)/shard_map/ppermute | solution.py:629
  100.7 2.3 %collective-permute-done.29 = bf16[32,1024]{1,0:T(8,128)(2,1)S(1)} collective-permute-done((bf16[32,1024]{1,0:T(8,128)(2,1)S(1)}, bf16[32,1024]{1,0:T(8,128)(2,1)S(1)}, u32[]{:S(2)}, u32[]{:S(2)}) %collective-permute-start.29) | collective-permute-done | bytes 65568 | tf_op jit(solution)/shard_map/ppermute | solution.py:629
  108.9 4.6 %collective-permute-done.31 = bf16[64,4096]{1,0:T(8,128)(2,1)S(1)} collective-permute-done((bf16[64,4096]{1,0:T(8,128)(2,1)S(1)}, bf16[64,4096]{1,0:T(8,128)(2,1)S(1)}, u32[]{:S(2)}, u32[]{:S(2)}) %collective-permute-start.31) | collective-permute-done | bytes 524320 | tf_op jit(solution)/shard_map/ppermute | solution.py:33
  114.4 4.7 %collective-permute-done.37 = bf16[64,4096]{1,0:T(8,128)(2,1)S(1)} collective-permute-done((bf16[64,4096]{1,0:T(8,128)(2,1)S(1)}, bf16[64,4096]{1,0:T(8,128)(2,1)S(1)}, u32[]{:S(2)}, u32[]{:S(2)}) %collective-permute-start.37) | collective-permute-done | bytes 524320 | tf_op jit(solution)/shard_map/ppermute | solution.py:33
  121.2 3.5 %collective-permute-done.32 = bf16[64,4096]{1,0:T(8,128)(2,1)S(1)} collective-permute-done((bf16[64,4096]{1,0:T(8,128)(2,1)S(1)}, bf16[64,4096]{1,0:T(8,128)(2,1)S(1)}, u32[]{:S(2)}, u32[]{:S(2)}) %collective-permute-start.32) | collective-permute-done | bytes 524320 | tf_op jit(solution)/shard_map/ppermute | solution.py:33
  125.7 4.7 %collective-permute-done.38 = bf16[64,4096]{1,0:T(8,128)(2,1)S(1)} collective-permute-done((bf16[64,4096]{1,0:T(8,128)(2,1)S(1)}, bf16[64,4096]{1,0:T(8,128)(2,1)S(1)}, u32[]{:S(2)}, u32[]{:S(2)}) %collective-permute-start.38) | collective-permute-done | bytes 524320 | tf_op jit(solution)/shard_map/ppermute | solution.py:33
  131.2 4.7 %collective-permute-done.34 = bf16[64,4096]{1,0:T(8,128)(2,1)S(1)} collective-permute-done((bf16[64,4096]{1,0:T(8,128)(2,1)S(1)}, bf16[64,4096]{1,0:T(8,128)(2,1)S(1)}, u32[]{:S(2)}, u32[]{:S(2)}) %collective-permute-start.34) | collective-permute-done | bytes 524320 | tf_op jit(solution)/shard_map/ppermute | solution.py:33
  136.9 4.7 %collective-permute-done.39 = bf16[64,4096]{1,0:T(8,128)(2,1)S(1)} collective-permute-done((bf16[64,4096]{1,0:T(8,128)(2,1)S(1)}, bf16[64,4096]{1,0:T(8,128)(2,1)S(1)}, u32[]{:S(2)}, u32[]{:S(2)}) %collective-permute-start.39) | collective-permute-done | bytes 524320 | tf_op jit(solution)/shard_map/ppermute | solution.py:33
  143.0 4.2 %collective-permute-done.36 = bf16[64,4096]{1,0:T(8,128)(2,1)S(1)} collective-permute-done((bf16[64,4096]{1,0:T(8,128)(2,1)S(1)}, bf16[64,4096]{1,0:T(8,128)(2,1)S(1)}, u32[]{:S(2)}, u32[]{:S(2)}) %collective-permute-start.36) | collective-permute-done | bytes 524320 | tf_op jit(solution)/shard_map/ppermute | solution.py:33
  (142 shorter events, 64.2 us)
Async XLA Ops:
  2.1 15.8 %collective-permute-start.4 = (bf16[4096,128]{1,0:T(8,128)(2,1)}, bf16[4096,128]{1,0:T(8,128)(2,1)}, u32[]{:S(2)}, u32[]{:S(2)}) collective-permute-start(bf16[4096,128]{1,0:T(8,128)(2,1)} %param.32), channel_id=1, source_target_pairs={{0,1},{1,0},{2,3},{3,2},{4,5},{5,4},{6,7},{7,6},{8,9},{9,8},{10,11... | collective-permute-start | bytes 3145736 | tf_op jit(solution)/shard_map/ppermute | solution.py:29
  2.1 12.7 %collective-permute-start = (bf16[64,4096]{1,0:T(8,128)(2,1)S(1)}, bf16[64,4096]{1,0:T(8,128)(2,1)S(1)}, u32[]{:S(2)}, u32[]{:S(2)}) collective-permute-start(bf16[64,4096]{1,0:T(8,128)(2,1)S(1)} %shard_map.217.refs_0_), channel_id=1, source_target_pairs={{0,4},{4,8},{8,12},{12,14},{14,10},{10,6},{6,2},{2,0},{1,3},{5,1},... | collective-permute-start | bytes 1572872 | tf_op jit(solution)/shard_map/ppermute | solution.py:33
  5.1 12.7 %collective-permute-start.3 = (bf16[64,4096]{1,0:T(8,128)(2,1)S(1)}, bf16[64,4096]{1,0:T(8,128)(2,1)S(1)}, u32[]{:S(2)}, u32[]{:S(2)}) collective-permute-start(bf16[64,4096]{1,0:T(8,128)(2,1)S(1)} %collective-permute-done.2.refs_1_), channel_id=1, source_target_pairs={{0,4},{4,8},{8,12},{12,14},{14,10},{10,6},{6,2},{2,0},{1,3},{5,1},... | collective-permute-start | bytes 1572872 | tf_op jit(solution)/shard_map/ppermute | solution.py:33
  7.5 10.8 %collective-permute-start.8 = (f32[1,128]{1,0:T(1,128)S(1)}, f32[1,128]{1,0:T(1,128)S(1)}, u32[]{:S(2)}, u32[]{:S(2)}) collective-permute-start(f32[1,128]{1,0:T(1,128)S(1)} %convert_element_type.71), channel_id=1, source_target_pairs={{0,1},{1,0},{2,3},{3,2},{4,5},{5,4},{6,7},{7,6},{8,9},{9,8},{10,11... | collective-permute-start | bytes 1544 | tf_op jit(solution)/shard_map/ppermute | solution.py:29
  7.5 37.4 %collective-permute-start.13 = (bf16[128,4096]{1,0:T(8,128)(2,1)}, bf16[128,4096]{1,0:T(8,128)(2,1)S(1)}, u32[]{:S(2)}, u32[]{:S(2)}) collective-permute-start(bf16[128,4096]{1,0:T(8,128)(2,1)} %param.37), channel_id=1, source_target_pairs={{0,1},{1,0},{2,3},{3,2},{4,5},{5,4},{6,7},{7,6},{8,9},{9,8},{10,11... | collective-permute-start | bytes 3145736 | tf_op jit(solution)/shard_map/ppermute | solution.py:29
  14.8 9.2 %collective-permute-start.1 = (bf16[64,4096]{1,0:T(8,128)(2,1)S(1)}, bf16[64,4096]{1,0:T(8,128)(2,1)S(1)}, u32[]{:S(2)}, u32[]{:S(2)}) collective-permute-start(bf16[64,4096]{1,0:T(8,128)(2,1)S(1)} %collective-permute-done.refs_2_.refs_0_), channel_id=1, source_target_pairs={{0,4},{4,8},{8,12},{12,14},{14,10},{10,6},{6,2},{2,0},{1,3},{5,1},... | collective-permute-start | bytes 1572872 | tf_op jit(solution)/shard_map/ppermute | solution.py:33
  19.9 15.4 %collective-permute-start.5 = (bf16[64,4096]{1,0:T(8,128)(2,1)S(1)}, bf16[64,4096]{1,0:T(8,128)(2,1)S(1)}, u32[]{:S(2)}, u32[]{:S(2)}) collective-permute-start(bf16[64,4096]{1,0:T(8,128)(2,1)S(1)} %collective-permute-done.3.refs_3_.refs_1_), channel_id=1, source_target_pairs={{0,4},{4,8},{8,12},{12,14},{14,10},{10,6},{6,2},{2,0},{1,3},{5,1},... | collective-permute-start | bytes 1572872 | tf_op jit(solution)/shard_map/ppermute | solution.py:33
  24.1 14.4 %collective-permute-start.12 = (bf16[64,4096]{1,0:T(8,128)(2,1)S(1)}, bf16[64,4096]{1,0:T(8,128)(2,1)S(1)}, u32[]{:S(2)}, u32[]{:S(2)}) collective-permute-start(bf16[64,4096]{1,0:T(8,128)(2,1)S(1)} %collective-permute-done.1.refs_0_), channel_id=1, source_target_pairs={{0,1},{1,0},{2,3},{3,2},{4,5},{5,4},{6,7},{7,6},{8,9},{9,8},{10,11... | collective-permute-start | bytes 1572872 | tf_op jit(solution)/shard_map/ppermute | solution.py:29
  24.1 12.9 %collective-permute-start.14 = (bf16[64,4096]{1,0:T(8,128)(2,1)S(1)}, bf16[64,4096]{1,0:T(8,128)(2,1)S(1)}, u32[]{:S(2)}, u32[]{:S(2)}) collective-permute-start(bf16[64,4096]{1,0:T(8,128)(2,1)S(1)} %collective-permute-done.1.refs_0_), channel_id=1, source_target_pairs={{0,4},{4,8},{8,12},{12,14},{14,10},{10,6},{6,2},{2,0},{1,3},{5,1},... | collective-permute-start | bytes 1572872 | tf_op jit(solution)/shard_map/ppermute | solution.py:33
  25.7 9.6 %collective-permute-start.9 = (bf16[128,512]{1,0:T(8,128)(2,1)S(1)}, bf16[128,512]{1,0:T(8,128)(2,1)S(1)}, u32[]{:S(2)}, u32[]{:S(2)}) collective-permute-start(bf16[128,512]{1,0:T(8,128)(2,1)S(1)} %get-tuple-element.120), channel_id=1, source_target_pairs={{0,16},{1,17},{2,18},{3,19},{4,20},{5,21},{6,22},{7,23},{8,24},{9,... | collective-permute-start | bytes 393224 | tf_op jit(solution)/shard_map/ppermute | solution.py:509
  35.4 9.6 %collective-permute-start.10 = (bf16[64,4096]{1,0:T(8,128)(2,1)S(1)}, bf16[64,4096]{1,0:T(8,128)(2,1)S(1)}, u32[]{:S(2)}, u32[]{:S(2)}) collective-permute-start(bf16[64,4096]{1,0:T(8,128)(2,1)S(1)} %collective-permute-done.5.refs_1_), channel_id=1, source_target_pairs={{0,4},{4,8},{8,12},{12,14},{14,10},{10,6},{6,2},{2,0},{1,3},{5,1},... | collective-permute-start | bytes 1572872 | tf_op jit(solution)/shard_map/ppermute | solution.py:33
  37.0 13.3 %collective-permute-start.15 = (bf16[64,4096]{1,0:T(8,128)(2,1)S(1)}, bf16[64,4096]{1,0:T(8,128)(2,1)S(1)}, u32[]{:S(2)}, u32[]{:S(2)}) collective-permute-start(bf16[64,4096]{1,0:T(8,128)(2,1)S(1)} %collective-permute-done.14.refs_0_), channel_id=1, source_target_pairs={{0,4},{4,8},{8,12},{12,14},{14,10},{10,6},{6,2},{2,0},{1,3},{5,1},... | collective-permute-start | bytes 1572872 | tf_op jit(solution)/shard_map/ppermute | solution.py:33
  38.5 9.8 %collective-permute-start.16 = (bf16[256,512]{1,0:T(8,128)(2,1)S(1)}, bf16[256,512]{1,0:T(8,128)(2,1)S(1)}, u32[]{:S(2)}, u32[]{:S(2)}) collective-permute-start(bf16[256,512]{1,0:T(8,128)(2,1)S(1)} %get-tuple-element.134), channel_id=1, source_target_pairs={{0,16},{1,17},{2,18},{3,19},{4,20},{5,21},{6,22},{7,23},{8,24},{9,... | collective-permute-start | bytes 786440 | tf_op jit(solution)/shard_map/ppermute | solution.py:509
  40.5 9.8 %collective-permute-start.18 = (bf16[64,4096]{1,0:T(8,128)(2,1)S(1)}, bf16[64,4096]{1,0:T(8,128)(2,1)S(1)}, u32[]{:S(2)}, u32[]{:S(2)}) collective-permute-start(bf16[64,4096]{1,0:T(8,128)(2,1)S(1)} %collective-permute-done.14.refs_0_), channel_id=1, source_target_pairs={{0,1},{1,0},{2,3},{3,2},{4,5},{5,4},{6,7},{7,6},{8,9},{9,8},{10,11... | collective-permute-start | bytes 1572872 | tf_op jit(solution)/shard_map/ppermute | solution.py:29
  58.0 19.1 %collective-permute-start.23 = (bf16[640,512]{1,0:T(8,128)(2,1)S(1)}, bf16[640,512]{1,0:T(8,128)(2,1)S(1)}, u32[]{:S(2)}, u32[]{:S(2)}) collective-permute-start(bf16[640,512]{1,0:T(8,128)(2,1)S(1)} %pad_maximum_fusion), channel_id=1, source_target_pairs={{0,16},{1,17},{2,18},{3,19},{4,20},{5,21},{6,22},{7,23},{8,24},{9,... | collective-permute-start | bytes 1966088 | tf_op jit(solution)/shard_map/ppermute | solution.py:509
  91.3 11.7 %collective-permute-start.30 = (bf16[128,4096]{1,0:T(8,128)(2,1)S(1)}, bf16[128,4096]{1,0:T(8,128)(2,1)S(1)}, u32[]{:S(2)}, u32[]{:S(2)}) collective-permute-start(bf16[128,4096]{1,0:T(8,128)(2,1)S(1)} %get-tuple-element.180), channel_id=1, source_target_pairs={{0,1},{1,0},{2,3},{3,2},{4,5},{5,4},{6,7},{7,6},{8,9},{9,8},{10,11... | collective-permute-start | bytes 3145736 | tf_op jit(solution)/shard_map/ppermute | solution.py:29
  95.9 11.7 %collective-permute-start.33 = (bf16[128,4096]{1,0:T(8,128)(2,1)S(1)}, bf16[128,4096]{1,0:T(8,128)(2,1)S(1)}, u32[]{:S(2)}, u32[]{:S(2)}) collective-permute-start(bf16[128,4096]{1,0:T(8,128)(2,1)S(1)} %get-tuple-element.189), channel_id=1, source_target_pairs={{0,1},{1,0},{2,3},{3,2},{4,5},{5,4},{6,7},{7,6},{8,9},{9,8},{10,11... | collective-permute-start | bytes 3145736 | tf_op jit(solution)/shard_map/ppermute | solution.py:29
  105.1 14.9 %collective-permute-start.35 = (bf16[128,4096]{1,0:T(8,128)(2,1)S(1)}, bf16[128,4096]{1,0:T(8,128)(2,1)S(1)}, u32[]{:S(2)}, u32[]{:S(2)}) collective-permute-start(bf16[128,4096]{1,0:T(8,128)(2,1)S(1)} %get-tuple-element.192), channel_id=1, source_target_pairs={{0,1},{1,0},{2,3},{3,2},{4,5},{5,4},{6,7},{7,6},{8,9},{9,8},{10,11... | collective-permute-start | bytes 3145736 | tf_op jit(solution)/shard_map/ppermute | solution.py:29
  106.4 12.7 %collective-permute-start.37 = (bf16[64,4096]{1,0:T(8,128)(2,1)S(1)}, bf16[64,4096]{1,0:T(8,128)(2,1)S(1)}, u32[]{:S(2)}, u32[]{:S(2)}) collective-permute-start(bf16[64,4096]{1,0:T(8,128)(2,1)S(1)} %convert_element_type.79), channel_id=1, source_target_pairs={{0,4},{4,8},{8,12},{12,14},{14,10},{10,6},{6,2},{2,0},{1,3},{5,1},... | collective-permute-start | bytes 1572872 | tf_op jit(solution)/shard_map/ppermute | solution.py:33
  113.6 11.1 %collective-permute-start.32 = (bf16[64,4096]{1,0:T(8,128)(2,1)S(1)}, bf16[64,4096]{1,0:T(8,128)(2,1)S(1)}, u32[]{:S(2)}, u32[]{:S(2)}) collective-permute-start(bf16[64,4096]{1,0:T(8,128)(2,1)S(1)} %add_convert_fusion.6), channel_id=1, source_target_pairs={{0,4},{4,8},{8,12},{12,14},{14,10},{10,6},{6,2},{2,0},{1,3},{5,1},... | collective-permute-start | bytes 1572872 | tf_op jit(solution)/shard_map/ppermute | solution.py:33
  119.2 11.1 %collective-permute-start.38 = (bf16[64,4096]{1,0:T(8,128)(2,1)S(1)}, bf16[64,4096]{1,0:T(8,128)(2,1)S(1)}, u32[]{:S(2)}, u32[]{:S(2)}) collective-permute-start(bf16[64,4096]{1,0:T(8,128)(2,1)S(1)} %add_convert_fusion.3), channel_id=1, source_target_pairs={{0,4},{4,8},{8,12},{12,14},{14,10},{10,6},{6,2},{2,0},{1,3},{5,1},... | collective-permute-start | bytes 1572872 | tf_op jit(solution)/shard_map/ppermute | solution.py:33
  124.9 11.1 %collective-permute-start.34 = (bf16[64,4096]{1,0:T(8,128)(2,1)S(1)}, bf16[64,4096]{1,0:T(8,128)(2,1)S(1)}, u32[]{:S(2)}, u32[]{:S(2)}) collective-permute-start(bf16[64,4096]{1,0:T(8,128)(2,1)S(1)} %add_convert_fusion.5), channel_id=1, source_target_pairs={{0,4},{4,8},{8,12},{12,14},{14,10},{10,6},{6,2},{2,0},{1,3},{5,1},... | collective-permute-start | bytes 1572872 | tf_op jit(solution)/shard_map/ppermute | solution.py:33
  130.4 11.1 %collective-permute-start.39 = (bf16[64,4096]{1,0:T(8,128)(2,1)S(1)}, bf16[64,4096]{1,0:T(8,128)(2,1)S(1)}, u32[]{:S(2)}, u32[]{:S(2)}) collective-permute-start(bf16[64,4096]{1,0:T(8,128)(2,1)S(1)} %add_convert_fusion.2), channel_id=1, source_target_pairs={{0,4},{4,8},{8,12},{12,14},{14,10},{10,6},{6,2},{2,0},{1,3},{5,1},... | collective-permute-start | bytes 1572872 | tf_op jit(solution)/shard_map/ppermute | solution.py:33
  136.1 11.1 %collective-permute-start.36 = (bf16[64,4096]{1,0:T(8,128)(2,1)S(1)}, bf16[64,4096]{1,0:T(8,128)(2,1)S(1)}, u32[]{:S(2)}, u32[]{:S(2)}) collective-permute-start(bf16[64,4096]{1,0:T(8,128)(2,1)S(1)} %add_convert_fusion.4), channel_id=1, source_target_pairs={{0,4},{4,8},{8,12},{12,14},{14,10},{10,6},{6,2},{2,0},{1,3},{5,1},... | collective-permute-start | bytes 1572872 | tf_op jit(solution)/shard_map/ppermute | solution.py:33
  (32 other events, 222.7 us)

commit v10 on v9

--- a/solution.py
+++ b/solution.py
@@ -209,9 +209,9 @@
 
 def block_rows_of(refs, block):
     if block == 0:
-        return jnp.concatenate([refs[0][...], refs[4][128:]], axis=0)
+        return jnp.concatenate([refs[0][...], refs[5][...]], axis=0)
     if block == 3:
-        return jnp.concatenate([refs[3][...], refs[4][:128]], axis=0)
+        return jnp.concatenate([refs[3][...], refs[4][...]], axis=0)
     return refs[block][...]
 
 
@@ -220,9 +220,9 @@
 
 
 def inner_kernel(info, *refs):
-    base_refs, up_refs, (rank_ref, meta_ref, turn_ref, first_ref, last_ref) = refs[:5], refs[5:10], refs[10:15]
-    qkv_right_ref, up_right_ref, bias_ref, left_ref = refs[15:19]
-    q_ref, k_ref, v_ref, hidden_ref, out_ref = refs[19:]
+    base_refs, up_refs, (rank_ref, meta_ref, turn_ref, first_ref, last_ref) = refs[:6], refs[6:12], refs[12:17]
+    qkv_right_ref, up_right_ref, bias_ref, left_ref = refs[17:21]
+    q_ref, k_ref, v_ref, hidden_ref, out_ref = refs[21:]
     rows = 1024
     columns = qkv_right_ref.shape[0]
     for block in range(BLOCKS // 4):
@@ -246,7 +246,7 @@
 
 
 def far_kernel(first_row, info, *refs):
-    shared_refs, (rank_ref, meta_ref, turn_ref, spread_ref, right_ref, k_ref, v_ref) = refs[:5], refs[5:]
+    shared_refs, (rank_ref, meta_ref, turn_ref, spread_ref, right_ref, k_ref, v_ref) = refs[:6], refs[6:]
     rows = 1024
     for block in range(BLOCKS // 4):
         at = slice(block * rows, (block + 1) * rows)
@@ -563,14 +563,16 @@
     third = products_of(held_rows, 2000000000)
     ranks = add_ranks(held_rows, (6,), ranks)
     ring_a, ranks, third, far_early = tie((ring_a, ranks, third, far_early))
-    part = part[2:] + (ring_a, to_partner(ring_a))
-    ranks = add_ranks(part, (7, 1), ranks)
+    fourth = products_of(part[2:])
+    swapped, fourth = tie((to_partner(ring_a), fourth))
+    opposite = (ring_a, swapped)
+    ranks = add_ranks(part[2:] + opposite, (7, 1), ranks)
     moved = lax.ppermute(ranks, "mlp", [(i, i ^ 2) for i in range(16)])
-    fourth = products_of(part)
-    ranks, fourth = tie((ranks + moved, fourth))
-    far_late = to_groups(jnp.concatenate([second[2], third[2], fourth[2]], axis=0))
+    fifth = products_of(opposite)
+    ranks, fifth = tie((ranks + moved, fifth))
+    far_late = to_groups(jnp.concatenate([second[2], third[2], fourth[2], fifth[2]], axis=0))
     rank_in = sum_over_mlp(ranks, (4, 8))
-    products = (zeroth, first, second, third, fourth)
+    products = (zeroth, first, second, third, fourth, fifth)
 
     bias_row = input_bias.reshape(1, -1)
     far_rank = to_groups(rank_in)
@@ -586,8 +588,8 @@
     keys, values = [own_keys], [own_values]
     for d in range(1, req_count):
         early, late = far_early[d - 1], far_late[d - 1]
-        ends = (0, block_rows, block_rows + pair_rows, 2 * block_rows + pair_rows)
-        shared = [far_own[d - 1], early] + [late[ends[k] : ends[k + 1]] for k in range(3)]
+        ends = (0, block_rows, block_rows + pair_rows, 2 * block_rows, 2 * block_rows + pair_rows)
+        shared = [far_own[d - 1], early] + [late[ends[k] : ends[k + 1]] for k in range(4)]
         far_keys, far_values = call(
             functools.partial(far_kernel, d * group_rows),
             shared + [far_rank[d - 1], meta, turns, spread_first, qkv_right],

time: 149 us -> 148 us (level)
    ppermute x16, waiting for transfers between devices: 1.94 us -> 0.38 us  [to_partner(): return lax.ppermute(value, 'mlp', CORE_PERM)]
    pallas_call x23 -> x24, Pallas kernels: 50.8 us -> 51.1 us  [call(): pl.pallas_call(kernel, in_specs=specs, out_specs=[vmem] * len(outs), out_...]
  transfers between devices with their start and end apart: 41 -> 41, of which waited for: 16 -> 17; matrix products, arithmetic and copies ran while one was open for 3% -> 3% of each run, Pallas kernels for 27% -> 27%
where the time goes in v10:
time: 148 us
  Pallas kernels  51.1 us (35%)
  waiting for transfers between devices  47.8 us (32%)
  starting transfers between devices  41.7 us (28%)
  local copies, waits for them, and re-layouts  3.6 us (2%)
  other arithmetic  3.18 us (2%)
    pallas_call x24, Pallas kernels, call(): pl.pallas_call(kernel, in_specs=specs, out_specs=[vmem] * len(outs), out_...  51.1 us
    ppermute x14, waiting for transfers between devices, along_ring(): return lax.ppermute(value, 'mlp', RING_PERM)  36.3 us
    ppermute x14, starting transfers between devices, along_ring(): return lax.ppermute(value, 'mlp', RING_PERM)  19 us
    ppermute x4, starting transfers between devices, to_group(): lax.ppermute(value, 'req', [(g, g + d) for g in range(req_count - d)])  8.21 us
    ppermute x4, starting transfers between devices, per_device(): moved = lax.ppermute(rank_out, 'mlp', [(i, i ^ bit) for i in range(16)])  6.26 us
    ppermute x2, waiting for transfers between devices, sum_over_mlp(): lax.ppermute(value, 'mlp', [(i, i ^ bit) for i in range(16)])  5.43 us
    ppermute x4, waiting for transfers between devices, per_device(): moved = lax.ppermute(rank_out, 'mlp', [(i, i ^ bit) for i in range(16)])  4.33 us
    ppermute x2, starting transfers between devices, sum_over_mlp(): lax.ppermute(value, 'mlp', [(i, i ^ bit) for i in range(16)])  4.13 us
  transfers between devices with their start and end apart: 41, of which 17 were waited for; matrix products, arithmetic and copies ran while one was open for 3% of the time, Pallas kernels for 27%

profile of v10, /device:TPU:0, one launch (start us, length us, event | category | flops | bytes accessed | tf_op | source)
XLA Modules:
  0.0 148.1 jit_solution(9704591216221917295)
XLA Ops:
  2.1 3.0 %collective-permute-start = (bf16[64,4096]{1,0:T(8,128)(2,1)S(1)}, bf16[64,4096]{1,0:T(8,128)(2,1)S(1)}, u32[]{:S(2)}, u32[]{:S(2)}) collective-permute-start(bf16[64,4096]{1,0:T(8,128)(2,1)S(1)} %shard_map.217.refs_0_), channel_id=1, source_target_pairs={{0,4},{4,8},{8,12},{12,14},{14,10},{10,6},{6,2},{2,0},{1,3},{5,1},... | collective-permute-start | bytes 1572872 | tf_op jit(solution)/shard_map/ppermute | solution.py:33
  10.2 4.6 %shard_map.218 = (f32[2048,128]{1,0:T(8,128)S(1)}, f32[2048,128]{1,0:T(8,128)S(1)}, bf16[4096,768]{1,0:T(8,128)(2,1)S(1)}, bf16[4096,512]{1,0:T(8,128)(2,1)S(1)}) custom-call(s32[34]{0:T(128)S(1)} %dynamic-slice_bitcast_fusion.info, f32[65,1]{1,0:T(8,128)S(1)} %copy.24.column_ref, f32[1,65]{1,0:T(1,128)S(1)} %get-tuple-element.216.row_ref, ...), custom_call_target="tpu_custom_call" | custom-call | flops 1000 | bytes 1000 | tf_op jit(solution)/shard_map/pallas_call | solution.py:393
  19.9 2.1 %collective-permute-start.5 = (bf16[64,4096]{1,0:T(8,128)(2,1)S(1)}, bf16[64,4096]{1,0:T(8,128)(2,1)S(1)}, u32[]{:S(2)}, u32[]{:S(2)}) collective-permute-start(bf16[64,4096]{1,0:T(8,128)(2,1)S(1)} %collective-permute-done.3.refs_3_.refs_1_), channel_id=1, source_target_pairs={{0,4},{4,8},{8,12},{12,14},{14,10},{10,6},{6,2},{2,0},{1,3},{5,1},... | collective-permute-start | bytes 1572872 | tf_op jit(solution)/shard_map/ppermute | solution.py:33
  22.2 1.8 %collective-permute-done.1.refs_0_ = bf16[64,4096]{1,0:T(8,128)(2,1)S(1)} collective-permute-done((bf16[64,4096]{1,0:T(8,128)(2,1)S(1)}, bf16[64,4096]{1,0:T(8,128)(2,1)S(1)}, u32[]{:S(2)}, u32[]{:S(2)}) %collective-permute-start.1) | collective-permute-done | bytes 524320 | tf_op jit(solution)/shard_map/ppermute | solution.py:33
  25.7 3.4 %collective-permute-start.9 = (bf16[128,512]{1,0:T(8,128)(2,1)S(1)}, bf16[128,512]{1,0:T(8,128)(2,1)S(1)}, u32[]{:S(2)}, u32[]{:S(2)}) collective-permute-start(bf16[128,512]{1,0:T(8,128)(2,1)S(1)} %get-tuple-element.127), channel_id=1, source_target_pairs={{0,16},{1,17},{2,18},{3,19},{4,20},{5,21},{6,22},{7,23},{8,24},{9,... | collective-permute-start | bytes 393224 | tf_op jit(solution)/shard_map/ppermute | solution.py:509
  30.5 2.9 %shard_map.221 = (f32[256,768]{1,0:T(8,128)S(1)}, f32[256,512]{1,0:T(8,128)S(1)}, bf16[256,512]{1,0:T(8,128)(2,1)S(1)}) custom-call(bf16[64,4096]{1,0:T(8,128)(2,1)S(1)} %collective-permute-done.refs_2_.refs_0_, bf16[64,4096]{1,0:T(8,128)(2,1)S(1)} %collective-permute-done.3.refs_3_.refs_1_, bf16[64,4096]{1,0:T(8,128)(2,1)S(1)} %collective-permute-done.6.refs_4_.refs_2_, ...), custom_call_target="tpu_custom_call" | custom-call | flops 1000 | bytes 1000 | tf_op jit(solution)/shard_map/pallas_call | solution.py:393
  38.5 2.0 %collective-permute-start.16 = (bf16[256,512]{1,0:T(8,128)(2,1)S(1)}, bf16[256,512]{1,0:T(8,128)(2,1)S(1)}, u32[]{:S(2)}, u32[]{:S(2)}) collective-permute-start(bf16[256,512]{1,0:T(8,128)(2,1)S(1)} %get-tuple-element.141), channel_id=1, source_target_pairs={{0,16},{1,17},{2,18},{3,19},{4,20},{5,21},{6,22},{7,23},{8,24},{9,... | collective-permute-start | bytes 786440 | tf_op jit(solution)/shard_map/ppermute | solution.py:509
  40.6 2.9 %shard_map.223 = (f32[256,768]{1,0:T(8,128)S(1)}, f32[256,512]{1,0:T(8,128)S(1)}, bf16[256,512]{1,0:T(8,128)(2,1)S(1)}) custom-call(bf16[64,4096]{1,0:T(8,128)(2,1)S(1)} %collective-permute-done.1.refs_0_, bf16[64,4096]{1,0:T(8,128)(2,1)S(1)} %collective-permute-done.5.refs_1_, bf16[64,4096]{1,0:T(8,128)(2,1)S(1)} %collective-permute-done.11.refs_2_, ...), custom_call_target="tpu_custom_call" | custom-call | flops 1000 | bytes 1000 | tf_op jit(solution)/shard_map/pallas_call | solution.py:393
  48.3 2.0 %collective-permute-done.15.refs_2_.refs_0_ = bf16[64,4096]{1,0:T(8,128)(2,1)S(1)} collective-permute-done((bf16[64,4096]{1,0:T(8,128)(2,1)S(1)}, bf16[64,4096]{1,0:T(8,128)(2,1)S(1)}, u32[]{:S(2)}, u32[]{:S(2)}) %collective-permute-start.15) | collective-permute-done | bytes 524320 | tf_op jit(solution)/shard_map/ppermute | solution.py:33
  61.0 2.8 %collective-permute-done.21 = bf16[32,1024]{1,0:T(8,128)(2,1)S(1)} collective-permute-done((bf16[32,1024]{1,0:T(8,128)(2,1)S(1)}, bf16[32,1024]{1,0:T(8,128)(2,1)S(1)}, u32[]{:S(2)}, u32[]{:S(2)}) %collective-permute-start.21) | collective-permute-done | bytes 65568 | tf_op jit(solution)/shard_map/ppermute | solution.py:410
  63.7 2.6 %collective-permute-start.22 = (bf16[32,1024]{1,0:T(8,128)(2,1)S(1)}, bf16[32,1024]{1,0:T(8,128)(2,1)S(1)}, u32[]{:S(2)}, u32[]{:S(2)}) collective-permute-start(bf16[32,1024]{1,0:T(8,128)(2,1)S(1)} %add.62), channel_id=1, source_target_pairs={{0,8},{1,9},{2,10},{3,11},{4,12},{5,13},{6,14},{7,15},{8,0},{9,1},... | collective-permute-start | bytes 196616 | tf_op jit(solution)/shard_map/ppermute | solution.py:410
  66.3 2.7 %collective-permute-done.22 = bf16[32,1024]{1,0:T(8,128)(2,1)S(1)} collective-permute-done((bf16[32,1024]{1,0:T(8,128)(2,1)S(1)}, bf16[32,1024]{1,0:T(8,128)(2,1)S(1)}, u32[]{:S(2)}, u32[]{:S(2)}) %collective-permute-start.22) | collective-permute-done | bytes 65568 | tf_op jit(solution)/shard_map/ppermute | solution.py:410
  70.6 6.2 %shard_map.229 = (bf16[1024,256]{1,0:T(8,128)(2,1)S(1)}, bf16[1024,256]{1,0:T(8,128)(2,1)S(1)}, bf16[1024,256]{1,0:T(8,128)(2,1)S(1)}, bf16[1024,512]{1,0:T(8,128)(2,1)S(1)}, bf16[32,1024]{1,0:T(8,128)(2,1)S(1)}) custom-call(s32[34]{0:T(128)S(1)} %dynamic-slice_bitcast_fusion.info, f32[128,768]{1,0:T(8,128)S(1)} %get-tuple-element.119.refs_0_, ...), custom_call_target="tpu_custom_call" | custom-call | flops 1000 | bytes 1000 | tf_op jit(solution)/shard_map/pallas_call | solution.py:393
  76.8 2.3 %shard_map.230 = (bf16[1024,256]{1,0:T(8,128)(2,1)S(1)}, bf16[1024,256]{1,0:T(8,128)(2,1)S(1)}) custom-call(s32[34]{0:T(128)S(1)} %dynamic-slice_bitcast_fusion.info, bf16[128,512]{1,0:T(8,128)(2,1)S(1)} %collective-permute-done.9.refs_0_, bf16[256,512]{1,0:T(8,128)(2,1)S(1)} %collective-permute-done.16.refs_1_, bf16[256,512]{1,0:T(8,128)(2,1)S(1)} %slice.20.refs_2_, ...), custom_call_target="tpu_custom_call" | custom-call | flops 1000 | bytes 1000 | tf_op jit(solution)/shard_map/pallas_call | solution.py:393
  79.1 5.2 %shard_map.231 = (bf16[1024,256]{1,0:T(8,128)(2,1)S(1)}, bf16[32,1024]{1,0:T(8,128)(2,1)S(1)}) custom-call(s32[34]{0:T(128)S(1)} %dynamic-slice_bitcast_fusion.info, bf16[1024,256]{1,0:T(8,128)(2,1)S(1)} %get-tuple-element.162.refs_0_, bf16[1024,256]{1,0:T(8,128)(2,1)S(1)} %get-tuple-element.163.refs_1_, bf16[1024,256]{1,0:T(8,128)(2,1)S(1)} %get-tuple-element.170.refs_2_, ...), custom_call_target="tpu_custom_call" | custom-call | flops 1000 | bytes 1000 | tf_op jit(solution)/shard_map/pallas_call | solution.py:393
  95.7 3.0 %collective-permute-start.29 = (bf16[32,1024]{1,0:T(8,128)(2,1)S(1)}, bf16[32,1024]{1,0:T(8,128)(2,1)S(1)}, u32[]{:S(2)}, u32[]{:S(2)}) collective-permute-start(bf16[32,1024]{1,0:T(8,128)(2,1)S(1)} %add.66), channel_id=1, source_target_pairs={{0,8},{1,9},{2,10},{3,11},{4,12},{5,13},{6,14},{7,15},{8,0},{9,1},... | collective-permute-start | bytes 196616 | tf_op jit(solution)/shard_map/ppermute | solution.py:631
  100.5 2.3 %collective-permute-done.29 = bf16[32,1024]{1,0:T(8,128)(2,1)S(1)} collective-permute-done((bf16[32,1024]{1,0:T(8,128)(2,1)S(1)}, bf16[32,1024]{1,0:T(8,128)(2,1)S(1)}, u32[]{:S(2)}, u32[]{:S(2)}) %collective-permute-start.29) | collective-permute-done | bytes 65568 | tf_op jit(solution)/shard_map/ppermute | solution.py:631
  108.7 4.6 %collective-permute-done.31 = bf16[64,4096]{1,0:T(8,128)(2,1)S(1)} collective-permute-done((bf16[64,4096]{1,0:T(8,128)(2,1)S(1)}, bf16[64,4096]{1,0:T(8,128)(2,1)S(1)}, u32[]{:S(2)}, u32[]{:S(2)}) %collective-permute-start.31) | collective-permute-done | bytes 524320 | tf_op jit(solution)/shard_map/ppermute | solution.py:33
  114.3 4.7 %collective-permute-done.37 = bf16[64,4096]{1,0:T(8,128)(2,1)S(1)} collective-permute-done((bf16[64,4096]{1,0:T(8,128)(2,1)S(1)}, bf16[64,4096]{1,0:T(8,128)(2,1)S(1)}, u32[]{:S(2)}, u32[]{:S(2)}) %collective-permute-start.37) | collective-permute-done | bytes 524320 | tf_op jit(solution)/shard_map/ppermute | solution.py:33
  121.1 3.5 %collective-permute-done.32 = bf16[64,4096]{1,0:T(8,128)(2,1)S(1)} collective-permute-done((bf16[64,4096]{1,0:T(8,128)(2,1)S(1)}, bf16[64,4096]{1,0:T(8,128)(2,1)S(1)}, u32[]{:S(2)}, u32[]{:S(2)}) %collective-permute-start.32) | collective-permute-done | bytes 524320 | tf_op jit(solution)/shard_map/ppermute | solution.py:33
  125.5 4.7 %collective-permute-done.38 = bf16[64,4096]{1,0:T(8,128)(2,1)S(1)} collective-permute-done((bf16[64,4096]{1,0:T(8,128)(2,1)S(1)}, bf16[64,4096]{1,0:T(8,128)(2,1)S(1)}, u32[]{:S(2)}, u32[]{:S(2)}) %collective-permute-start.38) | collective-permute-done | bytes 524320 | tf_op jit(solution)/shard_map/ppermute | solution.py:33
  131.1 4.7 %collective-permute-done.34 = bf16[64,4096]{1,0:T(8,128)(2,1)S(1)} collective-permute-done((bf16[64,4096]{1,0:T(8,128)(2,1)S(1)}, bf16[64,4096]{1,0:T(8,128)(2,1)S(1)}, u32[]{:S(2)}, u32[]{:S(2)}) %collective-permute-start.34) | collective-permute-done | bytes 524320 | tf_op jit(solution)/shard_map/ppermute | solution.py:33
  136.7 4.7 %collective-permute-done.39 = bf16[64,4096]{1,0:T(8,128)(2,1)S(1)} collective-permute-done((bf16[64,4096]{1,0:T(8,128)(2,1)S(1)}, bf16[64,4096]{1,0:T(8,128)(2,1)S(1)}, u32[]{:S(2)}, u32[]{:S(2)}) %collective-permute-start.39) | collective-permute-done | bytes 524320 | tf_op jit(solution)/shard_map/ppermute | solution.py:33
  142.9 4.2 %collective-permute-done.36 = bf16[64,4096]{1,0:T(8,128)(2,1)S(1)} collective-permute-done((bf16[64,4096]{1,0:T(8,128)(2,1)S(1)}, bf16[64,4096]{1,0:T(8,128)(2,1)S(1)}, u32[]{:S(2)}, u32[]{:S(2)}) %collective-permute-start.36) | collective-permute-done | bytes 524320 | tf_op jit(solution)/shard_map/ppermute | solution.py:33
  (143 shorter events, 64.8 us)
Async XLA Ops:
  2.1 15.8 %collective-permute-start.4 = (bf16[4096,128]{1,0:T(8,128)(2,1)}, bf16[4096,128]{1,0:T(8,128)(2,1)}, u32[]{:S(2)}, u32[]{:S(2)}) collective-permute-start(bf16[4096,128]{1,0:T(8,128)(2,1)} %param.32), channel_id=1, source_target_pairs={{0,1},{1,0},{2,3},{3,2},{4,5},{5,4},{6,7},{7,6},{8,9},{9,8},{10,11... | collective-permute-start | bytes 3145736 | tf_op jit(solution)/shard_map/ppermute | solution.py:29
  2.1 12.7 %collective-permute-start = (bf16[64,4096]{1,0:T(8,128)(2,1)S(1)}, bf16[64,4096]{1,0:T(8,128)(2,1)S(1)}, u32[]{:S(2)}, u32[]{:S(2)}) collective-permute-start(bf16[64,4096]{1,0:T(8,128)(2,1)S(1)} %shard_map.217.refs_0_), channel_id=1, source_target_pairs={{0,4},{4,8},{8,12},{12,14},{14,10},{10,6},{6,2},{2,0},{1,3},{5,1},... | collective-permute-start | bytes 1572872 | tf_op jit(solution)/shard_map/ppermute | solution.py:33
  5.1 12.7 %collective-permute-start.3 = (bf16[64,4096]{1,0:T(8,128)(2,1)S(1)}, bf16[64,4096]{1,0:T(8,128)(2,1)S(1)}, u32[]{:S(2)}, u32[]{:S(2)}) collective-permute-start(bf16[64,4096]{1,0:T(8,128)(2,1)S(1)} %collective-permute-done.2.refs_1_), channel_id=1, source_target_pairs={{0,4},{4,8},{8,12},{12,14},{14,10},{10,6},{6,2},{2,0},{1,3},{5,1},... | collective-permute-start | bytes 1572872 | tf_op jit(solution)/shard_map/ppermute | solution.py:33
  7.5 10.8 %collective-permute-start.8 = (f32[1,128]{1,0:T(1,128)S(1)}, f32[1,128]{1,0:T(1,128)S(1)}, u32[]{:S(2)}, u32[]{:S(2)}) collective-permute-start(f32[1,128]{1,0:T(1,128)S(1)} %convert_element_type.71), channel_id=1, source_target_pairs={{0,1},{1,0},{2,3},{3,2},{4,5},{5,4},{6,7},{7,6},{8,9},{9,8},{10,11... | collective-permute-start | bytes 1544 | tf_op jit(solution)/shard_map/ppermute | solution.py:29
  7.5 37.4 %collective-permute-start.13 = (bf16[128,4096]{1,0:T(8,128)(2,1)}, bf16[128,4096]{1,0:T(8,128)(2,1)S(1)}, u32[]{:S(2)}, u32[]{:S(2)}) collective-permute-start(bf16[128,4096]{1,0:T(8,128)(2,1)} %param.37), channel_id=1, source_target_pairs={{0,1},{1,0},{2,3},{3,2},{4,5},{5,4},{6,7},{7,6},{8,9},{9,8},{10,11... | collective-permute-start | bytes 3145736 | tf_op jit(solution)/shard_map/ppermute | solution.py:29
  14.8 9.2 %collective-permute-start.1 = (bf16[64,4096]{1,0:T(8,128)(2,1)S(1)}, bf16[64,4096]{1,0:T(8,128)(2,1)S(1)}, u32[]{:S(2)}, u32[]{:S(2)}) collective-permute-start(bf16[64,4096]{1,0:T(8,128)(2,1)S(1)} %collective-permute-done.refs_2_.refs_0_), channel_id=1, source_target_pairs={{0,4},{4,8},{8,12},{12,14},{14,10},{10,6},{6,2},{2,0},{1,3},{5,1},... | collective-permute-start | bytes 1572872 | tf_op jit(solution)/shard_map/ppermute | solution.py:33
  19.9 15.4 %collective-permute-start.5 = (bf16[64,4096]{1,0:T(8,128)(2,1)S(1)}, bf16[64,4096]{1,0:T(8,128)(2,1)S(1)}, u32[]{:S(2)}, u32[]{:S(2)}) collective-permute-start(bf16[64,4096]{1,0:T(8,128)(2,1)S(1)} %collective-permute-done.3.refs_3_.refs_1_), channel_id=1, source_target_pairs={{0,4},{4,8},{8,12},{12,14},{14,10},{10,6},{6,2},{2,0},{1,3},{5,1},... | collective-permute-start | bytes 1572872 | tf_op jit(solution)/shard_map/ppermute | solution.py:33
  24.1 14.4 %collective-permute-start.12 = (bf16[64,4096]{1,0:T(8,128)(2,1)S(1)}, bf16[64,4096]{1,0:T(8,128)(2,1)S(1)}, u32[]{:S(2)}, u32[]{:S(2)}) collective-permute-start(bf16[64,4096]{1,0:T(8,128)(2,1)S(1)} %collective-permute-done.1.refs_0_), channel_id=1, source_target_pairs={{0,1},{1,0},{2,3},{3,2},{4,5},{5,4},{6,7},{7,6},{8,9},{9,8},{10,11... | collective-permute-start | bytes 1572872 | tf_op jit(solution)/shard_map/ppermute | solution.py:29
  24.1 12.9 %collective-permute-start.14 = (bf16[64,4096]{1,0:T(8,128)(2,1)S(1)}, bf16[64,4096]{1,0:T(8,128)(2,1)S(1)}, u32[]{:S(2)}, u32[]{:S(2)}) collective-permute-start(bf16[64,4096]{1,0:T(8,128)(2,1)S(1)} %collective-permute-done.1.refs_0_), channel_id=1, source_target_pairs={{0,4},{4,8},{8,12},{12,14},{14,10},{10,6},{6,2},{2,0},{1,3},{5,1},... | collective-permute-start | bytes 1572872 | tf_op jit(solution)/shard_map/ppermute | solution.py:33
  25.7 9.6 %collective-permute-start.9 = (bf16[128,512]{1,0:T(8,128)(2,1)S(1)}, bf16[128,512]{1,0:T(8,128)(2,1)S(1)}, u32[]{:S(2)}, u32[]{:S(2)}) collective-permute-start(bf16[128,512]{1,0:T(8,128)(2,1)S(1)} %get-tuple-element.127), channel_id=1, source_target_pairs={{0,16},{1,17},{2,18},{3,19},{4,20},{5,21},{6,22},{7,23},{8,24},{9,... | collective-permute-start | bytes 393224 | tf_op jit(solution)/shard_map/ppermute | solution.py:509
  35.4 9.6 %collective-permute-start.10 = (bf16[64,4096]{1,0:T(8,128)(2,1)S(1)}, bf16[64,4096]{1,0:T(8,128)(2,1)S(1)}, u32[]{:S(2)}, u32[]{:S(2)}) collective-permute-start(bf16[64,4096]{1,0:T(8,128)(2,1)S(1)} %collective-permute-done.5.refs_1_), channel_id=1, source_target_pairs={{0,4},{4,8},{8,12},{12,14},{14,10},{10,6},{6,2},{2,0},{1,3},{5,1},... | collective-permute-start | bytes 1572872 | tf_op jit(solution)/shard_map/ppermute | solution.py:33
  37.0 13.3 %collective-permute-start.15 = (bf16[64,4096]{1,0:T(8,128)(2,1)S(1)}, bf16[64,4096]{1,0:T(8,128)(2,1)S(1)}, u32[]{:S(2)}, u32[]{:S(2)}) collective-permute-start(bf16[64,4096]{1,0:T(8,128)(2,1)S(1)} %collective-permute-done.14.refs_0_), channel_id=1, source_target_pairs={{0,4},{4,8},{8,12},{12,14},{14,10},{10,6},{6,2},{2,0},{1,3},{5,1},... | collective-permute-start | bytes 1572872 | tf_op jit(solution)/shard_map/ppermute | solution.py:33
  38.5 9.8 %collective-permute-start.16 = (bf16[256,512]{1,0:T(8,128)(2,1)S(1)}, bf16[256,512]{1,0:T(8,128)(2,1)S(1)}, u32[]{:S(2)}, u32[]{:S(2)}) collective-permute-start(bf16[256,512]{1,0:T(8,128)(2,1)S(1)} %get-tuple-element.141), channel_id=1, source_target_pairs={{0,16},{1,17},{2,18},{3,19},{4,20},{5,21},{6,22},{7,23},{8,24},{9,... | collective-permute-start | bytes 786440 | tf_op jit(solution)/shard_map/ppermute | solution.py:509
  40.5 9.8 %collective-permute-start.19 = (bf16[64,4096]{1,0:T(8,128)(2,1)S(1)}, bf16[64,4096]{1,0:T(8,128)(2,1)S(1)}, u32[]{:S(2)}, u32[]{:S(2)}) collective-permute-start(bf16[64,4096]{1,0:T(8,128)(2,1)S(1)} %collective-permute-done.14.refs_0_), channel_id=1, source_target_pairs={{0,1},{1,0},{2,3},{3,2},{4,5},{5,4},{6,7},{7,6},{8,9},{9,8},{10,11... | collective-permute-start | bytes 1572872 | tf_op jit(solution)/shard_map/ppermute | solution.py:29
  58.0 18.7 %collective-permute-start.23 = (bf16[640,512]{1,0:T(8,128)(2,1)S(1)}, bf16[640,512]{1,0:T(8,128)(2,1)S(1)}, u32[]{:S(2)}, u32[]{:S(2)}) collective-permute-start(bf16[640,512]{1,0:T(8,128)(2,1)S(1)} %pad_maximum_fusion), channel_id=1, source_target_pairs={{0,16},{1,17},{2,18},{3,19},{4,20},{5,21},{6,22},{7,23},{8,24},{9,... | collective-permute-start | bytes 1966088 | tf_op jit(solution)/shard_map/ppermute | solution.py:509
  90.9 11.9 %collective-permute-start.30 = (bf16[128,4096]{1,0:T(8,128)(2,1)S(1)}, bf16[128,4096]{1,0:T(8,128)(2,1)S(1)}, u32[]{:S(2)}, u32[]{:S(2)}) collective-permute-start(bf16[128,4096]{1,0:T(8,128)(2,1)S(1)} %get-tuple-element.194), channel_id=1, source_target_pairs={{0,1},{1,0},{2,3},{3,2},{4,5},{5,4},{6,7},{7,6},{8,9},{9,8},{10,11... | collective-permute-start | bytes 3145736 | tf_op jit(solution)/shard_map/ppermute | solution.py:29
  95.5 11.9 %collective-permute-start.33 = (bf16[128,4096]{1,0:T(8,128)(2,1)S(1)}, bf16[128,4096]{1,0:T(8,128)(2,1)S(1)}, u32[]{:S(2)}, u32[]{:S(2)}) collective-permute-start(bf16[128,4096]{1,0:T(8,128)(2,1)S(1)} %get-tuple-element.203), channel_id=1, source_target_pairs={{0,1},{1,0},{2,3},{3,2},{4,5},{5,4},{6,7},{7,6},{8,9},{9,8},{10,11... | collective-permute-start | bytes 3145736 | tf_op jit(solution)/shard_map/ppermute | solution.py:29
  104.9 14.9 %collective-permute-start.35 = (bf16[128,4096]{1,0:T(8,128)(2,1)S(1)}, bf16[128,4096]{1,0:T(8,128)(2,1)S(1)}, u32[]{:S(2)}, u32[]{:S(2)}) collective-permute-start(bf16[128,4096]{1,0:T(8,128)(2,1)S(1)} %get-tuple-element.206), channel_id=1, source_target_pairs={{0,1},{1,0},{2,3},{3,2},{4,5},{5,4},{6,7},{7,6},{8,9},{9,8},{10,11... | collective-permute-start | bytes 3145736 | tf_op jit(solution)/shard_map/ppermute | solution.py:29
  106.2 12.7 %collective-permute-start.37 = (bf16[64,4096]{1,0:T(8,128)(2,1)S(1)}, bf16[64,4096]{1,0:T(8,128)(2,1)S(1)}, u32[]{:S(2)}, u32[]{:S(2)}) collective-permute-start(bf16[64,4096]{1,0:T(8,128)(2,1)S(1)} %convert_element_type.79), channel_id=1, source_target_pairs={{0,4},{4,8},{8,12},{12,14},{14,10},{10,6},{6,2},{2,0},{1,3},{5,1},... | collective-permute-start | bytes 1572872 | tf_op jit(solution)/shard_map/ppermute | solution.py:33
  113.5 11.1 %collective-permute-start.32 = (bf16[64,4096]{1,0:T(8,128)(2,1)S(1)}, bf16[64,4096]{1,0:T(8,128)(2,1)S(1)}, u32[]{:S(2)}, u32[]{:S(2)}) collective-permute-start(bf16[64,4096]{1,0:T(8,128)(2,1)S(1)} %add_convert_fusion.6), channel_id=1, source_target_pairs={{0,4},{4,8},{8,12},{12,14},{14,10},{10,6},{6,2},{2,0},{1,3},{5,1},... | collective-permute-start | bytes 1572872 | tf_op jit(solution)/shard_map/ppermute | solution.py:33
  119.1 11.1 %collective-permute-start.38 = (bf16[64,4096]{1,0:T(8,128)(2,1)S(1)}, bf16[64,4096]{1,0:T(8,128)(2,1)S(1)}, u32[]{:S(2)}, u32[]{:S(2)}) collective-permute-start(bf16[64,4096]{1,0:T(8,128)(2,1)S(1)} %add_convert_fusion.3), channel_id=1, source_target_pairs={{0,4},{4,8},{8,12},{12,14},{14,10},{10,6},{6,2},{2,0},{1,3},{5,1},... | collective-permute-start | bytes 1572872 | tf_op jit(solution)/shard_map/ppermute | solution.py:33
  124.7 11.1 %collective-permute-start.34 = (bf16[64,4096]{1,0:T(8,128)(2,1)S(1)}, bf16[64,4096]{1,0:T(8,128)(2,1)S(1)}, u32[]{:S(2)}, u32[]{:S(2)}) collective-permute-start(bf16[64,4096]{1,0:T(8,128)(2,1)S(1)} %add_convert_fusion.5), channel_id=1, source_target_pairs={{0,4},{4,8},{8,12},{12,14},{14,10},{10,6},{6,2},{2,0},{1,3},{5,1},... | collective-permute-start | bytes 1572872 | tf_op jit(solution)/shard_map/ppermute | solution.py:33
  130.3 11.1 %collective-permute-start.39 = (bf16[64,4096]{1,0:T(8,128)(2,1)S(1)}, bf16[64,4096]{1,0:T(8,128)(2,1)S(1)}, u32[]{:S(2)}, u32[]{:S(2)}) collective-permute-start(bf16[64,4096]{1,0:T(8,128)(2,1)S(1)} %add_convert_fusion.2), channel_id=1, source_target_pairs={{0,4},{4,8},{8,12},{12,14},{14,10},{10,6},{6,2},{2,0},{1,3},{5,1},... | collective-permute-start | bytes 1572872 | tf_op jit(solution)/shard_map/ppermute | solution.py:33
  135.9 11.1 %collective-permute-start.36 = (bf16[64,4096]{1,0:T(8,128)(2,1)S(1)}, bf16[64,4096]{1,0:T(8,128)(2,1)S(1)}, u32[]{:S(2)}, u32[]{:S(2)}) collective-permute-start(bf16[64,4096]{1,0:T(8,128)(2,1)S(1)} %add_convert_fusion.4), channel_id=1, source_target_pairs={{0,4},{4,8},{8,12},{12,14},{14,10},{10,6},{6,2},{2,0},{1,3},{5,1},... | collective-permute-start | bytes 1572872 | tf_op jit(solution)/shard_map/ppermute | solution.py:33
  (32 other events, 222.0 us)
